TPU v7x, 128 devices: a whole 4x4x4 slice. The times are simulated.
128 devices in a mesh: section: 8 (over x, core), et: 16 (over y, z).
Axes of the slice: x: 4, y: 4, z: 4, core: 2. Of those that a mesh axis runs over, the one named last changes fastest.
Arguments:
- tokens_in: bfloat16 [512, 6144], P(('section', 'et')), may hold values from -6 to 6
- out_grad: bfloat16 [512, 6144], P('section', 'et'), may hold values from -6 to 6
- gate_weight: bfloat16 [2, 6144, 16384], P(None, None, ('section', 'et')), may hold values from -0.078125 to 0.078125
- up_weight: bfloat16 [2, 6144, 16384], P(None, None, ('section', 'et')), may hold values from -0.078125 to 0.078125
- down_weight: bfloat16 [2, 16384, 6144], P(None, ('section', 'et')), may hold values from -0.046875 to 0.046875
- slot_tokens: int32 [2, 256], replicated, may hold values from 0 to 511, as said below
- slot_counts: int32 [2], replicated, may hold values from 86 to 256, as said below
- slot_gates: float32 [2, 256], replicated, may hold values from 0.05 to 0.95
Outputs:
- input_grad: bfloat16 [512, 6144], P(('section', 'et'))
- gate_grad: bfloat16 [2, 6144, 16384], P(None, None, ('section', 'et'))
- up_grad: bfloat16 [2, 6144, 16384], P(None, None, ('section', 'et'))
- down_grad: bfloat16 [2, 16384, 6144], P(None, ('section', 'et'))
- router_grad: float32 [2, 256], replicated
Inputs may be any that keep to these rules, and one draw needn't show every extreme that they name: `slot_tokens`: each expert's slots hold distinct tokens in ascending order. `slot_counts`: in every draw some expert has all 256 slots live.
All inputs are finite; a program needn't handle non-finite values.
Results may differ from a plain program's by a relative error of at most 0.01.
Values may be sent and summed in bfloat16 or wider, within the bound.
No kernel may reach another device: no remote copies, remote signals or barrier semaphores. Data moves between devices by JAX's collectives and lax.ppermute only.
A program may use at most 192 MiB of HBM per device.

v0:
```python
import jax
import jax.numpy as jnp
from jax import lax
from jax.experimental import pallas as pl
from jax.experimental.pallas import tpu as pltpu
from jax.sharding import PartitionSpec as P

AXES = ("section", "et")
BF = jnp.bfloat16
F32 = jnp.float32
D = 6144
NX, NC, NY, NZ = 4, 2, 4, 4
H = 128
SHORT = 64
HALF = 256


def linear(x, c, y, z):
    return ((x * NC + c) * NY + y) * NZ + z


def shift_pairs(axis, step, by_core):
    pairs = []
    for x in range(NX):
        for c in range(NC):
            for y in range(NY):
                for z in range(NZ):
                    d = -step if (by_core and c == 1) else step
                    to = {
                        "x": ((x + d) % NX, c, y, z),
                        "y": (x, c, (y + d) % NY, z),
                        "z": (x, c, y, (z + d) % NZ),
                    }[axis]
                    pairs.append((linear(x, c, y, z), linear(*to)))
    return pairs


def shift(value, axis, step, by_core=False):
    return lax.ppermute(value, AXES, shift_pairs(axis, step, by_core))


def swap(value):
    pairs = [
        (linear(x, c, y, z), linear(x, 1 - c, y, z))
        for x in range(NX)
        for c in range(NC)
        for y in range(NY)
        for z in range(NZ)
    ]
    return lax.ppermute(value, AXES, pairs)


def position():
    section = lax.axis_index("section")
    et = lax.axis_index("et")
    return section // NC, section % NC, et // NZ, et % NZ


def nt(left, right):
    return lax.dot_general(left, right, (((1,), (1,)), ((), ())), preferred_element_type=F32)


def tn(left, right):
    return lax.dot_general(left, right, (((0,), (0,)), ((), ())), preferred_element_type=F32)


def total(first, rest):
    out = first.astype(F32)
    for r in rest:
        out = out + r.astype(F32)
    return out


KT = 1024
FT = 512
MIB = 2**20


def vmem_specs(n):
    return [pl.BlockSpec(memory_space=pltpu.VMEM)] * n


SMEM_SPEC = pl.BlockSpec(memory_space=pltpu.SMEM)


def first_stage_kernel(where, *refs):
    t, g, t_out, g_out, buf = refs[0:4], refs[4:8], refs[8], refs[9], refs[10]
    for k in range(NZ):
        buf[(where[2] - k) % NZ] = t[k][...].astype(F32)
    t_out[...] = jnp.concatenate([buf[k] for k in range(NZ)], axis=0).astype(BF)
    for k in range(NX):
        g_out[k * 64 : (k + 1) * 64, :] = g[k][...]


def run_first_stage(where, t, g):
    return pl.pallas_call(
        first_stage_kernel,
        out_shape=[jax.ShapeDtypeStruct((16, D), BF), jax.ShapeDtypeStruct((HALF, 384), BF)],
        in_specs=[SMEM_SPEC] + vmem_specs(8),
        out_specs=vmem_specs(2),
        scratch_shapes=[pltpu.VMEM((NZ, 4, D), F32)],
        compiler_params=pltpu.CompilerParams(vmem_limit_bytes=4 * MIB),
        name="first_stage",
    )(where, *t, *g)


def second_stage_kernel(where, *refs):
    t, g, t_out, g_out = refs[0:4], refs[4:8], refs[8], refs[9]
    for k in range(NY):
        start = pl.multiple_of(16 * ((where[1] - k) % NY), 16)
        t_out[pl.ds(start, 16), :] = t[k][...]
    for k in range(NZ):
        start = pl.multiple_of(384 * ((where[2] - k) % NZ), 128)
        g_out[:, pl.ds(start, 384)] = g[k][...]


def run_second_stage(where, t, g):
    return pl.pallas_call(
        second_stage_kernel,
        out_shape=[jax.ShapeDtypeStruct((64, D), BF), jax.ShapeDtypeStruct((HALF, 1536), BF)],
        in_specs=[SMEM_SPEC] + vmem_specs(8),
        out_specs=vmem_specs(2),
        compiler_params=pltpu.CompilerParams(vmem_limit_bytes=4 * MIB),
        name="second_stage",
    )(where, *t, *g)


def relay_kernel(*refs):
    value, (out, sem) = refs[0], refs[-2:]
    copy = pltpu.make_async_copy(value, out, sem)
    copy.start()
    copy.wait()


def run_relay(value, before):
    hbm = [pl.BlockSpec(memory_space=pltpu.HBM)]
    return pl.pallas_call(
        relay_kernel,
        out_shape=jax.ShapeDtypeStruct(value.shape, value.dtype),
        in_specs=hbm * (1 + len(before)),
        out_specs=hbm[0],
        scratch_shapes=[pltpu.SemaphoreType.DMA],
        compiler_params=pltpu.CompilerParams(vmem_limit_bytes=1 * MIB),
        cost_estimate=pl.CostEstimate(flops=0, bytes_accessed=6_000_000, transcendentals=0),
        name="relay",
    )(value, *before)


def row_copies(pieces, rows, sem):
    return [
        pltpu.make_async_copy(piece, rows.at[pl.ds(r * 64, 64), :], sem.at[r])
        for r, piece in enumerate(pieces)
    ]


def grad_copies(pieces, grads, sem, y, sign):
    copies = []
    for j, piece in enumerate(pieces):
        start = pl.multiple_of(((y - sign * j) % NY) * 1536, 128)
        copies.append(
            pltpu.make_async_copy(piece, grads.at[:, pl.ds(start, 1536)], sem.at[j])
        )
    return copies


def main_kernel(where, *refs):
    t_in, g_in = refs[0:4], refs[4:8]
    weights = (refs[8:11], refs[11:14])
    slots_ref, gates_ref = refs[14:16]
    pa_out, pb_out = refs[16:20], refs[20:24]
    own_out, sib_out, rp_ref, rows_out, grads_out = refs[24:29]
    rows, grads, wv, dv, pa, pb = refs[29:35]
    acc_g, acc_b, deltas, tile, rbuf, packed = refs[35:41]
    sem_t, sem_g, sem_w, sem_d, sem_o = refs[41:46]
    x, y, sign, core = where[0], where[1], where[3], where[4]
    copies_t = row_copies(t_in, rows, sem_t)
    copies_g = grad_copies(g_in, grads, sem_g, y, sign)
    tiles = D // KT

    def wide_copies(i):
        k = pl.ds(pl.multiple_of(i * KT, KT), KT)
        return [
            pltpu.make_async_copy(
                weights[s][n].at[:, k, :], wv.at[s, n, :, k, :], sem_w.at[i, s * 2 + n]
            )
            for s in range(2)
            for n in range(2)
        ]

    def tall_copies(i):
        k = pl.ds(pl.multiple_of(i * KT, KT), KT)
        return [
            pltpu.make_async_copy(weights[s][2].at[:, :, k], dv.at[s, :, :, k], sem_d.at[i, s])
            for s in range(2)
        ]

    for copy in copies_t:
        copy.start()
    for i in range(tiles):
        for copy in wide_copies(i):
            copy.start()
    for copy in copies_g:
        copy.start()
    for i in range(tiles):
        for copy in tall_copies(i):
            copy.start()
    acc_g[...] = jnp.zeros(acc_g.shape, F32)
    acc_b[...] = jnp.zeros(acc_b.shape, F32)
    scales = []
    slot = lax.broadcasted_iota(jnp.int32, (HALF, 256), 1)
    row = lax.broadcasted_iota(jnp.int32, (HALF, 256), 0)
    block = row // 64
    token = ((x - sign * block + NX) % NX) * 128 + core * 64 + (row - block * 64)
    for e in range(2):
        hit = (token == slots_ref[e : e + 1, :]) & (slot < where[5 + e])
        gate = jnp.broadcast_to(gates_ref[e : e + 1, :], (HALF, 256))
        scales.append(jnp.sum(jnp.where(hit, gate, 0.0), axis=1, keepdims=True))
    for copy in copies_t:
        copy.wait()
    rows_copy = pltpu.make_async_copy(rows, rows_out, sem_o.at[0])
    grads_copy = pltpu.make_async_copy(grads, grads_out, sem_o.at[1])

    @pl.loop(0, tiles)
    def _(i):
        for copy in wide_copies(i):
            copy.wait()
        k = pl.ds(pl.multiple_of(i * KT, KT), KT)
        wide = jnp.concatenate(
            [wv[s, n, e, k, :] for s in range(2) for e in range(2) for n in range(2)], axis=1
        )
        acc_g[...] += jnp.dot(rows[:, k], wide, preferred_element_type=F32)

    for copy in copies_g:
        copy.wait()

    @pl.loop(0, tiles)
    def _(i):
        for copy in tall_copies(i):
            copy.wait()
        k = pl.ds(pl.multiple_of(i * KT, KT), KT)
        tall = jnp.concatenate([dv[s, e, :, k] for s in range(2) for e in range(2)], axis=0)
        acc_b[...] += nt(grads[:, k], tall)

    rows_copy.start()
    grads_copy.start()
    router = [0.0, 0.0]
    for s in range(2):
        for e in range(2):
            j = s * 2 + e
            pre_gate = acc_g[:, j * 256 : j * 256 + H]
            pre_up = acc_g[:, j * 256 + H : (j + 1) * 256]
            back = acc_b[:, j * H : (j + 1) * H]
            scale = scales[e]
            sigma = jax.nn.sigmoid(pre_gate)
            active = pre_gate * sigma
            hidden = active * pre_up
            router[e] += jnp.sum(hidden.astype(BF).astype(F32) * back, axis=1, keepdims=True)
            hidden_grad = back * scale
            gate_delta = (hidden_grad * pre_up * sigma * (1.0 + pre_gate * (1.0 - sigma))).astype(BF)
            up_delta = (hidden_grad * active).astype(BF)
            deltas[:, j * 256 : j * 256 + H] = gate_delta
            deltas[:, j * 256 + H : (j + 1) * 256] = up_delta
            packed[s, :, e * 256 : e * 256 + H] = gate_delta
            packed[s, :, e * 256 + H : (e + 1) * 256] = up_delta
            packed[s, :, 512 + e * H : 512 + (e + 1) * H] = (hidden * scale).astype(BF)
    own_copy = pltpu.make_async_copy(packed.at[0], own_out, sem_o.at[2])
    sib_copy = pltpu.make_async_copy(packed.at[1], sib_out, sem_o.at[3])
    own_copy.start()
    sib_copy.start()
    lane = lax.broadcasted_iota(jnp.int32, (HALF, 128), 1)
    spread = jnp.where(lane == 0, router[0], jnp.where(lane == 1, router[1], 0.0))
    for k in range(NX):
        to = pl.multiple_of(((x - sign * k) % NX) * 64, 64)
        rbuf[pl.ds(to, 64), :] = spread[k * 64 : (k + 1) * 64]
    rp_ref[...] = rbuf[...].T[0:8]

    def partial(i):
        f = pl.ds(pl.multiple_of(i * FT, FT), FT)
        wide = jnp.concatenate(
            [wv[s, n, e, f, :] for s in range(2) for e in range(2) for n in range(2)], axis=1
        )
        return nt(deltas[...], wide)

    half = D // 2 // FT

    @pl.loop(0, half)
    def _(i):
        f = pl.ds(pl.multiple_of(i * FT, FT), FT)
        part = partial(i).astype(BF)
        for k in range(NX):
            pa[k, :, f] = part[k * 64 : (k + 1) * 64, :]

    copies = [pltpu.make_async_copy(pa.at[k], pa_out[k], sem_o.at[4 + k]) for k in range(NX)]
    for copy in copies:
        copy.start()

    @pl.loop(0, half)
    def _(i):
        f = pl.ds(pl.multiple_of(i * FT, FT), FT)
        tile[...] = partial(i + half).astype(BF)
        for k in range(NY):
            for b in range(NX):
                src = pl.multiple_of(b * 64 + ((y + k) % NY) * 16, 16)
                pb[k, b, :, f] = tile[pl.ds(src, 16), :]

    more = [pltpu.make_async_copy(pb.at[k], pb_out[k], sem_o.at[8 + k]) for k in range(NY)]
    for copy in more:
        copy.start()
    for copy in [rows_copy, grads_copy, own_copy, sib_copy] + copies + more:
        copy.wait()


def run_main(where, t, g, weights, slots, gates):
    hbm = [pl.BlockSpec(memory_space=pltpu.HBM)]
    out_shape = (
        [jax.ShapeDtypeStruct((64, D // 2), BF)] * 4
        + [jax.ShapeDtypeStruct((4, 16, D // 2), BF)] * 4
        + [jax.ShapeDtypeStruct((HALF, 768), BF)] * 2
        + [jax.ShapeDtypeStruct((8, 256), F32)]
        + [jax.ShapeDtypeStruct((HALF, D), BF)] * 2
    )
    return pl.pallas_call(
        main_kernel,
        out_shape=out_shape,
        in_specs=[SMEM_SPEC] + hbm * 14 + vmem_specs(2),
        out_specs=hbm * 10 + vmem_specs(1) + hbm * 2,
        scratch_shapes=[
            pltpu.VMEM((HALF, D), BF),
            pltpu.VMEM((HALF, D), BF),
            pltpu.VMEM((2, 2, 2, D, H), BF),
            pltpu.VMEM((2, 2, H, D), BF),
            pltpu.VMEM((4, 64, D // 2), BF),
            pltpu.VMEM((4, 4, 16, D // 2), BF),
            pltpu.VMEM((HALF, 1024), F32),
            pltpu.VMEM((HALF, 512), F32),
            pltpu.VMEM((HALF, 1024), BF),
            pltpu.VMEM((HALF, FT), BF),
            pltpu.VMEM((HALF, 128), F32),
            pltpu.VMEM((2, HALF, 768), BF),
            pltpu.SemaphoreType.DMA((4,)),
            pltpu.SemaphoreType.DMA((4,)),
            pltpu.SemaphoreType.DMA((D // KT, 4)),
            pltpu.SemaphoreType.DMA((D // KT, 2)),
            pltpu.SemaphoreType.DMA((12,)),
        ],
        compiler_params=pltpu.CompilerParams(vmem_limit_bytes=44 * MIB),
        cost_estimate=pl.CostEstimate(
            flops=8_000_000_000, bytes_accessed=30_000_000, transcendentals=262144
        ),
        name="main",
    )(where, *t, *g, *weights, slots, gates)


def up_kernel(*refs):
    rows_own, rows_sib, own, sib = refs[0:4]
    gate_out, up_out, token = refs[-3:]
    token[...] = jnp.zeros(token.shape, F32)
    part = tn(rows_own[...], own[:, 0:512]) + tn(rows_sib[...], sib[:, 0:512])
    for e in range(2):
        gate_out[e] = part[:, e * 256 : e * 256 + H].astype(BF)
        up_out[e] = part[:, e * 256 + H : (e + 1) * 256].astype(BF)


def run_up(rows_own, rows_sib, own, sib, before):
    tile = pl.BlockSpec((HALF, FT), lambda i: (0, i))
    whole = pl.BlockSpec((HALF, 768), lambda i: (0, 0))
    out = pl.BlockSpec((2, FT, H), lambda i: (0, i, 0))
    return pl.pallas_call(
        up_kernel,
        grid=(D // FT,),
        out_shape=[
            jax.ShapeDtypeStruct((2, D, H), BF),
            jax.ShapeDtypeStruct((2, D, H), BF),
            jax.ShapeDtypeStruct((8, 128), F32),
        ],
        in_specs=[tile, tile, whole, whole]
        + [pl.BlockSpec(memory_space=pl.ANY)] * len(before),
        out_specs=[out, out, pl.BlockSpec((8, 128), lambda i: (0, 0))],
        compiler_params=pltpu.CompilerParams(
            dimension_semantics=("arbitrary",), vmem_limit_bytes=16 * MIB
        ),
        cost_estimate=pl.CostEstimate(
            flops=3_200_000_000, bytes_accessed=13_000_000, transcendentals=0
        ),
        name="up_grads",
    )(rows_own, rows_sib, own, sib, *before)


def down_kernel(grads_own, grads_sib, own, sib, out, token, hidden):
    token[...] = jnp.zeros(token.shape, F32)

    @pl.when(pl.program_id(0) == 0)
    def _():
        hidden[:, 0:HALF] = own[:, 512:768].T
        hidden[:, HALF:512] = sib[:, 512:768].T

    part = jnp.dot(hidden[:, 0:HALF], grads_own[...], preferred_element_type=F32)
    part += jnp.dot(hidden[:, HALF:512], grads_sib[...], preferred_element_type=F32)
    for e in range(2):
        out[e] = part[e * H : (e + 1) * H].astype(BF)


def run_down(grads_own, grads_sib, own, sib):
    tile = pl.BlockSpec((HALF, 2 * FT), lambda i: (0, i))
    whole = pl.BlockSpec((HALF, 768), lambda i: (0, 0))
    return pl.pallas_call(
        down_kernel,
        grid=(D // FT // 2,),
        out_shape=[
            jax.ShapeDtypeStruct((2, H, D), BF),
            jax.ShapeDtypeStruct((8, 128), F32),
        ],
        in_specs=[tile, tile, whole, whole],
        out_specs=[
            pl.BlockSpec((2, H, 2 * FT), lambda i: (0, 0, i)),
            pl.BlockSpec((8, 128), lambda i: (0, 0)),
        ],
        scratch_shapes=[pltpu.VMEM((256, 512), BF)],
        compiler_params=pltpu.CompilerParams(
            dimension_semantics=("arbitrary",), vmem_limit_bytes=16 * MIB
        ),
        cost_estimate=pl.CostEstimate(
            flops=1_600_000_000, bytes_accessed=10_000_000, transcendentals=0
        ),
        name="down_grads",
    )(grads_own, grads_sib, own, sib)


def first_sum_kernel(where, *refs):
    ra, rb, rp, qa, qb, rp_out, buf = (
        refs[0:4],
        refs[4:8],
        refs[8:12],
        refs[12:16],
        refs[16:20],
        refs[20],
        refs[21],
    )
    y = where[1]
    rp_out[...] = total(rp[0][...], [r[...] for r in rp[1:]])
    buf[...] = total(ra[0][...], [r[...] for r in ra[1:]]).astype(BF)
    for k in range(NY):
        start = pl.multiple_of(((y + k) % NY) * 16, 16)
        qa[k][...] = buf[pl.ds(start, 16), :]
    for k in range(NX):
        qb[k][...] = total(rb[0][k], [r[k] for r in rb[1:]]).astype(BF)


def run_first_sum(where, ra, rb, rp):
    return pl.pallas_call(
        first_sum_kernel,
        out_shape=[jax.ShapeDtypeStruct((16, D // 2), BF)] * 8
        + [jax.ShapeDtypeStruct((8, 256), F32)],
        in_specs=[SMEM_SPEC] + vmem_specs(12),
        out_specs=vmem_specs(9),
        scratch_shapes=[pltpu.VMEM((64, D // 2), BF)],
        compiler_params=pltpu.CompilerParams(vmem_limit_bytes=8 * MIB),
        name="first_sum",
    )(where, *ra, *rb, *rp)


def second_sum_kernel(where, *refs):
    ra, rb, rp, own, out, rp_out, buf = (
        refs[0:4],
        refs[4:8],
        refs[8:12],
        refs[14],
        refs[15:18],
        refs[18],
        refs[19],
    )
    z = where[2]
    rp_out[...] = total(rp[0][...], [r[...] for r in rp[1:]])
    for n, r in enumerate((ra, rb)):
        part = total(r[0][...], [p[...] for p in r[1:]])
        for k in range(NZ):
            buf[k, :, n * (D // 2) : (n + 1) * (D // 2)] = part[4 * k : 4 * k + 4]
    for k in range(NZ):
        rows = buf[(z + k) % NZ]
        if k == 0:
            own[...] = rows
        else:
            out[k - 1][...] = rows.astype(BF)


def run_second_sum(where, ra, rb, rp, token, other):
    return pl.pallas_call(
        second_sum_kernel,
        out_shape=[jax.ShapeDtypeStruct((4, D), F32)]
        + [jax.ShapeDtypeStruct((4, D), BF)] * 3
        + [jax.ShapeDtypeStruct((8, 256), F32)],
        in_specs=[SMEM_SPEC] + vmem_specs(14),
        out_specs=vmem_specs(5),
        scratch_shapes=[pltpu.VMEM((NZ, 4, D), F32)],
        compiler_params=pltpu.CompilerParams(vmem_limit_bytes=8 * MIB),
        name="second_sum",
    )(where, *ra, *rb, *rp, token, other)


def last_sum_kernel(*refs):
    out, rp_out = refs[8], refs[9]
    out[...] = total(refs[0][...], [r[...] for r in refs[1:4]]).astype(BF)
    rp_out[...] = total(refs[4][...], [r[...] for r in refs[5:8]])


def run_last_sum(pieces, rp):
    return pl.pallas_call(
        last_sum_kernel,
        out_shape=[jax.ShapeDtypeStruct((4, D), BF), jax.ShapeDtypeStruct((8, 256), F32)],
        in_specs=vmem_specs(8),
        out_specs=vmem_specs(2),
        compiler_params=pltpu.CompilerParams(vmem_limit_bytes=4 * MIB),
        name="last_sum",
    )(*pieces, *rp)


def router_kernel(where, own, other, slots_ref, out):
    first = jnp.where(where[4] == 0, own[...], other[...])
    second = jnp.where(where[4] == 0, other[...], own[...])
    slots = slots_ref[...].T
    index = lax.broadcasted_iota(jnp.int32, (256, 256), 1)
    lane = lax.broadcasted_iota(jnp.int32, (256, 128), 1)
    spread = jnp.zeros((256, 128), F32)
    for e in range(2):
        picked = jnp.zeros((256, 1), F32)
        for core, values in enumerate((first, second)):
            token = (index // 64) * 128 + core * 64 + index % 64
            hit = slots[:, e : e + 1] == token
            line = jnp.broadcast_to(values[e : e + 1, :], (256, 256))
            picked += jnp.sum(jnp.where(hit, line, 0.0), axis=1, keepdims=True)
        spread = jnp.where(lane == e, picked, spread)
    lines = spread.T
    at = lax.broadcasted_iota(jnp.int32, (1, 256), 1)
    for e in range(2):
        out[e : e + 1, :] = jnp.where(at < where[5 + e], lines[e : e + 1, :], 0.0)


def run_router(where, own, other, slots):
    return pl.pallas_call(
        router_kernel,
        out_shape=jax.ShapeDtypeStruct((2, 256), F32),
        in_specs=[SMEM_SPEC] + vmem_specs(3),
        out_specs=vmem_specs(1)[0],
        compiler_params=pltpu.CompilerParams(vmem_limit_bytes=4 * MIB),
        name="router",
    )(where, own, other, slots)


def on_device(
    tokens_in, out_grad, gate_weight, up_weight, down_weight, slot_tokens, slot_counts, slot_gates
):
    x, c, y, z = position()
    where = jnp.stack([x, y, z, 1 - 2 * c, c, slot_counts[0], slot_counts[1]]).astype(jnp.int32)

    t = [tokens_in] + [shift(tokens_in, "z", k) for k in (1, 2, 3)]
    g = [out_grad] + [shift(out_grad, "x", k, True) for k in (1, 2, 3)]
    t16, g4 = run_first_stage(where, t, g)
    weights = (gate_weight, up_weight, down_weight)
    weights += tuple(swap(w) for w in weights)
    t = [t16] + [shift(t16, "y", k) for k in (1, 2, 3)]
    g = [g4] + [shift(g4, "z", k) for k in (1, 2, 3)]
    t64, g_z = run_second_stage(where, t, g)
    t, g = [t64], [g_z]
    for _ in range(3):
        t.append(shift(t[-1], "x", 1, True))
        g.append(shift(g[-1], "y", 1, True))
    outs = run_main(where, t, g, weights, slot_tokens, slot_gates)
    pa, pb = outs[0:4], outs[4:8]
    dl_own, dl_sib, rp, rows, grads = outs[8:]

    ra = [pa[0]] + [shift(pa[k], "x", -k, True) for k in (1, 2, 3)]
    rb = [pb[0]] + [shift(pb[k], "y", k) for k in (1, 2, 3)]
    dl_got, rows_sib = swap(dl_sib), swap(rows)
    before = [ra[1], ra[3], rb[1], rb[3]]
    grads_sib = swap(run_relay(grads, before))
    gate_grad, up_grad, up_token = run_up(rows, rows_sib, dl_own, dl_got, before)
    rps = [rp] + [shift(rp, "z", k) for k in (1, 2, 3)]
    q = run_first_sum(where, ra, rb, rps)
    qa, qb, rp = q[0:4], q[4:8], q[8]
    ra = [qa[0]] + [shift(qa[k], "y", k) for k in (1, 2, 3)]
    rb = [qb[0]] + [shift(qb[k], "x", -k, True) for k in (1, 2, 3)]
    rps = [rp] + [shift(rp, "x", k) for k in (1, 2, 3)]
    down_grad, token = run_down(grads, grads_sib, dl_own, dl_got)
    q = run_second_sum(where, ra, rb, rps, up_token, token)
    rz = [q[0]] + [shift(q[k], "z", k) for k in (1, 2, 3)]
    rps = [q[4]] + [shift(q[4], "y", k) for k in (1, 2, 3)]
    input_grad, rp = run_last_sum(rz, rps)
    router_grad = run_router(where, rp, swap(rp), slot_tokens)
    return (input_grad, gate_grad, up_grad, down_grad, router_grad)


def solution(mesh):
    return jax.shard_map(
        on_device,
        mesh=mesh,
        in_specs=(
            P(("section", "et"), None),
            P("section", "et"),
            P(None, None, ("section", "et")),
            P(None, None, ("section", "et")),
            P(None, ("section", "et"), None),
            P(),
            P(),
            P(),
        ),
        out_specs=(
            P(("section", "et"), None),
            P(None, None, ("section", "et")),
            P(None, None, ("section", "et")),
            P(None, ("section", "et"), None),
            P(),
        ),
        check_vma=False,
    )
```

profile of v0, /device:TPU:1, one launch (start us, length us, event | category | flops | bytes accessed | tf_op | source)
XLA Modules:
  0.0 193.4 jit_solution(15786352313775395907)
XLA Ops:
  2.6 3.7 %collective-permute-start.1 = (bf16[4,6144]{1,0:T(4,128)(2,1)}, bf16[4,6144]{1,0:T(4,128)(2,1)S(1)}, u32[]{:S(2)}, u32[]{:S(2)}) collective-permute-start(bf16[4,6144]{1,0:T(4,128)(2,1)} %refs_0_.1), channel_id=1, source_target_pairs={{0,2},{1,3},{2,0},{3,1},{4,6},{5,7},{6,4},{7,5},{8,10},{9,11},{10,... | collective-permute-start | bytes 147464 | tf_op jit(solution)/shard_map/ppermute | solution.py:39
  8.6 2.6 %collective-permute-start.2 = (bf16[4,6144]{1,0:T(4,128)(2,1)}, bf16[4,6144]{1,0:T(4,128)(2,1)S(1)}, u32[]{:S(2)}, u32[]{:S(2)}) collective-permute-start(bf16[4,6144]{1,0:T(4,128)(2,1)} %refs_0_.1), channel_id=1, source_target_pairs={{0,3},{1,0},{2,1},{3,2},{4,7},{5,4},{6,5},{7,6},{8,11},{9,8},{10,9... | collective-permute-start | bytes 147464 | tf_op jit(solution)/shard_map/ppermute | solution.py:39
  11.2 2.7 %collective-permute-start.4 = (bf16[64,384]{1,0:T(8,128)(2,1)}, bf16[64,384]{1,0:T(8,128)(2,1)S(1)}, u32[]{:S(2)}, u32[]{:S(2)}) collective-permute-start(bf16[64,384]{1,0:T(8,128)(2,1)} %refs_4_.1), channel_id=1, source_target_pairs={{0,64},{1,65},{2,66},{3,67},{4,68},{5,69},{6,70},{7,71},{8,72},{9,... | collective-permute-start | bytes 147464 | tf_op jit(solution)/shard_map/ppermute | solution.py:39
  17.8 2.9 %collective-permute-done.5.refs_7_ = bf16[64,384]{1,0:T(8,128)(2,1)S(1)} collective-permute-done((bf16[64,384]{1,0:T(8,128)(2,1)}, bf16[64,384]{1,0:T(8,128)(2,1)S(1)}, u32[]{:S(2)}, u32[]{:S(2)}) %collective-permute-start.5) | collective-permute-done | bytes 49184 | tf_op jit(solution)/shard_map/ppermute | solution.py:39
  22.9 2.8 %collective-permute-start.8 = (bf16[16,6144]{1,0:T(8,128)(2,1)S(1)}, bf16[16,6144]{1,0:T(8,128)(2,1)S(1)}, u32[]{:S(2)}, u32[]{:S(2)}) collective-permute-start(bf16[16,6144]{1,0:T(8,128)(2,1)S(1)} %get-tuple-element.43.refs_0_), channel_id=1, source_target_pairs={{0,12},{1,13},{2,14},{3,15},{4,0},{5,1},{6,2},{7,3},{8,4},{9,5},{1... | collective-permute-start | bytes 589832 | tf_op jit(solution)/shard_map/ppermute | solution.py:39
  26.1 4.7 %collective-permute-done.8.refs_3_ = bf16[16,6144]{1,0:T(8,128)(2,1)S(1)} collective-permute-done((bf16[16,6144]{1,0:T(8,128)(2,1)S(1)}, bf16[16,6144]{1,0:T(8,128)(2,1)S(1)}, u32[]{:S(2)}, u32[]{:S(2)}) %collective-permute-start.8) | collective-permute-done | bytes 196640 | tf_op jit(solution)/shard_map/ppermute | solution.py:39
  31.7 2.8 %collective-permute-start.11 = (bf16[256,384]{1,0:T(8,128)(2,1)S(1)}, bf16[256,384]{1,0:T(8,128)(2,1)S(1)}, u32[]{:S(2)}, u32[]{:S(2)}) collective-permute-start(bf16[256,384]{1,0:T(8,128)(2,1)S(1)} %get-tuple-element.44.refs_4_), channel_id=1, source_target_pairs={{0,3},{1,0},{2,1},{3,2},{4,7},{5,4},{6,5},{7,6},{8,11},{9,8},{10,9... | collective-permute-start | bytes 589832 | tf_op jit(solution)/shard_map/ppermute | solution.py:39
  34.6 2.8 %collective-permute-done.6.refs_1_ = bf16[16,6144]{1,0:T(8,128)(2,1)S(1)} collective-permute-done((bf16[16,6144]{1,0:T(8,128)(2,1)S(1)}, bf16[16,6144]{1,0:T(8,128)(2,1)S(1)}, u32[]{:S(2)}, u32[]{:S(2)}) %collective-permute-start.6) | collective-permute-done | bytes 196640 | tf_op jit(solution)/shard_map/ppermute | solution.py:39
  37.8 5.2 %collective-permute-start.9 = (bf16[256,384]{1,0:T(8,128)(2,1)S(1)}, bf16[256,384]{1,0:T(8,128)(2,1)S(1)}, u32[]{:S(2)}, u32[]{:S(2)}) collective-permute-start(bf16[256,384]{1,0:T(8,128)(2,1)S(1)} %get-tuple-element.44.refs_4_), channel_id=1, source_target_pairs={{0,1},{1,2},{2,3},{3,0},{4,5},{5,6},{6,7},{7,4},{8,9},{9,10},{10,1... | collective-permute-start | bytes 589832 | tf_op jit(solution)/shard_map/ppermute | solution.py:39
  43.4 4.0 %collective-permute-done.9.refs_5_ = bf16[256,384]{1,0:T(8,128)(2,1)S(1)} collective-permute-done((bf16[256,384]{1,0:T(8,128)(2,1)S(1)}, bf16[256,384]{1,0:T(8,128)(2,1)S(1)}, u32[]{:S(2)}, u32[]{:S(2)}) %collective-permute-start.9) | collective-permute-done | bytes 196640 | tf_op jit(solution)/shard_map/ppermute | solution.py:39
  49.6 9.7 %collective-permute-done.12.refs_1_ = bf16[64,6144]{1,0:T(8,128)(2,1)S(1)} collective-permute-done((bf16[64,6144]{1,0:T(8,128)(2,1)S(1)}, bf16[64,6144]{1,0:T(8,128)(2,1)S(1)}, u32[]{:S(2)}, u32[]{:S(2)}) %collective-permute-start.12) | collective-permute-done | bytes 786464 | tf_op jit(solution)/shard_map/ppermute | solution.py:39
  61.9 8.5 %collective-permute-done.13.refs_2_ = bf16[64,6144]{1,0:T(8,128)(2,1)S(1)} collective-permute-done((bf16[64,6144]{1,0:T(8,128)(2,1)S(1)}, bf16[64,6144]{1,0:T(8,128)(2,1)S(1)}, u32[]{:S(2)}, u32[]{:S(2)}) %collective-permute-start.13) | collective-permute-done | bytes 786464 | tf_op jit(solution)/shard_map/ppermute | solution.py:39
  70.4 2.1 %collective-permute-start.14 = (bf16[64,6144]{1,0:T(8,128)(2,1)S(1)}, bf16[64,6144]{1,0:T(8,128)(2,1)S(1)}, u32[]{:S(2)}, u32[]{:S(2)}) collective-permute-start(bf16[64,6144]{1,0:T(8,128)(2,1)S(1)} %collective-permute-done.13.refs_2_), channel_id=1, source_target_pairs={{0,32},{1,33},{2,34},{3,35},{4,36},{5,37},{6,38},{7,39},{8,40},{9,... | collective-permute-start | bytes 2359304 | tf_op jit(solution)/shard_map/ppermute | solution.py:39
  74.2 7.2 %collective-permute-done.14.refs_3_ = bf16[64,6144]{1,0:T(8,128)(2,1)S(1)} collective-permute-done((bf16[64,6144]{1,0:T(8,128)(2,1)S(1)}, bf16[64,6144]{1,0:T(8,128)(2,1)S(1)}, u32[]{:S(2)}, u32[]{:S(2)}) %collective-permute-start.14) | collective-permute-done | bytes 786464 | tf_op jit(solution)/shard_map/ppermute | solution.py:39
  81.5 2.9 %collective-permute-done.17.refs_7_ = bf16[256,1536]{1,0:T(8,128)(2,1)S(1)} collective-permute-done((bf16[256,1536]{1,0:T(8,128)(2,1)S(1)}, bf16[256,1536]{1,0:T(8,128)(2,1)S(1)}, u32[]{:S(2)}, u32[]{:S(2)}) %collective-permute-start.17) | collective-permute-done | bytes 786464 | tf_op jit(solution)/shard_map/ppermute | solution.py:39
  87.5 18.4 %main.1 = (bf16[64,3072]{1,0:T(8,128)(2,1)S(1)}, bf16[64,3072]{1,0:T(8,128)(2,1)S(1)}, bf16[64,3072]{1,0:T(8,128)(2,1)S(1)}, bf16[64,3072]{1,0:T(8,128)(2,1)S(1)...) custom-call(s32[7]{0:T(128)S(1)} %stack.23.where, ...), custom_call_target="tpu_custom_call" | custom-call | flops 8000000000 | bytes 30000000 | tf_op jit(solution)/shard_map/main/pallas_call | solution.py:322
  106.0 2.7 %collective-permute-start.23 = (bf16[64,3072]{1,0:T(8,128)(2,1)S(1)}, bf16[64,3072]{1,0:T(8,128)(2,1)S(1)}, u32[]{:S(2)}, u32[]{:S(2)}) collective-permute-start(bf16[64,3072]{1,0:T(8,128)(2,1)S(1)} %get-tuple-element.50), channel_id=1, source_target_pairs={{0,32},{1,33},{2,34},{3,35},{4,36},{5,37},{6,38},{7,39},{8,40},{9,... | collective-permute-start | bytes 1179656 | tf_op jit(solution)/shard_map/ppermute | solution.py:39
  111.3 8.7 %collective-permute-start.39 = (bf16[256,6144]{1,0:T(8,128)(2,1)}, bf16[256,6144]{1,0:T(8,128)(2,1)S(1)}, u32[]{:S(2)}, u32[]{:S(2)}) collective-permute-start(bf16[256,6144]{1,0:T(8,128)(2,1)} %get-tuple-element.65.refs_0_), channel_id=1, source_target_pairs={{0,16},{1,17},{2,18},{3,19},{4,20},{5,21},{6,22},{7,23},{8,24},{9,... | collective-permute-start | bytes 9437192 | tf_op jit(solution)/shard_map/ppermute | solution.py:50
  120.0 1.9 copy-done
  122.2 7.1 %collective-permute-start.41 = (bf16[256,6144]{1,0:T(8,128)(2,1)S(1)}, bf16[256,6144]{1,0:T(8,128)(2,1)S(1)}, u32[]{:S(2)}, u32[]{:S(2)}) collective-permute-start(bf16[256,6144]{1,0:T(8,128)(2,1)S(1)} %relay.1), channel_id=1, source_target_pairs={{0,16},{1,17},{2,18},{3,19},{4,20},{5,21},{6,22},{7,23},{8,24},{9,... | collective-permute-start | bytes 9437192 | tf_op jit(solution)/shard_map/ppermute | solution.py:50
  133.1 1.9 %collective-permute-done.28.refs_10_ = f32[8,256]{1,0:T(8,128)S(1)} collective-permute-done((f32[8,256]{1,0:T(8,128)S(1)}, f32[8,256]{1,0:T(8,128)S(1)}, u32[]{:S(2)}, u32[]{:S(2)}) %collective-permute-start.28) | collective-permute-done | bytes 8224 | tf_op jit(solution)/shard_map/ppermute | solution.py:39
  135.1 3.0 %collective-permute-start.25 = (bf16[4,16,3072]{2,1,0:T(8,128)(2,1)S(1)}, bf16[4,16,3072]{2,1,0:T(8,128)(2,1)S(1)}, u32[]{:S(2)}, u32[]{:S(2)}) collective-permute-start(bf16[4,16,3072]{2,1,0:T(8,128)(2,1)S(1)} %get-tuple-element.53), channel_id=1, source_target_pairs={{0,8},{1,9},{2,10},{3,11},{4,12},{5,13},{6,14},{7,15},{8,0},{9,1},... | collective-permute-start | bytes 1179656 | tf_op jit(solution)/shard_map/ppermute | solution.py:39
  138.1 1.8 collective-permute-start.40
  139.8 2.9 %collective-permute-done.22.refs_2_ = bf16[64,3072]{1,0:T(8,128)(2,1)S(1)} collective-permute-done((bf16[64,3072]{1,0:T(8,128)(2,1)S(1)}, bf16[64,3072]{1,0:T(8,128)(2,1)S(1)}, u32[]{:S(2)}, u32[]{:S(2)}) %collective-permute-start.22) | collective-permute-done | bytes 393248 | tf_op jit(solution)/shard_map/ppermute | solution.py:39
  142.8 3.0 %collective-permute-done.25.refs_6_ = bf16[4,16,3072]{2,1,0:T(8,128)(2,1)S(1)} collective-permute-done((bf16[4,16,3072]{2,1,0:T(8,128)(2,1)S(1)}, bf16[4,16,3072]{2,1,0:T(8,128)(2,1)S(1)}, u32[]{:S(2)}, u32[]{:S(2)}) %collective-permute-start.25) | collective-permute-done | bytes 393248 | tf_op jit(solution)/shard_map/ppermute | solution.py:39
  146.9 3.0 %collective-permute-start.38 = (f32[8,256]{1,0:T(8,128)S(1)}, f32[8,256]{1,0:T(8,128)S(1)}, u32[]{:S(2)}, u32[]{:S(2)}) collective-permute-start(f32[8,256]{1,0:T(8,128)S(1)} %get-tuple-element.64.refs_8_), channel_id=1, source_target_pairs={{0,96},{1,97},{2,98},{3,99},{4,100},{5,101},{6,102},{7,103},{8,104... | collective-permute-start | bytes 24584 | tf_op jit(solution)/shard_map/ppermute | solution.py:39
  152.3 8.3 %up_grads.1 = (bf16[2,6144,128]{2,1,0:T(8,128)(2,1)}, bf16[2,6144,128]{2,1,0:T(8,128)(2,1)}, f32[8,128]{1,0:T(8,128)S(1)}) custom-call(bf16[256,6144]{1,0:T(8,128)(2,1)S(1)} %copy-done.5, bf16[256,6144]{1,0:T(8,128)(2,1)S(1)} %collective-permute-done.39.refs_1_, bf16[256,768]{1,0:T(8,128)(2,1)S(1)} %get-tuple-element.66.refs_2_.own, ...), custom_call_target="tpu_custom_call" | custom-call | flops 3200000000 | bytes 13000000 | tf_op jit(solution)/shard_map/up_grads/pallas_call | solution.py:368
  163.1 2.0 %collective-permute-start.33 = (bf16[16,3072]{1,0:T(8,128)(2,1)S(1)}, bf16[16,3072]{1,0:T(8,128)(2,1)S(1)}, u32[]{:S(2)}, u32[]{:S(2)}) collective-permute-start(bf16[16,3072]{1,0:T(8,128)(2,1)S(1)} %get-tuple-element.61), channel_id=1, source_target_pairs={{0,96},{1,97},{2,98},{3,99},{4,100},{5,101},{6,102},{7,103},{8,104... | collective-permute-start | bytes 294920 | tf_op jit(solution)/shard_map/ppermute | solution.py:39
  167.5 4.6 %down_grads.1 = (bf16[2,128,6144]{2,1,0:T(8,128)(2,1)}, f32[8,128]{1,0:T(8,128)S(1)}) custom-call(bf16[256,6144]{1,0:T(8,128)(2,1)S(1)} %copy-done.1, bf16[256,6144]{1,0:T(8,128)(2,1)S(1)} %collective-permute-done.41.grads_sib, bf16[256,768]{1,0:T(8,128)(2,1)S(1)} %get-tuple-element.66.refs_2_.own, bf16[256,768]{1,0:T(8,128)(2,1)S(1)} %collective-permute-done.40.refs_3_.sib), custom_call_target="tpu_custom_call" | custom-call | flops 1600000000 | bytes 10000000 | tf_op jit(solution)/shard_map/down_grads/pallas_call | solution.py:406
  173.1 1.9 collective-permute-start.43
  178.8 1.9 collective-permute-done.46.refs_6_
  183.0 7.9 %collective-permute-start.48 = (f32[8,256]{1,0:T(8,128)S(1)}, f32[8,256]{1,0:T(8,128)S(1)}, u32[]{:S(2)}, u32[]{:S(2)}) collective-permute-start(f32[8,256]{1,0:T(8,128)S(1)} %get-tuple-element.80.own), channel_id=1, source_target_pairs={{0,16},{1,17},{2,18},{3,19},{4,20},{5,21},{6,22},{7,23},{8,24},{9,... | collective-permute-start | bytes 24584 | tf_op jit(solution)/shard_map/ppermute | solution.py:50
  (93 shorter events, 46.8 us)
Async XLA Ops:
  0.6 83.8 %collective-permute-start.18 = (bf16[2,6144,128]{2,1,0:T(8,128)(2,1)}, bf16[2,6144,128]{2,1,0:T(8,128)(2,1)S(1)}, u32[]{:S(2)}, u32[]{:S(2)}) collective-permute-start(bf16[2,6144,128]{2,1,0:T(8,128)(2,1)} %refs_8_.1), channel_id=1, source_target_pairs={{0,16},{1,17},{2,18},{3,19},{4,20},{5,21},{6,22},{7,23},{8,24},{9,... | collective-permute-start | bytes 9437192 | tf_op jit(solution)/shard_map/ppermute | solution.py:50
  2.1 82.3 %collective-permute-start.19 = (bf16[2,6144,128]{2,1,0:T(8,128)(2,1)}, bf16[2,6144,128]{2,1,0:T(8,128)(2,1)}, u32[]{:S(2)}, u32[]{:S(2)}) collective-permute-start(bf16[2,6144,128]{2,1,0:T(8,128)(2,1)} %refs_9_.1), channel_id=1, source_target_pairs={{0,16},{1,17},{2,18},{3,19},{4,20},{5,21},{6,22},{7,23},{8,24},{9,... | collective-permute-start | bytes 9437192 | tf_op jit(solution)/shard_map/ppermute | solution.py:50
  2.2 82.2 %collective-permute-start.20 = (bf16[2,128,6144]{2,1,0:T(8,128)(2,1)}, bf16[2,128,6144]{2,1,0:T(8,128)(2,1)}, u32[]{:S(2)}, u32[]{:S(2)}) collective-permute-start(bf16[2,128,6144]{2,1,0:T(8,128)(2,1)} %refs_10_.1), channel_id=1, source_target_pairs={{0,16},{1,17},{2,18},{3,19},{4,20},{5,21},{6,22},{7,23},{8,24},{9,... | collective-permute-start | bytes 9437192 | tf_op jit(solution)/shard_map/ppermute | solution.py:50
  22.9 7.9 %collective-permute-start.8 = (bf16[16,6144]{1,0:T(8,128)(2,1)S(1)}, bf16[16,6144]{1,0:T(8,128)(2,1)S(1)}, u32[]{:S(2)}, u32[]{:S(2)}) collective-permute-start(bf16[16,6144]{1,0:T(8,128)(2,1)S(1)} %get-tuple-element.43.refs_0_), channel_id=1, source_target_pairs={{0,12},{1,13},{2,14},{3,15},{4,0},{5,1},{6,2},{7,3},{8,4},{9,5},{1... | collective-permute-start | bytes 589832 | tf_op jit(solution)/shard_map/ppermute | solution.py:39
  37.8 9.6 %collective-permute-start.9 = (bf16[256,384]{1,0:T(8,128)(2,1)S(1)}, bf16[256,384]{1,0:T(8,128)(2,1)S(1)}, u32[]{:S(2)}, u32[]{:S(2)}) collective-permute-start(bf16[256,384]{1,0:T(8,128)(2,1)S(1)} %get-tuple-element.44.refs_4_), channel_id=1, source_target_pairs={{0,1},{1,2},{2,3},{3,0},{4,5},{5,6},{6,7},{7,4},{8,9},{9,10},{10,1... | collective-permute-start | bytes 589832 | tf_op jit(solution)/shard_map/ppermute | solution.py:39
  48.1 11.2 %collective-permute-start.12 = (bf16[64,6144]{1,0:T(8,128)(2,1)S(1)}, bf16[64,6144]{1,0:T(8,128)(2,1)S(1)}, u32[]{:S(2)}, u32[]{:S(2)}) collective-permute-start(bf16[64,6144]{1,0:T(8,128)(2,1)S(1)} %get-tuple-element.45.refs_0_), channel_id=1, source_target_pairs={{0,32},{1,33},{2,34},{3,35},{4,36},{5,37},{6,38},{7,39},{8,40},{9,... | collective-permute-start | bytes 2359304 | tf_op jit(solution)/shard_map/ppermute | solution.py:39
  48.2 12.3 %collective-permute-start.15 = (bf16[256,1536]{1,0:T(8,128)(2,1)S(1)}, bf16[256,1536]{1,0:T(8,128)(2,1)S(1)}, u32[]{:S(2)}, u32[]{:S(2)}) collective-permute-start(bf16[256,1536]{1,0:T(8,128)(2,1)S(1)} %get-tuple-element.46.refs_4_), channel_id=1, source_target_pairs={{0,4},{1,5},{2,6},{3,7},{4,8},{5,9},{6,10},{7,11},{8,12},{9,13},{1... | collective-permute-start | bytes 2359304 | tf_op jit(solution)/shard_map/ppermute | solution.py:39
  59.3 11.1 %collective-permute-start.13 = (bf16[64,6144]{1,0:T(8,128)(2,1)S(1)}, bf16[64,6144]{1,0:T(8,128)(2,1)S(1)}, u32[]{:S(2)}, u32[]{:S(2)}) collective-permute-start(bf16[64,6144]{1,0:T(8,128)(2,1)S(1)} %collective-permute-done.12.refs_1_), channel_id=1, source_target_pairs={{0,32},{1,33},{2,34},{3,35},{4,36},{5,37},{6,38},{7,39},{8,40},{9,... | collective-permute-start | bytes 2359304 | tf_op jit(solution)/shard_map/ppermute | solution.py:39
  60.5 12.1 %collective-permute-start.16 = (bf16[256,1536]{1,0:T(8,128)(2,1)S(1)}, bf16[256,1536]{1,0:T(8,128)(2,1)S(1)}, u32[]{:S(2)}, u32[]{:S(2)}) collective-permute-start(bf16[256,1536]{1,0:T(8,128)(2,1)S(1)} %collective-permute-done.15.refs_5_), channel_id=1, source_target_pairs={{0,4},{1,5},{2,6},{3,7},{4,8},{5,9},{6,10},{7,11},{8,12},{9,13},{1... | collective-permute-start | bytes 2359304 | tf_op jit(solution)/shard_map/ppermute | solution.py:39
  70.4 11.1 %collective-permute-start.14 = (bf16[64,6144]{1,0:T(8,128)(2,1)S(1)}, bf16[64,6144]{1,0:T(8,128)(2,1)S(1)}, u32[]{:S(2)}, u32[]{:S(2)}) collective-permute-start(bf16[64,6144]{1,0:T(8,128)(2,1)S(1)} %collective-permute-done.13.refs_2_), channel_id=1, source_target_pairs={{0,32},{1,33},{2,34},{3,35},{4,36},{5,37},{6,38},{7,39},{8,40},{9,... | collective-permute-start | bytes 2359304 | tf_op jit(solution)/shard_map/ppermute | solution.py:39
  72.6 11.9 %collective-permute-start.17 = (bf16[256,1536]{1,0:T(8,128)(2,1)S(1)}, bf16[256,1536]{1,0:T(8,128)(2,1)S(1)}, u32[]{:S(2)}, u32[]{:S(2)}) collective-permute-start(bf16[256,1536]{1,0:T(8,128)(2,1)S(1)} %collective-permute-done.16.refs_6_), channel_id=1, source_target_pairs={{0,4},{1,5},{2,6},{3,7},{4,8},{5,9},{6,10},{7,11},{8,12},{9,13},{1... | collective-permute-start | bytes 2359304 | tf_op jit(solution)/shard_map/ppermute | solution.py:39
  105.9 14.1 %collective-permute-start.21 = (bf16[64,3072]{1,0:T(8,128)(2,1)S(1)}, bf16[64,3072]{1,0:T(8,128)(2,1)S(1)}, u32[]{:S(2)}, u32[]{:S(2)}) collective-permute-start(bf16[64,3072]{1,0:T(8,128)(2,1)S(1)} %get-tuple-element.48), channel_id=1, source_target_pairs={{0,96},{1,97},{2,98},{3,99},{4,100},{5,101},{6,102},{7,103},{8,104... | collective-permute-start | bytes 1179656 | tf_op jit(solution)/shard_map/ppermute | solution.py:39
  106.0 14.1 %collective-permute-start.23 = (bf16[64,3072]{1,0:T(8,128)(2,1)S(1)}, bf16[64,3072]{1,0:T(8,128)(2,1)S(1)}, u32[]{:S(2)}, u32[]{:S(2)}) collective-permute-start(bf16[64,3072]{1,0:T(8,128)(2,1)S(1)} %get-tuple-element.50), channel_id=1, source_target_pairs={{0,32},{1,33},{2,34},{3,35},{4,36},{5,37},{6,38},{7,39},{8,40},{9,... | collective-permute-start | bytes 1179656 | tf_op jit(solution)/shard_map/ppermute | solution.py:39
  108.6 11.4 %collective-permute-start.24 = (bf16[4,16,3072]{2,1,0:T(8,128)(2,1)S(1)}, bf16[4,16,3072]{2,1,0:T(8,128)(2,1)S(1)}, u32[]{:S(2)}, u32[]{:S(2)}) collective-permute-start(bf16[4,16,3072]{2,1,0:T(8,128)(2,1)S(1)} %get-tuple-element.52), channel_id=1, source_target_pairs={{0,4},{1,5},{2,6},{3,7},{4,8},{5,9},{6,10},{7,11},{8,12},{9,13},{1... | collective-permute-start | bytes 1179656 | tf_op jit(solution)/shard_map/ppermute | solution.py:39
  110.1 9.9 %collective-permute-start.26 = (bf16[4,16,3072]{2,1,0:T(8,128)(2,1)S(1)}, bf16[4,16,3072]{2,1,0:T(8,128)(2,1)S(1)}, u32[]{:S(2)}, u32[]{:S(2)}) collective-permute-start(bf16[4,16,3072]{2,1,0:T(8,128)(2,1)S(1)} %get-tuple-element.54), channel_id=1, source_target_pairs={{0,12},{1,13},{2,14},{3,15},{4,0},{5,1},{6,2},{7,3},{8,4},{9,5},{1... | collective-permute-start | bytes 1179656 | tf_op jit(solution)/shard_map/ppermute | solution.py:39
  111.3 39.2 %collective-permute-start.39 = (bf16[256,6144]{1,0:T(8,128)(2,1)}, bf16[256,6144]{1,0:T(8,128)(2,1)S(1)}, u32[]{:S(2)}, u32[]{:S(2)}) collective-permute-start(bf16[256,6144]{1,0:T(8,128)(2,1)} %get-tuple-element.65.refs_0_), channel_id=1, source_target_pairs={{0,16},{1,17},{2,18},{3,19},{4,20},{5,21},{6,22},{7,23},{8,24},{9,... | collective-permute-start | bytes 9437192 | tf_op jit(solution)/shard_map/ppermute | solution.py:50
  122.2 44.1 %collective-permute-start.41 = (bf16[256,6144]{1,0:T(8,128)(2,1)S(1)}, bf16[256,6144]{1,0:T(8,128)(2,1)S(1)}, u32[]{:S(2)}, u32[]{:S(2)}) collective-permute-start(bf16[256,6144]{1,0:T(8,128)(2,1)S(1)} %relay.1), channel_id=1, source_target_pairs={{0,16},{1,17},{2,18},{3,19},{4,20},{5,21},{6,22},{7,23},{8,24},{9,... | collective-permute-start | bytes 9437192 | tf_op jit(solution)/shard_map/ppermute | solution.py:50
  131.9 10.9 %collective-permute-start.22 = (bf16[64,3072]{1,0:T(8,128)(2,1)S(1)}, bf16[64,3072]{1,0:T(8,128)(2,1)S(1)}, u32[]{:S(2)}, u32[]{:S(2)}) collective-permute-start(bf16[64,3072]{1,0:T(8,128)(2,1)S(1)} %get-tuple-element.49), channel_id=1, source_target_pairs={{0,64},{1,65},{2,66},{3,67},{4,68},{5,69},{6,70},{7,71},{8,72},{9,... | collective-permute-start | bytes 1179656 | tf_op jit(solution)/shard_map/ppermute | solution.py:39
  135.1 10.7 %collective-permute-start.25 = (bf16[4,16,3072]{2,1,0:T(8,128)(2,1)S(1)}, bf16[4,16,3072]{2,1,0:T(8,128)(2,1)S(1)}, u32[]{:S(2)}, u32[]{:S(2)}) collective-permute-start(bf16[4,16,3072]{2,1,0:T(8,128)(2,1)S(1)} %get-tuple-element.53), channel_id=1, source_target_pairs={{0,8},{1,9},{2,10},{3,11},{4,12},{5,13},{6,14},{7,15},{8,0},{9,1},... | collective-permute-start | bytes 1179656 | tf_op jit(solution)/shard_map/ppermute | solution.py:39
  138.1 11.8 %collective-permute-start.40 = (bf16[256,768]{1,0:T(8,128)(2,1)S(1)}, bf16[256,768]{1,0:T(8,128)(2,1)S(1)}, u32[]{:S(2)}, u32[]{:S(2)}) collective-permute-start(bf16[256,768]{1,0:T(8,128)(2,1)S(1)} %get-tuple-element.67), channel_id=1, source_target_pairs={{0,16},{1,17},{2,18},{3,19},{4,20},{5,21},{6,22},{7,23},{8,24},{9,... | collective-permute-start | bytes 1179656 | tf_op jit(solution)/shard_map/ppermute | solution.py:50
  146.9 13.7 %collective-permute-start.38 = (f32[8,256]{1,0:T(8,128)S(1)}, f32[8,256]{1,0:T(8,128)S(1)}, u32[]{:S(2)}, u32[]{:S(2)}) collective-permute-start(f32[8,256]{1,0:T(8,128)S(1)} %get-tuple-element.64.refs_8_), channel_id=1, source_target_pairs={{0,96},{1,97},{2,98},{3,99},{4,100},{5,101},{6,102},{7,103},{8,104... | collective-permute-start | bytes 24584 | tf_op jit(solution)/shard_map/ppermute | solution.py:39
  149.9 11.7 %collective-permute-start.37 = (f32[8,256]{1,0:T(8,128)S(1)}, f32[8,256]{1,0:T(8,128)S(1)}, u32[]{:S(2)}, u32[]{:S(2)}) collective-permute-start(f32[8,256]{1,0:T(8,128)S(1)} %get-tuple-element.64.refs_8_), channel_id=1, source_target_pairs={{0,64},{1,65},{2,66},{3,67},{4,68},{5,69},{6,70},{7,71},{8,72},{9,... | collective-permute-start | bytes 24584 | tf_op jit(solution)/shard_map/ppermute | solution.py:39
  149.9 13.2 %collective-permute-start.36 = (f32[8,256]{1,0:T(8,128)S(1)}, f32[8,256]{1,0:T(8,128)S(1)}, u32[]{:S(2)}, u32[]{:S(2)}) collective-permute-start(f32[8,256]{1,0:T(8,128)S(1)} %get-tuple-element.64.refs_8_), channel_id=1, source_target_pairs={{0,32},{1,33},{2,34},{3,35},{4,36},{5,37},{6,38},{7,39},{8,40},{9,... | collective-permute-start | bytes 24584 | tf_op jit(solution)/shard_map/ppermute | solution.py:39
  150.6 14.5 %collective-permute-start.30 = (bf16[16,3072]{1,0:T(8,128)(2,1)S(1)}, bf16[16,3072]{1,0:T(8,128)(2,1)S(1)}, u32[]{:S(2)}, u32[]{:S(2)}) collective-permute-start(bf16[16,3072]{1,0:T(8,128)(2,1)S(1)} %get-tuple-element.57), channel_id=1, source_target_pairs={{0,4},{1,5},{2,6},{3,7},{4,8},{5,9},{6,10},{7,11},{8,12},{9,13},{1... | collective-permute-start | bytes 294920 | tf_op jit(solution)/shard_map/ppermute | solution.py:39
  160.6 11.5 %collective-permute-start.31 = (bf16[16,3072]{1,0:T(8,128)(2,1)S(1)}, bf16[16,3072]{1,0:T(8,128)(2,1)S(1)}, u32[]{:S(2)}, u32[]{:S(2)}) collective-permute-start(bf16[16,3072]{1,0:T(8,128)(2,1)S(1)} %get-tuple-element.58), channel_id=1, source_target_pairs={{0,8},{1,9},{2,10},{3,11},{4,12},{5,13},{6,14},{7,15},{8,0},{9,1},... | collective-permute-start | bytes 294920 | tf_op jit(solution)/shard_map/ppermute | solution.py:39
  161.6 10.5 %collective-permute-start.32 = (bf16[16,3072]{1,0:T(8,128)(2,1)S(1)}, bf16[16,3072]{1,0:T(8,128)(2,1)S(1)}, u32[]{:S(2)}, u32[]{:S(2)}) collective-permute-start(bf16[16,3072]{1,0:T(8,128)(2,1)S(1)} %get-tuple-element.59), channel_id=1, source_target_pairs={{0,12},{1,13},{2,14},{3,15},{4,0},{5,1},{6,2},{7,3},{8,4},{9,5},{1... | collective-permute-start | bytes 294920 | tf_op jit(solution)/shard_map/ppermute | solution.py:39
  163.1 9.1 %collective-permute-start.33 = (bf16[16,3072]{1,0:T(8,128)(2,1)S(1)}, bf16[16,3072]{1,0:T(8,128)(2,1)S(1)}, u32[]{:S(2)}, u32[]{:S(2)}) collective-permute-start(bf16[16,3072]{1,0:T(8,128)(2,1)S(1)} %get-tuple-element.61), channel_id=1, source_target_pairs={{0,96},{1,97},{2,98},{3,99},{4,100},{5,101},{6,102},{7,103},{8,104... | collective-permute-start | bytes 294920 | tf_op jit(solution)/shard_map/ppermute | solution.py:39
  165.1 7.1 %collective-permute-start.34 = (bf16[16,3072]{1,0:T(8,128)(2,1)S(1)}, bf16[16,3072]{1,0:T(8,128)(2,1)S(1)}, u32[]{:S(2)}, u32[]{:S(2)}) collective-permute-start(bf16[16,3072]{1,0:T(8,128)(2,1)S(1)} %get-tuple-element.62), channel_id=1, source_target_pairs={{0,64},{1,65},{2,66},{3,67},{4,68},{5,69},{6,70},{7,71},{8,72},{9,... | collective-permute-start | bytes 294920 | tf_op jit(solution)/shard_map/ppermute | solution.py:39
  172.9 9.4 %collective-permute-start.42 = (bf16[4,6144]{1,0:T(4,128)(2,1)S(1)}, bf16[4,6144]{1,0:T(4,128)(2,1)S(1)}, u32[]{:S(2)}, u32[]{:S(2)}) collective-permute-start(bf16[4,6144]{1,0:T(4,128)(2,1)S(1)} %get-tuple-element.72), channel_id=1, source_target_pairs={{0,1},{1,2},{2,3},{3,0},{4,5},{5,6},{6,7},{7,4},{8,9},{9,10},{10,1... | collective-permute-start | bytes 147464 | tf_op jit(solution)/shard_map/ppermute | solution.py:39
  173.1 9.2 %collective-permute-start.43 = (bf16[4,6144]{1,0:T(4,128)(2,1)S(1)}, bf16[4,6144]{1,0:T(4,128)(2,1)S(1)}, u32[]{:S(2)}, u32[]{:S(2)}) collective-permute-start(bf16[4,6144]{1,0:T(4,128)(2,1)S(1)} %get-tuple-element.73), channel_id=1, source_target_pairs={{0,2},{1,3},{2,0},{3,1},{4,6},{5,7},{6,4},{7,5},{8,10},{9,11},{10,... | collective-permute-start | bytes 147464 | tf_op jit(solution)/shard_map/ppermute | solution.py:39
  175.0 7.3 %collective-permute-start.44 = (bf16[4,6144]{1,0:T(4,128)(2,1)S(1)}, bf16[4,6144]{1,0:T(4,128)(2,1)S(1)}, u32[]{:S(2)}, u32[]{:S(2)}) collective-permute-start(bf16[4,6144]{1,0:T(4,128)(2,1)S(1)} %get-tuple-element.74), channel_id=1, source_target_pairs={{0,3},{1,0},{2,1},{3,2},{4,7},{5,4},{6,5},{7,6},{8,11},{9,8},{10,9... | collective-permute-start | bytes 147464 | tf_op jit(solution)/shard_map/ppermute | solution.py:39
  183.0 8.7 %collective-permute-start.48 = (f32[8,256]{1,0:T(8,128)S(1)}, f32[8,256]{1,0:T(8,128)S(1)}, u32[]{:S(2)}, u32[]{:S(2)}) collective-permute-start(f32[8,256]{1,0:T(8,128)S(1)} %get-tuple-element.80.own), channel_id=1, source_target_pairs={{0,16},{1,17},{2,18},{3,19},{4,20},{5,21},{6,22},{7,23},{8,24},{9,... | collective-permute-start | bytes 24584 | tf_op jit(solution)/shard_map/ppermute | solution.py:50
  (25 other events, 136.1 us)
where the time goes:
time: 194 us; the launch traced here: 193 us
  starting transfers between devices  89.1 us (46%)
  waiting for transfers between devices  59.2 us (31%)
  Pallas kernels  37.1 us (19%)
  local copies, waits for them, and re-layouts  7.23 us (4%)
    ppermute x42, starting transfers between devices, shift(): return lax.ppermute(value, AXES, shift_pairs(axis, step, by_core))  61.6 us
    ppermute x42, waiting for transfers between devices, shift(): return lax.ppermute(value, AXES, shift_pairs(axis, step, by_core))  58.4 us
    ppermute x7, starting transfers between devices, swap(): return lax.ppermute(value, AXES, pairs)  27.5 us
    pallas_call x1, Pallas kernels, run_main(): pl.pallas_call(main_kernel, out_shape=out_shape, in_specs=[SMEM_SPEC] + h...  18.4 us
    pallas_call x1, Pallas kernels, run_up(): pl.pallas_call(up_kernel, grid=(D // FT,), out_shape=[jax.ShapeDtypeStruc...  8.33 us
    unnamed x16, local copies, waits for them, and re-layouts  6.5 us
    pallas_call x1, Pallas kernels, run_down(): pl.pallas_call(down_kernel, grid=(D // FT // 2,), out_shape=[jax.ShapeDty...  4.58 us
  transfers between devices with their start and end apart: 49, of which 20 were waited for; matrix products, arithmetic and copies ran while one was open for 0% of the time, Pallas kernels for 8%

commit v1 on v0

--- a/solution.py
+++ b/solution.py
@@ -19,24 +19,23 @@
     return ((x * NC + c) * NY + y) * NZ + z
 
 
-def shift_pairs(axis, step, by_core):
+def shift_pairs(axis, step):
     pairs = []
     for x in range(NX):
         for c in range(NC):
             for y in range(NY):
                 for z in range(NZ):
-                    d = -step if (by_core and c == 1) else step
                     to = {
-                        "x": ((x + d) % NX, c, y, z),
-                        "y": (x, c, (y + d) % NY, z),
-                        "z": (x, c, y, (z + d) % NZ),
+                        "x": ((x + step) % NX, c, y, z),
+                        "y": (x, c, (y + step) % NY, z),
+                        "z": (x, c, y, (z + step) % NZ),
                     }[axis]
                     pairs.append((linear(x, c, y, z), linear(*to)))
     return pairs
 
 
-def shift(value, axis, step, by_core=False):
-    return lax.ppermute(value, AXES, shift_pairs(axis, step, by_core))
+def shift(value, axis, step):
+    return lax.ppermute(value, AXES, shift_pairs(axis, step))
 
 
 def swap(value):
@@ -74,6 +73,7 @@
 KT = 1024
 FT = 512
 MIB = 2**20
+WIDE = D // 2 + 384
 
 
 def vmem_specs(n):
@@ -83,46 +83,86 @@
 SMEM_SPEC = pl.BlockSpec(memory_space=pltpu.SMEM)
 
 
+def pack_kernel(tokens, grads, out):
+    out[0:64, :] = grads[...]
+    rows = tokens[...].astype(F32)
+    for b in range(0, 16, 4):
+        four = [rows[:, (b + i) * 384 : (b + i + 1) * 384] for i in range(4)]
+        out[64 + 4 * b : 80 + 4 * b, :] = jnp.concatenate(four, axis=0).astype(BF)
+
+
+def run_pack(tokens, grads):
+    return pl.pallas_call(
+        pack_kernel,
+        out_shape=jax.ShapeDtypeStruct((128, 384), BF),
+        in_specs=vmem_specs(2),
+        out_specs=vmem_specs(1)[0],
+        compiler_params=pltpu.CompilerParams(vmem_limit_bytes=4 * MIB),
+        name="pack",
+    )(tokens, grads)
+
+
 def first_stage_kernel(where, *refs):
-    t, g, t_out, g_out, buf = refs[0:4], refs[4:8], refs[8], refs[9], refs[10]
+    packed, t_out, g_out, buf = refs[0:4], refs[4], refs[5], refs[6]
     for k in range(NZ):
-        buf[(where[2] - k) % NZ] = t[k][...].astype(F32)
+        at = (where[2] - k) % NZ
+        rows = packed[k][64:128, :].astype(F32)
+        for b in range(16):
+            buf[at, :, 384 * b : 384 * (b + 1)] = rows[4 * b : 4 * b + 4]
+        start = pl.multiple_of(384 * at, 128)
+        g_out[:, pl.ds(start, 384)] = packed[k][0:64, :]
     t_out[...] = jnp.concatenate([buf[k] for k in range(NZ)], axis=0).astype(BF)
-    for k in range(NX):
-        g_out[k * 64 : (k + 1) * 64, :] = g[k][...]
-
-
-def run_first_stage(where, t, g):
+
+
+def run_first_stage(where, packed):
     return pl.pallas_call(
         first_stage_kernel,
-        out_shape=[jax.ShapeDtypeStruct((16, D), BF), jax.ShapeDtypeStruct((HALF, 384), BF)],
-        in_specs=[SMEM_SPEC] + vmem_specs(8),
+        out_shape=[jax.ShapeDtypeStruct((16, D), BF), jax.ShapeDtypeStruct((64, 1536), BF)],
+        in_specs=[SMEM_SPEC] + vmem_specs(4),
         out_specs=vmem_specs(2),
         scratch_shapes=[pltpu.VMEM((NZ, 4, D), F32)],
         compiler_params=pltpu.CompilerParams(vmem_limit_bytes=4 * MIB),
         name="first_stage",
-    )(where, *t, *g)
+    )(where, *packed)
 
 
 def second_stage_kernel(where, *refs):
-    t, g, t_out, g_out = refs[0:4], refs[4:8], refs[8], refs[9]
+    t, g, t_out, g_out = refs[0:4], refs[4:8], refs[-2], refs[-1]
     for k in range(NY):
         start = pl.multiple_of(16 * ((where[1] - k) % NY), 16)
         t_out[pl.ds(start, 16), :] = t[k][...]
-    for k in range(NZ):
-        start = pl.multiple_of(384 * ((where[2] - k) % NZ), 128)
-        g_out[:, pl.ds(start, 384)] = g[k][...]
-
-
-def run_second_stage(where, t, g):
+    for k in range(NX):
+        g_out[k * 64 : (k + 1) * 64, :] = g[k][...]
+
+
+def run_second_stage(where, t, g, before):
     return pl.pallas_call(
         second_stage_kernel,
         out_shape=[jax.ShapeDtypeStruct((64, D), BF), jax.ShapeDtypeStruct((HALF, 1536), BF)],
-        in_specs=[SMEM_SPEC] + vmem_specs(8),
+        in_specs=[SMEM_SPEC] + vmem_specs(8) + [pl.BlockSpec(memory_space=pl.ANY)] * len(before),
         out_specs=vmem_specs(2),
         compiler_params=pltpu.CompilerParams(vmem_limit_bytes=4 * MIB),
         name="second_stage",
-    )(where, *t, *g)
+    )(where, *t, *g, *before)
+
+
+def halves_kernel(t_low, t_high, g_low, g_high, a, b, c, d):
+    a[...] = t_low[0:32, :]
+    b[...] = t_high[32:64, :]
+    c[...] = g_low[0:128, :]
+    d[...] = g_high[128:256, :]
+
+
+def run_halves(t_low, t_high, g_low, g_high):
+    return pl.pallas_call(
+        halves_kernel,
+        out_shape=[jax.ShapeDtypeStruct((32, D), BF)] * 2
+        + [jax.ShapeDtypeStruct((128, 1536), BF)] * 2,
+        in_specs=vmem_specs(4),
+        out_specs=vmem_specs(4),
+        compiler_params=pltpu.CompilerParams(vmem_limit_bytes=4 * MIB),
+        name="halves",
+    )(t_low, t_high, g_low, g_high)
 
 
 def relay_kernel(*refs):
@@ -147,34 +187,51 @@
 
 
 def row_copies(pieces, rows, sem):
+    places = (0, 64, 192, 128, 160)
     return [
-        pltpu.make_async_copy(piece, rows.at[pl.ds(r * 64, 64), :], sem.at[r])
-        for r, piece in enumerate(pieces)
+        pltpu.make_async_copy(piece, rows.at[pl.ds(at, piece.shape[0]), :], sem.at[r])
+        for r, (piece, at) in enumerate(zip(pieces, places))
     ]
 
 
-def grad_copies(pieces, grads, sem, y, sign):
+def grad_copies(pieces, grads, sem, y):
+    places = ((0, 0), (-1, 0), (1, 0), (2, 0), (2, 128))
     copies = []
-    for j, piece in enumerate(pieces):
-        start = pl.multiple_of(((y - sign * j) % NY) * 1536, 128)
+    for j, (piece, (step, at)) in enumerate(zip(pieces, places)):
+        start = pl.multiple_of(((y + step + NY) % NY) * 1536, 128)
         copies.append(
-            pltpu.make_async_copy(piece, grads.at[:, pl.ds(start, 1536)], sem.at[j])
+            pltpu.make_async_copy(
+                piece, grads.at[pl.ds(at, piece.shape[0]), pl.ds(start, 1536)], sem.at[j]
+            )
         )
     return copies
 
 
+def split_three(value):
+    high = value.astype(BF)
+    rest = value - high.astype(F32)
+    middle = rest.astype(BF)
+    low = (rest - middle.astype(F32)).astype(BF)
+    return jnp.concatenate([high, middle, low], axis=1)
+
+
+def join_three(parts):
+    out = parts.astype(F32)
+    return out[:, 0:128] + out[:, 128:256] + out[:, 256:384]
+
+
 def main_kernel(where, *refs):
-    t_in, g_in = refs[0:4], refs[4:8]
-    weights = (refs[8:11], refs[11:14])
-    slots_ref, gates_ref = refs[14:16]
-    pa_out, pb_out = refs[16:20], refs[20:24]
-    own_out, sib_out, rp_ref, rows_out, grads_out = refs[24:29]
+    t_in, g_in = refs[0:5], refs[5:10]
+    weights = (refs[10:13], refs[13:16])
+    slots_ref, gates_ref = refs[16:18]
+    pa_out, pb_out = refs[18:22], refs[22:26]
+    own_out, rows_out, grads_out = refs[26:29]
     rows, grads, wv, dv, pa, pb = refs[29:35]
     acc_g, acc_b, deltas, tile, rbuf, packed = refs[35:41]
     sem_t, sem_g, sem_w, sem_d, sem_o = refs[41:46]
-    x, y, sign, core = where[0], where[1], where[3], where[4]
+    x, y, core = where[0], where[1], where[4]
     copies_t = row_copies(t_in, rows, sem_t)
-    copies_g = grad_copies(g_in, grads, sem_g, y, sign)
+    copies_g = grad_copies(g_in, grads, sem_g, y)
     tiles = D // KT
 
     def wide_copies(i):
@@ -210,14 +267,14 @@
     slot = lax.broadcasted_iota(jnp.int32, (HALF, 256), 1)
     row = lax.broadcasted_iota(jnp.int32, (HALF, 256), 0)
     block = row // 64
-    token = ((x - sign * block + NX) % NX) * 128 + core * 64 + (row - block * 64)
+    token = ((x - block + NX) % NX) * 128 + core * 64 + (row - block * 64)
     for e in range(2):
         hit = (token == slots_ref[e : e + 1, :]) & (slot < where[5 + e])
         gate = jnp.broadcast_to(gates_ref[e : e + 1, :], (HALF, 256))
         scales.append(jnp.sum(jnp.where(hit, gate, 0.0), axis=1, keepdims=True))
     for copy in copies_t:
         copy.wait()
-    rows_copy = pltpu.make_async_copy(rows, rows_out, sem_o.at[0])
+    rows_copy = pltpu.make_async_copy(rows, rows_out.at[:, pl.ds(0, D)], sem_o.at[0])
     grads_copy = pltpu.make_async_copy(grads, grads_out, sem_o.at[1])
 
     @pl.loop(0, tiles)
@@ -264,15 +321,20 @@
             packed[s, :, e * 256 + H : (e + 1) * 256] = up_delta
             packed[s, :, 512 + e * H : 512 + (e + 1) * H] = (hidden * scale).astype(BF)
     own_copy = pltpu.make_async_copy(packed.at[0], own_out, sem_o.at[2])
-    sib_copy = pltpu.make_async_copy(packed.at[1], sib_out, sem_o.at[3])
+    sib_copy = pltpu.make_async_copy(packed.at[1], rows_out.at[:, pl.ds(D, 768)], sem_o.at[3])
     own_copy.start()
     sib_copy.start()
     lane = lax.broadcasted_iota(jnp.int32, (HALF, 128), 1)
     spread = jnp.where(lane == 0, router[0], jnp.where(lane == 1, router[1], 0.0))
     for k in range(NX):
-        to = pl.multiple_of(((x - sign * k) % NX) * 64, 64)
+        to = pl.multiple_of(((x - k) % NX) * 64, 64)
         rbuf[pl.ds(to, 64), :] = spread[k * 64 : (k + 1) * 64]
-    rp_ref[...] = rbuf[...].T[0:8]
+    line = rbuf[...].T[0:2]
+    four = [line[e : e + 1, h * 128 : (h + 1) * 128] for e in range(2) for h in range(2)]
+    sums = split_three(jnp.concatenate(four + [jnp.zeros((12, 128), F32)], axis=0))
+    for k in range(NX):
+        pa[k, :, D // 2 :] = jnp.zeros((64, 384), BF)
+        pa[k, 0:16, D // 2 :] = sums
 
     def partial(i):
         f = pl.ds(pl.multiple_of(i * FT, FT), FT)
@@ -313,23 +375,23 @@
 def run_main(where, t, g, weights, slots, gates):
     hbm = [pl.BlockSpec(memory_space=pltpu.HBM)]
     out_shape = (
-        [jax.ShapeDtypeStruct((64, D // 2), BF)] * 4
+        [jax.ShapeDtypeStruct((64, WIDE), BF)] * 4
         + [jax.ShapeDtypeStruct((4, 16, D // 2), BF)] * 4
-        + [jax.ShapeDtypeStruct((HALF, 768), BF)] * 2
-        + [jax.ShapeDtypeStruct((8, 256), F32)]
-        + [jax.ShapeDtypeStruct((HALF, D), BF)] * 2
+        + [jax.ShapeDtypeStruct((HALF, 768), BF)]
+        + [jax.ShapeDtypeStruct((HALF, D + 768), BF)]
+        + [jax.ShapeDtypeStruct((HALF, D), BF)]
     )
     return pl.pallas_call(
         main_kernel,
         out_shape=out_shape,
-        in_specs=[SMEM_SPEC] + hbm * 14 + vmem_specs(2),
-        out_specs=hbm * 10 + vmem_specs(1) + hbm * 2,
+        in_specs=[SMEM_SPEC] + hbm * 16 + vmem_specs(2),
+        out_specs=hbm * 11,
         scratch_shapes=[
             pltpu.VMEM((HALF, D), BF),
             pltpu.VMEM((HALF, D), BF),
             pltpu.VMEM((2, 2, 2, D, H), BF),
             pltpu.VMEM((2, 2, H, D), BF),
-            pltpu.VMEM((4, 64, D // 2), BF),
+            pltpu.VMEM((4, 64, WIDE), BF),
             pltpu.VMEM((4, 4, 16, D // 2), BF),
             pltpu.VMEM((HALF, 1024), F32),
             pltpu.VMEM((HALF, 512), F32),
@@ -337,8 +399,8 @@
             pltpu.VMEM((HALF, FT), BF),
             pltpu.VMEM((HALF, 128), F32),
             pltpu.VMEM((2, HALF, 768), BF),
-            pltpu.SemaphoreType.DMA((4,)),
-            pltpu.SemaphoreType.DMA((4,)),
+            pltpu.SemaphoreType.DMA((5,)),
+            pltpu.SemaphoreType.DMA((5,)),
             pltpu.SemaphoreType.DMA((D // KT, 4)),
             pltpu.SemaphoreType.DMA((D // KT, 2)),
             pltpu.SemaphoreType.DMA((12,)),
@@ -361,9 +423,10 @@
         up_out[e] = part[:, e * 256 + H : (e + 1) * 256].astype(BF)
 
 
-def run_up(rows_own, rows_sib, own, sib, before):
+def run_up(rows_own, rows_sib, own, before):
     tile = pl.BlockSpec((HALF, FT), lambda i: (0, i))
     whole = pl.BlockSpec((HALF, 768), lambda i: (0, 0))
+    tail = pl.BlockSpec((HALF, 768), lambda i: (0, D // 768))
     out = pl.BlockSpec((2, FT, H), lambda i: (0, i, 0))
     return pl.pallas_call(
         up_kernel,
@@ -373,7 +436,7 @@
             jax.ShapeDtypeStruct((2, D, H), BF),
             jax.ShapeDtypeStruct((8, 128), F32),
         ],
-        in_specs=[tile, tile, whole, whole]
+        in_specs=[tile, tile, whole, tail]
         + [pl.BlockSpec(memory_space=pl.ANY)] * len(before),
         out_specs=[out, out, pl.BlockSpec((8, 128), lambda i: (0, 0))],
         compiler_params=pltpu.CompilerParams(
@@ -383,7 +446,7 @@
             flops=3_200_000_000, bytes_accessed=13_000_000, transcendentals=0
         ),
         name="up_grads",
-    )(rows_own, rows_sib, own, sib, *before)
+    )(rows_own, rows_sib, own, rows_sib, *before)
 
 
 def down_kernel(grads_own, grads_sib, own, sib, out, token, hidden):
@@ -400,9 +463,10 @@
         out[e] = part[e * H : (e + 1) * H].astype(BF)
 
 
-def run_down(grads_own, grads_sib, own, sib):
+def run_down(grads_own, grads_sib, own, rows_sib):
     tile = pl.BlockSpec((HALF, 2 * FT), lambda i: (0, i))
     whole = pl.BlockSpec((HALF, 768), lambda i: (0, 0))
+    tail = pl.BlockSpec((HALF, 768), lambda i: (0, D // 768))
     return pl.pallas_call(
         down_kernel,
         grid=(D // FT // 2,),
@@ -410,7 +474,7 @@
             jax.ShapeDtypeStruct((2, H, D), BF),
             jax.ShapeDtypeStruct((8, 128), F32),
         ],
-        in_specs=[tile, tile, whole, whole],
+        in_specs=[tile, tile, whole, tail],
         out_specs=[
             pl.BlockSpec((2, H, 2 * FT), lambda i: (0, 0, i)),
             pl.BlockSpec((8, 128), lambda i: (0, 0)),
@@ -423,112 +487,109 @@
             flops=1_600_000_000, bytes_accessed=10_000_000, transcendentals=0
         ),
         name="down_grads",
-    )(grads_own, grads_sib, own, sib)
+    )(grads_own, grads_sib, own, rows_sib)
 
 
 def first_sum_kernel(where, *refs):
-    ra, rb, rp, qa, qb, rp_out, buf = (
-        refs[0:4],
-        refs[4:8],
-        refs[8:12],
-        refs[12:16],
-        refs[16:20],
-        refs[20],
-        refs[21],
-    )
-    y = where[1]
-    rp_out[...] = total(rp[0][...], [r[...] for r in rp[1:]])
-    buf[...] = total(ra[0][...], [r[...] for r in ra[1:]]).astype(BF)
+    ra, rb, qa, qb, buf = refs[0:4], refs[4:8], refs[9:13], refs[13:17], refs[17]
+    half = D // 2
+    buf[...] = total(ra[0][:, 0:half], [r[:, 0:half] for r in ra[1:]]).astype(BF)
+    sums = join_three(ra[0][0:16, half:])
+    for r in ra[1:]:
+        sums += join_three(r[0:16, half:])
+    sums = split_three(sums)
     for k in range(NY):
-        start = pl.multiple_of(((y + k) % NY) * 16, 16)
-        qa[k][...] = buf[pl.ds(start, 16), :]
+        start = pl.multiple_of(((where[1] + k) % NY) * 16, 16)
+        qa[k][:, 0:half] = buf[pl.ds(start, 16), :]
+        qa[k][:, half:] = sums
     for k in range(NX):
         qb[k][...] = total(rb[0][k], [r[k] for r in rb[1:]]).astype(BF)
 
 
-def run_first_sum(where, ra, rb, rp):
+def run_first_sum(where, ra, rb, token):
     return pl.pallas_call(
         first_sum_kernel,
-        out_shape=[jax.ShapeDtypeStruct((16, D // 2), BF)] * 8
-        + [jax.ShapeDtypeStruct((8, 256), F32)],
-        in_specs=[SMEM_SPEC] + vmem_specs(12),
-        out_specs=vmem_specs(9),
+        out_shape=[jax.ShapeDtypeStruct((16, WIDE), BF)] * 4
+        + [jax.ShapeDtypeStruct((16, D // 2), BF)] * 4,
+        in_specs=[SMEM_SPEC] + vmem_specs(9),
+        out_specs=vmem_specs(8),
         scratch_shapes=[pltpu.VMEM((64, D // 2), BF)],
         compiler_params=pltpu.CompilerParams(vmem_limit_bytes=8 * MIB),
         name="first_sum",
-    )(where, *ra, *rb, *rp)
+    )(where, *ra, *rb, token)
 
 
 def second_sum_kernel(where, *refs):
-    ra, rb, rp, own, out, rp_out, buf = (
-        refs[0:4],
-        refs[4:8],
-        refs[8:12],
-        refs[14],
-        refs[15:18],
-        refs[18],
-        refs[19],
-    )
-    z = where[2]
-    rp_out[...] = total(rp[0][...], [r[...] for r in rp[1:]])
+    ra, rb, own, out, buf = refs[0:4], refs[4:8], refs[9], refs[10:13], refs[13]
+    half = D // 2
     for n, r in enumerate((ra, rb)):
-        part = total(r[0][...], [p[...] for p in r[1:]])
+        part = total(r[0][:, 0:half], [p[:, 0:half] for p in r[1:]])
         for k in range(NZ):
-            buf[k, :, n * (D // 2) : (n + 1) * (D // 2)] = part[4 * k : 4 * k + 4]
+            buf[k, :, n * half : (n + 1) * half] = part[4 * k : 4 * k + 4]
+    sums = join_three(ra[0][:, half:])
+    for r in ra[1:]:
+        sums += join_three(r[:, half:])
+    parts = split_three(sums)[0:4]
     for k in range(NZ):
-        rows = buf[(z + k) % NZ]
+        rows = buf[(where[2] + k) % NZ]
         if k == 0:
-            own[...] = rows
+            own[:, 0:D] = rows
+            own[:, D:] = sums[0:4]
         else:
-            out[k - 1][...] = rows.astype(BF)
-
-
-def run_second_sum(where, ra, rb, rp, token, other):
+            out[k - 1][:, 0:D] = rows.astype(BF)
+            out[k - 1][:, D:] = parts
+
+
+def run_second_sum(where, ra, rb, token):
     return pl.pallas_call(
         second_sum_kernel,
-        out_shape=[jax.ShapeDtypeStruct((4, D), F32)]
-        + [jax.ShapeDtypeStruct((4, D), BF)] * 3
-        + [jax.ShapeDtypeStruct((8, 256), F32)],
-        in_specs=[SMEM_SPEC] + vmem_specs(14),
-        out_specs=vmem_specs(5),
+        out_shape=[jax.ShapeDtypeStruct((4, D + 128), F32)]
+        + [jax.ShapeDtypeStruct((4, D + 384), BF)] * 3,
+        in_specs=[SMEM_SPEC] + vmem_specs(9),
+        out_specs=vmem_specs(4),
         scratch_shapes=[pltpu.VMEM((NZ, 4, D), F32)],
         compiler_params=pltpu.CompilerParams(vmem_limit_bytes=8 * MIB),
         name="second_sum",
-    )(where, *ra, *rb, *rp, token, other)
-
-
-def last_sum_kernel(*refs):
-    out, rp_out = refs[8], refs[9]
-    out[...] = total(refs[0][...], [r[...] for r in refs[1:4]]).astype(BF)
-    rp_out[...] = total(refs[4][...], [r[...] for r in refs[5:8]])
-
-
-def run_last_sum(pieces, rp):
+    )(where, *ra, *rb, token)
+
+
+def last_sum_kernel(own, *refs):
+    out, sums_out = refs[3], refs[4]
+    out[...] = total(own[:, 0:D], [r[:, 0:D] for r in refs[0:3]]).astype(BF)
+    sums = own[:, D:]
+    for r in refs[0:3]:
+        sums += join_three(r[:, D:])
+    sums_out[0:4, :] = sums
+    sums_out[4:8, :] = jnp.zeros((4, 128), F32)
+
+
+def run_last_sum(pieces):
     return pl.pallas_call(
         last_sum_kernel,
-        out_shape=[jax.ShapeDtypeStruct((4, D), BF), jax.ShapeDtypeStruct((8, 256), F32)],
-        in_specs=vmem_specs(8),
+        out_shape=[jax.ShapeDtypeStruct((4, D), BF), jax.ShapeDtypeStruct((8, 128), F32)],
+        in_specs=vmem_specs(4),
         out_specs=vmem_specs(2),
         compiler_params=pltpu.CompilerParams(vmem_limit_bytes=4 * MIB),
         name="last_sum",
-    )(*pieces, *rp)
+    )(*pieces)
 
 
 def router_kernel(where, own, other, slots_ref, out):
     first = jnp.where(where[4] == 0, own[...], other[...])
     second = jnp.where(where[4] == 0, other[...], own[...])
     slots = slots_ref[...].T
-    index = lax.broadcasted_iota(jnp.int32, (256, 256), 1)
-    lane = lax.broadcasted_iota(jnp.int32, (256, 128), 1)
+    index = lax.broadcasted_iota(jnp.int32, (256, 128), 1)
     spread = jnp.zeros((256, 128), F32)
     for e in range(2):
         picked = jnp.zeros((256, 1), F32)
         for core, values in enumerate((first, second)):
-            token = (index // 64) * 128 + core * 64 + index % 64
-            hit = slots[:, e : e + 1] == token
-            line = jnp.broadcast_to(values[e : e + 1, :], (256, 256))
-            picked += jnp.sum(jnp.where(hit, line, 0.0), axis=1, keepdims=True)
-        spread = jnp.where(lane == e, picked, spread)
+            for h in range(2):
+                at = index + h * 128
+                token = (at // 64) * 128 + core * 64 + at % 64
+                hit = slots[:, e : e + 1] == token
+                line = jnp.broadcast_to(values[2 * e + h : 2 * e + h + 1, :], (256, 128))
+                picked += jnp.sum(jnp.where(hit, line, 0.0), axis=1, keepdims=True)
+        spread = jnp.where(index == e, picked, spread)
     lines = spread.T
     at = lax.broadcasted_iota(jnp.int32, (1, 256), 1)
     for e in range(2):
@@ -550,42 +611,39 @@
     tokens_in, out_grad, gate_weight, up_weight, down_weight, slot_tokens, slot_counts, slot_gates
 ):
     x, c, y, z = position()
-    where = jnp.stack([x, y, z, 1 - 2 * c, c, slot_counts[0], slot_counts[1]]).astype(jnp.int32)
-
-    t = [tokens_in] + [shift(tokens_in, "z", k) for k in (1, 2, 3)]
-    g = [out_grad] + [shift(out_grad, "x", k, True) for k in (1, 2, 3)]
-    t16, g4 = run_first_stage(where, t, g)
-    weights = (gate_weight, up_weight, down_weight)
-    weights += tuple(swap(w) for w in weights)
+    where = jnp.stack([x, y, z, c, c, slot_counts[0], slot_counts[1]]).astype(jnp.int32)
+    gate_sib, up_sib = swap(gate_weight), swap(up_weight)
+
+    packed = run_pack(tokens_in, out_grad)
+    t16, g64 = run_first_stage(where, [packed] + [shift(packed, "z", k) for k in (1, 2, 3)])
     t = [t16] + [shift(t16, "y", k) for k in (1, 2, 3)]
-    g = [g4] + [shift(g4, "z", k) for k in (1, 2, 3)]
-    t64, g_z = run_second_stage(where, t, g)
-    t, g = [t64], [g_z]
-    for _ in range(3):
-        t.append(shift(t[-1], "x", 1, True))
-        g.append(shift(g[-1], "y", 1, True))
+    g = [g64] + [shift(g64, "x", k) for k in (1, 2, 3)]
+    down_sib = swap(down_weight)
+    t64, g256 = run_second_stage(where, t, g, [gate_sib, up_sib])
+    t_low, t_high = shift(t64, "x", 1), shift(t64, "x", -1)
+    g_low, g_high = shift(g256, "y", 1), shift(g256, "y", -1)
+    a, b, e, f = run_halves(t_low, t_high, g_low, g_high)
+    t = (t64, t_low, t_high, shift(a, "x", 1), shift(b, "x", -1))
+    g = (g256, g_low, g_high, shift(e, "y", 1), shift(f, "y", -1))
+    weights = (gate_weight, up_weight, down_weight, gate_sib, up_sib, down_sib)
     outs = run_main(where, t, g, weights, slot_tokens, slot_gates)
     pa, pb = outs[0:4], outs[4:8]
-    dl_own, dl_sib, rp, rows, grads = outs[8:]
-
-    ra = [pa[0]] + [shift(pa[k], "x", -k, True) for k in (1, 2, 3)]
+    dl_own, rows, grads = outs[8:]
+
+    ra = [pa[0]] + [shift(pa[k], "x", -k) for k in (1, 2, 3)]
     rb = [pb[0]] + [shift(pb[k], "y", k) for k in (1, 2, 3)]
-    dl_got, rows_sib = swap(dl_sib), swap(rows)
+    rows_sib = swap(rows)
     before = [ra[1], ra[3], rb[1], rb[3]]
     grads_sib = swap(run_relay(grads, before))
-    gate_grad, up_grad, up_token = run_up(rows, rows_sib, dl_own, dl_got, before)
-    rps = [rp] + [shift(rp, "z", k) for k in (1, 2, 3)]
-    q = run_first_sum(where, ra, rb, rps)
-    qa, qb, rp = q[0:4], q[4:8], q[8]
+    gate_grad, up_grad, token = run_up(rows, rows_sib, dl_own, before)
+    q = run_first_sum(where, ra, rb, token)
+    qa, qb = q[0:4], q[4:8]
     ra = [qa[0]] + [shift(qa[k], "y", k) for k in (1, 2, 3)]
-    rb = [qb[0]] + [shift(qb[k], "x", -k, True) for k in (1, 2, 3)]
-    rps = [rp] + [shift(rp, "x", k) for k in (1, 2, 3)]
-    down_grad, token = run_down(grads, grads_sib, dl_own, dl_got)
-    q = run_second_sum(where, ra, rb, rps, up_token, token)
-    rz = [q[0]] + [shift(q[k], "z", k) for k in (1, 2, 3)]
-    rps = [q[4]] + [shift(q[4], "y", k) for k in (1, 2, 3)]
-    input_grad, rp = run_last_sum(rz, rps)
-    router_grad = run_router(where, rp, swap(rp), slot_tokens)
+    rb = [qb[0]] + [shift(qb[k], "x", -k) for k in (1, 2, 3)]
+    down_grad, token = run_down(grads, grads_sib, dl_own, rows_sib)
+    q = run_second_sum(where, ra, rb, token)
+    input_grad, sums = run_last_sum([q[0]] + [shift(q[k], "z", k) for k in (1, 2, 3)])
+    router_grad = run_router(where, sums, swap(sums), slot_tokens)
     return (input_grad, gate_grad, up_grad, down_grad, router_grad)
 
 

time: 194 us -> 163 us (0.84)
  starting transfers between devices: 89.1 us -> 54.3 us
  waiting for transfers between devices: 59.2 us -> 64.1 us
  local copies, waits for them, and re-layouts: 7.23 us -> 5.22 us
    ppermute x42 -> x32, starting transfers between devices: 61.6 us -> 39.7 us  [shift(): return lax.ppermute(value, AXES, shift_pairs(axis, step))]
    ppermute x7 -> x6, starting transfers between devices: 27.5 us -> 14.5 us  [swap(): return lax.ppermute(value, AXES, pairs)]
    ppermute x42 -> x32, waiting for transfers between devices: 58.4 us -> 63.2 us  [shift(): return lax.ppermute(value, AXES, shift_pairs(axis, step))]
    unnamed x16, local copies, waits for them, and re-layouts: 6.5 us -> 4.49 us
  transfers between devices with their start and end apart: 49 -> 38, of which waited for: 20 -> 20; matrix products, arithmetic and copies ran while one was open for 0% -> 0% of each run, Pallas kernels for 8% -> 10%
where the time goes in v1:
time: 163 us
  waiting for transfers between devices  64.1 us (39%)
  starting transfers between devices  54.3 us (33%)
  Pallas kernels  38.2 us (23%)
  local copies, waits for them, and re-layouts  5.22 us (3%)
    ppermute x32, waiting for transfers between devices, shift(): return lax.ppermute(value, AXES, shift_pairs(axis, step))  63.2 us
    ppermute x32, starting transfers between devices, shift(): return lax.ppermute(value, AXES, shift_pairs(axis, step))  39.7 us
    pallas_call x1, Pallas kernels, run_main(): pl.pallas_call(main_kernel, out_shape=out_shape, in_specs=[SMEM_SPEC] + h...  18.9 us
    ppermute x6, starting transfers between devices, swap(): return lax.ppermute(value, AXES, pairs)  14.5 us
    pallas_call x1, Pallas kernels, run_up(): pl.pallas_call(up_kernel, grid=(D // FT,), out_shape=[jax.ShapeDtypeStruc...  8.67 us
    pallas_call x1, Pallas kernels, run_down(): pl.pallas_call(down_kernel, grid=(D // FT // 2,), out_shape=[jax.ShapeDty...  4.6 us
    unnamed x16, local copies, waits for them, and re-layouts  4.49 us
  transfers between devices with their start and end apart: 38, of which 20 were waited for; matrix products, arithmetic and copies ran while one was open for 0% of the time, Pallas kernels for 10%

profile of v1, /device:TPU:1, one launch (start us, length us, event | category | flops | bytes accessed | tf_op | source)
XLA Modules:
  0.0 162.5 jit_solution(947875288867722695)
XLA Ops:
  0.6 1.5 collective-permute-start.9
  4.3 3.9 %collective-permute-start.2 = (bf16[128,384]{1,0:T(8,128)(2,1)S(1)}, bf16[128,384]{1,0:T(8,128)(2,1)S(1)}, u32[]{:S(2)}, u32[]{:S(2)}) collective-permute-start(bf16[128,384]{1,0:T(8,128)(2,1)S(1)} %pack.1.refs_0_), channel_id=1, source_target_pairs={{0,3},{1,0},{2,1},{3,2},{4,7},{5,4},{6,5},{7,6},{8,11},{9,8},{10,9... | collective-permute-start | bytes 294920 | tf_op jit(solution)/shard_map/ppermute | solution.py:38
  8.2 4.1 %collective-permute-done.2.refs_3_ = bf16[128,384]{1,0:T(8,128)(2,1)S(1)} collective-permute-done((bf16[128,384]{1,0:T(8,128)(2,1)S(1)}, bf16[128,384]{1,0:T(8,128)(2,1)S(1)}, u32[]{:S(2)}, u32[]{:S(2)}) %collective-permute-start.2) | collective-permute-done | bytes 98336 | tf_op jit(solution)/shard_map/ppermute | solution.py:38
  13.7 4.5 %collective-permute-done.refs_1_ = bf16[128,384]{1,0:T(8,128)(2,1)S(1)} collective-permute-done((bf16[128,384]{1,0:T(8,128)(2,1)S(1)}, bf16[128,384]{1,0:T(8,128)(2,1)S(1)}, u32[]{:S(2)}, u32[]{:S(2)}) %collective-permute-start) | collective-permute-done | bytes 98336 | tf_op jit(solution)/shard_map/ppermute | solution.py:38
  18.8 2.8 %collective-permute-start.5 = (bf16[16,6144]{1,0:T(8,128)(2,1)S(1)}, bf16[16,6144]{1,0:T(8,128)(2,1)S(1)}, u32[]{:S(2)}, u32[]{:S(2)}) collective-permute-start(bf16[16,6144]{1,0:T(8,128)(2,1)S(1)} %get-tuple-element.43.refs_0_), channel_id=1, source_target_pairs={{0,12},{1,13},{2,14},{3,15},{4,0},{5,1},{6,2},{7,3},{8,4},{9,5},{1... | collective-permute-start | bytes 589832 | tf_op jit(solution)/shard_map/ppermute | solution.py:38
  22.0 4.6 %collective-permute-done.5.refs_3_ = bf16[16,6144]{1,0:T(8,128)(2,1)S(1)} collective-permute-done((bf16[16,6144]{1,0:T(8,128)(2,1)S(1)}, bf16[16,6144]{1,0:T(8,128)(2,1)S(1)}, u32[]{:S(2)}, u32[]{:S(2)}) %collective-permute-start.5) | collective-permute-done | bytes 196640 | tf_op jit(solution)/shard_map/ppermute | solution.py:38
  27.7 2.5 %collective-permute-start.8 = (bf16[64,1536]{1,0:T(8,128)(2,1)S(1)}, bf16[64,1536]{1,0:T(8,128)(2,1)S(1)}, u32[]{:S(2)}, u32[]{:S(2)}) collective-permute-start(bf16[64,1536]{1,0:T(8,128)(2,1)S(1)} %get-tuple-element.44.refs_4_), channel_id=1, source_target_pairs={{0,96},{1,97},{2,98},{3,99},{4,100},{5,101},{6,102},{7,103},{8,104... | collective-permute-start | bytes 589832 | tf_op jit(solution)/shard_map/ppermute | solution.py:38
  30.2 5.9 %collective-permute-done.3.refs_1_ = bf16[16,6144]{1,0:T(8,128)(2,1)S(1)} collective-permute-done((bf16[16,6144]{1,0:T(8,128)(2,1)S(1)}, bf16[16,6144]{1,0:T(8,128)(2,1)S(1)}, u32[]{:S(2)}, u32[]{:S(2)}) %collective-permute-start.3) | collective-permute-done | bytes 196640 | tf_op jit(solution)/shard_map/ppermute | solution.py:38
  36.0 2.7 %collective-permute-start.7 = (bf16[64,1536]{1,0:T(8,128)(2,1)S(1)}, bf16[64,1536]{1,0:T(8,128)(2,1)S(1)}, u32[]{:S(2)}, u32[]{:S(2)}) collective-permute-start(bf16[64,1536]{1,0:T(8,128)(2,1)S(1)} %get-tuple-element.44.refs_4_), channel_id=1, source_target_pairs={{0,64},{1,65},{2,66},{3,67},{4,68},{5,69},{6,70},{7,71},{8,72},{9,... | collective-permute-start | bytes 589832 | tf_op jit(solution)/shard_map/ppermute | solution.py:38
  39.1 3.0 %collective-permute-done.7.refs_6_ = bf16[64,1536]{1,0:T(8,128)(2,1)S(1)} collective-permute-done((bf16[64,1536]{1,0:T(8,128)(2,1)S(1)}, bf16[64,1536]{1,0:T(8,128)(2,1)S(1)}, u32[]{:S(2)}, u32[]{:S(2)}) %collective-permute-start.7) | collective-permute-done | bytes 196640 | tf_op jit(solution)/shard_map/ppermute | solution.py:38
  42.1 5.0 %collective-permute-done.6.refs_5_ = bf16[64,1536]{1,0:T(8,128)(2,1)S(1)} collective-permute-done((bf16[64,1536]{1,0:T(8,128)(2,1)S(1)}, bf16[64,1536]{1,0:T(8,128)(2,1)S(1)}, u32[]{:S(2)}, u32[]{:S(2)}) %collective-permute-start.6) | collective-permute-done | bytes 196640 | tf_op jit(solution)/shard_map/ppermute | solution.py:38
  48.8 1.5 collective-permute-start.11
  51.7 13.8 %collective-permute-done.12.t_high.refs_2_ = bf16[64,6144]{1,0:T(8,128)(2,1)S(1)} collective-permute-done((bf16[64,6144]{1,0:T(8,128)(2,1)S(1)}, bf16[64,6144]{1,0:T(8,128)(2,1)S(1)}, u32[]{:S(2)}, u32[]{:S(2)}) %collective-permute-start.12) | collective-permute-done | bytes 786464 | tf_op jit(solution)/shard_map/ppermute | solution.py:38
  67.6 2.0 %collective-permute-start.16 = (bf16[32,6144]{1,0:T(8,128)(2,1)S(1)}, bf16[32,6144]{1,0:T(8,128)(2,1)S(1)}, u32[]{:S(2)}, u32[]{:S(2)}) collective-permute-start(bf16[32,6144]{1,0:T(8,128)(2,1)S(1)} %get-tuple-element.48), channel_id=1, source_target_pairs={{0,96},{1,97},{2,98},{3,99},{4,100},{5,101},{6,102},{7,103},{8,104... | collective-permute-start | bytes 1179656 | tf_op jit(solution)/shard_map/ppermute | solution.py:38
  70.4 1.9 %collective-permute-start.18 = (bf16[128,1536]{1,0:T(8,128)(2,1)S(1)}, bf16[128,1536]{1,0:T(8,128)(2,1)S(1)}, u32[]{:S(2)}, u32[]{:S(2)}) collective-permute-start(bf16[128,1536]{1,0:T(8,128)(2,1)S(1)} %get-tuple-element.50), channel_id=1, source_target_pairs={{0,12},{1,13},{2,14},{3,15},{4,0},{5,1},{6,2},{7,3},{8,4},{9,5},{1... | collective-permute-start | bytes 1179656 | tf_op jit(solution)/shard_map/ppermute | solution.py:38
  72.3 2.5 %collective-permute-done.15.refs_3_ = bf16[32,6144]{1,0:T(8,128)(2,1)S(1)} collective-permute-done((bf16[32,6144]{1,0:T(8,128)(2,1)S(1)}, bf16[32,6144]{1,0:T(8,128)(2,1)S(1)}, u32[]{:S(2)}, u32[]{:S(2)}) %collective-permute-start.15) | collective-permute-done | bytes 393248 | tf_op jit(solution)/shard_map/ppermute | solution.py:38
  74.8 3.0 %collective-permute-done.17.refs_8_ = bf16[128,1536]{1,0:T(8,128)(2,1)S(1)} collective-permute-done((bf16[128,1536]{1,0:T(8,128)(2,1)S(1)}, bf16[128,1536]{1,0:T(8,128)(2,1)S(1)}, u32[]{:S(2)}, u32[]{:S(2)}) %collective-permute-start.17) | collective-permute-done | bytes 393248 | tf_op jit(solution)/shard_map/ppermute | solution.py:38
  77.8 18.9 %main.1 = (bf16[64,3456]{1,0:T(8,128)(2,1)S(1)}, bf16[64,3456]{1,0:T(8,128)(2,1)S(1)}, bf16[64,3456]{1,0:T(8,128)(2,1)S(1)}, bf16[64,3456]{1,0:T(8,128)(2,1)S(1)...) custom-call(s32[7]{0:T(128)S(1)} %stack.20.where, ...), custom_call_target="tpu_custom_call" | custom-call | flops 8000000000 | bytes 30000000 | tf_op jit(solution)/shard_map/main/pallas_call | solution.py:384
  96.7 7.2 %collective-permute-start.26 = (bf16[256,6912]{1,0:T(8,128)(2,1)}, bf16[256,6912]{1,0:T(8,128)(2,1)S(1)}, u32[]{:S(2)}, u32[]{:S(2)}) collective-permute-start(bf16[256,6912]{1,0:T(8,128)(2,1)} %get-tuple-element.59.refs_0_), channel_id=1, source_target_pairs={{0,16},{1,17},{2,18},{3,19},{4,20},{5,21},{6,22},{7,23},{8,24},{9,... | collective-permute-start | bytes 10616840 | tf_op jit(solution)/shard_map/ppermute | solution.py:49
  103.9 1.5 collective-permute-start.22
  105.9 2.4 %collective-permute-start.25 = (bf16[4,16,3072]{2,1,0:T(8,128)(2,1)S(1)}, bf16[4,16,3072]{2,1,0:T(8,128)(2,1)S(1)}, u32[]{:S(2)}, u32[]{:S(2)}) collective-permute-start(bf16[4,16,3072]{2,1,0:T(8,128)(2,1)S(1)} %get-tuple-element.58), channel_id=1, source_target_pairs={{0,12},{1,13},{2,14},{3,15},{4,0},{5,1},{6,2},{7,3},{8,4},{9,5},{1... | collective-permute-start | bytes 1179656 | tf_op jit(solution)/shard_map/ppermute | solution.py:38
  108.3 8.8 %collective-permute-done.23.refs_6_.refs_5_.refs_3_ = bf16[4,16,3072]{2,1,0:T(8,128)(2,1)S(1)} collective-permute-done((bf16[4,16,3072]{2,1,0:T(8,128)(2,1)S(1)}, bf16[4,16,3072]{2,1,0:T(8,128)(2,1)S(1)}, u32[]{:S(2)}, u32[]{:S(2)}) %collective-permute-start.23) | collective-permute-done | bytes 393248 | tf_op jit(solution)/shard_map/ppermute | solution.py:38
  117.1 1.9 %copy-done = bf16[256,6144]{1,0:T(8,128)(2,1)S(1)} copy-done((bf16[256,6144]{1,0:T(8,128)(2,1)S(1)}, bf16[256,6144]{1,0:T(8,128)(2,1)}, u32[]{:S(2)}) %copy-start) | copy-done | bytes 3145752
  119.2 1.3 collective-permute-start.33
  120.7 2.6 %collective-permute-start.24 = (bf16[4,16,3072]{2,1,0:T(8,128)(2,1)S(1)}, bf16[4,16,3072]{2,1,0:T(8,128)(2,1)S(1)}, u32[]{:S(2)}, u32[]{:S(2)}) collective-permute-start(bf16[4,16,3072]{2,1,0:T(8,128)(2,1)S(1)} %get-tuple-element.57), channel_id=1, source_target_pairs={{0,8},{1,9},{2,10},{3,11},{4,12},{5,13},{6,14},{7,15},{8,0},{9,1},... | collective-permute-start | bytes 1179656 | tf_op jit(solution)/shard_map/ppermute | solution.py:38
  123.4 8.7 %up_grads.1 = (bf16[2,6144,128]{2,1,0:T(8,128)(2,1)}, bf16[2,6144,128]{2,1,0:T(8,128)(2,1)}, f32[8,128]{1,0:T(8,128)S(1)}) custom-call(bf16[256,6912]{1,0:T(8,128)(2,1)S(1)} %copy-done.2, bf16[256,6912]{1,0:T(8,128)(2,1)S(1)} %collective-permute-done.26.refs_1_.refs_3_.sib, bf16[256,768]{1,0:T(8,128)(2,1)S(1)} %get-tuple-element.60.refs_2_.own, ...), custom_call_target="tpu_custom_call" | custom-call | flops 3200000000 | bytes 13000000 | tf_op jit(solution)/shard_map/up_grads/pallas_call | solution.py:431
  138.4 3.0 %collective-permute-start.28 = (bf16[16,3456]{1,0:T(8,128)(2,1)S(1)}, bf16[16,3456]{1,0:T(8,128)(2,1)S(1)}, u32[]{:S(2)}, u32[]{:S(2)}) collective-permute-start(bf16[16,3456]{1,0:T(8,128)(2,1)S(1)} %get-tuple-element.64), channel_id=1, source_target_pairs={{0,8},{1,9},{2,10},{3,11},{4,12},{5,13},{6,14},{7,15},{8,0},{9,1},... | collective-permute-start | bytes 331784 | tf_op jit(solution)/shard_map/ppermute | solution.py:38
  142.2 4.6 %down_grads.1 = (bf16[2,128,6144]{2,1,0:T(8,128)(2,1)}, f32[8,128]{1,0:T(8,128)S(1)}) custom-call(bf16[256,6144]{1,0:T(8,128)(2,1)S(1)} %copy-done.1, bf16[256,6144]{1,0:T(8,128)(2,1)S(1)} %collective-permute-done.33.grads_sib, bf16[256,768]{1,0:T(8,128)(2,1)S(1)} %get-tuple-element.60.refs_2_.own, ...), custom_call_target="tpu_custom_call" | custom-call | flops 1600000000 | bytes 10000000 | tf_op jit(solution)/shard_map/down_grads/pallas_call | solution.py:470
  147.7 4.3 %collective-permute-start.35 = (bf16[4,6528]{1,0:T(4,128)(2,1)S(1)}, bf16[4,6528]{1,0:T(4,128)(2,1)S(1)}, u32[]{:S(2)}, u32[]{:S(2)}) collective-permute-start(bf16[4,6528]{1,0:T(4,128)(2,1)S(1)} %get-tuple-element.74), channel_id=1, source_target_pairs={{0,2},{1,3},{2,0},{3,1},{4,6},{5,7},{6,4},{7,5},{8,10},{9,11},{10,... | collective-permute-start | bytes 156680 | tf_op jit(solution)/shard_map/ppermute | solution.py:38
  152.3 1.7 %collective-permute-done.35.refs_1_ = bf16[4,6528]{1,0:T(4,128)(2,1)S(1)} collective-permute-done((bf16[4,6528]{1,0:T(4,128)(2,1)S(1)}, bf16[4,6528]{1,0:T(4,128)(2,1)S(1)}, u32[]{:S(2)}, u32[]{:S(2)}) %collective-permute-start.35) | collective-permute-done | bytes 52256 | tf_op jit(solution)/shard_map/ppermute | solution.py:38
  155.9 4.0 %collective-permute-start.37 = (f32[8,128]{1,0:T(8,128)S(1)}, f32[8,128]{1,0:T(8,128)S(1)}, u32[]{:S(2)}, u32[]{:S(2)}) collective-permute-start(f32[8,128]{1,0:T(8,128)S(1)} %get-tuple-element.80.own), channel_id=1, source_target_pairs={{0,16},{1,17},{2,18},{3,19},{4,20},{5,21},{6,22},{7,23},{8,24},{9,... | collective-permute-start | bytes 12296 | tf_op jit(solution)/shard_map/ppermute | solution.py:49
  160.7 1.8 %router.1 = f32[2,256]{1,0:T(2,128)} custom-call(s32[7]{0:T(128)S(1)} %stack.20.where, f32[8,128]{1,0:T(8,128)S(1)} %get-tuple-element.80.own, f32[8,128]{1,0:T(8,128)S(1)} %collective-permute-done.37.other, s32[2,256]{1,0:T(2,128)S(1)} %copy-done.6), custom_call_target="tpu_custom_call" | custom-call | tf_op jit(solution)/shard_map/router/pallas_call | solution.py:600
  (73 shorter events, 23.9 us)
Async XLA Ops:
  0.6 46.5 %collective-permute-start.9 = (bf16[2,6144,128]{2,1,0:T(8,128)(2,1)}, bf16[2,6144,128]{2,1,0:T(8,128)(2,1)S(1)}, u32[]{:S(2)}, u32[]{:S(2)}) collective-permute-start(bf16[2,6144,128]{2,1,0:T(8,128)(2,1)} %refs_10_.1), channel_id=1, source_target_pairs={{0,16},{1,17},{2,18},{3,19},{4,20},{5,21},{6,22},{7,23},{8,24},{9,... | collective-permute-start | bytes 9437192 | tf_op jit(solution)/shard_map/ppermute | solution.py:49
  2.1 45.0 %collective-permute-start.10 = (bf16[2,6144,128]{2,1,0:T(8,128)(2,1)}, bf16[2,6144,128]{2,1,0:T(8,128)(2,1)}, u32[]{:S(2)}, u32[]{:S(2)}) collective-permute-start(bf16[2,6144,128]{2,1,0:T(8,128)(2,1)} %refs_11_.1), channel_id=1, source_target_pairs={{0,16},{1,17},{2,18},{3,19},{4,20},{5,21},{6,22},{7,23},{8,24},{9,... | collective-permute-start | bytes 9437192 | tf_op jit(solution)/shard_map/ppermute | solution.py:49
  2.2 70.1 %collective-permute-start.19 = (bf16[2,128,6144]{2,1,0:T(8,128)(2,1)}, bf16[2,128,6144]{2,1,0:T(8,128)(2,1)}, u32[]{:S(2)}, u32[]{:S(2)}) collective-permute-start(bf16[2,128,6144]{2,1,0:T(8,128)(2,1)} %refs_12_.1), channel_id=1, source_target_pairs={{0,16},{1,17},{2,18},{3,19},{4,20},{5,21},{6,22},{7,23},{8,24},{9,... | collective-permute-start | bytes 9437192 | tf_op jit(solution)/shard_map/ppermute | solution.py:49
  4.3 8.0 %collective-permute-start.2 = (bf16[128,384]{1,0:T(8,128)(2,1)S(1)}, bf16[128,384]{1,0:T(8,128)(2,1)S(1)}, u32[]{:S(2)}, u32[]{:S(2)}) collective-permute-start(bf16[128,384]{1,0:T(8,128)(2,1)S(1)} %pack.1.refs_0_), channel_id=1, source_target_pairs={{0,3},{1,0},{2,1},{3,2},{4,7},{5,4},{6,5},{7,6},{8,11},{9,8},{10,9... | collective-permute-start | bytes 294920 | tf_op jit(solution)/shard_map/ppermute | solution.py:38
  18.8 7.7 %collective-permute-start.5 = (bf16[16,6144]{1,0:T(8,128)(2,1)S(1)}, bf16[16,6144]{1,0:T(8,128)(2,1)S(1)}, u32[]{:S(2)}, u32[]{:S(2)}) collective-permute-start(bf16[16,6144]{1,0:T(8,128)(2,1)S(1)} %get-tuple-element.43.refs_0_), channel_id=1, source_target_pairs={{0,12},{1,13},{2,14},{3,15},{4,0},{5,1},{6,2},{7,3},{8,4},{9,5},{1... | collective-permute-start | bytes 589832 | tf_op jit(solution)/shard_map/ppermute | solution.py:38
  21.7 6.0 %collective-permute-start.4 = (bf16[16,6144]{1,0:T(8,128)(2,1)S(1)}, bf16[16,6144]{1,0:T(8,128)(2,1)S(1)}, u32[]{:S(2)}, u32[]{:S(2)}) collective-permute-start(bf16[16,6144]{1,0:T(8,128)(2,1)S(1)} %get-tuple-element.43.refs_0_), channel_id=1, source_target_pairs={{0,8},{1,9},{2,10},{3,11},{4,12},{5,13},{6,14},{7,15},{8,0},{9,1},... | collective-permute-start | bytes 589832 | tf_op jit(solution)/shard_map/ppermute | solution.py:38
  26.6 9.5 %collective-permute-start.3 = (bf16[16,6144]{1,0:T(8,128)(2,1)S(1)}, bf16[16,6144]{1,0:T(8,128)(2,1)S(1)}, u32[]{:S(2)}, u32[]{:S(2)}) collective-permute-start(bf16[16,6144]{1,0:T(8,128)(2,1)S(1)} %get-tuple-element.43.refs_0_), channel_id=1, source_target_pairs={{0,4},{1,5},{2,6},{3,7},{4,8},{5,9},{6,10},{7,11},{8,12},{9,13},{1... | collective-permute-start | bytes 589832 | tf_op jit(solution)/shard_map/ppermute | solution.py:38
  27.7 11.1 %collective-permute-start.8 = (bf16[64,1536]{1,0:T(8,128)(2,1)S(1)}, bf16[64,1536]{1,0:T(8,128)(2,1)S(1)}, u32[]{:S(2)}, u32[]{:S(2)}) collective-permute-start(bf16[64,1536]{1,0:T(8,128)(2,1)S(1)} %get-tuple-element.44.refs_4_), channel_id=1, source_target_pairs={{0,96},{1,97},{2,98},{3,99},{4,100},{5,101},{6,102},{7,103},{8,104... | collective-permute-start | bytes 589832 | tf_op jit(solution)/shard_map/ppermute | solution.py:38
  36.0 6.0 %collective-permute-start.7 = (bf16[64,1536]{1,0:T(8,128)(2,1)S(1)}, bf16[64,1536]{1,0:T(8,128)(2,1)S(1)}, u32[]{:S(2)}, u32[]{:S(2)}) collective-permute-start(bf16[64,1536]{1,0:T(8,128)(2,1)S(1)} %get-tuple-element.44.refs_4_), channel_id=1, source_target_pairs={{0,64},{1,65},{2,66},{3,67},{4,68},{5,69},{6,70},{7,71},{8,72},{9,... | collective-permute-start | bytes 589832 | tf_op jit(solution)/shard_map/ppermute | solution.py:38
  38.8 8.3 %collective-permute-start.6 = (bf16[64,1536]{1,0:T(8,128)(2,1)S(1)}, bf16[64,1536]{1,0:T(8,128)(2,1)S(1)}, u32[]{:S(2)}, u32[]{:S(2)}) collective-permute-start(bf16[64,1536]{1,0:T(8,128)(2,1)S(1)} %get-tuple-element.44.refs_4_), channel_id=1, source_target_pairs={{0,32},{1,33},{2,34},{3,35},{4,36},{5,37},{6,38},{7,39},{8,40},{9,... | collective-permute-start | bytes 589832 | tf_op jit(solution)/shard_map/ppermute | solution.py:38
  48.8 16.7 %collective-permute-start.12 = (bf16[64,6144]{1,0:T(8,128)(2,1)S(1)}, bf16[64,6144]{1,0:T(8,128)(2,1)S(1)}, u32[]{:S(2)}, u32[]{:S(2)}) collective-permute-start(bf16[64,6144]{1,0:T(8,128)(2,1)S(1)} %get-tuple-element.45.refs_0_), channel_id=1, source_target_pairs={{0,96},{1,97},{2,98},{3,99},{4,100},{5,101},{6,102},{7,103},{8,104... | collective-permute-start | bytes 2359304 | tf_op jit(solution)/shard_map/ppermute | solution.py:38
  48.8 17.8 %collective-permute-start.11 = (bf16[64,6144]{1,0:T(8,128)(2,1)S(1)}, bf16[64,6144]{1,0:T(8,128)(2,1)S(1)}, u32[]{:S(2)}, u32[]{:S(2)}) collective-permute-start(bf16[64,6144]{1,0:T(8,128)(2,1)S(1)} %get-tuple-element.45.refs_0_), channel_id=1, source_target_pairs={{0,32},{1,33},{2,34},{3,35},{4,36},{5,37},{6,38},{7,39},{8,40},{9,... | collective-permute-start | bytes 2359304 | tf_op jit(solution)/shard_map/ppermute | solution.py:38
  50.2 16.3 %collective-permute-start.14 = (bf16[256,1536]{1,0:T(8,128)(2,1)S(1)}, bf16[256,1536]{1,0:T(8,128)(2,1)S(1)}, u32[]{:S(2)}, u32[]{:S(2)}) collective-permute-start(bf16[256,1536]{1,0:T(8,128)(2,1)S(1)} %get-tuple-element.46.refs_5_), channel_id=1, source_target_pairs={{0,12},{1,13},{2,14},{3,15},{4,0},{5,1},{6,2},{7,3},{8,4},{9,5},{1... | collective-permute-start | bytes 2359304 | tf_op jit(solution)/shard_map/ppermute | solution.py:38
  51.3 15.5 %collective-permute-start.13 = (bf16[256,1536]{1,0:T(8,128)(2,1)S(1)}, bf16[256,1536]{1,0:T(8,128)(2,1)S(1)}, u32[]{:S(2)}, u32[]{:S(2)}) collective-permute-start(bf16[256,1536]{1,0:T(8,128)(2,1)S(1)} %get-tuple-element.46.refs_5_), channel_id=1, source_target_pairs={{0,4},{1,5},{2,6},{3,7},{4,8},{5,9},{6,10},{7,11},{8,12},{9,13},{1... | collective-permute-start | bytes 2359304 | tf_op jit(solution)/shard_map/ppermute | solution.py:38
  66.9 7.9 %collective-permute-start.15 = (bf16[32,6144]{1,0:T(8,128)(2,1)S(1)}, bf16[32,6144]{1,0:T(8,128)(2,1)S(1)}, u32[]{:S(2)}, u32[]{:S(2)}) collective-permute-start(bf16[32,6144]{1,0:T(8,128)(2,1)S(1)} %get-tuple-element.47), channel_id=1, source_target_pairs={{0,32},{1,33},{2,34},{3,35},{4,36},{5,37},{6,38},{7,39},{8,40},{9,... | collective-permute-start | bytes 1179656 | tf_op jit(solution)/shard_map/ppermute | solution.py:38
  67.6 7.2 %collective-permute-start.16 = (bf16[32,6144]{1,0:T(8,128)(2,1)S(1)}, bf16[32,6144]{1,0:T(8,128)(2,1)S(1)}, u32[]{:S(2)}, u32[]{:S(2)}) collective-permute-start(bf16[32,6144]{1,0:T(8,128)(2,1)S(1)} %get-tuple-element.48), channel_id=1, source_target_pairs={{0,96},{1,97},{2,98},{3,99},{4,100},{5,101},{6,102},{7,103},{8,104... | collective-permute-start | bytes 1179656 | tf_op jit(solution)/shard_map/ppermute | solution.py:38
  69.6 8.1 %collective-permute-start.17 = (bf16[128,1536]{1,0:T(8,128)(2,1)S(1)}, bf16[128,1536]{1,0:T(8,128)(2,1)S(1)}, u32[]{:S(2)}, u32[]{:S(2)}) collective-permute-start(bf16[128,1536]{1,0:T(8,128)(2,1)S(1)} %get-tuple-element.49), channel_id=1, source_target_pairs={{0,4},{1,5},{2,6},{3,7},{4,8},{5,9},{6,10},{7,11},{8,12},{9,13},{1... | collective-permute-start | bytes 1179656 | tf_op jit(solution)/shard_map/ppermute | solution.py:38
  70.4 7.3 %collective-permute-start.18 = (bf16[128,1536]{1,0:T(8,128)(2,1)S(1)}, bf16[128,1536]{1,0:T(8,128)(2,1)S(1)}, u32[]{:S(2)}, u32[]{:S(2)}) collective-permute-start(bf16[128,1536]{1,0:T(8,128)(2,1)S(1)} %get-tuple-element.50), channel_id=1, source_target_pairs={{0,12},{1,13},{2,14},{3,15},{4,0},{5,1},{6,2},{7,3},{8,4},{9,5},{1... | collective-permute-start | bytes 1179656 | tf_op jit(solution)/shard_map/ppermute | solution.py:38
  96.7 26.7 %collective-permute-start.26 = (bf16[256,6912]{1,0:T(8,128)(2,1)}, bf16[256,6912]{1,0:T(8,128)(2,1)S(1)}, u32[]{:S(2)}, u32[]{:S(2)}) collective-permute-start(bf16[256,6912]{1,0:T(8,128)(2,1)} %get-tuple-element.59.refs_0_), channel_id=1, source_target_pairs={{0,16},{1,17},{2,18},{3,19},{4,20},{5,21},{6,22},{7,23},{8,24},{9,... | collective-permute-start | bytes 10616840 | tf_op jit(solution)/shard_map/ppermute | solution.py:49
  103.9 13.2 %collective-permute-start.20 = (bf16[64,3456]{1,0:T(8,128)(2,1)S(1)}, bf16[64,3456]{1,0:T(8,128)(2,1)S(1)}, u32[]{:S(2)}, u32[]{:S(2)}) collective-permute-start(bf16[64,3456]{1,0:T(8,128)(2,1)S(1)} %get-tuple-element.52), channel_id=1, source_target_pairs={{0,96},{1,97},{2,98},{3,99},{4,100},{5,101},{6,102},{7,103},{8,104... | collective-permute-start | bytes 1327112 | tf_op jit(solution)/shard_map/ppermute | solution.py:38
  103.9 13.2 %collective-permute-start.22 = (bf16[64,3456]{1,0:T(8,128)(2,1)S(1)}, bf16[64,3456]{1,0:T(8,128)(2,1)S(1)}, u32[]{:S(2)}, u32[]{:S(2)}) collective-permute-start(bf16[64,3456]{1,0:T(8,128)(2,1)S(1)} %get-tuple-element.54), channel_id=1, source_target_pairs={{0,32},{1,33},{2,34},{3,35},{4,36},{5,37},{6,38},{7,39},{8,40},{9,... | collective-permute-start | bytes 1327112 | tf_op jit(solution)/shard_map/ppermute | solution.py:38
  105.4 11.7 %collective-permute-start.23 = (bf16[4,16,3072]{2,1,0:T(8,128)(2,1)S(1)}, bf16[4,16,3072]{2,1,0:T(8,128)(2,1)S(1)}, u32[]{:S(2)}, u32[]{:S(2)}) collective-permute-start(bf16[4,16,3072]{2,1,0:T(8,128)(2,1)S(1)} %get-tuple-element.56), channel_id=1, source_target_pairs={{0,4},{1,5},{2,6},{3,7},{4,8},{5,9},{6,10},{7,11},{8,12},{9,13},{1... | collective-permute-start | bytes 1179656 | tf_op jit(solution)/shard_map/ppermute | solution.py:38
  105.9 11.3 %collective-permute-start.25 = (bf16[4,16,3072]{2,1,0:T(8,128)(2,1)S(1)}, bf16[4,16,3072]{2,1,0:T(8,128)(2,1)S(1)}, u32[]{:S(2)}, u32[]{:S(2)}) collective-permute-start(bf16[4,16,3072]{2,1,0:T(8,128)(2,1)S(1)} %get-tuple-element.58), channel_id=1, source_target_pairs={{0,12},{1,13},{2,14},{3,15},{4,0},{5,1},{6,2},{7,3},{8,4},{9,5},{1... | collective-permute-start | bytes 1179656 | tf_op jit(solution)/shard_map/ppermute | solution.py:38
  119.2 19.1 %collective-permute-start.33 = (bf16[256,6144]{1,0:T(8,128)(2,1)S(1)}, bf16[256,6144]{1,0:T(8,128)(2,1)S(1)}, u32[]{:S(2)}, u32[]{:S(2)}) collective-permute-start(bf16[256,6144]{1,0:T(8,128)(2,1)S(1)} %relay.1), channel_id=1, source_target_pairs={{0,16},{1,17},{2,18},{3,19},{4,20},{5,21},{6,22},{7,23},{8,24},{9,... | collective-permute-start | bytes 9437192 | tf_op jit(solution)/shard_map/ppermute | solution.py:49
  120.6 13.2 %collective-permute-start.21 = (bf16[64,3456]{1,0:T(8,128)(2,1)S(1)}, bf16[64,3456]{1,0:T(8,128)(2,1)S(1)}, u32[]{:S(2)}, u32[]{:S(2)}) collective-permute-start(bf16[64,3456]{1,0:T(8,128)(2,1)S(1)} %get-tuple-element.53), channel_id=1, source_target_pairs={{0,64},{1,65},{2,66},{3,67},{4,68},{5,69},{6,70},{7,71},{8,72},{9,... | collective-permute-start | bytes 1327112 | tf_op jit(solution)/shard_map/ppermute | solution.py:38
  120.7 11.8 %collective-permute-start.24 = (bf16[4,16,3072]{2,1,0:T(8,128)(2,1)S(1)}, bf16[4,16,3072]{2,1,0:T(8,128)(2,1)S(1)}, u32[]{:S(2)}, u32[]{:S(2)}) collective-permute-start(bf16[4,16,3072]{2,1,0:T(8,128)(2,1)S(1)} %get-tuple-element.57), channel_id=1, source_target_pairs={{0,8},{1,9},{2,10},{3,11},{4,12},{5,13},{6,14},{7,15},{8,0},{9,1},... | collective-permute-start | bytes 1179656 | tf_op jit(solution)/shard_map/ppermute | solution.py:38
  135.0 6.4 %collective-permute-start.30 = (bf16[16,3072]{1,0:T(8,128)(2,1)S(1)}, bf16[16,3072]{1,0:T(8,128)(2,1)S(1)}, u32[]{:S(2)}, u32[]{:S(2)}) collective-permute-start(bf16[16,3072]{1,0:T(8,128)(2,1)S(1)} %get-tuple-element.67), channel_id=1, source_target_pairs={{0,96},{1,97},{2,98},{3,99},{4,100},{5,101},{6,102},{7,103},{8,104... | collective-permute-start | bytes 294920 | tf_op jit(solution)/shard_map/ppermute | solution.py:38
  136.3 10.6 %collective-permute-start.31 = (bf16[16,3072]{1,0:T(8,128)(2,1)S(1)}, bf16[16,3072]{1,0:T(8,128)(2,1)S(1)}, u32[]{:S(2)}, u32[]{:S(2)}) collective-permute-start(bf16[16,3072]{1,0:T(8,128)(2,1)S(1)} %get-tuple-element.68), channel_id=1, source_target_pairs={{0,64},{1,65},{2,66},{3,67},{4,68},{5,69},{6,70},{7,71},{8,72},{9,... | collective-permute-start | bytes 294920 | tf_op jit(solution)/shard_map/ppermute | solution.py:38
  137.3 9.6 %collective-permute-start.32 = (bf16[16,3072]{1,0:T(8,128)(2,1)S(1)}, bf16[16,3072]{1,0:T(8,128)(2,1)S(1)}, u32[]{:S(2)}, u32[]{:S(2)}) collective-permute-start(bf16[16,3072]{1,0:T(8,128)(2,1)S(1)} %get-tuple-element.69), channel_id=1, source_target_pairs={{0,32},{1,33},{2,34},{3,35},{4,36},{5,37},{6,38},{7,39},{8,40},{9,... | collective-permute-start | bytes 294920 | tf_op jit(solution)/shard_map/ppermute | solution.py:38
  137.5 9.3 %collective-permute-start.27 = (bf16[16,3456]{1,0:T(8,128)(2,1)S(1)}, bf16[16,3456]{1,0:T(8,128)(2,1)S(1)}, u32[]{:S(2)}, u32[]{:S(2)}) collective-permute-start(bf16[16,3456]{1,0:T(8,128)(2,1)S(1)} %get-tuple-element.63), channel_id=1, source_target_pairs={{0,4},{1,5},{2,6},{3,7},{4,8},{5,9},{6,10},{7,11},{8,12},{9,13},{1... | collective-permute-start | bytes 331784 | tf_op jit(solution)/shard_map/ppermute | solution.py:38
  138.4 8.5 %collective-permute-start.28 = (bf16[16,3456]{1,0:T(8,128)(2,1)S(1)}, bf16[16,3456]{1,0:T(8,128)(2,1)S(1)}, u32[]{:S(2)}, u32[]{:S(2)}) collective-permute-start(bf16[16,3456]{1,0:T(8,128)(2,1)S(1)} %get-tuple-element.64), channel_id=1, source_target_pairs={{0,8},{1,9},{2,10},{3,11},{4,12},{5,13},{6,14},{7,15},{8,0},{9,1},... | collective-permute-start | bytes 331784 | tf_op jit(solution)/shard_map/ppermute | solution.py:38
  147.7 6.3 %collective-permute-start.35 = (bf16[4,6528]{1,0:T(4,128)(2,1)S(1)}, bf16[4,6528]{1,0:T(4,128)(2,1)S(1)}, u32[]{:S(2)}, u32[]{:S(2)}) collective-permute-start(bf16[4,6528]{1,0:T(4,128)(2,1)S(1)} %get-tuple-element.74), channel_id=1, source_target_pairs={{0,2},{1,3},{2,0},{3,1},{4,6},{5,7},{6,4},{7,5},{8,10},{9,11},{10,... | collective-permute-start | bytes 156680 | tf_op jit(solution)/shard_map/ppermute | solution.py:38
  (14 other events, 107.4 us)

commit v2 on v1

--- a/solution.py
+++ b/solution.py
@@ -5,7 +5,7 @@
 from jax.experimental.pallas import tpu as pltpu
 from jax.sharding import PartitionSpec as P
 
-AXES = ("section", "et")
+AXES = ("x", "core", "y", "z")
 BF = jnp.bfloat16
 F32 = jnp.float32
 D = 6144
@@ -50,9 +50,7 @@
 
 
 def position():
-    section = lax.axis_index("section")
-    et = lax.axis_index("et")
-    return section // NC, section % NC, et // NZ, et % NZ
+    return tuple(lax.axis_index(axis) for axis in AXES)
 
 
 def nt(left, right):
@@ -222,7 +220,8 @@
 
 def main_kernel(where, *refs):
     t_in, g_in = refs[0:5], refs[5:10]
-    weights = (refs[10:13], refs[13:16])
+    other = 1 - where[4]
+    weights = (refs[10:13], (refs[13].at[other], refs[14].at[other], refs[15]))
     slots_ref, gates_ref = refs[16:18]
     pa_out, pb_out = refs[18:22], refs[22:26]
     own_out, rows_out, grads_out = refs[26:29]
@@ -405,7 +404,7 @@
             pltpu.SemaphoreType.DMA((D // KT, 2)),
             pltpu.SemaphoreType.DMA((12,)),
         ],
-        compiler_params=pltpu.CompilerParams(vmem_limit_bytes=44 * MIB),
+        compiler_params=pltpu.CompilerParams(vmem_limit_bytes=58 * MIB),
         cost_estimate=pl.CostEstimate(
             flops=8_000_000_000, bytes_accessed=30_000_000, transcendentals=262144
         ),
@@ -612,20 +611,20 @@
 ):
     x, c, y, z = position()
     where = jnp.stack([x, y, z, c, c, slot_counts[0], slot_counts[1]]).astype(jnp.int32)
-    gate_sib, up_sib = swap(gate_weight), swap(up_weight)
+    gates, ups = (lax.all_gather(w, "core", axis=0) for w in (gate_weight, up_weight))
 
     packed = run_pack(tokens_in, out_grad)
     t16, g64 = run_first_stage(where, [packed] + [shift(packed, "z", k) for k in (1, 2, 3)])
     t = [t16] + [shift(t16, "y", k) for k in (1, 2, 3)]
     g = [g64] + [shift(g64, "x", k) for k in (1, 2, 3)]
     down_sib = swap(down_weight)
-    t64, g256 = run_second_stage(where, t, g, [gate_sib, up_sib])
+    t64, g256 = run_second_stage(where, t, g, [])
     t_low, t_high = shift(t64, "x", 1), shift(t64, "x", -1)
     g_low, g_high = shift(g256, "y", 1), shift(g256, "y", -1)
     a, b, e, f = run_halves(t_low, t_high, g_low, g_high)
     t = (t64, t_low, t_high, shift(a, "x", 1), shift(b, "x", -1))
     g = (g256, g_low, g_high, shift(e, "y", 1), shift(f, "y", -1))
-    weights = (gate_weight, up_weight, down_weight, gate_sib, up_sib, down_sib)
+    weights = (gate_weight, up_weight, down_weight, gates, ups, down_sib)
     outs = run_main(where, t, g, weights, slot_tokens, slot_gates)
     pa, pb = outs[0:4], outs[4:8]
     dl_own, rows, grads = outs[8:]
@@ -648,25 +647,21 @@
 
 
 def solution(mesh):
+    by_axis = jax.sharding.Mesh(mesh.devices.reshape(NX, NC, NY, NZ), AXES)
+    section, et = AXES[0:2], AXES[2:4]
     return jax.shard_map(
         on_device,
-        mesh=mesh,
+        mesh=by_axis,
         in_specs=(
-            P(("section", "et"), None),
-            P("section", "et"),
-            P(None, None, ("section", "et")),
-            P(None, None, ("section", "et")),
-            P(None, ("section", "et"), None),
+            P(AXES, None),
+            P(section, et),
+            P(None, None, AXES),
+            P(None, None, AXES),
+            P(None, AXES, None),
             P(),
             P(),
             P(),
         ),
-        out_specs=(
-            P(("section", "et"), None),
-            P(None, None, ("section", "et")),
-            P(None, None, ("section", "et")),
-            P(None, ("section", "et"), None),
-            P(),
-        ),
+        out_specs=(P(AXES, None), P(None, None, AXES), P(None, None, AXES), P(None, AXES, None), P()),
         check_vma=False,
     )

time: 163 us -> 172 us (1.055)
  between operations: 0.77 us -> 14.3 us
  waiting for transfers between devices: 64.1 us -> 50.6 us
  starting transfers between devices: 54.3 us -> 60.8 us
  Pallas kernels: 38.2 us -> 42.8 us
    ppermute x32, waiting for transfers between devices: 63.2 us -> 48.4 us  [shift(): return lax.ppermute(value, AXES, shift_pairs(axis, step))]
    ppermute x32, starting transfers between devices: 39.7 us -> 47.7 us  [shift(): return lax.ppermute(value, AXES, shift_pairs(axis, step))]
    pallas_call x1, Pallas kernels: 18.9 us -> 23.5 us  [run_main(): pl.pallas_call(main_kernel, out_shape=out_shape, in_specs=[SMEM_SPEC] + h...]
    ppermute x6 -> x4, starting transfers between devices: 14.5 us -> 13 us  [swap(): return lax.ppermute(value, AXES, pairs)]
    unnamed x16 -> x48, local copies, waits for them, and re-layouts: 4.49 us -> 3.46 us
  transfers between devices with their start and end apart: 38 -> 38, of which waited for: 20 -> 18; matrix products, arithmetic and copies ran while one was open for 0% -> 0% of each run, Pallas kernels for 10% -> 9%
where the time goes in v2:
time: 172 us
  starting transfers between devices  60.8 us (35%)
  waiting for transfers between devices  50.6 us (29%)
  Pallas kernels  42.8 us (25%)
  between operations  14.3 us (8%)
  local copies, waits for them, and re-layouts  3.55 us (2%)
    ppermute x32, waiting for transfers between devices, shift(): return lax.ppermute(value, AXES, shift_pairs(axis, step))  48.4 us
    ppermute x32, starting transfers between devices, shift(): return lax.ppermute(value, AXES, shift_pairs(axis, step))  47.7 us
    pallas_call x1, Pallas kernels, run_main(): pl.pallas_call(main_kernel, out_shape=out_shape, in_specs=[SMEM_SPEC] + h...  23.5 us
    ppermute x4, starting transfers between devices, swap(): return lax.ppermute(value, AXES, pairs)  13 us
    pallas_call x1, Pallas kernels, run_up(): pl.pallas_call(up_kernel, grid=(D // FT,), out_shape=[jax.ShapeDtypeStruc...  8.67 us
    pallas_call x1, Pallas kernels, run_down(): pl.pallas_call(down_kernel, grid=(D // FT // 2,), out_shape=[jax.ShapeDty...  4.6 us
    unnamed x48, local copies, waits for them, and re-layouts  3.46 us
  transfers between devices with their start and end apart: 38, of which 18 were waited for; matrix products, arithmetic and copies ran while one was open for 0% of the time, Pallas kernels for 9%

profile of v2, /device:TPU:1, one launch (start us, length us, event | category | flops | bytes accessed | tf_op | source)
XLA Modules:
  0.0 172.1 jit_solution(13593183237951579099)
XLA Ops:
  8.7 1.5 collective-permute-start.17
  10.2 3.9 %collective-permute-start.2 = (bf16[128,384]{1,0:T(8,128)(2,1)S(1)}, bf16[128,384]{1,0:T(8,128)(2,1)S(1)}, u32[]{:S(2)}, u32[]{:S(2)}) collective-permute-start(bf16[128,384]{1,0:T(8,128)(2,1)S(1)} %pack.1.refs_0_), channel_id=1, source_target_pairs={{0,3},{1,0},{2,1},{3,2},{4,7},{5,4},{6,5},{7,6},{8,11},{9,8},{10,9... | collective-permute-start | bytes 294920 | tf_op jit(solution)/shard_map/ppermute | solution.py:38
  14.9 3.4 %collective-permute-done.2.refs_3_ = bf16[128,384]{1,0:T(8,128)(2,1)S(1)} collective-permute-done((bf16[128,384]{1,0:T(8,128)(2,1)S(1)}, bf16[128,384]{1,0:T(8,128)(2,1)S(1)}, u32[]{:S(2)}, u32[]{:S(2)}) %collective-permute-start.2) | collective-permute-done | bytes 98336 | tf_op jit(solution)/shard_map/ppermute | solution.py:38
  18.3 1.5 collective-permute-done.1.refs_2_
  19.7 2.2 %collective-permute-done.refs_1_ = bf16[128,384]{1,0:T(8,128)(2,1)S(1)} collective-permute-done((bf16[128,384]{1,0:T(8,128)(2,1)S(1)}, bf16[128,384]{1,0:T(8,128)(2,1)S(1)}, u32[]{:S(2)}, u32[]{:S(2)}) %collective-permute-start) | collective-permute-done | bytes 98336 | tf_op jit(solution)/shard_map/ppermute | solution.py:38
  22.6 2.8 %collective-permute-start.5 = (bf16[16,6144]{1,0:T(8,128)(2,1)S(1)}, bf16[16,6144]{1,0:T(8,128)(2,1)S(1)}, u32[]{:S(2)}, u32[]{:S(2)}) collective-permute-start(bf16[16,6144]{1,0:T(8,128)(2,1)S(1)} %get-tuple-element.43.refs_0_), channel_id=1, source_target_pairs={{0,12},{1,13},{2,14},{3,15},{4,0},{5,1},{6,2},{7,3},{8,4},{9,5},{1... | collective-permute-start | bytes 589832 | tf_op jit(solution)/shard_map/ppermute | solution.py:38
  26.4 2.5 %collective-permute-start.8 = (bf16[64,1536]{1,0:T(8,128)(2,1)S(1)}, bf16[64,1536]{1,0:T(8,128)(2,1)S(1)}, u32[]{:S(2)}, u32[]{:S(2)}) collective-permute-start(bf16[64,1536]{1,0:T(8,128)(2,1)S(1)} %get-tuple-element.44.refs_4_), channel_id=1, source_target_pairs={{0,96},{1,97},{2,98},{3,99},{4,100},{5,101},{6,102},{7,103},{8,104... | collective-permute-start | bytes 589832 | tf_op jit(solution)/shard_map/ppermute | solution.py:38
  29.9 2.7 %collective-permute-start.7 = (bf16[64,1536]{1,0:T(8,128)(2,1)S(1)}, bf16[64,1536]{1,0:T(8,128)(2,1)S(1)}, u32[]{:S(2)}, u32[]{:S(2)}) collective-permute-start(bf16[64,1536]{1,0:T(8,128)(2,1)S(1)} %get-tuple-element.44.refs_4_), channel_id=1, source_target_pairs={{0,64},{1,65},{2,66},{3,67},{4,68},{5,69},{6,70},{7,71},{8,72},{9,... | collective-permute-start | bytes 589832 | tf_op jit(solution)/shard_map/ppermute | solution.py:38
  33.5 4.4 %collective-permute-done.3.refs_1_ = bf16[16,6144]{1,0:T(8,128)(2,1)S(1)} collective-permute-done((bf16[16,6144]{1,0:T(8,128)(2,1)S(1)}, bf16[16,6144]{1,0:T(8,128)(2,1)S(1)}, u32[]{:S(2)}, u32[]{:S(2)}) %collective-permute-start.3) | collective-permute-done | bytes 196640 | tf_op jit(solution)/shard_map/ppermute | solution.py:38
  39.1 2.1 %collective-permute-start.10 = (bf16[64,6144]{1,0:T(8,128)(2,1)S(1)}, bf16[64,6144]{1,0:T(8,128)(2,1)S(1)}, u32[]{:S(2)}, u32[]{:S(2)}) collective-permute-start(bf16[64,6144]{1,0:T(8,128)(2,1)S(1)} %get-tuple-element.45.refs_0_), channel_id=1, source_target_pairs={{0,96},{1,97},{2,98},{3,99},{4,100},{5,101},{6,102},{7,103},{8,104... | collective-permute-start | bytes 2359304 | tf_op jit(solution)/shard_map/ppermute | solution.py:38
  41.2 9.1 %collective-permute-start.12 = (bf16[256,1536]{1,0:T(8,128)(2,1)S(1)}, bf16[256,1536]{1,0:T(8,128)(2,1)S(1)}, u32[]{:S(2)}, u32[]{:S(2)}) collective-permute-start(bf16[256,1536]{1,0:T(8,128)(2,1)S(1)} %get-tuple-element.46.refs_5_), channel_id=1, source_target_pairs={{0,12},{1,13},{2,14},{3,15},{4,0},{5,1},{6,2},{7,3},{8,4},{9,5},{1... | collective-permute-start | bytes 2359304 | tf_op jit(solution)/shard_map/ppermute | solution.py:38
  50.3 3.8 %collective-permute-done.10.t_high.refs_2_ = bf16[64,6144]{1,0:T(8,128)(2,1)S(1)} collective-permute-done((bf16[64,6144]{1,0:T(8,128)(2,1)S(1)}, bf16[64,6144]{1,0:T(8,128)(2,1)S(1)}, u32[]{:S(2)}, u32[]{:S(2)}) %collective-permute-start.10) | collective-permute-done | bytes 786464 | tf_op jit(solution)/shard_map/ppermute | solution.py:38
  54.0 2.5 %collective-permute-done.9.t_low.refs_1_ = bf16[64,6144]{1,0:T(8,128)(2,1)S(1)} collective-permute-done((bf16[64,6144]{1,0:T(8,128)(2,1)S(1)}, bf16[64,6144]{1,0:T(8,128)(2,1)S(1)}, u32[]{:S(2)}, u32[]{:S(2)}) %collective-permute-start.9) | collective-permute-done | bytes 786464 | tf_op jit(solution)/shard_map/ppermute | solution.py:38
  56.6 8.3 %collective-permute-done.12.g_high.refs_7_ = bf16[256,1536]{1,0:T(8,128)(2,1)S(1)} collective-permute-done((bf16[256,1536]{1,0:T(8,128)(2,1)S(1)}, bf16[256,1536]{1,0:T(8,128)(2,1)S(1)}, u32[]{:S(2)}, u32[]{:S(2)}) %collective-permute-start.12) | collective-permute-done | bytes 786464 | tf_op jit(solution)/shard_map/ppermute | solution.py:38
  64.9 3.1 %collective-permute-done.11.g_low.refs_6_ = bf16[256,1536]{1,0:T(8,128)(2,1)S(1)} collective-permute-done((bf16[256,1536]{1,0:T(8,128)(2,1)S(1)}, bf16[256,1536]{1,0:T(8,128)(2,1)S(1)}, u32[]{:S(2)}, u32[]{:S(2)}) %collective-permute-start.11) | collective-permute-done | bytes 786464 | tf_op jit(solution)/shard_map/ppermute | solution.py:38
  68.2 2.7 %collective-permute-start.14 = (bf16[32,6144]{1,0:T(8,128)(2,1)S(1)}, bf16[32,6144]{1,0:T(8,128)(2,1)S(1)}, u32[]{:S(2)}, u32[]{:S(2)}) collective-permute-start(bf16[32,6144]{1,0:T(8,128)(2,1)S(1)} %get-tuple-element.48), channel_id=1, source_target_pairs={{0,96},{1,97},{2,98},{3,99},{4,100},{5,101},{6,102},{7,103},{8,104... | collective-permute-start | bytes 1179656 | tf_op jit(solution)/shard_map/ppermute | solution.py:38
  70.9 2.7 %collective-permute-start.16 = (bf16[128,1536]{1,0:T(8,128)(2,1)S(1)}, bf16[128,1536]{1,0:T(8,128)(2,1)S(1)}, u32[]{:S(2)}, u32[]{:S(2)}) collective-permute-start(bf16[128,1536]{1,0:T(8,128)(2,1)S(1)} %get-tuple-element.50), channel_id=1, source_target_pairs={{0,12},{1,13},{2,14},{3,15},{4,0},{5,1},{6,2},{7,3},{8,4},{9,5},{1... | collective-permute-start | bytes 1179656 | tf_op jit(solution)/shard_map/ppermute | solution.py:38
  73.6 3.1 %collective-permute-done.13.refs_3_ = bf16[32,6144]{1,0:T(8,128)(2,1)S(1)} collective-permute-done((bf16[32,6144]{1,0:T(8,128)(2,1)S(1)}, bf16[32,6144]{1,0:T(8,128)(2,1)S(1)}, u32[]{:S(2)}, u32[]{:S(2)}) %collective-permute-start.13) | collective-permute-done | bytes 393248 | tf_op jit(solution)/shard_map/ppermute | solution.py:38
  76.6 2.4 %collective-permute-done.15.refs_8_ = bf16[128,1536]{1,0:T(8,128)(2,1)S(1)} collective-permute-done((bf16[128,1536]{1,0:T(8,128)(2,1)S(1)}, bf16[128,1536]{1,0:T(8,128)(2,1)S(1)}, u32[]{:S(2)}, u32[]{:S(2)}) %collective-permute-start.15) | collective-permute-done | bytes 393248 | tf_op jit(solution)/shard_map/ppermute | solution.py:38
  80.6 23.5 %main.1 = (bf16[64,3456]{1,0:T(8,128)(2,1)}, bf16[64,3456]{1,0:T(8,128)(2,1)}, bf16[64,3456]{1,0:T(8,128)(2,1)}, bf16[64,3456]{1,0:T(8,128)(2,1)}, bf16[4,16,307...) custom-call(s32[7]{0:T(128)} %copy-done.14, ...), custom_call_target="tpu_custom_call" | custom-call | flops 8000000000 | bytes 30000000 | tf_op jit(solution)/shard_map/main/pallas_call | solution.py:383
  104.1 4.9 %collective-permute-start.24 = (bf16[256,6912]{1,0:T(8,128)(2,1)}, bf16[256,6912]{1,0:T(8,128)(2,1)S(1)}, u32[]{:S(2)}, u32[]{:S(2)}) collective-permute-start(bf16[256,6912]{1,0:T(8,128)(2,1)} %get-tuple-element.59.refs_0_), channel_id=1, source_target_pairs={{0,16},{1,17},{2,18},{3,19},{4,20},{5,21},{6,22},{7,23},{8,24},{9,... | collective-permute-start | bytes 10616840 | tf_op jit(solution)/shard_map/ppermute | solution.py:49
  110.5 2.7 %collective-permute-start.23 = (bf16[4,16,3072]{2,1,0:T(8,128)(2,1)}, bf16[4,16,3072]{2,1,0:T(8,128)(2,1)S(1)}, u32[]{:S(2)}, u32[]{:S(2)}) collective-permute-start(bf16[4,16,3072]{2,1,0:T(8,128)(2,1)} %get-tuple-element.58), channel_id=1, source_target_pairs={{0,12},{1,13},{2,14},{3,15},{4,0},{5,1},{6,2},{7,3},{8,4},{9,5},{1... | collective-permute-start | bytes 1179656 | tf_op jit(solution)/shard_map/ppermute | solution.py:38
  113.2 8.8 %collective-permute-done.21.refs_6_.refs_5_.refs_3_ = bf16[4,16,3072]{2,1,0:T(8,128)(2,1)S(1)} collective-permute-done((bf16[4,16,3072]{2,1,0:T(8,128)(2,1)}, bf16[4,16,3072]{2,1,0:T(8,128)(2,1)S(1)}, u32[]{:S(2)}, u32[]{:S(2)}) %collective-permute-start.21) | collective-permute-done | bytes 393248 | tf_op jit(solution)/shard_map/ppermute | solution.py:38
  122.0 1.9 %copy-done = bf16[256,6144]{1,0:T(8,128)(2,1)S(1)} copy-done((bf16[256,6144]{1,0:T(8,128)(2,1)S(1)}, bf16[256,6144]{1,0:T(8,128)(2,1)}, u32[]{:S(2)}) %copy-start) | copy-done | bytes 3145752
  124.1 1.6 collective-permute-start.31
  126.4 2.2 %collective-permute-start.22 = (bf16[4,16,3072]{2,1,0:T(8,128)(2,1)S(1)}, bf16[4,16,3072]{2,1,0:T(8,128)(2,1)S(1)}, u32[]{:S(2)}, u32[]{:S(2)}) collective-permute-start(bf16[4,16,3072]{2,1,0:T(8,128)(2,1)S(1)} %copy-done.23), channel_id=1, source_target_pairs={{0,8},{1,9},{2,10},{3,11},{4,12},{5,13},{6,14},{7,15},{8,0},{9,1},... | collective-permute-start | bytes 1179656 | tf_op jit(solution)/shard_map/ppermute | solution.py:38
  128.6 8.7 %up_grads.1 = (bf16[2,6144,128]{2,1,0:T(8,128)(2,1)}, bf16[2,6144,128]{2,1,0:T(8,128)(2,1)}, f32[8,128]{1,0:T(8,128)S(1)}) custom-call(bf16[256,6912]{1,0:T(8,128)(2,1)S(1)} %copy-done.2, bf16[256,6912]{1,0:T(8,128)(2,1)S(1)} %collective-permute-done.24.refs_1_.refs_3_.sib, bf16[256,768]{1,0:T(8,128)(2,1)S(1)} %copy-done.7, ...), custom_call_target="tpu_custom_call" | custom-call | flops 3200000000 | bytes 13000000 | tf_op jit(solution)/shard_map/up_grads/pallas_call | solution.py:430
  142.8 3.0 %collective-permute-start.26 = (bf16[16,3456]{1,0:T(8,128)(2,1)S(1)}, bf16[16,3456]{1,0:T(8,128)(2,1)S(1)}, u32[]{:S(2)}, u32[]{:S(2)}) collective-permute-start(bf16[16,3456]{1,0:T(8,128)(2,1)S(1)} %get-tuple-element.64), channel_id=1, source_target_pairs={{0,8},{1,9},{2,10},{3,11},{4,12},{5,13},{6,14},{7,15},{8,0},{9,1},... | collective-permute-start | bytes 331784 | tf_op jit(solution)/shard_map/ppermute | solution.py:38
  146.2 4.6 %down_grads.1 = (bf16[2,128,6144]{2,1,0:T(8,128)(2,1)}, f32[8,128]{1,0:T(8,128)S(1)}) custom-call(bf16[256,6144]{1,0:T(8,128)(2,1)S(1)} %copy-done.1, bf16[256,6144]{1,0:T(8,128)(2,1)S(1)} %collective-permute-done.31.grads_sib, bf16[256,768]{1,0:T(8,128)(2,1)S(1)} %copy-done.7, bf16[256,6912]{1,0:T(8,128)(2,1)S(1)} %collective-permute-done.24.refs_1_.refs_3_.sib), custom_call_target="tpu_custom_call" | custom-call | flops 1600000000 | bytes 10000000 | tf_op jit(solution)/shard_map/down_grads/pallas_call | solution.py:469
  154.3 2.1 %collective-permute-done.32.refs_0_ = bf16[4,6528]{1,0:T(4,128)(2,1)S(1)} collective-permute-done((bf16[4,6528]{1,0:T(4,128)(2,1)S(1)}, bf16[4,6528]{1,0:T(4,128)(2,1)S(1)}, u32[]{:S(2)}, u32[]{:S(2)}) %collective-permute-start.32) | collective-permute-done | bytes 52256 | tf_op jit(solution)/shard_map/ppermute | solution.py:38
  157.6 5.0 %collective-permute-start.35 = (f32[8,128]{1,0:T(8,128)S(1)}, f32[8,128]{1,0:T(8,128)S(1)}, u32[]{:S(2)}, u32[]{:S(2)}) collective-permute-start(f32[8,128]{1,0:T(8,128)S(1)} %get-tuple-element.80.own), channel_id=1, source_target_pairs={{0,16},{1,17},{2,18},{3,19},{4,20},{5,21},{6,22},{7,23},{8,24},{9,... | collective-permute-start | bytes 12296 | tf_op jit(solution)/shard_map/ppermute | solution.py:49
  163.4 1.8 %router.1 = f32[2,256]{1,0:T(2,128)} custom-call(s32[7]{0:T(128)S(1)} %copy-done.15, f32[8,128]{1,0:T(8,128)S(1)} %get-tuple-element.80.own, f32[8,128]{1,0:T(8,128)S(1)} %collective-permute-done.35.other, s32[2,256]{1,0:T(2,128)S(1)} %copy-done.16), custom_call_target="tpu_custom_call" | custom-call | tf_op jit(solution)/shard_map/router/pallas_call | solution.py:599
  (107 shorter events, 22.6 us)
Async XLA Ops:
  7.2 73.3 %all-gather.5.cloned.1.call-start = ((), (), s32[]{:S(2)}) async-start(), calls=%async_computation | async-start | bytes 9437184 | tf_op jit(solution)/shard_map/all_gather | solution.py:614
  7.9 72.6 %all-gather.7.cloned.1.call-start = ((), (), s32[]{:S(2)}) async-start(), calls=%async_computation.1 | async-start | bytes 9437184 | tf_op jit(solution)/shard_map/all_gather | solution.py:614
  8.7 71.8 %collective-permute-start.17 = (bf16[2,128,6144]{2,1,0:T(8,128)(2,1)}, bf16[2,128,6144]{2,1,0:T(8,128)(2,1)}, u32[]{:S(2)}, u32[]{:S(2)}) collective-permute-start(bf16[2,128,6144]{2,1,0:T(8,128)(2,1)} %refs_12_.1), channel_id=1, source_target_pairs={{0,16},{1,17},{2,18},{3,19},{4,20},{5,21},{6,22},{7,23},{8,24},{9,... | collective-permute-start | bytes 9437192 | tf_op jit(solution)/shard_map/ppermute | solution.py:49
  10.2 8.1 %collective-permute-start.2 = (bf16[128,384]{1,0:T(8,128)(2,1)S(1)}, bf16[128,384]{1,0:T(8,128)(2,1)S(1)}, u32[]{:S(2)}, u32[]{:S(2)}) collective-permute-start(bf16[128,384]{1,0:T(8,128)(2,1)S(1)} %pack.1.refs_0_), channel_id=1, source_target_pairs={{0,3},{1,0},{2,1},{3,2},{4,7},{5,4},{6,5},{7,6},{8,11},{9,8},{10,9... | collective-permute-start | bytes 294920 | tf_op jit(solution)/shard_map/ppermute | solution.py:38
  14.1 7.8 %collective-permute-start = (bf16[128,384]{1,0:T(8,128)(2,1)S(1)}, bf16[128,384]{1,0:T(8,128)(2,1)S(1)}, u32[]{:S(2)}, u32[]{:S(2)}) collective-permute-start(bf16[128,384]{1,0:T(8,128)(2,1)S(1)} %pack.1.refs_0_), channel_id=1, source_target_pairs={{0,1},{1,2},{2,3},{3,0},{4,5},{5,6},{6,7},{7,4},{8,9},{9,10},{10,1... | collective-permute-start | bytes 294920 | tf_op jit(solution)/shard_map/ppermute | solution.py:38
  22.6 7.3 %collective-permute-start.5 = (bf16[16,6144]{1,0:T(8,128)(2,1)S(1)}, bf16[16,6144]{1,0:T(8,128)(2,1)S(1)}, u32[]{:S(2)}, u32[]{:S(2)}) collective-permute-start(bf16[16,6144]{1,0:T(8,128)(2,1)S(1)} %get-tuple-element.43.refs_0_), channel_id=1, source_target_pairs={{0,12},{1,13},{2,14},{3,15},{4,0},{5,1},{6,2},{7,3},{8,4},{9,5},{1... | collective-permute-start | bytes 589832 | tf_op jit(solution)/shard_map/ppermute | solution.py:38
  25.4 7.3 %collective-permute-start.4 = (bf16[16,6144]{1,0:T(8,128)(2,1)S(1)}, bf16[16,6144]{1,0:T(8,128)(2,1)S(1)}, u32[]{:S(2)}, u32[]{:S(2)}) collective-permute-start(bf16[16,6144]{1,0:T(8,128)(2,1)S(1)} %get-tuple-element.43.refs_0_), channel_id=1, source_target_pairs={{0,8},{1,9},{2,10},{3,11},{4,12},{5,13},{6,14},{7,15},{8,0},{9,1},... | collective-permute-start | bytes 589832 | tf_op jit(solution)/shard_map/ppermute | solution.py:38
  25.7 12.2 %collective-permute-start.3 = (bf16[16,6144]{1,0:T(8,128)(2,1)S(1)}, bf16[16,6144]{1,0:T(8,128)(2,1)S(1)}, u32[]{:S(2)}, u32[]{:S(2)}) collective-permute-start(bf16[16,6144]{1,0:T(8,128)(2,1)S(1)} %get-tuple-element.43.refs_0_), channel_id=1, source_target_pairs={{0,4},{1,5},{2,6},{3,7},{4,8},{5,9},{6,10},{7,11},{8,12},{9,13},{1... | collective-permute-start | bytes 589832 | tf_op jit(solution)/shard_map/ppermute | solution.py:38
  26.4 11.5 %collective-permute-start.8 = (bf16[64,1536]{1,0:T(8,128)(2,1)S(1)}, bf16[64,1536]{1,0:T(8,128)(2,1)S(1)}, u32[]{:S(2)}, u32[]{:S(2)}) collective-permute-start(bf16[64,1536]{1,0:T(8,128)(2,1)S(1)} %get-tuple-element.44.refs_4_), channel_id=1, source_target_pairs={{0,96},{1,97},{2,98},{3,99},{4,100},{5,101},{6,102},{7,103},{8,104... | collective-permute-start | bytes 589832 | tf_op jit(solution)/shard_map/ppermute | solution.py:38
  29.9 8.0 %collective-permute-start.7 = (bf16[64,1536]{1,0:T(8,128)(2,1)S(1)}, bf16[64,1536]{1,0:T(8,128)(2,1)S(1)}, u32[]{:S(2)}, u32[]{:S(2)}) collective-permute-start(bf16[64,1536]{1,0:T(8,128)(2,1)S(1)} %get-tuple-element.44.refs_4_), channel_id=1, source_target_pairs={{0,64},{1,65},{2,66},{3,67},{4,68},{5,69},{6,70},{7,71},{8,72},{9,... | collective-permute-start | bytes 589832 | tf_op jit(solution)/shard_map/ppermute | solution.py:38
  39.1 15.0 %collective-permute-start.10 = (bf16[64,6144]{1,0:T(8,128)(2,1)S(1)}, bf16[64,6144]{1,0:T(8,128)(2,1)S(1)}, u32[]{:S(2)}, u32[]{:S(2)}) collective-permute-start(bf16[64,6144]{1,0:T(8,128)(2,1)S(1)} %get-tuple-element.45.refs_0_), channel_id=1, source_target_pairs={{0,96},{1,97},{2,98},{3,99},{4,100},{5,101},{6,102},{7,103},{8,104... | collective-permute-start | bytes 2359304 | tf_op jit(solution)/shard_map/ppermute | solution.py:38
  41.2 15.4 %collective-permute-start.9 = (bf16[64,6144]{1,0:T(8,128)(2,1)S(1)}, bf16[64,6144]{1,0:T(8,128)(2,1)S(1)}, u32[]{:S(2)}, u32[]{:S(2)}) collective-permute-start(bf16[64,6144]{1,0:T(8,128)(2,1)S(1)} %get-tuple-element.45.refs_0_), channel_id=1, source_target_pairs={{0,32},{1,33},{2,34},{3,35},{4,36},{5,37},{6,38},{7,39},{8,40},{9,... | collective-permute-start | bytes 2359304 | tf_op jit(solution)/shard_map/ppermute | solution.py:38
  41.2 23.7 %collective-permute-start.12 = (bf16[256,1536]{1,0:T(8,128)(2,1)S(1)}, bf16[256,1536]{1,0:T(8,128)(2,1)S(1)}, u32[]{:S(2)}, u32[]{:S(2)}) collective-permute-start(bf16[256,1536]{1,0:T(8,128)(2,1)S(1)} %get-tuple-element.46.refs_5_), channel_id=1, source_target_pairs={{0,12},{1,13},{2,14},{3,15},{4,0},{5,1},{6,2},{7,3},{8,4},{9,5},{1... | collective-permute-start | bytes 2359304 | tf_op jit(solution)/shard_map/ppermute | solution.py:38
  50.3 17.8 %collective-permute-start.11 = (bf16[256,1536]{1,0:T(8,128)(2,1)S(1)}, bf16[256,1536]{1,0:T(8,128)(2,1)S(1)}, u32[]{:S(2)}, u32[]{:S(2)}) collective-permute-start(bf16[256,1536]{1,0:T(8,128)(2,1)S(1)} %get-tuple-element.46.refs_5_), channel_id=1, source_target_pairs={{0,4},{1,5},{2,6},{3,7},{4,8},{5,9},{6,10},{7,11},{8,12},{9,13},{1... | collective-permute-start | bytes 2359304 | tf_op jit(solution)/shard_map/ppermute | solution.py:38
  68.1 8.5 %collective-permute-start.13 = (bf16[32,6144]{1,0:T(8,128)(2,1)S(1)}, bf16[32,6144]{1,0:T(8,128)(2,1)S(1)}, u32[]{:S(2)}, u32[]{:S(2)}) collective-permute-start(bf16[32,6144]{1,0:T(8,128)(2,1)S(1)} %get-tuple-element.47), channel_id=1, source_target_pairs={{0,32},{1,33},{2,34},{3,35},{4,36},{5,37},{6,38},{7,39},{8,40},{9,... | collective-permute-start | bytes 1179656 | tf_op jit(solution)/shard_map/ppermute | solution.py:38
  68.2 8.4 %collective-permute-start.14 = (bf16[32,6144]{1,0:T(8,128)(2,1)S(1)}, bf16[32,6144]{1,0:T(8,128)(2,1)S(1)}, u32[]{:S(2)}, u32[]{:S(2)}) collective-permute-start(bf16[32,6144]{1,0:T(8,128)(2,1)S(1)} %get-tuple-element.48), channel_id=1, source_target_pairs={{0,96},{1,97},{2,98},{3,99},{4,100},{5,101},{6,102},{7,103},{8,104... | collective-permute-start | bytes 1179656 | tf_op jit(solution)/shard_map/ppermute | solution.py:38
  70.9 8.1 %collective-permute-start.15 = (bf16[128,1536]{1,0:T(8,128)(2,1)S(1)}, bf16[128,1536]{1,0:T(8,128)(2,1)S(1)}, u32[]{:S(2)}, u32[]{:S(2)}) collective-permute-start(bf16[128,1536]{1,0:T(8,128)(2,1)S(1)} %get-tuple-element.49), channel_id=1, source_target_pairs={{0,4},{1,5},{2,6},{3,7},{4,8},{5,9},{6,10},{7,11},{8,12},{9,13},{1... | collective-permute-start | bytes 1179656 | tf_op jit(solution)/shard_map/ppermute | solution.py:38
  70.9 8.1 %collective-permute-start.16 = (bf16[128,1536]{1,0:T(8,128)(2,1)S(1)}, bf16[128,1536]{1,0:T(8,128)(2,1)S(1)}, u32[]{:S(2)}, u32[]{:S(2)}) collective-permute-start(bf16[128,1536]{1,0:T(8,128)(2,1)S(1)} %get-tuple-element.50), channel_id=1, source_target_pairs={{0,12},{1,13},{2,14},{3,15},{4,0},{5,1},{6,2},{7,3},{8,4},{9,5},{1... | collective-permute-start | bytes 1179656 | tf_op jit(solution)/shard_map/ppermute | solution.py:38
  104.1 24.5 %collective-permute-start.24 = (bf16[256,6912]{1,0:T(8,128)(2,1)}, bf16[256,6912]{1,0:T(8,128)(2,1)S(1)}, u32[]{:S(2)}, u32[]{:S(2)}) collective-permute-start(bf16[256,6912]{1,0:T(8,128)(2,1)} %get-tuple-element.59.refs_0_), channel_id=1, source_target_pairs={{0,16},{1,17},{2,18},{3,19},{4,20},{5,21},{6,22},{7,23},{8,24},{9,... | collective-permute-start | bytes 10616840 | tf_op jit(solution)/shard_map/ppermute | solution.py:49
  109.0 12.9 %collective-permute-start.18 = (bf16[64,3456]{1,0:T(8,128)(2,1)}, bf16[64,3456]{1,0:T(8,128)(2,1)S(1)}, u32[]{:S(2)}, u32[]{:S(2)}) collective-permute-start(bf16[64,3456]{1,0:T(8,128)(2,1)} %get-tuple-element.52), channel_id=1, source_target_pairs={{0,96},{1,97},{2,98},{3,99},{4,100},{5,101},{6,102},{7,103},{8,104... | collective-permute-start | bytes 1327112 | tf_op jit(solution)/shard_map/ppermute | solution.py:38
  109.1 12.8 %collective-permute-start.20 = (bf16[64,3456]{1,0:T(8,128)(2,1)}, bf16[64,3456]{1,0:T(8,128)(2,1)S(1)}, u32[]{:S(2)}, u32[]{:S(2)}) collective-permute-start(bf16[64,3456]{1,0:T(8,128)(2,1)} %get-tuple-element.54), channel_id=1, source_target_pairs={{0,32},{1,33},{2,34},{3,35},{4,36},{5,37},{6,38},{7,39},{8,40},{9,... | collective-permute-start | bytes 1327112 | tf_op jit(solution)/shard_map/ppermute | solution.py:38
  110.5 11.5 %collective-permute-start.21 = (bf16[4,16,3072]{2,1,0:T(8,128)(2,1)}, bf16[4,16,3072]{2,1,0:T(8,128)(2,1)S(1)}, u32[]{:S(2)}, u32[]{:S(2)}) collective-permute-start(bf16[4,16,3072]{2,1,0:T(8,128)(2,1)} %get-tuple-element.56), channel_id=1, source_target_pairs={{0,4},{1,5},{2,6},{3,7},{4,8},{5,9},{6,10},{7,11},{8,12},{9,13},{1... | collective-permute-start | bytes 1179656 | tf_op jit(solution)/shard_map/ppermute | solution.py:38
  110.5 11.5 %collective-permute-start.23 = (bf16[4,16,3072]{2,1,0:T(8,128)(2,1)}, bf16[4,16,3072]{2,1,0:T(8,128)(2,1)S(1)}, u32[]{:S(2)}, u32[]{:S(2)}) collective-permute-start(bf16[4,16,3072]{2,1,0:T(8,128)(2,1)} %get-tuple-element.58), channel_id=1, source_target_pairs={{0,12},{1,13},{2,14},{3,15},{4,0},{5,1},{6,2},{7,3},{8,4},{9,5},{1... | collective-permute-start | bytes 1179656 | tf_op jit(solution)/shard_map/ppermute | solution.py:38
  124.1 18.7 %collective-permute-start.31 = (bf16[256,6144]{1,0:T(8,128)(2,1)S(1)}, bf16[256,6144]{1,0:T(8,128)(2,1)S(1)}, u32[]{:S(2)}, u32[]{:S(2)}) collective-permute-start(bf16[256,6144]{1,0:T(8,128)(2,1)S(1)} %relay.1), channel_id=1, source_target_pairs={{0,16},{1,17},{2,18},{3,19},{4,20},{5,21},{6,22},{7,23},{8,24},{9,... | collective-permute-start | bytes 9437192 | tf_op jit(solution)/shard_map/ppermute | solution.py:49
  125.7 12.5 %collective-permute-start.19 = (bf16[64,3456]{1,0:T(8,128)(2,1)S(1)}, bf16[64,3456]{1,0:T(8,128)(2,1)S(1)}, u32[]{:S(2)}, u32[]{:S(2)}) collective-permute-start(bf16[64,3456]{1,0:T(8,128)(2,1)S(1)} %copy-done.22), channel_id=1, source_target_pairs={{0,64},{1,65},{2,66},{3,67},{4,68},{5,69},{6,70},{7,71},{8,72},{9,... | collective-permute-start | bytes 1327112 | tf_op jit(solution)/shard_map/ppermute | solution.py:38
  126.4 11.1 %collective-permute-start.22 = (bf16[4,16,3072]{2,1,0:T(8,128)(2,1)S(1)}, bf16[4,16,3072]{2,1,0:T(8,128)(2,1)S(1)}, u32[]{:S(2)}, u32[]{:S(2)}) collective-permute-start(bf16[4,16,3072]{2,1,0:T(8,128)(2,1)S(1)} %copy-done.23), channel_id=1, source_target_pairs={{0,8},{1,9},{2,10},{3,11},{4,12},{5,13},{6,14},{7,15},{8,0},{9,1},... | collective-permute-start | bytes 1179656 | tf_op jit(solution)/shard_map/ppermute | solution.py:38
  139.4 6.4 %collective-permute-start.28 = (bf16[16,3072]{1,0:T(8,128)(2,1)S(1)}, bf16[16,3072]{1,0:T(8,128)(2,1)S(1)}, u32[]{:S(2)}, u32[]{:S(2)}) collective-permute-start(bf16[16,3072]{1,0:T(8,128)(2,1)S(1)} %get-tuple-element.67), channel_id=1, source_target_pairs={{0,96},{1,97},{2,98},{3,99},{4,100},{5,101},{6,102},{7,103},{8,104... | collective-permute-start | bytes 294920 | tf_op jit(solution)/shard_map/ppermute | solution.py:38
  140.8 10.0 %collective-permute-start.29 = (bf16[16,3072]{1,0:T(8,128)(2,1)S(1)}, bf16[16,3072]{1,0:T(8,128)(2,1)S(1)}, u32[]{:S(2)}, u32[]{:S(2)}) collective-permute-start(bf16[16,3072]{1,0:T(8,128)(2,1)S(1)} %get-tuple-element.68), channel_id=1, source_target_pairs={{0,64},{1,65},{2,66},{3,67},{4,68},{5,69},{6,70},{7,71},{8,72},{9,... | collective-permute-start | bytes 294920 | tf_op jit(solution)/shard_map/ppermute | solution.py:38
  141.8 9.0 %collective-permute-start.30 = (bf16[16,3072]{1,0:T(8,128)(2,1)S(1)}, bf16[16,3072]{1,0:T(8,128)(2,1)S(1)}, u32[]{:S(2)}, u32[]{:S(2)}) collective-permute-start(bf16[16,3072]{1,0:T(8,128)(2,1)S(1)} %get-tuple-element.69), channel_id=1, source_target_pairs={{0,32},{1,33},{2,34},{3,35},{4,36},{5,37},{6,38},{7,39},{8,40},{9,... | collective-permute-start | bytes 294920 | tf_op jit(solution)/shard_map/ppermute | solution.py:38
  141.9 8.9 %collective-permute-start.25 = (bf16[16,3456]{1,0:T(8,128)(2,1)S(1)}, bf16[16,3456]{1,0:T(8,128)(2,1)S(1)}, u32[]{:S(2)}, u32[]{:S(2)}) collective-permute-start(bf16[16,3456]{1,0:T(8,128)(2,1)S(1)} %get-tuple-element.63), channel_id=1, source_target_pairs={{0,4},{1,5},{2,6},{3,7},{4,8},{5,9},{6,10},{7,11},{8,12},{9,13},{1... | collective-permute-start | bytes 331784 | tf_op jit(solution)/shard_map/ppermute | solution.py:38
  142.8 8.0 %collective-permute-start.26 = (bf16[16,3456]{1,0:T(8,128)(2,1)S(1)}, bf16[16,3456]{1,0:T(8,128)(2,1)S(1)}, u32[]{:S(2)}, u32[]{:S(2)}) collective-permute-start(bf16[16,3456]{1,0:T(8,128)(2,1)S(1)} %get-tuple-element.64), channel_id=1, source_target_pairs={{0,8},{1,9},{2,10},{3,11},{4,12},{5,13},{6,14},{7,15},{8,0},{9,1},... | collective-permute-start | bytes 331784 | tf_op jit(solution)/shard_map/ppermute | solution.py:38
  157.6 5.8 %collective-permute-start.35 = (f32[8,128]{1,0:T(8,128)S(1)}, f32[8,128]{1,0:T(8,128)S(1)}, u32[]{:S(2)}, u32[]{:S(2)}) collective-permute-start(f32[8,128]{1,0:T(8,128)S(1)} %get-tuple-element.80.own), channel_id=1, source_target_pairs={{0,16},{1,17},{2,18},{3,19},{4,20},{5,21},{6,22},{7,23},{8,24},{9,... | collective-permute-start | bytes 12296 | tf_op jit(solution)/shard_map/ppermute | solution.py:49
  (30 other events, 321.7 us)
Sparse Core Ops, SparseCore 0:
  9.7 23.0 all-gather.4
  34.5 20.7 all-gather.6

commit v3 on v1

--- a/solution.py
+++ b/solution.py
@@ -220,18 +220,10 @@
     return out[:, 0:128] + out[:, 128:256] + out[:, 256:384]
 
 
-def main_kernel(where, *refs):
-    t_in, g_in = refs[0:5], refs[5:10]
-    weights = (refs[10:13], refs[13:16])
-    slots_ref, gates_ref = refs[16:18]
-    pa_out, pb_out = refs[18:22], refs[22:26]
-    own_out, rows_out, grads_out = refs[26:29]
-    rows, grads, wv, dv, pa, pb = refs[29:35]
-    acc_g, acc_b, deltas, tile, rbuf, packed = refs[35:41]
-    sem_t, sem_g, sem_w, sem_d, sem_o = refs[41:46]
-    x, y, core = where[0], where[1], where[4]
-    copies_t = row_copies(t_in, rows, sem_t)
-    copies_g = grad_copies(g_in, grads, sem_g, y)
+def early_kernel(where, *refs):
+    t, g, weights = refs[0:3], refs[3:6], (refs[6:9], refs[9:12])
+    acc_g, acc_b, wv, dv, sem_w, sem_d = refs[12:18]
+    y = where[1]
     tiles = D // KT
 
     def wide_copies(i):
@@ -244,25 +236,104 @@
             for n in range(2)
         ]
 
-    def tall_copies(i):
+    tall_copies = []
+    for j, step in enumerate((0, -1, 1)):
+        block = pl.ds(pl.multiple_of(((y + step + NY) % NY) * 1536, 128), 1536)
+        tall_copies.append(
+            [
+                pltpu.make_async_copy(weights[s][2].at[:, :, block], dv.at[j, s], sem_d.at[j, s])
+                for s in range(2)
+            ]
+        )
+    for i in range(tiles):
+        for copy in wide_copies(i):
+            copy.start()
+    for group in tall_copies:
+        for copy in group:
+            copy.start()
+    acc_g[...] = jnp.zeros(acc_g.shape, F32)
+    acc_b[...] = jnp.zeros(acc_b.shape, F32)
+
+    @pl.loop(0, tiles)
+    def _(i):
+        for copy in wide_copies(i):
+            copy.wait()
+        k = pl.ds(pl.multiple_of(i * KT, KT), KT)
+        wide = jnp.concatenate(
+            [wv[s, n, e, k, :] for s in range(2) for e in range(2) for n in range(2)], axis=1
+        )
+        rows = jnp.concatenate([piece[:, k] for piece in t], axis=0)
+        acc_g[...] += jnp.dot(rows, wide, preferred_element_type=F32)
+
+    for j, group in enumerate(tall_copies):
+        for copy in group:
+            copy.wait()
+        tall = jnp.concatenate([dv[j, s, e] for s in range(2) for e in range(2)], axis=0)
+        acc_b[...] += nt(g[j][...], tall)
+
+
+def run_early(where, t, g, weights):
+    hbm = [pl.BlockSpec(memory_space=pltpu.HBM)]
+    return pl.pallas_call(
+        early_kernel,
+        out_shape=[
+            jax.ShapeDtypeStruct((192, 1024), F32),
+            jax.ShapeDtypeStruct((HALF, 512), F32),
+        ],
+        in_specs=[SMEM_SPEC] + vmem_specs(6) + hbm * 6,
+        out_specs=vmem_specs(2),
+        scratch_shapes=[
+            pltpu.VMEM((2, 2, 2, D, H), BF),
+            pltpu.VMEM((3, 2, 2, H, 1536), BF),
+            pltpu.SemaphoreType.DMA((D // KT, 4)),
+            pltpu.SemaphoreType.DMA((3, 2)),
+        ],
+        compiler_params=pltpu.CompilerParams(vmem_limit_bytes=30 * MIB),
+        cost_estimate=pl.CostEstimate(
+            flops=3_600_000_000, bytes_accessed=20_000_000, transcendentals=0
+        ),
+        name="early",
+    )(where, *t, *g, *weights)
+
+
+def main_kernel(where, *refs):
+    t_in, g_in = refs[0:5], refs[5:10]
+    weights = (refs[10:13], refs[13:16])
+    slots_ref, gates_ref, early_g, early_b = refs[16:20]
+    pa_out, pb_out = refs[20:25], refs[25:30]
+    own_out, rows_out, grads_out = refs[30:33]
+    rows, grads, wv, dv, pa, pb = refs[33:39]
+    acc_g, acc_b, deltas, tile, rbuf, packed = refs[39:45]
+    sem_t, sem_g, sem_w, sem_d, sem_o = refs[45:50]
+    x, y, core = where[0], where[1], where[4]
+    copies_t = row_copies(t_in, rows, sem_t)
+    copies_g = grad_copies(g_in, grads, sem_g, y)
+    tiles = D // KT
+
+    def wide_copies(i):
         k = pl.ds(pl.multiple_of(i * KT, KT), KT)
         return [
-            pltpu.make_async_copy(weights[s][2].at[:, :, k], dv.at[s, :, :, k], sem_d.at[i, s])
+            pltpu.make_async_copy(
+                weights[s][n].at[:, k, :], wv.at[s, n, :, k, :], sem_w.at[i, s * 2 + n]
+            )
             for s in range(2)
+            for n in range(2)
         ]
 
+    far = pl.ds(pl.multiple_of(((y + 2) % NY) * 1536, 128), 1536)
+    tall_copies = [
+        pltpu.make_async_copy(weights[s][2].at[:, :, far], dv.at[s], sem_d.at[s]) for s in range(2)
+    ]
     for copy in copies_t:
         copy.start()
     for i in range(tiles):
         for copy in wide_copies(i):
             copy.start()
-    for copy in copies_g:
+    for copy in copies_g + tall_copies:
         copy.start()
-    for i in range(tiles):
-        for copy in tall_copies(i):
-            copy.start()
-    acc_g[...] = jnp.zeros(acc_g.shape, F32)
-    acc_b[...] = jnp.zeros(acc_b.shape, F32)
+    acc_g[0:128, :] = early_g[0:128, :]
+    acc_g[128:192, :] = jnp.zeros((64, 1024), F32)
+    acc_g[192:256, :] = early_g[128:192, :]
     scales = []
     slot = lax.broadcasted_iota(jnp.int32, (HALF, 256), 1)
     row = lax.broadcasted_iota(jnp.int32, (HALF, 256), 0)
@@ -285,19 +356,12 @@
         wide = jnp.concatenate(
             [wv[s, n, e, k, :] for s in range(2) for e in range(2) for n in range(2)], axis=1
         )
-        acc_g[...] += jnp.dot(rows[:, k], wide, preferred_element_type=F32)
-
-    for copy in copies_g:
+        acc_g[128:192, :] += jnp.dot(rows[128:192, k], wide, preferred_element_type=F32)
+
+    for copy in copies_g + tall_copies:
         copy.wait()
-
-    @pl.loop(0, tiles)
-    def _(i):
-        for copy in tall_copies(i):
-            copy.wait()
-        k = pl.ds(pl.multiple_of(i * KT, KT), KT)
-        tall = jnp.concatenate([dv[s, e, :, k] for s in range(2) for e in range(2)], axis=0)
-        acc_b[...] += nt(grads[:, k], tall)
-
+    tall = jnp.concatenate([dv[s, e] for s in range(2) for e in range(2)], axis=0)
+    acc_b[...] = early_b[...] + nt(grads[:, far], tall)
     rows_copy.start()
     grads_copy.start()
     router = [0.0, 0.0]
@@ -352,7 +416,10 @@
         for k in range(NX):
             pa[k, :, f] = part[k * 64 : (k + 1) * 64, :]
 
-    copies = [pltpu.make_async_copy(pa.at[k], pa_out[k], sem_o.at[4 + k]) for k in range(NX)]
+    parts = (pa.at[0], pa.at[1], pa.at[3], pa.at[2, pl.ds(0, 32), :], pa.at[2, pl.ds(32, 32), :])
+    copies = [
+        pltpu.make_async_copy(part, pa_out[k], sem_o.at[4 + k]) for k, part in enumerate(parts)
+    ]
     for copy in copies:
         copy.start()
 
@@ -365,18 +432,23 @@
                 src = pl.multiple_of(b * 64 + ((y + k) % NY) * 16, 16)
                 pb[k, b, :, f] = tile[pl.ds(src, 16), :]
 
-    more = [pltpu.make_async_copy(pb.at[k], pb_out[k], sem_o.at[8 + k]) for k in range(NY)]
+    parts = (pb.at[0], pb.at[1], pb.at[3], pb.at[2, pl.ds(0, 2)], pb.at[2, pl.ds(2, 2)])
+    more = [
+        pltpu.make_async_copy(part, pb_out[k], sem_o.at[9 + k]) for k, part in enumerate(parts)
+    ]
     for copy in more:
         copy.start()
     for copy in [rows_copy, grads_copy, own_copy, sib_copy] + copies + more:
         copy.wait()
 
 
-def run_main(where, t, g, weights, slots, gates):
+def run_main(where, t, g, weights, slots, gates, early):
     hbm = [pl.BlockSpec(memory_space=pltpu.HBM)]
     out_shape = (
-        [jax.ShapeDtypeStruct((64, WIDE), BF)] * 4
-        + [jax.ShapeDtypeStruct((4, 16, D // 2), BF)] * 4
+        [jax.ShapeDtypeStruct((64, WIDE), BF)] * 3
+        + [jax.ShapeDtypeStruct((32, WIDE), BF)] * 2
+        + [jax.ShapeDtypeStruct((4, 16, D // 2), BF)] * 3
+        + [jax.ShapeDtypeStruct((2, 16, D // 2), BF)] * 2
         + [jax.ShapeDtypeStruct((HALF, 768), BF)]
         + [jax.ShapeDtypeStruct((HALF, D + 768), BF)]
         + [jax.ShapeDtypeStruct((HALF, D), BF)]
@@ -384,13 +456,13 @@
     return pl.pallas_call(
         main_kernel,
         out_shape=out_shape,
-        in_specs=[SMEM_SPEC] + hbm * 16 + vmem_specs(2),
-        out_specs=hbm * 11,
+        in_specs=[SMEM_SPEC] + hbm * 16 + vmem_specs(4),
+        out_specs=hbm * 13,
         scratch_shapes=[
             pltpu.VMEM((HALF, D), BF),
             pltpu.VMEM((HALF, D), BF),
             pltpu.VMEM((2, 2, 2, D, H), BF),
-            pltpu.VMEM((2, 2, H, D), BF),
+            pltpu.VMEM((2, 2, H, 1536), BF),
             pltpu.VMEM((4, 64, WIDE), BF),
             pltpu.VMEM((4, 4, 16, D // 2), BF),
             pltpu.VMEM((HALF, 1024), F32),
@@ -402,15 +474,15 @@
             pltpu.SemaphoreType.DMA((5,)),
             pltpu.SemaphoreType.DMA((5,)),
             pltpu.SemaphoreType.DMA((D // KT, 4)),
-            pltpu.SemaphoreType.DMA((D // KT, 2)),
-            pltpu.SemaphoreType.DMA((12,)),
+            pltpu.SemaphoreType.DMA((2,)),
+            pltpu.SemaphoreType.DMA((14,)),
         ],
-        compiler_params=pltpu.CompilerParams(vmem_limit_bytes=44 * MIB),
+        compiler_params=pltpu.CompilerParams(vmem_limit_bytes=38 * MIB),
         cost_estimate=pl.CostEstimate(
             flops=8_000_000_000, bytes_accessed=30_000_000, transcendentals=262144
         ),
         name="main",
-    )(where, *t, *g, *weights, slots, gates)
+    )(where, *t, *g, *weights, slots, gates, *early)
 
 
 def up_kernel(*refs):
@@ -490,8 +562,39 @@
     )(grads_own, grads_sib, own, rows_sib)
 
 
+def middle_sum_kernel(*refs):
+    a_down, a_up, b_up, b_down = refs[0:4]
+    low_a, high_a, low_b, high_b = refs[4:8]
+    out_a_down, out_a_up, out_b_up, out_b_down = refs[8:12]
+    half = D // 2
+    out_a_down[0:32, 0:half] = total(a_down[0:32, 0:half], [low_a[:, 0:half]]).astype(BF)
+    out_a_down[32:64, :] = a_down[32:64, :]
+    sums = join_three(a_down[0:16, half:]) + join_three(low_a[0:16, half:])
+    out_a_down[0:16, half:] = split_three(sums)
+    out_a_down[16:32, half:] = a_down[16:32, half:]
+    out_a_up[0:32, :] = a_up[0:32, :]
+    out_a_up[32:64, :] = total(a_up[32:64, :], [high_a[...]]).astype(BF)
+    for k in range(2):
+        out_b_up[k] = total(b_up[k], [low_b[k]]).astype(BF)
+        out_b_up[2 + k] = b_up[2 + k]
+        out_b_down[k] = b_down[k]
+        out_b_down[2 + k] = total(b_down[2 + k], [high_b[k]]).astype(BF)
+
+
+def run_middle_sum(blocks, halves):
+    return pl.pallas_call(
+        middle_sum_kernel,
+        out_shape=[jax.ShapeDtypeStruct((64, WIDE), BF)] * 2
+        + [jax.ShapeDtypeStruct((4, 16, D // 2), BF)] * 2,
+        in_specs=vmem_specs(8),
+        out_specs=vmem_specs(4),
+        compiler_params=pltpu.CompilerParams(vmem_limit_bytes=8 * MIB),
+        name="middle_sum",
+    )(*blocks, *halves)
+
+
 def first_sum_kernel(where, *refs):
-    ra, rb, qa, qb, buf = refs[0:4], refs[4:8], refs[9:13], refs[13:17], refs[17]
+    ra, rb, qa, qb, buf = refs[0:3], refs[3:6], refs[7:11], refs[11:15], refs[15]
     half = D // 2
     buf[...] = total(ra[0][:, 0:half], [r[:, 0:half] for r in ra[1:]]).astype(BF)
     sums = join_three(ra[0][0:16, half:])
@@ -511,7 +614,7 @@
         first_sum_kernel,
         out_shape=[jax.ShapeDtypeStruct((16, WIDE), BF)] * 4
         + [jax.ShapeDtypeStruct((16, D // 2), BF)] * 4,
-        in_specs=[SMEM_SPEC] + vmem_specs(9),
+        in_specs=[SMEM_SPEC] + vmem_specs(7),
         out_specs=vmem_specs(8),
         scratch_shapes=[pltpu.VMEM((64, D // 2), BF)],
         compiler_params=pltpu.CompilerParams(vmem_limit_bytes=8 * MIB),
@@ -626,16 +729,20 @@
     t = (t64, t_low, t_high, shift(a, "x", 1), shift(b, "x", -1))
     g = (g256, g_low, g_high, shift(e, "y", 1), shift(f, "y", -1))
     weights = (gate_weight, up_weight, down_weight, gate_sib, up_sib, down_sib)
-    outs = run_main(where, t, g, weights, slot_tokens, slot_gates)
-    pa, pb = outs[0:4], outs[4:8]
-    dl_own, rows, grads = outs[8:]
-
-    ra = [pa[0]] + [shift(pa[k], "x", -k) for k in (1, 2, 3)]
-    rb = [pb[0]] + [shift(pb[k], "y", k) for k in (1, 2, 3)]
+    early = run_early(where, t[0:3], g[0:3], weights)
+    outs = run_main(where, t, g, weights, slot_tokens, slot_gates, early)
+    a_own, a_down, a_up, a_low, a_high = outs[0:5]
+    b_own, b_up, b_down, b_low, b_high = outs[5:10]
+    dl_own, rows, grads = outs[10:]
+
+    halves = [shift(a_low, "x", -1), shift(a_high, "x", 1)]
+    halves += [shift(b_low, "y", 1), shift(b_high, "y", -1)]
     rows_sib = swap(rows)
-    before = [ra[1], ra[3], rb[1], rb[3]]
-    grads_sib = swap(run_relay(grads, before))
-    gate_grad, up_grad, token = run_up(rows, rows_sib, dl_own, before)
+    grads_sib = swap(run_relay(grads, halves))
+    a_down, a_up, b_up, b_down = run_middle_sum((a_down, a_up, b_up, b_down), halves)
+    gate_grad, up_grad, token = run_up(rows, rows_sib, dl_own, [a_down])
+    ra = [a_own, shift(a_down, "x", -1), shift(a_up, "x", 1)]
+    rb = [b_own, shift(b_up, "y", 1), shift(b_down, "y", -1)]
     q = run_first_sum(where, ra, rb, token)
     qa, qb = q[0:4], q[4:8]
     ra = [qa[0]] + [shift(qa[k], "y", k) for k in (1, 2, 3)]

time: 163 us -> 155 us (0.951)
  waiting for transfers between devices: 64.1 us -> 51.7 us
  Pallas kernels: 38.2 us -> 43.4 us
  local copies, waits for them, and re-layouts: 5.22 us -> 2.36 us
  starting transfers between devices: 54.3 us -> 56.5 us
    ppermute x32 -> x34, waiting for transfers between devices: 63.2 us -> 50.9 us  [shift(): return lax.ppermute(value, AXES, shift_pairs(axis, step))]
    pallas_call x0 -> x2, Pallas kernels: none -> 7.37 us  [the longest x1 7.15 us: run_early(): pl.pallas_call(early_kernel, out_shape=[jax.ShapeDtypeStruct((192, 1024),...]
    unnamed x16 -> x18, local copies, waits for them, and re-layouts: 4.49 us -> 1.63 us
    pallas_call x1, Pallas kernels: 18.9 us -> 16.9 us  [run_main(): pl.pallas_call(main_kernel, out_shape=out_shape, in_specs=[SMEM_SPEC] + h...]
    ppermute x32 -> x34, starting transfers between devices: 39.7 us -> 41 us  [shift(): return lax.ppermute(value, AXES, shift_pairs(axis, step))]
  transfers between devices with their start and end apart: 38 -> 40, of which waited for: 20 -> 15; matrix products, arithmetic and copies ran while one was open for 0% -> 0% of each run, Pallas kernels for 10% -> 15%
where the time goes in v3:
time: 155 us
  starting transfers between devices  56.5 us (36%)
  waiting for transfers between devices  51.7 us (33%)
  Pallas kernels  43.4 us (28%)
  local copies, waits for them, and re-layouts  2.36 us (2%)
    ppermute x34, waiting for transfers between devices, shift(): return lax.ppermute(value, AXES, shift_pairs(axis, step))  50.9 us
    ppermute x34, starting transfers between devices, shift(): return lax.ppermute(value, AXES, shift_pairs(axis, step))  41 us
    pallas_call x1, Pallas kernels, run_main(): pl.pallas_call(main_kernel, out_shape=out_shape, in_specs=[SMEM_SPEC] + h...  16.9 us
    ppermute x6, starting transfers between devices, swap(): return lax.ppermute(value, AXES, pairs)  15.5 us
    pallas_call x1, Pallas kernels, run_up(): pl.pallas_call(up_kernel, grid=(D // FT,), out_shape=[jax.ShapeDtypeStruc...  8.64 us
    pallas_call x1, Pallas kernels, run_early(): pl.pallas_call(early_kernel, out_shape=[jax.ShapeDtypeStruct((192, 1024),...  7.15 us
    pallas_call x1, Pallas kernels, run_down(): pl.pallas_call(down_kernel, grid=(D // FT // 2,), out_shape=[jax.ShapeDty...  4.6 us
  transfers between devices with their start and end apart: 40, of which 15 were waited for; matrix products, arithmetic and copies ran while one was open for 0% of the time, Pallas kernels for 15%

profile of v3, /device:TPU:1, one launch (start us, length us, event | category | flops | bytes accessed | tf_op | source)
XLA Modules:
  0.0 154.8 jit_solution(18205382630175430949)
XLA Ops:
  0.6 1.5 collective-permute-start.9
  4.3 3.9 %collective-permute-start.2 = (bf16[128,384]{1,0:T(8,128)(2,1)S(1)}, bf16[128,384]{1,0:T(8,128)(2,1)S(1)}, u32[]{:S(2)}, u32[]{:S(2)}) collective-permute-start(bf16[128,384]{1,0:T(8,128)(2,1)S(1)} %pack.1.refs_0_), channel_id=1, source_target_pairs={{0,3},{1,0},{2,1},{3,2},{4,7},{5,4},{6,5},{7,6},{8,11},{9,8},{10,9... | collective-permute-start | bytes 294920 | tf_op jit(solution)/shard_map/ppermute | solution.py:38
  8.2 4.1 %collective-permute-done.2.refs_3_ = bf16[128,384]{1,0:T(8,128)(2,1)S(1)} collective-permute-done((bf16[128,384]{1,0:T(8,128)(2,1)S(1)}, bf16[128,384]{1,0:T(8,128)(2,1)S(1)}, u32[]{:S(2)}, u32[]{:S(2)}) %collective-permute-start.2) | collective-permute-done | bytes 98336 | tf_op jit(solution)/shard_map/ppermute | solution.py:38
  13.7 4.5 %collective-permute-done.refs_1_ = bf16[128,384]{1,0:T(8,128)(2,1)S(1)} collective-permute-done((bf16[128,384]{1,0:T(8,128)(2,1)S(1)}, bf16[128,384]{1,0:T(8,128)(2,1)S(1)}, u32[]{:S(2)}, u32[]{:S(2)}) %collective-permute-start) | collective-permute-done | bytes 98336 | tf_op jit(solution)/shard_map/ppermute | solution.py:38
  18.8 2.8 %collective-permute-start.5 = (bf16[16,6144]{1,0:T(8,128)(2,1)S(1)}, bf16[16,6144]{1,0:T(8,128)(2,1)S(1)}, u32[]{:S(2)}, u32[]{:S(2)}) collective-permute-start(bf16[16,6144]{1,0:T(8,128)(2,1)S(1)} %get-tuple-element.51.refs_0_), channel_id=1, source_target_pairs={{0,12},{1,13},{2,14},{3,15},{4,0},{5,1},{6,2},{7,3},{8,4},{9,5},{1... | collective-permute-start | bytes 589832 | tf_op jit(solution)/shard_map/ppermute | solution.py:38
  22.0 4.6 %collective-permute-done.5.refs_3_ = bf16[16,6144]{1,0:T(8,128)(2,1)S(1)} collective-permute-done((bf16[16,6144]{1,0:T(8,128)(2,1)S(1)}, bf16[16,6144]{1,0:T(8,128)(2,1)S(1)}, u32[]{:S(2)}, u32[]{:S(2)}) %collective-permute-start.5) | collective-permute-done | bytes 196640 | tf_op jit(solution)/shard_map/ppermute | solution.py:38
  27.7 2.5 %collective-permute-start.8 = (bf16[64,1536]{1,0:T(8,128)(2,1)S(1)}, bf16[64,1536]{1,0:T(8,128)(2,1)S(1)}, u32[]{:S(2)}, u32[]{:S(2)}) collective-permute-start(bf16[64,1536]{1,0:T(8,128)(2,1)S(1)} %get-tuple-element.52.refs_4_), channel_id=1, source_target_pairs={{0,96},{1,97},{2,98},{3,99},{4,100},{5,101},{6,102},{7,103},{8,104... | collective-permute-start | bytes 589832 | tf_op jit(solution)/shard_map/ppermute | solution.py:38
  30.2 5.9 %collective-permute-done.3.refs_1_ = bf16[16,6144]{1,0:T(8,128)(2,1)S(1)} collective-permute-done((bf16[16,6144]{1,0:T(8,128)(2,1)S(1)}, bf16[16,6144]{1,0:T(8,128)(2,1)S(1)}, u32[]{:S(2)}, u32[]{:S(2)}) %collective-permute-start.3) | collective-permute-done | bytes 196640 | tf_op jit(solution)/shard_map/ppermute | solution.py:38
  36.0 2.7 %collective-permute-start.7 = (bf16[64,1536]{1,0:T(8,128)(2,1)S(1)}, bf16[64,1536]{1,0:T(8,128)(2,1)S(1)}, u32[]{:S(2)}, u32[]{:S(2)}) collective-permute-start(bf16[64,1536]{1,0:T(8,128)(2,1)S(1)} %get-tuple-element.52.refs_4_), channel_id=1, source_target_pairs={{0,64},{1,65},{2,66},{3,67},{4,68},{5,69},{6,70},{7,71},{8,72},{9,... | collective-permute-start | bytes 589832 | tf_op jit(solution)/shard_map/ppermute | solution.py:38
  39.1 3.0 %collective-permute-done.7.refs_6_ = bf16[64,1536]{1,0:T(8,128)(2,1)S(1)} collective-permute-done((bf16[64,1536]{1,0:T(8,128)(2,1)S(1)}, bf16[64,1536]{1,0:T(8,128)(2,1)S(1)}, u32[]{:S(2)}, u32[]{:S(2)}) %collective-permute-start.7) | collective-permute-done | bytes 196640 | tf_op jit(solution)/shard_map/ppermute | solution.py:38
  42.1 5.0 %collective-permute-done.6.refs_5_ = bf16[64,1536]{1,0:T(8,128)(2,1)S(1)} collective-permute-done((bf16[64,1536]{1,0:T(8,128)(2,1)S(1)}, bf16[64,1536]{1,0:T(8,128)(2,1)S(1)}, u32[]{:S(2)}, u32[]{:S(2)}) %collective-permute-start.6) | collective-permute-done | bytes 196640 | tf_op jit(solution)/shard_map/ppermute | solution.py:38
  47.9 1.5 collective-permute-start.11
  50.8 13.8 %collective-permute-done.12.t_high.refs_2_ = bf16[64,6144]{1,0:T(8,128)(2,1)S(1)} collective-permute-done((bf16[64,6144]{1,0:T(8,128)(2,1)S(1)}, bf16[64,6144]{1,0:T(8,128)(2,1)S(1)}, u32[]{:S(2)}, u32[]{:S(2)}) %collective-permute-start.12) | collective-permute-done | bytes 786464 | tf_op jit(solution)/shard_map/ppermute | solution.py:38
  64.6 1.2 collective-permute-done.11.t_low.refs_1_
  66.7 1.9 %collective-permute-start.16 = (bf16[32,6144]{1,0:T(8,128)(2,1)S(1)}, bf16[32,6144]{1,0:T(8,128)(2,1)S(1)}, u32[]{:S(2)}, u32[]{:S(2)}) collective-permute-start(bf16[32,6144]{1,0:T(8,128)(2,1)S(1)} %get-tuple-element.56), channel_id=1, source_target_pairs={{0,96},{1,97},{2,98},{3,99},{4,100},{5,101},{6,102},{7,103},{8,104... | collective-permute-start | bytes 1179656 | tf_op jit(solution)/shard_map/ppermute | solution.py:38
  69.5 1.7 %collective-permute-start.18 = (bf16[128,1536]{1,0:T(8,128)(2,1)S(1)}, bf16[128,1536]{1,0:T(8,128)(2,1)S(1)}, u32[]{:S(2)}, u32[]{:S(2)}) collective-permute-start(bf16[128,1536]{1,0:T(8,128)(2,1)S(1)} %get-tuple-element.58), channel_id=1, source_target_pairs={{0,12},{1,13},{2,14},{3,15},{4,0},{5,1},{6,2},{7,3},{8,4},{9,5},{1... | collective-permute-start | bytes 1179656 | tf_op jit(solution)/shard_map/ppermute | solution.py:38
  71.3 7.2 %early.1 = (f32[192,1024]{1,0:T(8,128)S(1)}, f32[256,512]{1,0:T(8,128)S(1)}) custom-call(s32[7]{0:T(128)S(1)} %stack.20.where, bf16[64,6144]{1,0:T(8,128)(2,1)S(1)} %get-tuple-element.53.refs_0_, bf16[64,6144]{1,0:T(8,128)(2,1)S(1)} %collective-permute-done.11.t_low.refs_1_, bf16[64,6144]{1,0:T(8,128)(2,1)S(1)} %collective-permute-done.12.t_high.refs_2_, ...), custom_call_target="tpu_custom_call" | custom-call | flops 3600000000 | bytes 20000000 | tf_op jit(solution)/shard_map/early/pallas_call | solution.py:277
  78.5 16.9 %main.1 = (bf16[64,3456]{1,0:T(8,128)(2,1)S(1)}, bf16[64,3456]{1,0:T(8,128)(2,1)S(1)}, bf16[64,3456]{1,0:T(8,128)(2,1)S(1)}, bf16[32,3456]{1,0:T(8,128)(2,1)S(1)...) custom-call(s32[7]{0:T(128)S(1)} %stack.20.where, ...), custom_call_target="tpu_custom_call" | custom-call | flops 8000000000 | bytes 30000000 | tf_op jit(solution)/shard_map/main/pallas_call | solution.py:456
  95.4 7.0 %collective-permute-start.28 = (bf16[256,6912]{1,0:T(8,128)(2,1)}, bf16[256,6912]{1,0:T(8,128)(2,1)S(1)}, u32[]{:S(2)}, u32[]{:S(2)}) collective-permute-start(bf16[256,6912]{1,0:T(8,128)(2,1)} %get-tuple-element.75.refs_0_), channel_id=1, source_target_pairs={{0,16},{1,17},{2,18},{3,19},{4,20},{5,21},{6,22},{7,23},{8,24},{9,... | collective-permute-start | bytes 10616840 | tf_op jit(solution)/shard_map/ppermute | solution.py:49
  102.6 1.4 collective-permute-start.21
  104.9 1.7 %collective-permute-start.23 = (bf16[2,16,3072]{2,1,0:T(8,128)(2,1)S(1)}, bf16[2,16,3072]{2,1,0:T(8,128)(2,1)S(1)}, u32[]{:S(2)}, u32[]{:S(2)}) collective-permute-start(bf16[2,16,3072]{2,1,0:T(8,128)(2,1)S(1)} %get-tuple-element.69), channel_id=1, source_target_pairs={{0,12},{1,13},{2,14},{3,15},{4,0},{5,1},{6,2},{7,3},{8,4},{9,5},{1... | collective-permute-start | bytes 589832 | tf_op jit(solution)/shard_map/ppermute | solution.py:38
  106.6 4.4 %collective-permute-done.22.refs_6_.refs_3_ = bf16[2,16,3072]{2,1,0:T(8,128)(2,1)S(1)} collective-permute-done((bf16[2,16,3072]{2,1,0:T(8,128)(2,1)S(1)}, bf16[2,16,3072]{2,1,0:T(8,128)(2,1)S(1)}, u32[]{:S(2)}, u32[]{:S(2)}) %collective-permute-start.22) | collective-permute-done | bytes 196640 | tf_op jit(solution)/shard_map/ppermute | solution.py:38
  111.2 1.6 %collective-permute-start.35 = (bf16[256,6144]{1,0:T(8,128)(2,1)S(1)}, bf16[256,6144]{1,0:T(8,128)(2,1)S(1)}, u32[]{:S(2)}, u32[]{:S(2)}) collective-permute-start(bf16[256,6144]{1,0:T(8,128)(2,1)S(1)} %relay.1), channel_id=1, source_target_pairs={{0,16},{1,17},{2,18},{3,19},{4,20},{5,21},{6,22},{7,23},{8,24},{9,... | collective-permute-start | bytes 9437192 | tf_op jit(solution)/shard_map/ppermute | solution.py:49
  113.1 2.7 %collective-permute-start.24 = (bf16[64,3456]{1,0:T(8,128)(2,1)S(1)}, bf16[64,3456]{1,0:T(8,128)(2,1)S(1)}, u32[]{:S(2)}, u32[]{:S(2)}) collective-permute-start(bf16[64,3456]{1,0:T(8,128)(2,1)S(1)} %get-tuple-element.70.refs_4_), channel_id=1, source_target_pairs={{0,96},{1,97},{2,98},{3,99},{4,100},{5,101},{6,102},{7,103},{8,104... | collective-permute-start | bytes 1327112 | tf_op jit(solution)/shard_map/ppermute | solution.py:38
  116.8 1.7 %collective-permute-start.27 = (bf16[4,16,3072]{2,1,0:T(8,128)(2,1)S(1)}, bf16[4,16,3072]{2,1,0:T(8,128)(2,1)S(1)}, u32[]{:S(2)}, u32[]{:S(2)}) collective-permute-start(bf16[4,16,3072]{2,1,0:T(8,128)(2,1)S(1)} %get-tuple-element.74), channel_id=1, source_target_pairs={{0,12},{1,13},{2,14},{3,15},{4,0},{5,1},{6,2},{7,3},{8,4},{9,5},{1... | collective-permute-start | bytes 1179656 | tf_op jit(solution)/shard_map/ppermute | solution.py:38
  118.5 8.6 %up_grads.1 = (bf16[2,6144,128]{2,1,0:T(8,128)(2,1)}, bf16[2,6144,128]{2,1,0:T(8,128)(2,1)}, f32[8,128]{1,0:T(8,128)S(1)}) custom-call(bf16[256,6912]{1,0:T(8,128)(2,1)S(1)} %copy-done.7, bf16[256,6912]{1,0:T(8,128)(2,1)S(1)} %collective-permute-done.28.refs_1_.refs_3_.sib, bf16[256,768]{1,0:T(8,128)(2,1)S(1)} %get-tuple-element.76.refs_2_.own, ...), custom_call_target="tpu_custom_call" | custom-call | flops 3200000000 | bytes 13000000 | tf_op jit(solution)/shard_map/up_grads/pallas_call | solution.py:503
  128.2 1.4 collective-permute-start.32
  131.2 2.9 %collective-permute-start.30 = (bf16[16,3456]{1,0:T(8,128)(2,1)S(1)}, bf16[16,3456]{1,0:T(8,128)(2,1)S(1)}, u32[]{:S(2)}, u32[]{:S(2)}) collective-permute-start(bf16[16,3456]{1,0:T(8,128)(2,1)S(1)} %get-tuple-element.80), channel_id=1, source_target_pairs={{0,8},{1,9},{2,10},{3,11},{4,12},{5,13},{6,14},{7,15},{8,0},{9,1},... | collective-permute-start | bytes 331784 | tf_op jit(solution)/shard_map/ppermute | solution.py:38
  135.0 4.6 %down_grads.1 = (bf16[2,128,6144]{2,1,0:T(8,128)(2,1)}, f32[8,128]{1,0:T(8,128)S(1)}) custom-call(bf16[256,6144]{1,0:T(8,128)(2,1)S(1)} %get-tuple-element.86.refs_0_.grads_own, bf16[256,6144]{1,0:T(8,128)(2,1)S(1)} %collective-permute-done.35.grads_sib, bf16[256,768]{1,0:T(8,128)(2,1)S(1)} %get-tuple-element.76.refs_2_.own, ...), custom_call_target="tpu_custom_call" | custom-call | flops 1600000000 | bytes 10000000 | tf_op jit(solution)/shard_map/down_grads/pallas_call | solution.py:542
  140.5 3.3 %collective-permute-start.37 = (bf16[4,6528]{1,0:T(4,128)(2,1)S(1)}, bf16[4,6528]{1,0:T(4,128)(2,1)S(1)}, u32[]{:S(2)}, u32[]{:S(2)}) collective-permute-start(bf16[4,6528]{1,0:T(4,128)(2,1)S(1)} %get-tuple-element.90), channel_id=1, source_target_pairs={{0,2},{1,3},{2,0},{3,1},{4,6},{5,7},{6,4},{7,5},{8,10},{9,11},{10,... | collective-permute-start | bytes 156680 | tf_op jit(solution)/shard_map/ppermute | solution.py:38
  147.3 4.8 %collective-permute-start.39 = (f32[8,128]{1,0:T(8,128)S(1)}, f32[8,128]{1,0:T(8,128)S(1)}, u32[]{:S(2)}, u32[]{:S(2)}) collective-permute-start(f32[8,128]{1,0:T(8,128)S(1)} %get-tuple-element.96.own), channel_id=1, source_target_pairs={{0,16},{1,17},{2,18},{3,19},{4,20},{5,21},{6,22},{7,23},{8,24},{9,... | collective-permute-start | bytes 12296 | tf_op jit(solution)/shard_map/ppermute | solution.py:49
  153.0 1.8 %router.1 = f32[2,256]{1,0:T(2,128)} custom-call(s32[7]{0:T(128)S(1)} %stack.20.where, f32[8,128]{1,0:T(8,128)S(1)} %get-tuple-element.96.own, f32[8,128]{1,0:T(8,128)S(1)} %collective-permute-done.39.other, s32[2,256]{1,0:T(2,128)S(1)} %copy-done.6), custom_call_target="tpu_custom_call" | custom-call | tf_op jit(solution)/shard_map/router/pallas_call | solution.py:703
  (81 shorter events, 21.6 us)
Async XLA Ops:
  0.6 46.5 %collective-permute-start.9 = (bf16[2,6144,128]{2,1,0:T(8,128)(2,1)}, bf16[2,6144,128]{2,1,0:T(8,128)(2,1)S(1)}, u32[]{:S(2)}, u32[]{:S(2)}) collective-permute-start(bf16[2,6144,128]{2,1,0:T(8,128)(2,1)} %refs_10_.1), channel_id=1, source_target_pairs={{0,16},{1,17},{2,18},{3,19},{4,20},{5,21},{6,22},{7,23},{8,24},{9,... | collective-permute-start | bytes 9437192 | tf_op jit(solution)/shard_map/ppermute | solution.py:49
  2.1 45.0 %collective-permute-start.10 = (bf16[2,6144,128]{2,1,0:T(8,128)(2,1)}, bf16[2,6144,128]{2,1,0:T(8,128)(2,1)}, u32[]{:S(2)}, u32[]{:S(2)}) collective-permute-start(bf16[2,6144,128]{2,1,0:T(8,128)(2,1)} %refs_11_.1), channel_id=1, source_target_pairs={{0,16},{1,17},{2,18},{3,19},{4,20},{5,21},{6,22},{7,23},{8,24},{9,... | collective-permute-start | bytes 9437192 | tf_op jit(solution)/shard_map/ppermute | solution.py:49
  2.2 69.1 %collective-permute-start.19 = (bf16[2,128,6144]{2,1,0:T(8,128)(2,1)}, bf16[2,128,6144]{2,1,0:T(8,128)(2,1)}, u32[]{:S(2)}, u32[]{:S(2)}) collective-permute-start(bf16[2,128,6144]{2,1,0:T(8,128)(2,1)} %refs_12_.1), channel_id=1, source_target_pairs={{0,16},{1,17},{2,18},{3,19},{4,20},{5,21},{6,22},{7,23},{8,24},{9,... | collective-permute-start | bytes 9437192 | tf_op jit(solution)/shard_map/ppermute | solution.py:49
  4.3 8.0 %collective-permute-start.2 = (bf16[128,384]{1,0:T(8,128)(2,1)S(1)}, bf16[128,384]{1,0:T(8,128)(2,1)S(1)}, u32[]{:S(2)}, u32[]{:S(2)}) collective-permute-start(bf16[128,384]{1,0:T(8,128)(2,1)S(1)} %pack.1.refs_0_), channel_id=1, source_target_pairs={{0,3},{1,0},{2,1},{3,2},{4,7},{5,4},{6,5},{7,6},{8,11},{9,8},{10,9... | collective-permute-start | bytes 294920 | tf_op jit(solution)/shard_map/ppermute | solution.py:38
  18.8 7.7 %collective-permute-start.5 = (bf16[16,6144]{1,0:T(8,128)(2,1)S(1)}, bf16[16,6144]{1,0:T(8,128)(2,1)S(1)}, u32[]{:S(2)}, u32[]{:S(2)}) collective-permute-start(bf16[16,6144]{1,0:T(8,128)(2,1)S(1)} %get-tuple-element.51.refs_0_), channel_id=1, source_target_pairs={{0,12},{1,13},{2,14},{3,15},{4,0},{5,1},{6,2},{7,3},{8,4},{9,5},{1... | collective-permute-start | bytes 589832 | tf_op jit(solution)/shard_map/ppermute | solution.py:38
  21.7 6.0 %collective-permute-start.4 = (bf16[16,6144]{1,0:T(8,128)(2,1)S(1)}, bf16[16,6144]{1,0:T(8,128)(2,1)S(1)}, u32[]{:S(2)}, u32[]{:S(2)}) collective-permute-start(bf16[16,6144]{1,0:T(8,128)(2,1)S(1)} %get-tuple-element.51.refs_0_), channel_id=1, source_target_pairs={{0,8},{1,9},{2,10},{3,11},{4,12},{5,13},{6,14},{7,15},{8,0},{9,1},... | collective-permute-start | bytes 589832 | tf_op jit(solution)/shard_map/ppermute | solution.py:38
  26.6 9.5 %collective-permute-start.3 = (bf16[16,6144]{1,0:T(8,128)(2,1)S(1)}, bf16[16,6144]{1,0:T(8,128)(2,1)S(1)}, u32[]{:S(2)}, u32[]{:S(2)}) collective-permute-start(bf16[16,6144]{1,0:T(8,128)(2,1)S(1)} %get-tuple-element.51.refs_0_), channel_id=1, source_target_pairs={{0,4},{1,5},{2,6},{3,7},{4,8},{5,9},{6,10},{7,11},{8,12},{9,13},{1... | collective-permute-start | bytes 589832 | tf_op jit(solution)/shard_map/ppermute | solution.py:38
  27.7 11.1 %collective-permute-start.8 = (bf16[64,1536]{1,0:T(8,128)(2,1)S(1)}, bf16[64,1536]{1,0:T(8,128)(2,1)S(1)}, u32[]{:S(2)}, u32[]{:S(2)}) collective-permute-start(bf16[64,1536]{1,0:T(8,128)(2,1)S(1)} %get-tuple-element.52.refs_4_), channel_id=1, source_target_pairs={{0,96},{1,97},{2,98},{3,99},{4,100},{5,101},{6,102},{7,103},{8,104... | collective-permute-start | bytes 589832 | tf_op jit(solution)/shard_map/ppermute | solution.py:38
  36.0 6.0 %collective-permute-start.7 = (bf16[64,1536]{1,0:T(8,128)(2,1)S(1)}, bf16[64,1536]{1,0:T(8,128)(2,1)S(1)}, u32[]{:S(2)}, u32[]{:S(2)}) collective-permute-start(bf16[64,1536]{1,0:T(8,128)(2,1)S(1)} %get-tuple-element.52.refs_4_), channel_id=1, source_target_pairs={{0,64},{1,65},{2,66},{3,67},{4,68},{5,69},{6,70},{7,71},{8,72},{9,... | collective-permute-start | bytes 589832 | tf_op jit(solution)/shard_map/ppermute | solution.py:38
  38.8 8.3 %collective-permute-start.6 = (bf16[64,1536]{1,0:T(8,128)(2,1)S(1)}, bf16[64,1536]{1,0:T(8,128)(2,1)S(1)}, u32[]{:S(2)}, u32[]{:S(2)}) collective-permute-start(bf16[64,1536]{1,0:T(8,128)(2,1)S(1)} %get-tuple-element.52.refs_4_), channel_id=1, source_target_pairs={{0,32},{1,33},{2,34},{3,35},{4,36},{5,37},{6,38},{7,39},{8,40},{9,... | collective-permute-start | bytes 589832 | tf_op jit(solution)/shard_map/ppermute | solution.py:38
  47.8 16.8 %collective-permute-start.12 = (bf16[64,6144]{1,0:T(8,128)(2,1)S(1)}, bf16[64,6144]{1,0:T(8,128)(2,1)S(1)}, u32[]{:S(2)}, u32[]{:S(2)}) collective-permute-start(bf16[64,6144]{1,0:T(8,128)(2,1)S(1)} %get-tuple-element.53.refs_0_), channel_id=1, source_target_pairs={{0,96},{1,97},{2,98},{3,99},{4,100},{5,101},{6,102},{7,103},{8,104... | collective-permute-start | bytes 2359304 | tf_op jit(solution)/shard_map/ppermute | solution.py:38
  47.9 17.9 %collective-permute-start.11 = (bf16[64,6144]{1,0:T(8,128)(2,1)S(1)}, bf16[64,6144]{1,0:T(8,128)(2,1)S(1)}, u32[]{:S(2)}, u32[]{:S(2)}) collective-permute-start(bf16[64,6144]{1,0:T(8,128)(2,1)S(1)} %get-tuple-element.53.refs_0_), channel_id=1, source_target_pairs={{0,32},{1,33},{2,34},{3,35},{4,36},{5,37},{6,38},{7,39},{8,40},{9,... | collective-permute-start | bytes 2359304 | tf_op jit(solution)/shard_map/ppermute | solution.py:38
  49.3 16.4 %collective-permute-start.14 = (bf16[256,1536]{1,0:T(8,128)(2,1)S(1)}, bf16[256,1536]{1,0:T(8,128)(2,1)S(1)}, u32[]{:S(2)}, u32[]{:S(2)}) collective-permute-start(bf16[256,1536]{1,0:T(8,128)(2,1)S(1)} %get-tuple-element.54.refs_3_.refs_5_), channel_id=1, source_target_pairs={{0,12},{1,13},{2,14},{3,15},{4,0},{5,1},{6,2},{7,3},{8,4},{9,5},{1... | collective-permute-start | bytes 2359304 | tf_op jit(solution)/shard_map/ppermute | solution.py:38
  50.4 15.3 %collective-permute-start.13 = (bf16[256,1536]{1,0:T(8,128)(2,1)S(1)}, bf16[256,1536]{1,0:T(8,128)(2,1)S(1)}, u32[]{:S(2)}, u32[]{:S(2)}) collective-permute-start(bf16[256,1536]{1,0:T(8,128)(2,1)S(1)} %get-tuple-element.54.refs_3_.refs_5_), channel_id=1, source_target_pairs={{0,4},{1,5},{2,6},{3,7},{4,8},{5,9},{6,10},{7,11},{8,12},{9,13},{1... | collective-permute-start | bytes 2359304 | tf_op jit(solution)/shard_map/ppermute | solution.py:38
  65.9 12.6 %collective-permute-start.15 = (bf16[32,6144]{1,0:T(8,128)(2,1)S(1)}, bf16[32,6144]{1,0:T(8,128)(2,1)S(1)}, u32[]{:S(2)}, u32[]{:S(2)}) collective-permute-start(bf16[32,6144]{1,0:T(8,128)(2,1)S(1)} %get-tuple-element.55), channel_id=1, source_target_pairs={{0,32},{1,33},{2,34},{3,35},{4,36},{5,37},{6,38},{7,39},{8,40},{9,... | collective-permute-start | bytes 1179656 | tf_op jit(solution)/shard_map/ppermute | solution.py:38
  66.7 11.8 %collective-permute-start.16 = (bf16[32,6144]{1,0:T(8,128)(2,1)S(1)}, bf16[32,6144]{1,0:T(8,128)(2,1)S(1)}, u32[]{:S(2)}, u32[]{:S(2)}) collective-permute-start(bf16[32,6144]{1,0:T(8,128)(2,1)S(1)} %get-tuple-element.56), channel_id=1, source_target_pairs={{0,96},{1,97},{2,98},{3,99},{4,100},{5,101},{6,102},{7,103},{8,104... | collective-permute-start | bytes 1179656 | tf_op jit(solution)/shard_map/ppermute | solution.py:38
  68.6 9.9 %collective-permute-start.17 = (bf16[128,1536]{1,0:T(8,128)(2,1)S(1)}, bf16[128,1536]{1,0:T(8,128)(2,1)S(1)}, u32[]{:S(2)}, u32[]{:S(2)}) collective-permute-start(bf16[128,1536]{1,0:T(8,128)(2,1)S(1)} %get-tuple-element.57), channel_id=1, source_target_pairs={{0,4},{1,5},{2,6},{3,7},{4,8},{5,9},{6,10},{7,11},{8,12},{9,13},{1... | collective-permute-start | bytes 1179656 | tf_op jit(solution)/shard_map/ppermute | solution.py:38
  69.5 9.0 %collective-permute-start.18 = (bf16[128,1536]{1,0:T(8,128)(2,1)S(1)}, bf16[128,1536]{1,0:T(8,128)(2,1)S(1)}, u32[]{:S(2)}, u32[]{:S(2)}) collective-permute-start(bf16[128,1536]{1,0:T(8,128)(2,1)S(1)} %get-tuple-element.58), channel_id=1, source_target_pairs={{0,12},{1,13},{2,14},{3,15},{4,0},{5,1},{6,2},{7,3},{8,4},{9,5},{1... | collective-permute-start | bytes 1179656 | tf_op jit(solution)/shard_map/ppermute | solution.py:38
  95.4 21.3 %collective-permute-start.28 = (bf16[256,6912]{1,0:T(8,128)(2,1)}, bf16[256,6912]{1,0:T(8,128)(2,1)S(1)}, u32[]{:S(2)}, u32[]{:S(2)}) collective-permute-start(bf16[256,6912]{1,0:T(8,128)(2,1)} %get-tuple-element.75.refs_0_), channel_id=1, source_target_pairs={{0,16},{1,17},{2,18},{3,19},{4,20},{5,21},{6,22},{7,23},{8,24},{9,... | collective-permute-start | bytes 10616840 | tf_op jit(solution)/shard_map/ppermute | solution.py:49
  102.5 8.5 %collective-permute-start.20 = (bf16[32,3456]{1,0:T(8,128)(2,1)S(1)}, bf16[32,3456]{1,0:T(8,128)(2,1)S(1)}, u32[]{:S(2)}, u32[]{:S(2)}) collective-permute-start(bf16[32,3456]{1,0:T(8,128)(2,1)S(1)} %get-tuple-element.66), channel_id=1, source_target_pairs={{0,96},{1,97},{2,98},{3,99},{4,100},{5,101},{6,102},{7,103},{8,104... | collective-permute-start | bytes 663560 | tf_op jit(solution)/shard_map/ppermute | solution.py:38
  102.6 8.4 %collective-permute-start.21 = (bf16[32,3456]{1,0:T(8,128)(2,1)S(1)}, bf16[32,3456]{1,0:T(8,128)(2,1)S(1)}, u32[]{:S(2)}, u32[]{:S(2)}) collective-permute-start(bf16[32,3456]{1,0:T(8,128)(2,1)S(1)} %get-tuple-element.67), channel_id=1, source_target_pairs={{0,32},{1,33},{2,34},{3,35},{4,36},{5,37},{6,38},{7,39},{8,40},{9,... | collective-permute-start | bytes 663560 | tf_op jit(solution)/shard_map/ppermute | solution.py:38
  103.9 7.0 %collective-permute-start.22 = (bf16[2,16,3072]{2,1,0:T(8,128)(2,1)S(1)}, bf16[2,16,3072]{2,1,0:T(8,128)(2,1)S(1)}, u32[]{:S(2)}, u32[]{:S(2)}) collective-permute-start(bf16[2,16,3072]{2,1,0:T(8,128)(2,1)S(1)} %get-tuple-element.68), channel_id=1, source_target_pairs={{0,4},{1,5},{2,6},{3,7},{4,8},{5,9},{6,10},{7,11},{8,12},{9,13},{1... | collective-permute-start | bytes 589832 | tf_op jit(solution)/shard_map/ppermute | solution.py:38
  104.9 6.1 %collective-permute-start.23 = (bf16[2,16,3072]{2,1,0:T(8,128)(2,1)S(1)}, bf16[2,16,3072]{2,1,0:T(8,128)(2,1)S(1)}, u32[]{:S(2)}, u32[]{:S(2)}) collective-permute-start(bf16[2,16,3072]{2,1,0:T(8,128)(2,1)S(1)} %get-tuple-element.69), channel_id=1, source_target_pairs={{0,12},{1,13},{2,14},{3,15},{4,0},{5,1},{6,2},{7,3},{8,4},{9,5},{1... | collective-permute-start | bytes 589832 | tf_op jit(solution)/shard_map/ppermute | solution.py:38
  111.2 20.0 %collective-permute-start.35 = (bf16[256,6144]{1,0:T(8,128)(2,1)S(1)}, bf16[256,6144]{1,0:T(8,128)(2,1)S(1)}, u32[]{:S(2)}, u32[]{:S(2)}) collective-permute-start(bf16[256,6144]{1,0:T(8,128)(2,1)S(1)} %relay.1), channel_id=1, source_target_pairs={{0,16},{1,17},{2,18},{3,19},{4,20},{5,21},{6,22},{7,23},{8,24},{9,... | collective-permute-start | bytes 9437192 | tf_op jit(solution)/shard_map/ppermute | solution.py:49
  113.0 14.1 %collective-permute-start.25 = (bf16[64,3456]{1,0:T(8,128)(2,1)S(1)}, bf16[64,3456]{1,0:T(8,128)(2,1)S(1)}, u32[]{:S(2)}, u32[]{:S(2)}) collective-permute-start(bf16[64,3456]{1,0:T(8,128)(2,1)S(1)} %get-tuple-element.71), channel_id=1, source_target_pairs={{0,32},{1,33},{2,34},{3,35},{4,36},{5,37},{6,38},{7,39},{8,40},{9,... | collective-permute-start | bytes 1327112 | tf_op jit(solution)/shard_map/ppermute | solution.py:38
  113.1 14.0 %collective-permute-start.24 = (bf16[64,3456]{1,0:T(8,128)(2,1)S(1)}, bf16[64,3456]{1,0:T(8,128)(2,1)S(1)}, u32[]{:S(2)}, u32[]{:S(2)}) collective-permute-start(bf16[64,3456]{1,0:T(8,128)(2,1)S(1)} %get-tuple-element.70.refs_4_), channel_id=1, source_target_pairs={{0,96},{1,97},{2,98},{3,99},{4,100},{5,101},{6,102},{7,103},{8,104... | collective-permute-start | bytes 1327112 | tf_op jit(solution)/shard_map/ppermute | solution.py:38
  115.8 11.3 %collective-permute-start.26 = (bf16[4,16,3072]{2,1,0:T(8,128)(2,1)S(1)}, bf16[4,16,3072]{2,1,0:T(8,128)(2,1)S(1)}, u32[]{:S(2)}, u32[]{:S(2)}) collective-permute-start(bf16[4,16,3072]{2,1,0:T(8,128)(2,1)S(1)} %get-tuple-element.73), channel_id=1, source_target_pairs={{0,4},{1,5},{2,6},{3,7},{4,8},{5,9},{6,10},{7,11},{8,12},{9,13},{1... | collective-permute-start | bytes 1179656 | tf_op jit(solution)/shard_map/ppermute | solution.py:38
  116.8 10.3 %collective-permute-start.27 = (bf16[4,16,3072]{2,1,0:T(8,128)(2,1)S(1)}, bf16[4,16,3072]{2,1,0:T(8,128)(2,1)S(1)}, u32[]{:S(2)}, u32[]{:S(2)}) collective-permute-start(bf16[4,16,3072]{2,1,0:T(8,128)(2,1)S(1)} %get-tuple-element.74), channel_id=1, source_target_pairs={{0,12},{1,13},{2,14},{3,15},{4,0},{5,1},{6,2},{7,3},{8,4},{9,5},{1... | collective-permute-start | bytes 1179656 | tf_op jit(solution)/shard_map/ppermute | solution.py:38
  129.5 10.1 %collective-permute-start.33 = (bf16[16,3072]{1,0:T(8,128)(2,1)S(1)}, bf16[16,3072]{1,0:T(8,128)(2,1)S(1)}, u32[]{:S(2)}, u32[]{:S(2)}) collective-permute-start(bf16[16,3072]{1,0:T(8,128)(2,1)S(1)} %get-tuple-element.84), channel_id=1, source_target_pairs={{0,64},{1,65},{2,66},{3,67},{4,68},{5,69},{6,70},{7,71},{8,72},{9,... | collective-permute-start | bytes 294920 | tf_op jit(solution)/shard_map/ppermute | solution.py:38
  129.6 10.1 %collective-permute-start.34 = (bf16[16,3072]{1,0:T(8,128)(2,1)S(1)}, bf16[16,3072]{1,0:T(8,128)(2,1)S(1)}, u32[]{:S(2)}, u32[]{:S(2)}) collective-permute-start(bf16[16,3072]{1,0:T(8,128)(2,1)S(1)} %get-tuple-element.85), channel_id=1, source_target_pairs={{0,32},{1,33},{2,34},{3,35},{4,36},{5,37},{6,38},{7,39},{8,40},{9,... | collective-permute-start | bytes 294920 | tf_op jit(solution)/shard_map/ppermute | solution.py:38
  130.2 9.4 %collective-permute-start.29 = (bf16[16,3456]{1,0:T(8,128)(2,1)S(1)}, bf16[16,3456]{1,0:T(8,128)(2,1)S(1)}, u32[]{:S(2)}, u32[]{:S(2)}) collective-permute-start(bf16[16,3456]{1,0:T(8,128)(2,1)S(1)} %get-tuple-element.79), channel_id=1, source_target_pairs={{0,4},{1,5},{2,6},{3,7},{4,8},{5,9},{6,10},{7,11},{8,12},{9,13},{1... | collective-permute-start | bytes 331784 | tf_op jit(solution)/shard_map/ppermute | solution.py:38
  131.2 8.4 %collective-permute-start.30 = (bf16[16,3456]{1,0:T(8,128)(2,1)S(1)}, bf16[16,3456]{1,0:T(8,128)(2,1)S(1)}, u32[]{:S(2)}, u32[]{:S(2)}) collective-permute-start(bf16[16,3456]{1,0:T(8,128)(2,1)S(1)} %get-tuple-element.80), channel_id=1, source_target_pairs={{0,8},{1,9},{2,10},{3,11},{4,12},{5,13},{6,14},{7,15},{8,0},{9,1},... | collective-permute-start | bytes 331784 | tf_op jit(solution)/shard_map/ppermute | solution.py:38
  (17 other events, 164.2 us)

commit v4 on v3

--- a/solution.py
+++ b/solution.py
@@ -103,7 +103,7 @@
 
 
 def first_stage_kernel(where, *refs):
-    packed, t_out, g_out, buf = refs[0:4], refs[4], refs[5], refs[6]
+    packed, t_out, g_out, buf = refs[0:4], refs[-3], refs[-2], refs[-1]
     for k in range(NZ):
         at = (where[2] - k) % NZ
         rows = packed[k][64:128, :].astype(F32)
@@ -114,36 +114,59 @@
     t_out[...] = jnp.concatenate([buf[k] for k in range(NZ)], axis=0).astype(BF)
 
 
-def run_first_stage(where, packed):
+def run_first_stage(where, packed, before):
     return pl.pallas_call(
         first_stage_kernel,
         out_shape=[jax.ShapeDtypeStruct((16, D), BF), jax.ShapeDtypeStruct((64, 1536), BF)],
-        in_specs=[SMEM_SPEC] + vmem_specs(4),
+        in_specs=[SMEM_SPEC] + vmem_specs(4) + [pl.BlockSpec(memory_space=pl.ANY)] * len(before),
         out_specs=vmem_specs(2),
         scratch_shapes=[pltpu.VMEM((NZ, 4, D), F32)],
         compiler_params=pltpu.CompilerParams(vmem_limit_bytes=4 * MIB),
         name="first_stage",
-    )(where, *packed)
+    )(where, *packed, *before)
+
+
+def near_halves_kernel(t_low, t_high, g_low, g_high, a, b, c, d):
+    a[...] = t_low[:, 0 : D // 2]
+    b[...] = t_high[:, D // 2 : D]
+    c[...] = g_low[0:32, :]
+    d[...] = g_high[32:64, :]
+
+
+def run_near_halves(t_low, t_high, g_low, g_high):
+    return pl.pallas_call(
+        near_halves_kernel,
+        out_shape=[jax.ShapeDtypeStruct((16, D // 2), BF)] * 2
+        + [jax.ShapeDtypeStruct((32, 1536), BF)] * 2,
+        in_specs=vmem_specs(4),
+        out_specs=vmem_specs(4),
+        compiler_params=pltpu.CompilerParams(vmem_limit_bytes=4 * MIB),
+        name="near_halves",
+    )(t_low, t_high, g_low, g_high)
 
 
 def second_stage_kernel(where, *refs):
-    t, g, t_out, g_out = refs[0:4], refs[4:8], refs[-2], refs[-1]
-    for k in range(NY):
-        start = pl.multiple_of(16 * ((where[1] - k) % NY), 16)
-        t_out[pl.ds(start, 16), :] = t[k][...]
-    for k in range(NX):
-        g_out[k * 64 : (k + 1) * 64, :] = g[k][...]
-
-
-def run_second_stage(where, t, g, before):
+    t, g, t_out, g_out = refs[0:5], refs[5:10], refs[10], refs[11]
+    y = where[1]
+    for piece, step in zip(t[0:3], (0, -1, 1)):
+        start = pl.multiple_of(16 * ((y + step + NY) % NY), 16)
+        t_out[pl.ds(start, 16), :] = piece[...]
+    start = pl.multiple_of(16 * ((y + 2) % NY), 16)
+    t_out[pl.ds(start, 16), 0 : D // 2] = t[3][...]
+    t_out[pl.ds(start, 16), D // 2 : D] = t[4][...]
+    for piece, at in zip(g, (0, 64, 192, 128, 160)):
+        g_out[at : at + piece.shape[0], :] = piece[...]
+
+
+def run_second_stage(where, t, g):
     return pl.pallas_call(
         second_stage_kernel,
         out_shape=[jax.ShapeDtypeStruct((64, D), BF), jax.ShapeDtypeStruct((HALF, 1536), BF)],
-        in_specs=[SMEM_SPEC] + vmem_specs(8) + [pl.BlockSpec(memory_space=pl.ANY)] * len(before),
+        in_specs=[SMEM_SPEC] + vmem_specs(10),
         out_specs=vmem_specs(2),
         compiler_params=pltpu.CompilerParams(vmem_limit_bytes=4 * MIB),
         name="second_stage",
-    )(where, *t, *g, *before)
+    )(where, *t, *g)
 
 
 def halves_kernel(t_low, t_high, g_low, g_high, a, b, c, d):
@@ -718,11 +741,15 @@
     gate_sib, up_sib = swap(gate_weight), swap(up_weight)
 
     packed = run_pack(tokens_in, out_grad)
-    t16, g64 = run_first_stage(where, [packed] + [shift(packed, "z", k) for k in (1, 2, 3)])
-    t = [t16] + [shift(t16, "y", k) for k in (1, 2, 3)]
-    g = [g64] + [shift(g64, "x", k) for k in (1, 2, 3)]
-    down_sib = swap(down_weight)
-    t64, g256 = run_second_stage(where, t, g, [gate_sib, up_sib])
+    packed = [packed] + [shift(packed, "z", k) for k in (1, 2, 3)]
+    t16, g64 = run_first_stage(where, packed, [gate_sib, up_sib])
+    down_sib = swap(run_relay(down_weight, [t16]))
+    t_low, t_high = shift(t16, "y", 1), shift(t16, "y", -1)
+    g_low, g_high = shift(g64, "x", 1), shift(g64, "x", -1)
+    a, b, e, f = run_near_halves(t_low, t_high, g_low, g_high)
+    t = (t16, t_low, t_high, shift(a, "y", 1), shift(b, "y", -1))
+    g = (g64, g_low, g_high, shift(e, "x", 1), shift(f, "x", -1))
+    t64, g256 = run_second_stage(where, t, g)
     t_low, t_high = shift(t64, "x", 1), shift(t64, "x", -1)
     g_low, g_high = shift(g256, "y", 1), shift(g256, "y", -1)
     a, b, e, f = run_halves(t_low, t_high, g_low, g_high)

time: 155 us -> 144 us (0.929)
  waiting for transfers between devices: 51.7 us -> 38.9 us
    ppermute x34 -> x36, waiting for transfers between devices: 50.9 us -> 38.1 us  [shift(): return lax.ppermute(value, AXES, shift_pairs(axis, step))]
    ppermute x34 -> x36, starting transfers between devices: 41 us -> 43.5 us  [shift(): return lax.ppermute(value, AXES, shift_pairs(axis, step))]
  transfers between devices with their start and end apart: 40 -> 42, of which waited for: 15 -> 14; matrix products, arithmetic and copies ran while one was open for 0% -> 1% of each run, Pallas kernels for 15% -> 16%
where the time goes in v4:
time: 144 us
  starting transfers between devices  57.8 us (40%)
  Pallas kernels  44 us (31%)
  waiting for transfers between devices  38.9 us (27%)
  local copies, waits for them, and re-layouts  2.37 us (2%)
    ppermute x36, starting transfers between devices, shift(): return lax.ppermute(value, AXES, shift_pairs(axis, step))  43.5 us
    ppermute x36, waiting for transfers between devices, shift(): return lax.ppermute(value, AXES, shift_pairs(axis, step))  38.1 us
    pallas_call x1, Pallas kernels, run_main(): pl.pallas_call(main_kernel, out_shape=out_shape, in_specs=[SMEM_SPEC] + h...  16.9 us
    ppermute x6, starting transfers between devices, swap(): return lax.ppermute(value, AXES, pairs)  14.3 us
    pallas_call x1, Pallas kernels, run_up(): pl.pallas_call(up_kernel, grid=(D // FT,), out_shape=[jax.ShapeDtypeStruc...  8.64 us
    pallas_call x1, Pallas kernels, run_early(): pl.pallas_call(early_kernel, out_shape=[jax.ShapeDtypeStruct((192, 1024),...  7.54 us
    pallas_call x1, Pallas kernels, run_down(): pl.pallas_call(down_kernel, grid=(D // FT // 2,), out_shape=[jax.ShapeDty...  4.6 us
  transfers between devices with their start and end apart: 42, of which 14 were waited for; matrix products, arithmetic and copies ran while one was open for 1% of the time, Pallas kernels for 16%

profile of v4, /device:TPU:1, one launch (start us, length us, event | category | flops | bytes accessed | tf_op | source)
XLA Modules:
  0.0 144.0 jit_solution(10722925033187758795)
XLA Ops:
  0.6 1.5 %collective-permute-start.3 = (bf16[2,6144,128]{2,1,0:T(8,128)(2,1)}, bf16[2,6144,128]{2,1,0:T(8,128)(2,1)S(1)}, u32[]{:S(2)}, u32[]{:S(2)}) collective-permute-start(bf16[2,6144,128]{2,1,0:T(8,128)(2,1)} %refs_10_.1), channel_id=1, source_target_pairs={{0,16},{1,17},{2,18},{3,19},{4,20},{5,21},{6,22},{7,23},{8,24},{9,... | collective-permute-start | bytes 9437192 | tf_op jit(solution)/shard_map/ppermute | solution.py:49
  3.8 3.9 %collective-permute-start.2 = (bf16[128,384]{1,0:T(8,128)(2,1)S(1)}, bf16[128,384]{1,0:T(8,128)(2,1)S(1)}, u32[]{:S(2)}, u32[]{:S(2)}) collective-permute-start(bf16[128,384]{1,0:T(8,128)(2,1)S(1)} %pack.1.refs_0_), channel_id=1, source_target_pairs={{0,3},{1,0},{2,1},{3,2},{4,7},{5,4},{6,5},{7,6},{8,11},{9,8},{10,9... | collective-permute-start | bytes 294920 | tf_op jit(solution)/shard_map/ppermute | solution.py:38
  9.2 2.6 %collective-permute-done.2.refs_3_ = bf16[128,384]{1,0:T(8,128)(2,1)S(1)} collective-permute-done((bf16[128,384]{1,0:T(8,128)(2,1)S(1)}, bf16[128,384]{1,0:T(8,128)(2,1)S(1)}, u32[]{:S(2)}, u32[]{:S(2)}) %collective-permute-start.2) | collective-permute-done | bytes 98336 | tf_op jit(solution)/shard_map/ppermute | solution.py:38
  12.8 2.6 %collective-permute-done.refs_1_ = bf16[128,384]{1,0:T(8,128)(2,1)S(1)} collective-permute-done((bf16[128,384]{1,0:T(8,128)(2,1)S(1)}, bf16[128,384]{1,0:T(8,128)(2,1)S(1)}, u32[]{:S(2)}, u32[]{:S(2)}) %collective-permute-start) | collective-permute-done | bytes 98336 | tf_op jit(solution)/shard_map/ppermute | solution.py:38
  17.3 2.5 %collective-permute-start.8 = (bf16[64,1536]{1,0:T(8,128)(2,1)S(1)}, bf16[64,1536]{1,0:T(8,128)(2,1)S(1)}, u32[]{:S(2)}, u32[]{:S(2)}) collective-permute-start(bf16[64,1536]{1,0:T(8,128)(2,1)S(1)} %get-tuple-element.56.refs_5_), channel_id=1, source_target_pairs={{0,96},{1,97},{2,98},{3,99},{4,100},{5,101},{6,102},{7,103},{8,104... | collective-permute-start | bytes 589832 | tf_op jit(solution)/shard_map/ppermute | solution.py:38
  19.8 2.7 %collective-permute-start.6 = (bf16[16,6144]{1,0:T(8,128)(2,1)S(1)}, bf16[16,6144]{1,0:T(8,128)(2,1)S(1)}, u32[]{:S(2)}, u32[]{:S(2)}) collective-permute-start(bf16[16,6144]{1,0:T(8,128)(2,1)S(1)} %get-tuple-element.55.refs_0_.refs_1_), channel_id=1, source_target_pairs={{0,12},{1,13},{2,14},{3,15},{4,0},{5,1},{6,2},{7,3},{8,4},{9,5},{1... | collective-permute-start | bytes 589832 | tf_op jit(solution)/shard_map/ppermute | solution.py:38
  22.5 1.5 %collective-permute-done.8.g_high.refs_7_ = bf16[64,1536]{1,0:T(8,128)(2,1)S(1)} collective-permute-done((bf16[64,1536]{1,0:T(8,128)(2,1)S(1)}, bf16[64,1536]{1,0:T(8,128)(2,1)S(1)}, u32[]{:S(2)}, u32[]{:S(2)}) %collective-permute-start.8) | collective-permute-done | bytes 196640 | tf_op jit(solution)/shard_map/ppermute | solution.py:38
  24.1 3.1 %collective-permute-done.7.g_low.refs_6_ = bf16[64,1536]{1,0:T(8,128)(2,1)S(1)} collective-permute-done((bf16[64,1536]{1,0:T(8,128)(2,1)S(1)}, bf16[64,1536]{1,0:T(8,128)(2,1)S(1)}, u32[]{:S(2)}, u32[]{:S(2)}) %collective-permute-start.7) | collective-permute-done | bytes 196640 | tf_op jit(solution)/shard_map/ppermute | solution.py:38
  27.2 2.4 %collective-permute-done.5.t_low.refs_1_ = bf16[16,6144]{1,0:T(8,128)(2,1)S(1)} collective-permute-done((bf16[16,6144]{1,0:T(8,128)(2,1)S(1)}, bf16[16,6144]{1,0:T(8,128)(2,1)S(1)}, u32[]{:S(2)}, u32[]{:S(2)}) %collective-permute-start.5) | collective-permute-done | bytes 196640 | tf_op jit(solution)/shard_map/ppermute | solution.py:38
  29.7 2.7 %collective-permute-start.10 = (bf16[16,3072]{1,0:T(8,128)(2,1)S(1)}, bf16[16,3072]{1,0:T(8,128)(2,1)S(1)}, u32[]{:S(2)}, u32[]{:S(2)}) collective-permute-start(bf16[16,3072]{1,0:T(8,128)(2,1)S(1)} %get-tuple-element.58), channel_id=1, source_target_pairs={{0,12},{1,13},{2,14},{3,15},{4,0},{5,1},{6,2},{7,3},{8,4},{9,5},{1... | collective-permute-start | bytes 294920 | tf_op jit(solution)/shard_map/ppermute | solution.py:38
  32.4 2.7 %collective-permute-start.12 = (bf16[32,1536]{1,0:T(8,128)(2,1)S(1)}, bf16[32,1536]{1,0:T(8,128)(2,1)S(1)}, u32[]{:S(2)}, u32[]{:S(2)}) collective-permute-start(bf16[32,1536]{1,0:T(8,128)(2,1)S(1)} %get-tuple-element.60), channel_id=1, source_target_pairs={{0,96},{1,97},{2,98},{3,99},{4,100},{5,101},{6,102},{7,103},{8,104... | collective-permute-start | bytes 294920 | tf_op jit(solution)/shard_map/ppermute | solution.py:38
  35.0 2.0 %collective-permute-done.11.refs_8_ = bf16[32,1536]{1,0:T(8,128)(2,1)S(1)} collective-permute-done((bf16[32,1536]{1,0:T(8,128)(2,1)S(1)}, bf16[32,1536]{1,0:T(8,128)(2,1)S(1)}, u32[]{:S(2)}, u32[]{:S(2)}) %collective-permute-start.11) | collective-permute-done | bytes 98336 | tf_op jit(solution)/shard_map/ppermute | solution.py:38
  37.7 2.7 %collective-permute-start.14 = (bf16[64,6144]{1,0:T(8,128)(2,1)S(1)}, bf16[64,6144]{1,0:T(8,128)(2,1)S(1)}, u32[]{:S(2)}, u32[]{:S(2)}) collective-permute-start(bf16[64,6144]{1,0:T(8,128)(2,1)S(1)} %get-tuple-element.61.refs_0_), channel_id=1, source_target_pairs={{0,96},{1,97},{2,98},{3,99},{4,100},{5,101},{6,102},{7,103},{8,104... | collective-permute-start | bytes 2359304 | tf_op jit(solution)/shard_map/ppermute | solution.py:38
  40.4 1.5 %collective-permute-start.15 = (bf16[256,1536]{1,0:T(8,128)(2,1)S(1)}, bf16[256,1536]{1,0:T(8,128)(2,1)S(1)}, u32[]{:S(2)}, u32[]{:S(2)}) collective-permute-start(bf16[256,1536]{1,0:T(8,128)(2,1)S(1)} %get-tuple-element.62.refs_3_.refs_5_), channel_id=1, source_target_pairs={{0,4},{1,5},{2,6},{3,7},{4,8},{5,9},{6,10},{7,11},{8,12},{9,13},{1... | collective-permute-start | bytes 2359304 | tf_op jit(solution)/shard_map/ppermute | solution.py:38
  41.9 11.9 %collective-permute-done.14.t_high.refs_2_ = bf16[64,6144]{1,0:T(8,128)(2,1)S(1)} collective-permute-done((bf16[64,6144]{1,0:T(8,128)(2,1)S(1)}, bf16[64,6144]{1,0:T(8,128)(2,1)S(1)}, u32[]{:S(2)}, u32[]{:S(2)}) %collective-permute-start.14) | collective-permute-done | bytes 786464 | tf_op jit(solution)/shard_map/ppermute | solution.py:38
  53.8 3.1 %collective-permute-done.13.t_low.refs_1_ = bf16[64,6144]{1,0:T(8,128)(2,1)S(1)} collective-permute-done((bf16[64,6144]{1,0:T(8,128)(2,1)S(1)}, bf16[64,6144]{1,0:T(8,128)(2,1)S(1)}, u32[]{:S(2)}, u32[]{:S(2)}) %collective-permute-start.13) | collective-permute-done | bytes 786464 | tf_op jit(solution)/shard_map/ppermute | solution.py:38
  57.1 2.7 %collective-permute-start.18 = (bf16[32,6144]{1,0:T(8,128)(2,1)S(1)}, bf16[32,6144]{1,0:T(8,128)(2,1)S(1)}, u32[]{:S(2)}, u32[]{:S(2)}) collective-permute-start(bf16[32,6144]{1,0:T(8,128)(2,1)S(1)} %get-tuple-element.64), channel_id=1, source_target_pairs={{0,96},{1,97},{2,98},{3,99},{4,100},{5,101},{6,102},{7,103},{8,104... | collective-permute-start | bytes 1179656 | tf_op jit(solution)/shard_map/ppermute | solution.py:38
  59.8 2.7 %collective-permute-start.20 = (bf16[128,1536]{1,0:T(8,128)(2,1)S(1)}, bf16[128,1536]{1,0:T(8,128)(2,1)S(1)}, u32[]{:S(2)}, u32[]{:S(2)}) collective-permute-start(bf16[128,1536]{1,0:T(8,128)(2,1)S(1)} %get-tuple-element.66), channel_id=1, source_target_pairs={{0,12},{1,13},{2,14},{3,15},{4,0},{5,1},{6,2},{7,3},{8,4},{9,5},{1... | collective-permute-start | bytes 1179656 | tf_op jit(solution)/shard_map/ppermute | solution.py:38
  62.5 7.5 %early.1 = (f32[192,1024]{1,0:T(8,128)S(1)}, f32[256,512]{1,0:T(8,128)S(1)}) custom-call(s32[7]{0:T(128)S(1)} %stack.20.where, bf16[64,6144]{1,0:T(8,128)(2,1)S(1)} %get-tuple-element.61.refs_0_, bf16[64,6144]{1,0:T(8,128)(2,1)S(1)} %collective-permute-done.13.t_low.refs_1_, bf16[64,6144]{1,0:T(8,128)(2,1)S(1)} %collective-permute-done.14.t_high.refs_2_, ...), custom_call_target="tpu_custom_call" | custom-call | flops 3600000000 | bytes 20000000 | tf_op jit(solution)/shard_map/early/pallas_call | solution.py:300
  70.1 16.9 %main.1 = (bf16[64,3456]{1,0:T(8,128)(2,1)S(1)}, bf16[64,3456]{1,0:T(8,128)(2,1)S(1)}, bf16[64,3456]{1,0:T(8,128)(2,1)S(1)}, bf16[32,3456]{1,0:T(8,128)(2,1)S(1)...) custom-call(s32[7]{0:T(128)S(1)} %stack.20.where, ...), custom_call_target="tpu_custom_call" | custom-call | flops 8000000000 | bytes 30000000 | tf_op jit(solution)/shard_map/main/pallas_call | solution.py:479
  87.0 6.0 %collective-permute-start.30 = (bf16[256,6912]{1,0:T(8,128)(2,1)}, bf16[256,6912]{1,0:T(8,128)(2,1)S(1)}, u32[]{:S(2)}, u32[]{:S(2)}) collective-permute-start(bf16[256,6912]{1,0:T(8,128)(2,1)} %get-tuple-element.83.refs_0_), channel_id=1, source_target_pairs={{0,16},{1,17},{2,18},{3,19},{4,20},{5,21},{6,22},{7,23},{8,24},{9,... | collective-permute-start | bytes 10616840 | tf_op jit(solution)/shard_map/ppermute | solution.py:49
  94.5 2.7 %collective-permute-start.25 = (bf16[2,16,3072]{2,1,0:T(8,128)(2,1)S(1)}, bf16[2,16,3072]{2,1,0:T(8,128)(2,1)S(1)}, u32[]{:S(2)}, u32[]{:S(2)}) collective-permute-start(bf16[2,16,3072]{2,1,0:T(8,128)(2,1)S(1)} %get-tuple-element.77), channel_id=1, source_target_pairs={{0,12},{1,13},{2,14},{3,15},{4,0},{5,1},{6,2},{7,3},{8,4},{9,5},{1... | collective-permute-start | bytes 589832 | tf_op jit(solution)/shard_map/ppermute | solution.py:38
  97.2 4.4 %collective-permute-done.24.refs_6_.refs_3_ = bf16[2,16,3072]{2,1,0:T(8,128)(2,1)S(1)} collective-permute-done((bf16[2,16,3072]{2,1,0:T(8,128)(2,1)S(1)}, bf16[2,16,3072]{2,1,0:T(8,128)(2,1)S(1)}, u32[]{:S(2)}, u32[]{:S(2)}) %collective-permute-start.24) | collective-permute-done | bytes 196640 | tf_op jit(solution)/shard_map/ppermute | solution.py:38
  104.0 2.7 %collective-permute-start.26 = (bf16[64,3456]{1,0:T(8,128)(2,1)S(1)}, bf16[64,3456]{1,0:T(8,128)(2,1)S(1)}, u32[]{:S(2)}, u32[]{:S(2)}) collective-permute-start(bf16[64,3456]{1,0:T(8,128)(2,1)S(1)} %get-tuple-element.78.refs_4_), channel_id=1, source_target_pairs={{0,96},{1,97},{2,98},{3,99},{4,100},{5,101},{6,102},{7,103},{8,104... | collective-permute-start | bytes 1327112 | tf_op jit(solution)/shard_map/ppermute | solution.py:38
  106.7 2.7 %collective-permute-start.29 = (bf16[4,16,3072]{2,1,0:T(8,128)(2,1)S(1)}, bf16[4,16,3072]{2,1,0:T(8,128)(2,1)S(1)}, u32[]{:S(2)}, u32[]{:S(2)}) collective-permute-start(bf16[4,16,3072]{2,1,0:T(8,128)(2,1)S(1)} %get-tuple-element.82), channel_id=1, source_target_pairs={{0,12},{1,13},{2,14},{3,15},{4,0},{5,1},{6,2},{7,3},{8,4},{9,5},{1... | collective-permute-start | bytes 1179656 | tf_op jit(solution)/shard_map/ppermute | solution.py:38
  109.4 8.6 %up_grads.1 = (bf16[2,6144,128]{2,1,0:T(8,128)(2,1)}, bf16[2,6144,128]{2,1,0:T(8,128)(2,1)}, f32[8,128]{1,0:T(8,128)S(1)}) custom-call(bf16[256,6912]{1,0:T(8,128)(2,1)S(1)} %copy-done.8, bf16[256,6912]{1,0:T(8,128)(2,1)S(1)} %collective-permute-done.30.refs_1_.refs_3_.sib, bf16[256,768]{1,0:T(8,128)(2,1)S(1)} %get-tuple-element.84.refs_2_.own, ...), custom_call_target="tpu_custom_call" | custom-call | flops 3200000000 | bytes 13000000 | tf_op jit(solution)/shard_map/up_grads/pallas_call | solution.py:526
  121.8 2.8 %collective-permute-start.32 = (bf16[16,3456]{1,0:T(8,128)(2,1)S(1)}, bf16[16,3456]{1,0:T(8,128)(2,1)S(1)}, u32[]{:S(2)}, u32[]{:S(2)}) collective-permute-start(bf16[16,3456]{1,0:T(8,128)(2,1)S(1)} %get-tuple-element.88), channel_id=1, source_target_pairs={{0,8},{1,9},{2,10},{3,11},{4,12},{5,13},{6,14},{7,15},{8,0},{9,1},... | collective-permute-start | bytes 331784 | tf_op jit(solution)/shard_map/ppermute | solution.py:38
  125.4 4.6 %down_grads.1 = (bf16[2,128,6144]{2,1,0:T(8,128)(2,1)}, f32[8,128]{1,0:T(8,128)S(1)}) custom-call(bf16[256,6144]{1,0:T(8,128)(2,1)S(1)} %get-tuple-element.94.refs_0_.grads_own, bf16[256,6144]{1,0:T(8,128)(2,1)S(1)} %collective-permute-done.37.grads_sib, bf16[256,768]{1,0:T(8,128)(2,1)S(1)} %get-tuple-element.84.refs_2_.own, ...), custom_call_target="tpu_custom_call" | custom-call | flops 1600000000 | bytes 10000000 | tf_op jit(solution)/shard_map/down_grads/pallas_call | solution.py:565
  130.8 1.8 %collective-permute-start.39 = (bf16[4,6528]{1,0:T(4,128)(2,1)S(1)}, bf16[4,6528]{1,0:T(4,128)(2,1)S(1)}, u32[]{:S(2)}, u32[]{:S(2)}) collective-permute-start(bf16[4,6528]{1,0:T(4,128)(2,1)S(1)} %get-tuple-element.98), channel_id=1, source_target_pairs={{0,2},{1,3},{2,0},{3,1},{4,6},{5,7},{6,4},{7,5},{8,10},{9,11},{10,... | collective-permute-start | bytes 156680 | tf_op jit(solution)/shard_map/ppermute | solution.py:38
  133.5 2.1 %collective-permute-done.38.refs_0_ = bf16[4,6528]{1,0:T(4,128)(2,1)S(1)} collective-permute-done((bf16[4,6528]{1,0:T(4,128)(2,1)S(1)}, bf16[4,6528]{1,0:T(4,128)(2,1)S(1)}, u32[]{:S(2)}, u32[]{:S(2)}) %collective-permute-start.38) | collective-permute-done | bytes 52256 | tf_op jit(solution)/shard_map/ppermute | solution.py:38
  136.8 4.6 %collective-permute-start.41 = (f32[8,128]{1,0:T(8,128)S(1)}, f32[8,128]{1,0:T(8,128)S(1)}, u32[]{:S(2)}, u32[]{:S(2)}) collective-permute-start(f32[8,128]{1,0:T(8,128)S(1)} %get-tuple-element.104.own), channel_id=1, source_target_pairs={{0,16},{1,17},{2,18},{3,19},{4,20},{5,21},{6,22},{7,23},{8,24},{9,... | collective-permute-start | bytes 12296 | tf_op jit(solution)/shard_map/ppermute | solution.py:49
  142.2 1.8 %router.1 = f32[2,256]{1,0:T(2,128)} custom-call(s32[7]{0:T(128)S(1)} %stack.20.where, f32[8,128]{1,0:T(8,128)S(1)} %get-tuple-element.104.own, f32[8,128]{1,0:T(8,128)S(1)} %collective-permute-done.41.other, s32[2,256]{1,0:T(2,128)S(1)} %copy-done.7), custom_call_target="tpu_custom_call" | custom-call | tf_op jit(solution)/shard_map/router/pallas_call | solution.py:726
  (89 shorter events, 19.1 us)
Async XLA Ops:
  0.6 14.9 %collective-permute-start.3 = (bf16[2,6144,128]{2,1,0:T(8,128)(2,1)}, bf16[2,6144,128]{2,1,0:T(8,128)(2,1)S(1)}, u32[]{:S(2)}, u32[]{:S(2)}) collective-permute-start(bf16[2,6144,128]{2,1,0:T(8,128)(2,1)} %refs_10_.1), channel_id=1, source_target_pairs={{0,16},{1,17},{2,18},{3,19},{4,20},{5,21},{6,22},{7,23},{8,24},{9,... | collective-permute-start | bytes 9437192 | tf_op jit(solution)/shard_map/ppermute | solution.py:49
  2.1 13.4 %collective-permute-start.4 = (bf16[2,6144,128]{2,1,0:T(8,128)(2,1)}, bf16[2,6144,128]{2,1,0:T(8,128)(2,1)}, u32[]{:S(2)}, u32[]{:S(2)}) collective-permute-start(bf16[2,6144,128]{2,1,0:T(8,128)(2,1)} %refs_11_.1), channel_id=1, source_target_pairs={{0,16},{1,17},{2,18},{3,19},{4,20},{5,21},{6,22},{7,23},{8,24},{9,... | collective-permute-start | bytes 9437192 | tf_op jit(solution)/shard_map/ppermute | solution.py:49
  3.8 8.0 %collective-permute-start.2 = (bf16[128,384]{1,0:T(8,128)(2,1)S(1)}, bf16[128,384]{1,0:T(8,128)(2,1)S(1)}, u32[]{:S(2)}, u32[]{:S(2)}) collective-permute-start(bf16[128,384]{1,0:T(8,128)(2,1)S(1)} %pack.1.refs_0_), channel_id=1, source_target_pairs={{0,3},{1,0},{2,1},{3,2},{4,7},{5,4},{6,5},{7,6},{8,11},{9,8},{10,9... | collective-permute-start | bytes 294920 | tf_op jit(solution)/shard_map/ppermute | solution.py:38
  7.8 7.7 %collective-permute-start = (bf16[128,384]{1,0:T(8,128)(2,1)S(1)}, bf16[128,384]{1,0:T(8,128)(2,1)S(1)}, u32[]{:S(2)}, u32[]{:S(2)}) collective-permute-start(bf16[128,384]{1,0:T(8,128)(2,1)S(1)} %pack.1.refs_0_), channel_id=1, source_target_pairs={{0,1},{1,2},{2,3},{3,0},{4,5},{5,6},{6,7},{7,4},{8,9},{9,10},{10,1... | collective-permute-start | bytes 294920 | tf_op jit(solution)/shard_map/ppermute | solution.py:38
  16.4 46.0 %collective-permute-start.21 = (bf16[2,128,6144]{2,1,0:T(8,128)(2,1)S(1)}, bf16[2,128,6144]{2,1,0:T(8,128)(2,1)S(1)}, u32[]{:S(2)}, u32[]{:S(2)}) collective-permute-start(bf16[2,128,6144]{2,1,0:T(8,128)(2,1)S(1)} %relay.2), channel_id=1, source_target_pairs={{0,16},{1,17},{2,18},{3,19},{4,20},{5,21},{6,22},{7,23},{8,24},{9,... | collective-permute-start | bytes 9437192 | tf_op jit(solution)/shard_map/ppermute | solution.py:49
  17.3 6.7 %collective-permute-start.8 = (bf16[64,1536]{1,0:T(8,128)(2,1)S(1)}, bf16[64,1536]{1,0:T(8,128)(2,1)S(1)}, u32[]{:S(2)}, u32[]{:S(2)}) collective-permute-start(bf16[64,1536]{1,0:T(8,128)(2,1)S(1)} %get-tuple-element.56.refs_5_), channel_id=1, source_target_pairs={{0,96},{1,97},{2,98},{3,99},{4,100},{5,101},{6,102},{7,103},{8,104... | collective-permute-start | bytes 589832 | tf_op jit(solution)/shard_map/ppermute | solution.py:38
  19.8 7.3 %collective-permute-start.7 = (bf16[64,1536]{1,0:T(8,128)(2,1)S(1)}, bf16[64,1536]{1,0:T(8,128)(2,1)S(1)}, u32[]{:S(2)}, u32[]{:S(2)}) collective-permute-start(bf16[64,1536]{1,0:T(8,128)(2,1)S(1)} %get-tuple-element.56.refs_5_), channel_id=1, source_target_pairs={{0,32},{1,33},{2,34},{3,35},{4,36},{5,37},{6,38},{7,39},{8,40},{9,... | collective-permute-start | bytes 589832 | tf_op jit(solution)/shard_map/ppermute | solution.py:38
  19.8 7.3 %collective-permute-start.6 = (bf16[16,6144]{1,0:T(8,128)(2,1)S(1)}, bf16[16,6144]{1,0:T(8,128)(2,1)S(1)}, u32[]{:S(2)}, u32[]{:S(2)}) collective-permute-start(bf16[16,6144]{1,0:T(8,128)(2,1)S(1)} %get-tuple-element.55.refs_0_.refs_1_), channel_id=1, source_target_pairs={{0,12},{1,13},{2,14},{3,15},{4,0},{5,1},{6,2},{7,3},{8,4},{9,5},{1... | collective-permute-start | bytes 589832 | tf_op jit(solution)/shard_map/ppermute | solution.py:38
  22.5 7.0 %collective-permute-start.5 = (bf16[16,6144]{1,0:T(8,128)(2,1)S(1)}, bf16[16,6144]{1,0:T(8,128)(2,1)S(1)}, u32[]{:S(2)}, u32[]{:S(2)}) collective-permute-start(bf16[16,6144]{1,0:T(8,128)(2,1)S(1)} %get-tuple-element.55.refs_0_.refs_1_), channel_id=1, source_target_pairs={{0,4},{1,5},{2,6},{3,7},{4,8},{5,9},{6,10},{7,11},{8,12},{9,13},{1... | collective-permute-start | bytes 589832 | tf_op jit(solution)/shard_map/ppermute | solution.py:38
  37.7 16.1 %collective-permute-start.14 = (bf16[64,6144]{1,0:T(8,128)(2,1)S(1)}, bf16[64,6144]{1,0:T(8,128)(2,1)S(1)}, u32[]{:S(2)}, u32[]{:S(2)}) collective-permute-start(bf16[64,6144]{1,0:T(8,128)(2,1)S(1)} %get-tuple-element.61.refs_0_), channel_id=1, source_target_pairs={{0,96},{1,97},{2,98},{3,99},{4,100},{5,101},{6,102},{7,103},{8,104... | collective-permute-start | bytes 2359304 | tf_op jit(solution)/shard_map/ppermute | solution.py:38
  40.4 16.5 %collective-permute-start.13 = (bf16[64,6144]{1,0:T(8,128)(2,1)S(1)}, bf16[64,6144]{1,0:T(8,128)(2,1)S(1)}, u32[]{:S(2)}, u32[]{:S(2)}) collective-permute-start(bf16[64,6144]{1,0:T(8,128)(2,1)S(1)} %get-tuple-element.61.refs_0_), channel_id=1, source_target_pairs={{0,32},{1,33},{2,34},{3,35},{4,36},{5,37},{6,38},{7,39},{8,40},{9,... | collective-permute-start | bytes 2359304 | tf_op jit(solution)/shard_map/ppermute | solution.py:38
  40.4 16.5 %collective-permute-start.16 = (bf16[256,1536]{1,0:T(8,128)(2,1)S(1)}, bf16[256,1536]{1,0:T(8,128)(2,1)S(1)}, u32[]{:S(2)}, u32[]{:S(2)}) collective-permute-start(bf16[256,1536]{1,0:T(8,128)(2,1)S(1)} %get-tuple-element.62.refs_3_.refs_5_), channel_id=1, source_target_pairs={{0,12},{1,13},{2,14},{3,15},{4,0},{5,1},{6,2},{7,3},{8,4},{9,5},{1... | collective-permute-start | bytes 2359304 | tf_op jit(solution)/shard_map/ppermute | solution.py:38
  40.4 16.5 %collective-permute-start.15 = (bf16[256,1536]{1,0:T(8,128)(2,1)S(1)}, bf16[256,1536]{1,0:T(8,128)(2,1)S(1)}, u32[]{:S(2)}, u32[]{:S(2)}) collective-permute-start(bf16[256,1536]{1,0:T(8,128)(2,1)S(1)} %get-tuple-element.62.refs_3_.refs_5_), channel_id=1, source_target_pairs={{0,4},{1,5},{2,6},{3,7},{4,8},{5,9},{6,10},{7,11},{8,12},{9,13},{1... | collective-permute-start | bytes 2359304 | tf_op jit(solution)/shard_map/ppermute | solution.py:38
  57.0 13.0 %collective-permute-start.17 = (bf16[32,6144]{1,0:T(8,128)(2,1)S(1)}, bf16[32,6144]{1,0:T(8,128)(2,1)S(1)}, u32[]{:S(2)}, u32[]{:S(2)}) collective-permute-start(bf16[32,6144]{1,0:T(8,128)(2,1)S(1)} %get-tuple-element.63), channel_id=1, source_target_pairs={{0,32},{1,33},{2,34},{3,35},{4,36},{5,37},{6,38},{7,39},{8,40},{9,... | collective-permute-start | bytes 1179656 | tf_op jit(solution)/shard_map/ppermute | solution.py:38
  57.1 13.0 %collective-permute-start.18 = (bf16[32,6144]{1,0:T(8,128)(2,1)S(1)}, bf16[32,6144]{1,0:T(8,128)(2,1)S(1)}, u32[]{:S(2)}, u32[]{:S(2)}) collective-permute-start(bf16[32,6144]{1,0:T(8,128)(2,1)S(1)} %get-tuple-element.64), channel_id=1, source_target_pairs={{0,96},{1,97},{2,98},{3,99},{4,100},{5,101},{6,102},{7,103},{8,104... | collective-permute-start | bytes 1179656 | tf_op jit(solution)/shard_map/ppermute | solution.py:38
  59.8 10.3 %collective-permute-start.19 = (bf16[128,1536]{1,0:T(8,128)(2,1)S(1)}, bf16[128,1536]{1,0:T(8,128)(2,1)S(1)}, u32[]{:S(2)}, u32[]{:S(2)}) collective-permute-start(bf16[128,1536]{1,0:T(8,128)(2,1)S(1)} %get-tuple-element.65), channel_id=1, source_target_pairs={{0,4},{1,5},{2,6},{3,7},{4,8},{5,9},{6,10},{7,11},{8,12},{9,13},{1... | collective-permute-start | bytes 1179656 | tf_op jit(solution)/shard_map/ppermute | solution.py:38
  59.8 10.3 %collective-permute-start.20 = (bf16[128,1536]{1,0:T(8,128)(2,1)S(1)}, bf16[128,1536]{1,0:T(8,128)(2,1)S(1)}, u32[]{:S(2)}, u32[]{:S(2)}) collective-permute-start(bf16[128,1536]{1,0:T(8,128)(2,1)S(1)} %get-tuple-element.66), channel_id=1, source_target_pairs={{0,12},{1,13},{2,14},{3,15},{4,0},{5,1},{6,2},{7,3},{8,4},{9,5},{1... | collective-permute-start | bytes 1179656 | tf_op jit(solution)/shard_map/ppermute | solution.py:38
  87.0 19.7 %collective-permute-start.30 = (bf16[256,6912]{1,0:T(8,128)(2,1)}, bf16[256,6912]{1,0:T(8,128)(2,1)S(1)}, u32[]{:S(2)}, u32[]{:S(2)}) collective-permute-start(bf16[256,6912]{1,0:T(8,128)(2,1)} %get-tuple-element.83.refs_0_), channel_id=1, source_target_pairs={{0,16},{1,17},{2,18},{3,19},{4,20},{5,21},{6,22},{7,23},{8,24},{9,... | collective-permute-start | bytes 10616840 | tf_op jit(solution)/shard_map/ppermute | solution.py:49
  93.0 8.5 %collective-permute-start.22 = (bf16[32,3456]{1,0:T(8,128)(2,1)S(1)}, bf16[32,3456]{1,0:T(8,128)(2,1)S(1)}, u32[]{:S(2)}, u32[]{:S(2)}) collective-permute-start(bf16[32,3456]{1,0:T(8,128)(2,1)S(1)} %get-tuple-element.74), channel_id=1, source_target_pairs={{0,96},{1,97},{2,98},{3,99},{4,100},{5,101},{6,102},{7,103},{8,104... | collective-permute-start | bytes 663560 | tf_op jit(solution)/shard_map/ppermute | solution.py:38
  94.4 7.9 %collective-permute-start.23 = (bf16[32,3456]{1,0:T(8,128)(2,1)S(1)}, bf16[32,3456]{1,0:T(8,128)(2,1)S(1)}, u32[]{:S(2)}, u32[]{:S(2)}) collective-permute-start(bf16[32,3456]{1,0:T(8,128)(2,1)S(1)} %get-tuple-element.75), channel_id=1, source_target_pairs={{0,32},{1,33},{2,34},{3,35},{4,36},{5,37},{6,38},{7,39},{8,40},{9,... | collective-permute-start | bytes 663560 | tf_op jit(solution)/shard_map/ppermute | solution.py:38
  94.5 7.0 %collective-permute-start.24 = (bf16[2,16,3072]{2,1,0:T(8,128)(2,1)S(1)}, bf16[2,16,3072]{2,1,0:T(8,128)(2,1)S(1)}, u32[]{:S(2)}, u32[]{:S(2)}) collective-permute-start(bf16[2,16,3072]{2,1,0:T(8,128)(2,1)S(1)} %get-tuple-element.76), channel_id=1, source_target_pairs={{0,4},{1,5},{2,6},{3,7},{4,8},{5,9},{6,10},{7,11},{8,12},{9,13},{1... | collective-permute-start | bytes 589832 | tf_op jit(solution)/shard_map/ppermute | solution.py:38
  94.5 7.0 %collective-permute-start.25 = (bf16[2,16,3072]{2,1,0:T(8,128)(2,1)S(1)}, bf16[2,16,3072]{2,1,0:T(8,128)(2,1)S(1)}, u32[]{:S(2)}, u32[]{:S(2)}) collective-permute-start(bf16[2,16,3072]{2,1,0:T(8,128)(2,1)S(1)} %get-tuple-element.77), channel_id=1, source_target_pairs={{0,12},{1,13},{2,14},{3,15},{4,0},{5,1},{6,2},{7,3},{8,4},{9,5},{1... | collective-permute-start | bytes 589832 | tf_op jit(solution)/shard_map/ppermute | solution.py:38
  102.5 19.4 %collective-permute-start.37 = (bf16[256,6144]{1,0:T(8,128)(2,1)S(1)}, bf16[256,6144]{1,0:T(8,128)(2,1)S(1)}, u32[]{:S(2)}, u32[]{:S(2)}) collective-permute-start(bf16[256,6144]{1,0:T(8,128)(2,1)S(1)} %relay.3), channel_id=1, source_target_pairs={{0,16},{1,17},{2,18},{3,19},{4,20},{5,21},{6,22},{7,23},{8,24},{9,... | collective-permute-start | bytes 9437192 | tf_op jit(solution)/shard_map/ppermute | solution.py:49
  104.0 14.1 %collective-permute-start.27 = (bf16[64,3456]{1,0:T(8,128)(2,1)S(1)}, bf16[64,3456]{1,0:T(8,128)(2,1)S(1)}, u32[]{:S(2)}, u32[]{:S(2)}) collective-permute-start(bf16[64,3456]{1,0:T(8,128)(2,1)S(1)} %get-tuple-element.79), channel_id=1, source_target_pairs={{0,32},{1,33},{2,34},{3,35},{4,36},{5,37},{6,38},{7,39},{8,40},{9,... | collective-permute-start | bytes 1327112 | tf_op jit(solution)/shard_map/ppermute | solution.py:38
  104.0 14.0 %collective-permute-start.26 = (bf16[64,3456]{1,0:T(8,128)(2,1)S(1)}, bf16[64,3456]{1,0:T(8,128)(2,1)S(1)}, u32[]{:S(2)}, u32[]{:S(2)}) collective-permute-start(bf16[64,3456]{1,0:T(8,128)(2,1)S(1)} %get-tuple-element.78.refs_4_), channel_id=1, source_target_pairs={{0,96},{1,97},{2,98},{3,99},{4,100},{5,101},{6,102},{7,103},{8,104... | collective-permute-start | bytes 1327112 | tf_op jit(solution)/shard_map/ppermute | solution.py:38
  106.7 11.3 %collective-permute-start.28 = (bf16[4,16,3072]{2,1,0:T(8,128)(2,1)S(1)}, bf16[4,16,3072]{2,1,0:T(8,128)(2,1)S(1)}, u32[]{:S(2)}, u32[]{:S(2)}) collective-permute-start(bf16[4,16,3072]{2,1,0:T(8,128)(2,1)S(1)} %get-tuple-element.81), channel_id=1, source_target_pairs={{0,4},{1,5},{2,6},{3,7},{4,8},{5,9},{6,10},{7,11},{8,12},{9,13},{1... | collective-permute-start | bytes 1179656 | tf_op jit(solution)/shard_map/ppermute | solution.py:38
  106.7 11.3 %collective-permute-start.29 = (bf16[4,16,3072]{2,1,0:T(8,128)(2,1)S(1)}, bf16[4,16,3072]{2,1,0:T(8,128)(2,1)S(1)}, u32[]{:S(2)}, u32[]{:S(2)}) collective-permute-start(bf16[4,16,3072]{2,1,0:T(8,128)(2,1)S(1)} %get-tuple-element.82), channel_id=1, source_target_pairs={{0,12},{1,13},{2,14},{3,15},{4,0},{5,1},{6,2},{7,3},{8,4},{9,5},{1... | collective-permute-start | bytes 1179656 | tf_op jit(solution)/shard_map/ppermute | solution.py:38
  119.1 5.6 %collective-permute-start.34 = (bf16[16,3072]{1,0:T(8,128)(2,1)S(1)}, bf16[16,3072]{1,0:T(8,128)(2,1)S(1)}, u32[]{:S(2)}, u32[]{:S(2)}) collective-permute-start(bf16[16,3072]{1,0:T(8,128)(2,1)S(1)} %get-tuple-element.91), channel_id=1, source_target_pairs={{0,96},{1,97},{2,98},{3,99},{4,100},{5,101},{6,102},{7,103},{8,104... | collective-permute-start | bytes 294920 | tf_op jit(solution)/shard_map/ppermute | solution.py:38
  120.5 9.5 %collective-permute-start.35 = (bf16[16,3072]{1,0:T(8,128)(2,1)S(1)}, bf16[16,3072]{1,0:T(8,128)(2,1)S(1)}, u32[]{:S(2)}, u32[]{:S(2)}) collective-permute-start(bf16[16,3072]{1,0:T(8,128)(2,1)S(1)} %get-tuple-element.92), channel_id=1, source_target_pairs={{0,64},{1,65},{2,66},{3,67},{4,68},{5,69},{6,70},{7,71},{8,72},{9,... | collective-permute-start | bytes 294920 | tf_op jit(solution)/shard_map/ppermute | solution.py:38
  120.5 9.5 %collective-permute-start.36 = (bf16[16,3072]{1,0:T(8,128)(2,1)S(1)}, bf16[16,3072]{1,0:T(8,128)(2,1)S(1)}, u32[]{:S(2)}, u32[]{:S(2)}) collective-permute-start(bf16[16,3072]{1,0:T(8,128)(2,1)S(1)} %get-tuple-element.93), channel_id=1, source_target_pairs={{0,32},{1,33},{2,34},{3,35},{4,36},{5,37},{6,38},{7,39},{8,40},{9,... | collective-permute-start | bytes 294920 | tf_op jit(solution)/shard_map/ppermute | solution.py:38
  121.1 8.8 %collective-permute-start.31 = (bf16[16,3456]{1,0:T(8,128)(2,1)S(1)}, bf16[16,3456]{1,0:T(8,128)(2,1)S(1)}, u32[]{:S(2)}, u32[]{:S(2)}) collective-permute-start(bf16[16,3456]{1,0:T(8,128)(2,1)S(1)} %get-tuple-element.87), channel_id=1, source_target_pairs={{0,4},{1,5},{2,6},{3,7},{4,8},{5,9},{6,10},{7,11},{8,12},{9,13},{1... | collective-permute-start | bytes 331784 | tf_op jit(solution)/shard_map/ppermute | solution.py:38
  121.8 8.2 %collective-permute-start.32 = (bf16[16,3456]{1,0:T(8,128)(2,1)S(1)}, bf16[16,3456]{1,0:T(8,128)(2,1)S(1)}, u32[]{:S(2)}, u32[]{:S(2)}) collective-permute-start(bf16[16,3456]{1,0:T(8,128)(2,1)S(1)} %get-tuple-element.88), channel_id=1, source_target_pairs={{0,8},{1,9},{2,10},{3,11},{4,12},{5,13},{6,14},{7,15},{8,0},{9,1},... | collective-permute-start | bytes 331784 | tf_op jit(solution)/shard_map/ppermute | solution.py:38
  (20 other events, 232.2 us)

commit v5 on v4

--- a/solution.py
+++ b/solution.py
@@ -212,7 +212,9 @@
 def row_copies(pieces, rows, sem):
     places = (0, 64, 192, 128, 160)
     return [
-        pltpu.make_async_copy(piece, rows.at[pl.ds(at, piece.shape[0]), :], sem.at[r])
+        pltpu.make_async_copy(
+            piece, rows.at[pl.ds(at, piece.shape[0]), pl.ds(0, D)], sem.at[r]
+        )
         for r, (piece, at) in enumerate(zip(pieces, places))
     ]
 
@@ -311,7 +313,7 @@
             pltpu.SemaphoreType.DMA((D // KT, 4)),
             pltpu.SemaphoreType.DMA((3, 2)),
         ],
-        compiler_params=pltpu.CompilerParams(vmem_limit_bytes=30 * MIB),
+        compiler_params=pltpu.CompilerParams(vmem_limit_bytes=22 * MIB),
         cost_estimate=pl.CostEstimate(
             flops=3_600_000_000, bytes_accessed=20_000_000, transcendentals=0
         ),
@@ -325,12 +327,11 @@
     slots_ref, gates_ref, early_g, early_b = refs[16:20]
     pa_out, pb_out = refs[20:25], refs[25:30]
     own_out, rows_out, grads_out = refs[30:33]
-    rows, grads, wv, dv, pa, pb = refs[33:39]
-    acc_g, acc_b, deltas, tile, rbuf, packed = refs[39:45]
-    sem_t, sem_g, sem_w, sem_d, sem_o = refs[45:50]
+    wv, dv, acc_g, acc_b, deltas, tile, rbuf = refs[33:40]
+    sem_t, sem_g, sem_w, sem_d = refs[40:44]
     x, y, core = where[0], where[1], where[4]
-    copies_t = row_copies(t_in, rows, sem_t)
-    copies_g = grad_copies(g_in, grads, sem_g, y)
+    copies_t = row_copies(t_in, rows_out, sem_t)
+    copies_g = grad_copies(g_in, grads_out, sem_g, y)
     tiles = D // KT
 
     def wide_copies(i):
@@ -368,8 +369,6 @@
         scales.append(jnp.sum(jnp.where(hit, gate, 0.0), axis=1, keepdims=True))
     for copy in copies_t:
         copy.wait()
-    rows_copy = pltpu.make_async_copy(rows, rows_out.at[:, pl.ds(0, D)], sem_o.at[0])
-    grads_copy = pltpu.make_async_copy(grads, grads_out, sem_o.at[1])
 
     @pl.loop(0, tiles)
     def _(i):
@@ -379,14 +378,12 @@
         wide = jnp.concatenate(
             [wv[s, n, e, k, :] for s in range(2) for e in range(2) for n in range(2)], axis=1
         )
-        acc_g[128:192, :] += jnp.dot(rows[128:192, k], wide, preferred_element_type=F32)
+        acc_g[128:192, :] += jnp.dot(rows_out[128:192, k], wide, preferred_element_type=F32)
 
     for copy in copies_g + tall_copies:
         copy.wait()
     tall = jnp.concatenate([dv[s, e] for s in range(2) for e in range(2)], axis=0)
-    acc_b[...] = early_b[...] + nt(grads[:, far], tall)
-    rows_copy.start()
-    grads_copy.start()
+    acc_b[...] = early_b[...] + nt(grads_out[:, far], tall)
     router = [0.0, 0.0]
     for s in range(2):
         for e in range(2):
@@ -404,13 +401,11 @@
             up_delta = (hidden_grad * active).astype(BF)
             deltas[:, j * 256 : j * 256 + H] = gate_delta
             deltas[:, j * 256 + H : (j + 1) * 256] = up_delta
-            packed[s, :, e * 256 : e * 256 + H] = gate_delta
-            packed[s, :, e * 256 + H : (e + 1) * 256] = up_delta
-            packed[s, :, 512 + e * H : 512 + (e + 1) * H] = (hidden * scale).astype(BF)
-    own_copy = pltpu.make_async_copy(packed.at[0], own_out, sem_o.at[2])
-    sib_copy = pltpu.make_async_copy(packed.at[1], rows_out.at[:, pl.ds(D, 768)], sem_o.at[3])
-    own_copy.start()
-    sib_copy.start()
+            out, at = (own_out, 0) if s == 0 else (rows_out, D)
+            out[:, at + e * 256 : at + e * 256 + H] = gate_delta
+            out[:, at + e * 256 + H : at + (e + 1) * 256] = up_delta
+            at += 512 + e * H
+            out[:, at : at + H] = (hidden * scale).astype(BF)
     lane = lax.broadcasted_iota(jnp.int32, (HALF, 128), 1)
     spread = jnp.where(lane == 0, router[0], jnp.where(lane == 1, router[1], 0.0))
     for k in range(NX):
@@ -419,9 +414,9 @@
     line = rbuf[...].T[0:2]
     four = [line[e : e + 1, h * 128 : (h + 1) * 128] for e in range(2) for h in range(2)]
     sums = split_three(jnp.concatenate(four + [jnp.zeros((12, 128), F32)], axis=0))
-    for k in range(NX):
-        pa[k, :, D // 2 :] = jnp.zeros((64, 384), BF)
-        pa[k, 0:16, D // 2 :] = sums
+    for out in pa_out:
+        out[:, D // 2 :] = jnp.zeros((out.shape[0], 384), BF)
+        out[0:16, D // 2 :] = sums
 
     def partial(i):
         f = pl.ds(pl.multiple_of(i * FT, FT), FT)
@@ -436,33 +431,17 @@
     def _(i):
         f = pl.ds(pl.multiple_of(i * FT, FT), FT)
         part = partial(i).astype(BF)
-        for k in range(NX):
-            pa[k, :, f] = part[k * 64 : (k + 1) * 64, :]
-
-    parts = (pa.at[0], pa.at[1], pa.at[3], pa.at[2, pl.ds(0, 32), :], pa.at[2, pl.ds(32, 32), :])
-    copies = [
-        pltpu.make_async_copy(part, pa_out[k], sem_o.at[4 + k]) for k, part in enumerate(parts)
-    ]
-    for copy in copies:
-        copy.start()
+        for out, at in zip(pa_out, (0, 64, 192, 128, 160)):
+            out[:, f] = part[at : at + out.shape[0], :]
 
     @pl.loop(0, half)
     def _(i):
         f = pl.ds(pl.multiple_of(i * FT, FT), FT)
         tile[...] = partial(i + half).astype(BF)
-        for k in range(NY):
-            for b in range(NX):
-                src = pl.multiple_of(b * 64 + ((y + k) % NY) * 16, 16)
-                pb[k, b, :, f] = tile[pl.ds(src, 16), :]
-
-    parts = (pb.at[0], pb.at[1], pb.at[3], pb.at[2, pl.ds(0, 2)], pb.at[2, pl.ds(2, 2)])
-    more = [
-        pltpu.make_async_copy(part, pb_out[k], sem_o.at[9 + k]) for k, part in enumerate(parts)
-    ]
-    for copy in more:
-        copy.start()
-    for copy in [rows_copy, grads_copy, own_copy, sib_copy] + copies + more:
-        copy.wait()
+        for out, k, first in zip(pb_out, (0, 1, 3, 2, 2), (0, 0, 0, 0, 2)):
+            for b in range(out.shape[0]):
+                src = pl.multiple_of((first + b) * 64 + ((y + k) % NY) * 16, 16)
+                out[b, :, f] = tile[pl.ds(src, 16), :]
 
 
 def run_main(where, t, g, weights, slots, gates, early):
@@ -480,27 +459,21 @@
         main_kernel,
         out_shape=out_shape,
         in_specs=[SMEM_SPEC] + hbm * 16 + vmem_specs(4),
-        out_specs=hbm * 13,
+        out_specs=vmem_specs(13),
         scratch_shapes=[
-            pltpu.VMEM((HALF, D), BF),
-            pltpu.VMEM((HALF, D), BF),
             pltpu.VMEM((2, 2, 2, D, H), BF),
             pltpu.VMEM((2, 2, H, 1536), BF),
-            pltpu.VMEM((4, 64, WIDE), BF),
-            pltpu.VMEM((4, 4, 16, D // 2), BF),
             pltpu.VMEM((HALF, 1024), F32),
             pltpu.VMEM((HALF, 512), F32),
             pltpu.VMEM((HALF, 1024), BF),
             pltpu.VMEM((HALF, FT), BF),
             pltpu.VMEM((HALF, 128), F32),
-            pltpu.VMEM((2, HALF, 768), BF),
             pltpu.SemaphoreType.DMA((5,)),
             pltpu.SemaphoreType.DMA((5,)),
             pltpu.SemaphoreType.DMA((D // KT, 4)),
             pltpu.SemaphoreType.DMA((2,)),
-            pltpu.SemaphoreType.DMA((14,)),
         ],
-        compiler_params=pltpu.CompilerParams(vmem_limit_bytes=38 * MIB),
+        compiler_params=pltpu.CompilerParams(vmem_limit_bytes=21 * MIB),
         cost_estimate=pl.CostEstimate(
             flops=8_000_000_000, bytes_accessed=30_000_000, transcendentals=262144
         ),
@@ -764,14 +737,14 @@
 
     halves = [shift(a_low, "x", -1), shift(a_high, "x", 1)]
     halves += [shift(b_low, "y", 1), shift(b_high, "y", -1)]
-    rows_sib = swap(rows)
-    grads_sib = swap(run_relay(grads, halves))
+    rows_sib = swap(run_relay(rows, halves))
     a_down, a_up, b_up, b_down = run_middle_sum((a_down, a_up, b_up, b_down), halves)
     gate_grad, up_grad, token = run_up(rows, rows_sib, dl_own, [a_down])
     ra = [a_own, shift(a_down, "x", -1), shift(a_up, "x", 1)]
     rb = [b_own, shift(b_up, "y", 1), shift(b_down, "y", -1)]
     q = run_first_sum(where, ra, rb, token)
     qa, qb = q[0:4], q[4:8]
+    grads_sib = swap(run_relay(grads, [qa[0]]))
     ra = [qa[0]] + [shift(qa[k], "y", k) for k in (1, 2, 3)]
     rb = [qb[0]] + [shift(qb[k], "x", -k) for k in (1, 2, 3)]
     down_grad, token = run_down(grads, grads_sib, dl_own, rows_sib)

time: 144 us -> 145 us (level)
  Pallas kernels: 44 us -> 41.1 us
  local copies, waits for them, and re-layouts: 2.37 us -> 4.35 us
    pallas_call x1, Pallas kernels: 16.9 us -> 13.9 us  [run_main(): pl.pallas_call(main_kernel, out_shape=out_shape, in_specs=[SMEM_SPEC] + h...]
    unnamed x20 -> x18, local copies, waits for them, and re-layouts: 1.63 us -> 3.62 us
  transfers between devices with their start and end apart: 42 -> 42, of which waited for: 14 -> 15; matrix products, arithmetic and copies ran while one was open for 1% -> 1% of each run, Pallas kernels for 16% -> 15%
where the time goes in v5:
time: 145 us; the launch traced here: 144 us
  starting transfers between devices  58.7 us (40%)
  Pallas kernels  41.1 us (28%)
  waiting for transfers between devices  38.8 us (27%)
  local copies, waits for them, and re-layouts  4.35 us (3%)
    ppermute x36, starting transfers between devices, shift(): return lax.ppermute(value, AXES, shift_pairs(axis, step))  43.9 us
    ppermute x36, waiting for transfers between devices, shift(): return lax.ppermute(value, AXES, shift_pairs(axis, step))  37.9 us
    ppermute x6, starting transfers between devices, swap(): return lax.ppermute(value, AXES, pairs)  14.9 us
    pallas_call x1, Pallas kernels, run_main(): pl.pallas_call(main_kernel, out_shape=out_shape, in_specs=[SMEM_SPEC] + h...  13.9 us
    pallas_call x1, Pallas kernels, run_up(): pl.pallas_call(up_kernel, grid=(D // FT,), out_shape=[jax.ShapeDtypeStruc...  8.67 us
    pallas_call x1, Pallas kernels, run_early(): pl.pallas_call(early_kernel, out_shape=[jax.ShapeDtypeStruct((192, 1024),...  7.16 us
    pallas_call x1, Pallas kernels, run_down(): pl.pallas_call(down_kernel, grid=(D // FT // 2,), out_shape=[jax.ShapeDty...  4.6 us
    unnamed x18, local copies, waits for them, and re-layouts  3.62 us
  transfers between devices with their start and end apart: 42, of which 15 were waited for; matrix products, arithmetic and copies ran while one was open for 1% of the time, Pallas kernels for 15%

profile of v5, /device:TPU:1, one launch (start us, length us, event | category | flops | bytes accessed | tf_op | source)
XLA Modules:
  0.0 143.9 jit_solution(17141964002674168745)
XLA Ops:
  3.8 3.9 %collective-permute-start.2 = (bf16[128,384]{1,0:T(8,128)(2,1)S(1)}, bf16[128,384]{1,0:T(8,128)(2,1)S(1)}, u32[]{:S(2)}, u32[]{:S(2)}) collective-permute-start(bf16[128,384]{1,0:T(8,128)(2,1)S(1)} %pack.1.refs_0_), channel_id=1, source_target_pairs={{0,3},{1,0},{2,1},{3,2},{4,7},{5,4},{6,5},{7,6},{8,11},{9,8},{10,9... | collective-permute-start | bytes 294920 | tf_op jit(solution)/shard_map/ppermute | solution.py:38
  9.2 2.6 %collective-permute-done.2.refs_3_ = bf16[128,384]{1,0:T(8,128)(2,1)S(1)} collective-permute-done((bf16[128,384]{1,0:T(8,128)(2,1)S(1)}, bf16[128,384]{1,0:T(8,128)(2,1)S(1)}, u32[]{:S(2)}, u32[]{:S(2)}) %collective-permute-start.2) | collective-permute-done | bytes 98336 | tf_op jit(solution)/shard_map/ppermute | solution.py:38
  12.8 2.6 %collective-permute-done.refs_1_ = bf16[128,384]{1,0:T(8,128)(2,1)S(1)} collective-permute-done((bf16[128,384]{1,0:T(8,128)(2,1)S(1)}, bf16[128,384]{1,0:T(8,128)(2,1)S(1)}, u32[]{:S(2)}, u32[]{:S(2)}) %collective-permute-start) | collective-permute-done | bytes 98336 | tf_op jit(solution)/shard_map/ppermute | solution.py:38
  17.3 2.5 %collective-permute-start.8 = (bf16[64,1536]{1,0:T(8,128)(2,1)S(1)}, bf16[64,1536]{1,0:T(8,128)(2,1)S(1)}, u32[]{:S(2)}, u32[]{:S(2)}) collective-permute-start(bf16[64,1536]{1,0:T(8,128)(2,1)S(1)} %get-tuple-element.56.refs_5_), channel_id=1, source_target_pairs={{0,96},{1,97},{2,98},{3,99},{4,100},{5,101},{6,102},{7,103},{8,104... | collective-permute-start | bytes 589832 | tf_op jit(solution)/shard_map/ppermute | solution.py:38
  19.8 2.7 %collective-permute-start.6 = (bf16[16,6144]{1,0:T(8,128)(2,1)S(1)}, bf16[16,6144]{1,0:T(8,128)(2,1)S(1)}, u32[]{:S(2)}, u32[]{:S(2)}) collective-permute-start(bf16[16,6144]{1,0:T(8,128)(2,1)S(1)} %get-tuple-element.55.refs_0_.refs_1_), channel_id=1, source_target_pairs={{0,12},{1,13},{2,14},{3,15},{4,0},{5,1},{6,2},{7,3},{8,4},{9,5},{1... | collective-permute-start | bytes 589832 | tf_op jit(solution)/shard_map/ppermute | solution.py:38
  22.5 1.5 %collective-permute-done.8.g_high.refs_7_ = bf16[64,1536]{1,0:T(8,128)(2,1)S(1)} collective-permute-done((bf16[64,1536]{1,0:T(8,128)(2,1)S(1)}, bf16[64,1536]{1,0:T(8,128)(2,1)S(1)}, u32[]{:S(2)}, u32[]{:S(2)}) %collective-permute-start.8) | collective-permute-done | bytes 196640 | tf_op jit(solution)/shard_map/ppermute | solution.py:38
  24.1 3.1 %collective-permute-done.7.g_low.refs_6_ = bf16[64,1536]{1,0:T(8,128)(2,1)S(1)} collective-permute-done((bf16[64,1536]{1,0:T(8,128)(2,1)S(1)}, bf16[64,1536]{1,0:T(8,128)(2,1)S(1)}, u32[]{:S(2)}, u32[]{:S(2)}) %collective-permute-start.7) | collective-permute-done | bytes 196640 | tf_op jit(solution)/shard_map/ppermute | solution.py:38
  27.1 2.4 %collective-permute-done.5.t_low.refs_1_ = bf16[16,6144]{1,0:T(8,128)(2,1)S(1)} collective-permute-done((bf16[16,6144]{1,0:T(8,128)(2,1)S(1)}, bf16[16,6144]{1,0:T(8,128)(2,1)S(1)}, u32[]{:S(2)}, u32[]{:S(2)}) %collective-permute-start.5) | collective-permute-done | bytes 196640 | tf_op jit(solution)/shard_map/ppermute | solution.py:38
  29.7 2.7 %collective-permute-start.10 = (bf16[16,3072]{1,0:T(8,128)(2,1)S(1)}, bf16[16,3072]{1,0:T(8,128)(2,1)S(1)}, u32[]{:S(2)}, u32[]{:S(2)}) collective-permute-start(bf16[16,3072]{1,0:T(8,128)(2,1)S(1)} %get-tuple-element.58), channel_id=1, source_target_pairs={{0,12},{1,13},{2,14},{3,15},{4,0},{5,1},{6,2},{7,3},{8,4},{9,5},{1... | collective-permute-start | bytes 294920 | tf_op jit(solution)/shard_map/ppermute | solution.py:38
  32.3 2.7 %collective-permute-start.12 = (bf16[32,1536]{1,0:T(8,128)(2,1)S(1)}, bf16[32,1536]{1,0:T(8,128)(2,1)S(1)}, u32[]{:S(2)}, u32[]{:S(2)}) collective-permute-start(bf16[32,1536]{1,0:T(8,128)(2,1)S(1)} %get-tuple-element.60), channel_id=1, source_target_pairs={{0,96},{1,97},{2,98},{3,99},{4,100},{5,101},{6,102},{7,103},{8,104... | collective-permute-start | bytes 294920 | tf_op jit(solution)/shard_map/ppermute | solution.py:38
  35.0 2.0 %collective-permute-done.11.refs_8_ = bf16[32,1536]{1,0:T(8,128)(2,1)S(1)} collective-permute-done((bf16[32,1536]{1,0:T(8,128)(2,1)S(1)}, bf16[32,1536]{1,0:T(8,128)(2,1)S(1)}, u32[]{:S(2)}, u32[]{:S(2)}) %collective-permute-start.11) | collective-permute-done | bytes 98336 | tf_op jit(solution)/shard_map/ppermute | solution.py:38
  37.7 2.7 %collective-permute-start.14 = (bf16[64,6144]{1,0:T(8,128)(2,1)S(1)}, bf16[64,6144]{1,0:T(8,128)(2,1)S(1)}, u32[]{:S(2)}, u32[]{:S(2)}) collective-permute-start(bf16[64,6144]{1,0:T(8,128)(2,1)S(1)} %get-tuple-element.61.refs_0_), channel_id=1, source_target_pairs={{0,96},{1,97},{2,98},{3,99},{4,100},{5,101},{6,102},{7,103},{8,104... | collective-permute-start | bytes 2359304 | tf_op jit(solution)/shard_map/ppermute | solution.py:38
  41.9 11.9 %collective-permute-done.14.t_high.refs_2_ = bf16[64,6144]{1,0:T(8,128)(2,1)S(1)} collective-permute-done((bf16[64,6144]{1,0:T(8,128)(2,1)S(1)}, bf16[64,6144]{1,0:T(8,128)(2,1)S(1)}, u32[]{:S(2)}, u32[]{:S(2)}) %collective-permute-start.14) | collective-permute-done | bytes 786464 | tf_op jit(solution)/shard_map/ppermute | solution.py:38
  53.8 3.1 %collective-permute-done.13.t_low.refs_1_ = bf16[64,6144]{1,0:T(8,128)(2,1)S(1)} collective-permute-done((bf16[64,6144]{1,0:T(8,128)(2,1)S(1)}, bf16[64,6144]{1,0:T(8,128)(2,1)S(1)}, u32[]{:S(2)}, u32[]{:S(2)}) %collective-permute-start.13) | collective-permute-done | bytes 786464 | tf_op jit(solution)/shard_map/ppermute | solution.py:38
  57.1 2.7 %collective-permute-start.18 = (bf16[32,6144]{1,0:T(8,128)(2,1)S(1)}, bf16[32,6144]{1,0:T(8,128)(2,1)S(1)}, u32[]{:S(2)}, u32[]{:S(2)}) collective-permute-start(bf16[32,6144]{1,0:T(8,128)(2,1)S(1)} %get-tuple-element.64), channel_id=1, source_target_pairs={{0,96},{1,97},{2,98},{3,99},{4,100},{5,101},{6,102},{7,103},{8,104... | collective-permute-start | bytes 1179656 | tf_op jit(solution)/shard_map/ppermute | solution.py:38
  59.8 2.7 %collective-permute-start.20 = (bf16[128,1536]{1,0:T(8,128)(2,1)S(1)}, bf16[128,1536]{1,0:T(8,128)(2,1)S(1)}, u32[]{:S(2)}, u32[]{:S(2)}) collective-permute-start(bf16[128,1536]{1,0:T(8,128)(2,1)S(1)} %get-tuple-element.66), channel_id=1, source_target_pairs={{0,12},{1,13},{2,14},{3,15},{4,0},{5,1},{6,2},{7,3},{8,4},{9,5},{1... | collective-permute-start | bytes 1179656 | tf_op jit(solution)/shard_map/ppermute | solution.py:38
  62.5 7.2 %early.1 = (f32[192,1024]{1,0:T(8,128)S(1)}, f32[256,512]{1,0:T(8,128)S(1)}) custom-call(s32[7]{0:T(128)S(1)} %stack.20.where, bf16[64,6144]{1,0:T(8,128)(2,1)S(1)} %get-tuple-element.61.refs_0_, bf16[64,6144]{1,0:T(8,128)(2,1)S(1)} %collective-permute-done.13.t_low.refs_1_, bf16[64,6144]{1,0:T(8,128)(2,1)S(1)} %collective-permute-done.14.t_high.refs_2_, ...), custom_call_target="tpu_custom_call" | custom-call | flops 3600000000 | bytes 20000000 | tf_op jit(solution)/shard_map/early/pallas_call | solution.py:302
  69.7 13.9 %main.1 = (bf16[64,3456]{1,0:T(8,128)(2,1)S(1)}, bf16[64,3456]{1,0:T(8,128)(2,1)S(1)}, bf16[64,3456]{1,0:T(8,128)(2,1)S(1)}, bf16[32,3456]{1,0:T(8,128)(2,1)S(1)...) custom-call(s32[7]{0:T(128)S(1)} %stack.20.where, ...), custom_call_target="tpu_custom_call" | custom-call | flops 8000000000 | bytes 30000000 | tf_op jit(solution)/shard_map/main/pallas_call | solution.py:458
  85.2 2.7 %collective-permute-start.25 = (bf16[2,16,3072]{2,1,0:T(8,128)(2,1)S(1)}, bf16[2,16,3072]{2,1,0:T(8,128)(2,1)S(1)}, u32[]{:S(2)}, u32[]{:S(2)}) collective-permute-start(bf16[2,16,3072]{2,1,0:T(8,128)(2,1)S(1)} %get-tuple-element.77), channel_id=1, source_target_pairs={{0,12},{1,13},{2,14},{3,15},{4,0},{5,1},{6,2},{7,3},{8,4},{9,5},{1... | collective-permute-start | bytes 589832 | tf_op jit(solution)/shard_map/ppermute | solution.py:38
  87.8 3.1 %collective-permute-done.24.refs_6_.refs_3_ = bf16[2,16,3072]{2,1,0:T(8,128)(2,1)S(1)} collective-permute-done((bf16[2,16,3072]{2,1,0:T(8,128)(2,1)S(1)}, bf16[2,16,3072]{2,1,0:T(8,128)(2,1)S(1)}, u32[]{:S(2)}, u32[]{:S(2)}) %collective-permute-start.24) | collective-permute-done | bytes 196640 | tf_op jit(solution)/shard_map/ppermute | solution.py:38
  90.9 2.0 %copy-done.1 = bf16[256,6912]{1,0:T(8,128)(2,1)S(1)} copy-done((bf16[256,6912]{1,0:T(8,128)(2,1)S(1)}, bf16[256,6912]{1,0:T(8,128)(2,1)}, u32[]{:S(2)}) %copy-start.1) | copy-done | bytes 3538968
  93.3 7.8 %collective-permute-start.30 = (bf16[256,6912]{1,0:T(8,128)(2,1)S(1)}, bf16[256,6912]{1,0:T(8,128)(2,1)S(1)}, u32[]{:S(2)}, u32[]{:S(2)}) collective-permute-start(bf16[256,6912]{1,0:T(8,128)(2,1)S(1)} %relay.4), channel_id=1, source_target_pairs={{0,16},{1,17},{2,18},{3,19},{4,20},{5,21},{6,22},{7,23},{8,24},{9,... | collective-permute-start | bytes 10616840 | tf_op jit(solution)/shard_map/ppermute | solution.py:49
  101.4 2.7 %collective-permute-start.26 = (bf16[64,3456]{1,0:T(8,128)(2,1)S(1)}, bf16[64,3456]{1,0:T(8,128)(2,1)S(1)}, u32[]{:S(2)}, u32[]{:S(2)}) collective-permute-start(bf16[64,3456]{1,0:T(8,128)(2,1)S(1)} %get-tuple-element.78.refs_4_), channel_id=1, source_target_pairs={{0,96},{1,97},{2,98},{3,99},{4,100},{5,101},{6,102},{7,103},{8,104... | collective-permute-start | bytes 1327112 | tf_op jit(solution)/shard_map/ppermute | solution.py:38
  104.1 3.0 %collective-permute-start.29 = (bf16[4,16,3072]{2,1,0:T(8,128)(2,1)S(1)}, bf16[4,16,3072]{2,1,0:T(8,128)(2,1)S(1)}, u32[]{:S(2)}, u32[]{:S(2)}) collective-permute-start(bf16[4,16,3072]{2,1,0:T(8,128)(2,1)S(1)} %get-tuple-element.82), channel_id=1, source_target_pairs={{0,12},{1,13},{2,14},{3,15},{4,0},{5,1},{6,2},{7,3},{8,4},{9,5},{1... | collective-permute-start | bytes 1179656 | tf_op jit(solution)/shard_map/ppermute | solution.py:38
  107.0 8.7 %up_grads.1 = (bf16[2,6144,128]{2,1,0:T(8,128)(2,1)}, bf16[2,6144,128]{2,1,0:T(8,128)(2,1)}, f32[8,128]{1,0:T(8,128)S(1)}) custom-call(bf16[256,6912]{1,0:T(8,128)(2,1)S(1)} %copy-done.2, bf16[256,6912]{1,0:T(8,128)(2,1)S(1)} %collective-permute-done.30.refs_1_.refs_3_.sib, bf16[256,768]{1,0:T(8,128)(2,1)S(1)} %get-tuple-element.84.refs_2_.own, ...), custom_call_target="tpu_custom_call" | custom-call | flops 3200000000 | bytes 13000000 | tf_op jit(solution)/shard_map/up_grads/pallas_call | solution.py:499
  121.2 1.6 %collective-permute-done.34.refs_5_ = bf16[16,3072]{1,0:T(8,128)(2,1)S(1)} collective-permute-done((bf16[16,3072]{1,0:T(8,128)(2,1)S(1)}, bf16[16,3072]{1,0:T(8,128)(2,1)S(1)}, u32[]{:S(2)}, u32[]{:S(2)}) %collective-permute-start.34) | collective-permute-done | bytes 98336 | tf_op jit(solution)/shard_map/ppermute | solution.py:38
  122.8 2.6 %collective-permute-start.32 = (bf16[16,3456]{1,0:T(8,128)(2,1)S(1)}, bf16[16,3456]{1,0:T(8,128)(2,1)S(1)}, u32[]{:S(2)}, u32[]{:S(2)}) collective-permute-start(bf16[16,3456]{1,0:T(8,128)(2,1)S(1)} %get-tuple-element.88), channel_id=1, source_target_pairs={{0,8},{1,9},{2,10},{3,11},{4,12},{5,13},{6,14},{7,15},{8,0},{9,1},... | collective-permute-start | bytes 331784 | tf_op jit(solution)/shard_map/ppermute | solution.py:38
  126.4 4.6 %down_grads.1 = (bf16[2,128,6144]{2,1,0:T(8,128)(2,1)}, f32[8,128]{1,0:T(8,128)S(1)}) custom-call(bf16[256,6144]{1,0:T(8,128)(2,1)S(1)} %get-tuple-element.94.refs_0_.grads_own, bf16[256,6144]{1,0:T(8,128)(2,1)S(1)} %collective-permute-done.37.grads_sib, bf16[256,768]{1,0:T(8,128)(2,1)S(1)} %get-tuple-element.84.refs_2_.own, ...), custom_call_target="tpu_custom_call" | custom-call | flops 1600000000 | bytes 10000000 | tf_op jit(solution)/shard_map/down_grads/pallas_call | solution.py:538
  131.8 1.8 %collective-permute-start.39 = (bf16[4,6528]{1,0:T(4,128)(2,1)S(1)}, bf16[4,6528]{1,0:T(4,128)(2,1)S(1)}, u32[]{:S(2)}, u32[]{:S(2)}) collective-permute-start(bf16[4,6528]{1,0:T(4,128)(2,1)S(1)} %get-tuple-element.98), channel_id=1, source_target_pairs={{0,2},{1,3},{2,0},{3,1},{4,6},{5,7},{6,4},{7,5},{8,10},{9,11},{10,... | collective-permute-start | bytes 156680 | tf_op jit(solution)/shard_map/ppermute | solution.py:38
  134.5 2.1 %collective-permute-done.38.refs_0_ = bf16[4,6528]{1,0:T(4,128)(2,1)S(1)} collective-permute-done((bf16[4,6528]{1,0:T(4,128)(2,1)S(1)}, bf16[4,6528]{1,0:T(4,128)(2,1)S(1)}, u32[]{:S(2)}, u32[]{:S(2)}) %collective-permute-start.38) | collective-permute-done | bytes 52256 | tf_op jit(solution)/shard_map/ppermute | solution.py:38
  137.8 3.4 %collective-permute-start.41 = (f32[8,128]{1,0:T(8,128)S(1)}, f32[8,128]{1,0:T(8,128)S(1)}, u32[]{:S(2)}, u32[]{:S(2)}) collective-permute-start(f32[8,128]{1,0:T(8,128)S(1)} %get-tuple-element.104.own), channel_id=1, source_target_pairs={{0,16},{1,17},{2,18},{3,19},{4,20},{5,21},{6,22},{7,23},{8,24},{9,... | collective-permute-start | bytes 12296 | tf_op jit(solution)/shard_map/ppermute | solution.py:49
  142.1 1.8 %router.1 = f32[2,256]{1,0:T(2,128)} custom-call(s32[7]{0:T(128)S(1)} %stack.20.where, f32[8,128]{1,0:T(8,128)S(1)} %get-tuple-element.104.own, f32[8,128]{1,0:T(8,128)S(1)} %collective-permute-done.41.other, s32[2,256]{1,0:T(2,128)S(1)} %copy-done.7), custom_call_target="tpu_custom_call" | custom-call | tf_op jit(solution)/shard_map/router/pallas_call | solution.py:699
  (88 shorter events, 22.3 us)
Async XLA Ops:
  0.6 14.9 %collective-permute-start.3 = (bf16[2,6144,128]{2,1,0:T(8,128)(2,1)}, bf16[2,6144,128]{2,1,0:T(8,128)(2,1)S(1)}, u32[]{:S(2)}, u32[]{:S(2)}) collective-permute-start(bf16[2,6144,128]{2,1,0:T(8,128)(2,1)} %refs_10_.1), channel_id=1, source_target_pairs={{0,16},{1,17},{2,18},{3,19},{4,20},{5,21},{6,22},{7,23},{8,24},{9,... | collective-permute-start | bytes 9437192 | tf_op jit(solution)/shard_map/ppermute | solution.py:49
  2.1 13.4 %collective-permute-start.4 = (bf16[2,6144,128]{2,1,0:T(8,128)(2,1)}, bf16[2,6144,128]{2,1,0:T(8,128)(2,1)}, u32[]{:S(2)}, u32[]{:S(2)}) collective-permute-start(bf16[2,6144,128]{2,1,0:T(8,128)(2,1)} %refs_11_.1), channel_id=1, source_target_pairs={{0,16},{1,17},{2,18},{3,19},{4,20},{5,21},{6,22},{7,23},{8,24},{9,... | collective-permute-start | bytes 9437192 | tf_op jit(solution)/shard_map/ppermute | solution.py:49
  3.8 8.0 %collective-permute-start.2 = (bf16[128,384]{1,0:T(8,128)(2,1)S(1)}, bf16[128,384]{1,0:T(8,128)(2,1)S(1)}, u32[]{:S(2)}, u32[]{:S(2)}) collective-permute-start(bf16[128,384]{1,0:T(8,128)(2,1)S(1)} %pack.1.refs_0_), channel_id=1, source_target_pairs={{0,3},{1,0},{2,1},{3,2},{4,7},{5,4},{6,5},{7,6},{8,11},{9,8},{10,9... | collective-permute-start | bytes 294920 | tf_op jit(solution)/shard_map/ppermute | solution.py:38
  7.8 7.7 %collective-permute-start = (bf16[128,384]{1,0:T(8,128)(2,1)S(1)}, bf16[128,384]{1,0:T(8,128)(2,1)S(1)}, u32[]{:S(2)}, u32[]{:S(2)}) collective-permute-start(bf16[128,384]{1,0:T(8,128)(2,1)S(1)} %pack.1.refs_0_), channel_id=1, source_target_pairs={{0,1},{1,2},{2,3},{3,0},{4,5},{5,6},{6,7},{7,4},{8,9},{9,10},{10,1... | collective-permute-start | bytes 294920 | tf_op jit(solution)/shard_map/ppermute | solution.py:38
  16.4 46.0 %collective-permute-start.21 = (bf16[2,128,6144]{2,1,0:T(8,128)(2,1)S(1)}, bf16[2,128,6144]{2,1,0:T(8,128)(2,1)S(1)}, u32[]{:S(2)}, u32[]{:S(2)}) collective-permute-start(bf16[2,128,6144]{2,1,0:T(8,128)(2,1)S(1)} %relay.3), channel_id=1, source_target_pairs={{0,16},{1,17},{2,18},{3,19},{4,20},{5,21},{6,22},{7,23},{8,24},{9,... | collective-permute-start | bytes 9437192 | tf_op jit(solution)/shard_map/ppermute | solution.py:49
  17.3 6.7 %collective-permute-start.8 = (bf16[64,1536]{1,0:T(8,128)(2,1)S(1)}, bf16[64,1536]{1,0:T(8,128)(2,1)S(1)}, u32[]{:S(2)}, u32[]{:S(2)}) collective-permute-start(bf16[64,1536]{1,0:T(8,128)(2,1)S(1)} %get-tuple-element.56.refs_5_), channel_id=1, source_target_pairs={{0,96},{1,97},{2,98},{3,99},{4,100},{5,101},{6,102},{7,103},{8,104... | collective-permute-start | bytes 589832 | tf_op jit(solution)/shard_map/ppermute | solution.py:38
  19.8 7.3 %collective-permute-start.7 = (bf16[64,1536]{1,0:T(8,128)(2,1)S(1)}, bf16[64,1536]{1,0:T(8,128)(2,1)S(1)}, u32[]{:S(2)}, u32[]{:S(2)}) collective-permute-start(bf16[64,1536]{1,0:T(8,128)(2,1)S(1)} %get-tuple-element.56.refs_5_), channel_id=1, source_target_pairs={{0,32},{1,33},{2,34},{3,35},{4,36},{5,37},{6,38},{7,39},{8,40},{9,... | collective-permute-start | bytes 589832 | tf_op jit(solution)/shard_map/ppermute | solution.py:38
  19.8 7.3 %collective-permute-start.6 = (bf16[16,6144]{1,0:T(8,128)(2,1)S(1)}, bf16[16,6144]{1,0:T(8,128)(2,1)S(1)}, u32[]{:S(2)}, u32[]{:S(2)}) collective-permute-start(bf16[16,6144]{1,0:T(8,128)(2,1)S(1)} %get-tuple-element.55.refs_0_.refs_1_), channel_id=1, source_target_pairs={{0,12},{1,13},{2,14},{3,15},{4,0},{5,1},{6,2},{7,3},{8,4},{9,5},{1... | collective-permute-start | bytes 589832 | tf_op jit(solution)/shard_map/ppermute | solution.py:38
  22.5 7.0 %collective-permute-start.5 = (bf16[16,6144]{1,0:T(8,128)(2,1)S(1)}, bf16[16,6144]{1,0:T(8,128)(2,1)S(1)}, u32[]{:S(2)}, u32[]{:S(2)}) collective-permute-start(bf16[16,6144]{1,0:T(8,128)(2,1)S(1)} %get-tuple-element.55.refs_0_.refs_1_), channel_id=1, source_target_pairs={{0,4},{1,5},{2,6},{3,7},{4,8},{5,9},{6,10},{7,11},{8,12},{9,13},{1... | collective-permute-start | bytes 589832 | tf_op jit(solution)/shard_map/ppermute | solution.py:38
  37.7 16.1 %collective-permute-start.14 = (bf16[64,6144]{1,0:T(8,128)(2,1)S(1)}, bf16[64,6144]{1,0:T(8,128)(2,1)S(1)}, u32[]{:S(2)}, u32[]{:S(2)}) collective-permute-start(bf16[64,6144]{1,0:T(8,128)(2,1)S(1)} %get-tuple-element.61.refs_0_), channel_id=1, source_target_pairs={{0,96},{1,97},{2,98},{3,99},{4,100},{5,101},{6,102},{7,103},{8,104... | collective-permute-start | bytes 2359304 | tf_op jit(solution)/shard_map/ppermute | solution.py:38
  40.4 16.5 %collective-permute-start.13 = (bf16[64,6144]{1,0:T(8,128)(2,1)S(1)}, bf16[64,6144]{1,0:T(8,128)(2,1)S(1)}, u32[]{:S(2)}, u32[]{:S(2)}) collective-permute-start(bf16[64,6144]{1,0:T(8,128)(2,1)S(1)} %get-tuple-element.61.refs_0_), channel_id=1, source_target_pairs={{0,32},{1,33},{2,34},{3,35},{4,36},{5,37},{6,38},{7,39},{8,40},{9,... | collective-permute-start | bytes 2359304 | tf_op jit(solution)/shard_map/ppermute | solution.py:38
  40.4 16.5 %collective-permute-start.16 = (bf16[256,1536]{1,0:T(8,128)(2,1)S(1)}, bf16[256,1536]{1,0:T(8,128)(2,1)S(1)}, u32[]{:S(2)}, u32[]{:S(2)}) collective-permute-start(bf16[256,1536]{1,0:T(8,128)(2,1)S(1)} %get-tuple-element.62.refs_3_.refs_5_), channel_id=1, source_target_pairs={{0,12},{1,13},{2,14},{3,15},{4,0},{5,1},{6,2},{7,3},{8,4},{9,5},{1... | collective-permute-start | bytes 2359304 | tf_op jit(solution)/shard_map/ppermute | solution.py:38
  40.4 16.5 %collective-permute-start.15 = (bf16[256,1536]{1,0:T(8,128)(2,1)S(1)}, bf16[256,1536]{1,0:T(8,128)(2,1)S(1)}, u32[]{:S(2)}, u32[]{:S(2)}) collective-permute-start(bf16[256,1536]{1,0:T(8,128)(2,1)S(1)} %get-tuple-element.62.refs_3_.refs_5_), channel_id=1, source_target_pairs={{0,4},{1,5},{2,6},{3,7},{4,8},{5,9},{6,10},{7,11},{8,12},{9,13},{1... | collective-permute-start | bytes 2359304 | tf_op jit(solution)/shard_map/ppermute | solution.py:38
  57.0 12.6 %collective-permute-start.17 = (bf16[32,6144]{1,0:T(8,128)(2,1)S(1)}, bf16[32,6144]{1,0:T(8,128)(2,1)S(1)}, u32[]{:S(2)}, u32[]{:S(2)}) collective-permute-start(bf16[32,6144]{1,0:T(8,128)(2,1)S(1)} %get-tuple-element.63), channel_id=1, source_target_pairs={{0,32},{1,33},{2,34},{3,35},{4,36},{5,37},{6,38},{7,39},{8,40},{9,... | collective-permute-start | bytes 1179656 | tf_op jit(solution)/shard_map/ppermute | solution.py:38
  57.1 12.5 %collective-permute-start.18 = (bf16[32,6144]{1,0:T(8,128)(2,1)S(1)}, bf16[32,6144]{1,0:T(8,128)(2,1)S(1)}, u32[]{:S(2)}, u32[]{:S(2)}) collective-permute-start(bf16[32,6144]{1,0:T(8,128)(2,1)S(1)} %get-tuple-element.64), channel_id=1, source_target_pairs={{0,96},{1,97},{2,98},{3,99},{4,100},{5,101},{6,102},{7,103},{8,104... | collective-permute-start | bytes 1179656 | tf_op jit(solution)/shard_map/ppermute | solution.py:38
  59.8 9.9 %collective-permute-start.19 = (bf16[128,1536]{1,0:T(8,128)(2,1)S(1)}, bf16[128,1536]{1,0:T(8,128)(2,1)S(1)}, u32[]{:S(2)}, u32[]{:S(2)}) collective-permute-start(bf16[128,1536]{1,0:T(8,128)(2,1)S(1)} %get-tuple-element.65), channel_id=1, source_target_pairs={{0,4},{1,5},{2,6},{3,7},{4,8},{5,9},{6,10},{7,11},{8,12},{9,13},{1... | collective-permute-start | bytes 1179656 | tf_op jit(solution)/shard_map/ppermute | solution.py:38
  59.8 9.9 %collective-permute-start.20 = (bf16[128,1536]{1,0:T(8,128)(2,1)S(1)}, bf16[128,1536]{1,0:T(8,128)(2,1)S(1)}, u32[]{:S(2)}, u32[]{:S(2)}) collective-permute-start(bf16[128,1536]{1,0:T(8,128)(2,1)S(1)} %get-tuple-element.66), channel_id=1, source_target_pairs={{0,12},{1,13},{2,14},{3,15},{4,0},{5,1},{6,2},{7,3},{8,4},{9,5},{1... | collective-permute-start | bytes 1179656 | tf_op jit(solution)/shard_map/ppermute | solution.py:38
  83.6 7.3 %collective-permute-start.22 = (bf16[32,3456]{1,0:T(8,128)(2,1)S(1)}, bf16[32,3456]{1,0:T(8,128)(2,1)S(1)}, u32[]{:S(2)}, u32[]{:S(2)}) collective-permute-start(bf16[32,3456]{1,0:T(8,128)(2,1)S(1)} %get-tuple-element.74), channel_id=1, source_target_pairs={{0,96},{1,97},{2,98},{3,99},{4,100},{5,101},{6,102},{7,103},{8,104... | collective-permute-start | bytes 663560 | tf_op jit(solution)/shard_map/ppermute | solution.py:38
  84.9 6.0 %collective-permute-start.23 = (bf16[32,3456]{1,0:T(8,128)(2,1)S(1)}, bf16[32,3456]{1,0:T(8,128)(2,1)S(1)}, u32[]{:S(2)}, u32[]{:S(2)}) collective-permute-start(bf16[32,3456]{1,0:T(8,128)(2,1)S(1)} %get-tuple-element.75), channel_id=1, source_target_pairs={{0,32},{1,33},{2,34},{3,35},{4,36},{5,37},{6,38},{7,39},{8,40},{9,... | collective-permute-start | bytes 663560 | tf_op jit(solution)/shard_map/ppermute | solution.py:38
  85.2 5.7 %collective-permute-start.24 = (bf16[2,16,3072]{2,1,0:T(8,128)(2,1)S(1)}, bf16[2,16,3072]{2,1,0:T(8,128)(2,1)S(1)}, u32[]{:S(2)}, u32[]{:S(2)}) collective-permute-start(bf16[2,16,3072]{2,1,0:T(8,128)(2,1)S(1)} %get-tuple-element.76), channel_id=1, source_target_pairs={{0,4},{1,5},{2,6},{3,7},{4,8},{5,9},{6,10},{7,11},{8,12},{9,13},{1... | collective-permute-start | bytes 589832 | tf_op jit(solution)/shard_map/ppermute | solution.py:38
  85.2 5.7 %collective-permute-start.25 = (bf16[2,16,3072]{2,1,0:T(8,128)(2,1)S(1)}, bf16[2,16,3072]{2,1,0:T(8,128)(2,1)S(1)}, u32[]{:S(2)}, u32[]{:S(2)}) collective-permute-start(bf16[2,16,3072]{2,1,0:T(8,128)(2,1)S(1)} %get-tuple-element.77), channel_id=1, source_target_pairs={{0,12},{1,13},{2,14},{3,15},{4,0},{5,1},{6,2},{7,3},{8,4},{9,5},{1... | collective-permute-start | bytes 589832 | tf_op jit(solution)/shard_map/ppermute | solution.py:38
  93.3 13.7 %collective-permute-start.30 = (bf16[256,6912]{1,0:T(8,128)(2,1)S(1)}, bf16[256,6912]{1,0:T(8,128)(2,1)S(1)}, u32[]{:S(2)}, u32[]{:S(2)}) collective-permute-start(bf16[256,6912]{1,0:T(8,128)(2,1)S(1)} %relay.4), channel_id=1, source_target_pairs={{0,16},{1,17},{2,18},{3,19},{4,20},{5,21},{6,22},{7,23},{8,24},{9,... | collective-permute-start | bytes 10616840 | tf_op jit(solution)/shard_map/ppermute | solution.py:49
  101.3 14.7 %collective-permute-start.27 = (bf16[64,3456]{1,0:T(8,128)(2,1)S(1)}, bf16[64,3456]{1,0:T(8,128)(2,1)S(1)}, u32[]{:S(2)}, u32[]{:S(2)}) collective-permute-start(bf16[64,3456]{1,0:T(8,128)(2,1)S(1)} %get-tuple-element.79), channel_id=1, source_target_pairs={{0,32},{1,33},{2,34},{3,35},{4,36},{5,37},{6,38},{7,39},{8,40},{9,... | collective-permute-start | bytes 1327112 | tf_op jit(solution)/shard_map/ppermute | solution.py:38
  101.4 14.6 %collective-permute-start.26 = (bf16[64,3456]{1,0:T(8,128)(2,1)S(1)}, bf16[64,3456]{1,0:T(8,128)(2,1)S(1)}, u32[]{:S(2)}, u32[]{:S(2)}) collective-permute-start(bf16[64,3456]{1,0:T(8,128)(2,1)S(1)} %get-tuple-element.78.refs_4_), channel_id=1, source_target_pairs={{0,96},{1,97},{2,98},{3,99},{4,100},{5,101},{6,102},{7,103},{8,104... | collective-permute-start | bytes 1327112 | tf_op jit(solution)/shard_map/ppermute | solution.py:38
  104.1 11.9 %collective-permute-start.28 = (bf16[4,16,3072]{2,1,0:T(8,128)(2,1)S(1)}, bf16[4,16,3072]{2,1,0:T(8,128)(2,1)S(1)}, u32[]{:S(2)}, u32[]{:S(2)}) collective-permute-start(bf16[4,16,3072]{2,1,0:T(8,128)(2,1)S(1)} %get-tuple-element.81), channel_id=1, source_target_pairs={{0,4},{1,5},{2,6},{3,7},{4,8},{5,9},{6,10},{7,11},{8,12},{9,13},{1... | collective-permute-start | bytes 1179656 | tf_op jit(solution)/shard_map/ppermute | solution.py:38
  104.1 11.9 %collective-permute-start.29 = (bf16[4,16,3072]{2,1,0:T(8,128)(2,1)S(1)}, bf16[4,16,3072]{2,1,0:T(8,128)(2,1)S(1)}, u32[]{:S(2)}, u32[]{:S(2)}) collective-permute-start(bf16[4,16,3072]{2,1,0:T(8,128)(2,1)S(1)} %get-tuple-element.82), channel_id=1, source_target_pairs={{0,12},{1,13},{2,14},{3,15},{4,0},{5,1},{6,2},{7,3},{8,4},{9,5},{1... | collective-permute-start | bytes 1179656 | tf_op jit(solution)/shard_map/ppermute | solution.py:38
  117.2 8.2 %collective-permute-start.37 = (bf16[256,6144]{1,0:T(8,128)(2,1)S(1)}, bf16[256,6144]{1,0:T(8,128)(2,1)S(1)}, u32[]{:S(2)}, u32[]{:S(2)}) collective-permute-start(bf16[256,6144]{1,0:T(8,128)(2,1)S(1)} %relay.5), channel_id=1, source_target_pairs={{0,16},{1,17},{2,18},{3,19},{4,20},{5,21},{6,22},{7,23},{8,24},{9,... | collective-permute-start | bytes 9437192 | tf_op jit(solution)/shard_map/ppermute | solution.py:49
  119.8 11.2 %collective-permute-start.35 = (bf16[16,3072]{1,0:T(8,128)(2,1)S(1)}, bf16[16,3072]{1,0:T(8,128)(2,1)S(1)}, u32[]{:S(2)}, u32[]{:S(2)}) collective-permute-start(bf16[16,3072]{1,0:T(8,128)(2,1)S(1)} %get-tuple-element.92), channel_id=1, source_target_pairs={{0,64},{1,65},{2,66},{3,67},{4,68},{5,69},{6,70},{7,71},{8,72},{9,... | collective-permute-start | bytes 294920 | tf_op jit(solution)/shard_map/ppermute | solution.py:38
  119.8 11.2 %collective-permute-start.36 = (bf16[16,3072]{1,0:T(8,128)(2,1)S(1)}, bf16[16,3072]{1,0:T(8,128)(2,1)S(1)}, u32[]{:S(2)}, u32[]{:S(2)}) collective-permute-start(bf16[16,3072]{1,0:T(8,128)(2,1)S(1)} %get-tuple-element.93), channel_id=1, source_target_pairs={{0,32},{1,33},{2,34},{3,35},{4,36},{5,37},{6,38},{7,39},{8,40},{9,... | collective-permute-start | bytes 294920 | tf_op jit(solution)/shard_map/ppermute | solution.py:38
  120.4 10.6 %collective-permute-start.31 = (bf16[16,3456]{1,0:T(8,128)(2,1)S(1)}, bf16[16,3456]{1,0:T(8,128)(2,1)S(1)}, u32[]{:S(2)}, u32[]{:S(2)}) collective-permute-start(bf16[16,3456]{1,0:T(8,128)(2,1)S(1)} %get-tuple-element.87), channel_id=1, source_target_pairs={{0,4},{1,5},{2,6},{3,7},{4,8},{5,9},{6,10},{7,11},{8,12},{9,13},{1... | collective-permute-start | bytes 331784 | tf_op jit(solution)/shard_map/ppermute | solution.py:38
  122.8 8.2 %collective-permute-start.32 = (bf16[16,3456]{1,0:T(8,128)(2,1)S(1)}, bf16[16,3456]{1,0:T(8,128)(2,1)S(1)}, u32[]{:S(2)}, u32[]{:S(2)}) collective-permute-start(bf16[16,3456]{1,0:T(8,128)(2,1)S(1)} %get-tuple-element.88), channel_id=1, source_target_pairs={{0,8},{1,9},{2,10},{3,11},{4,12},{5,13},{6,14},{7,15},{8,0},{9,1},... | collective-permute-start | bytes 331784 | tf_op jit(solution)/shard_map/ppermute | solution.py:38
  125.4 5.6 %collective-permute-start.33 = (bf16[16,3456]{1,0:T(8,128)(2,1)S(1)}, bf16[16,3456]{1,0:T(8,128)(2,1)S(1)}, u32[]{:S(2)}, u32[]{:S(2)}) collective-permute-start(bf16[16,3456]{1,0:T(8,128)(2,1)S(1)} %get-tuple-element.89), channel_id=1, source_target_pairs={{0,12},{1,13},{2,14},{3,15},{4,0},{5,1},{6,2},{7,3},{8,4},{9,5},{1... | collective-permute-start | bytes 331784 | tf_op jit(solution)/shard_map/ppermute | solution.py:38
  (19 other events, 183.7 us)

commit v6 on v5

--- a/solution.py
+++ b/solution.py
@@ -737,14 +737,14 @@
 
     halves = [shift(a_low, "x", -1), shift(a_high, "x", 1)]
     halves += [shift(b_low, "y", 1), shift(b_high, "y", -1)]
-    rows_sib = swap(run_relay(rows, halves))
+    rows_sib = swap(rows)
+    grads_sib = swap(run_relay(grads, halves))
     a_down, a_up, b_up, b_down = run_middle_sum((a_down, a_up, b_up, b_down), halves)
     gate_grad, up_grad, token = run_up(rows, rows_sib, dl_own, [a_down])
     ra = [a_own, shift(a_down, "x", -1), shift(a_up, "x", 1)]
     rb = [b_own, shift(b_up, "y", 1), shift(b_down, "y", -1)]
     q = run_first_sum(where, ra, rb, token)
     qa, qb = q[0:4], q[4:8]
-    grads_sib = swap(run_relay(grads, [qa[0]]))
     ra = [qa[0]] + [shift(qa[k], "y", k) for k in (1, 2, 3)]
     rb = [qb[0]] + [shift(qb[k], "x", -k) for k in (1, 2, 3)]
     down_grad, token = run_down(grads, grads_sib, dl_own, rows_sib)

time: 145 us -> 141 us (0.972)
  local copies, waits for them, and re-layouts: 4.35 us -> 2.36 us
    unnamed x18 -> x16, local copies, waits for them, and re-layouts: 3.62 us -> 1.62 us
  transfers between devices with their start and end apart: 42 -> 42, of which waited for: 15 -> 14; matrix products, arithmetic and copies ran while one was open for 1% -> 1% of each run, Pallas kernels for 15% -> 16%
where the time goes in v6:
time: 141 us
  starting transfers between devices  57.8 us (41%)
  Pallas kernels  40.8 us (29%)
  waiting for transfers between devices  38.9 us (28%)
  local copies, waits for them, and re-layouts  2.36 us (2%)
    ppermute x36, starting transfers between devices, shift(): return lax.ppermute(value, AXES, shift_pairs(axis, step))  43.5 us
    ppermute x36, waiting for transfers between devices, shift(): return lax.ppermute(value, AXES, shift_pairs(axis, step))  38.1 us
    ppermute x6, starting transfers between devices, swap(): return lax.ppermute(value, AXES, pairs)  14.3 us
    pallas_call x1, Pallas kernels, run_main(): pl.pallas_call(main_kernel, out_shape=out_shape, in_specs=[SMEM_SPEC] + h...  14 us
    pallas_call x1, Pallas kernels, run_up(): pl.pallas_call(up_kernel, grid=(D // FT,), out_shape=[jax.ShapeDtypeStruc...  8.64 us
    pallas_call x1, Pallas kernels, run_early(): pl.pallas_call(early_kernel, out_shape=[jax.ShapeDtypeStruct((192, 1024),...  7.16 us
    pallas_call x1, Pallas kernels, run_down(): pl.pallas_call(down_kernel, grid=(D // FT // 2,), out_shape=[jax.ShapeDty...  4.6 us
  transfers between devices with their start and end apart: 42, of which 14 were waited for; matrix products, arithmetic and copies ran while one was open for 1% of the time, Pallas kernels for 16%

profile of v6, /device:TPU:1, one launch (start us, length us, event | category | flops | bytes accessed | tf_op | source)
XLA Modules:
  0.0 140.7 jit_solution(2100191530238257163)
XLA Ops:
  0.6 1.5 %collective-permute-start.3 = (bf16[2,6144,128]{2,1,0:T(8,128)(2,1)}, bf16[2,6144,128]{2,1,0:T(8,128)(2,1)S(1)}, u32[]{:S(2)}, u32[]{:S(2)}) collective-permute-start(bf16[2,6144,128]{2,1,0:T(8,128)(2,1)} %refs_10_.1), channel_id=1, source_target_pairs={{0,16},{1,17},{2,18},{3,19},{4,20},{5,21},{6,22},{7,23},{8,24},{9,... | collective-permute-start | bytes 9437192 | tf_op jit(solution)/shard_map/ppermute | solution.py:49
  3.8 3.9 %collective-permute-start.2 = (bf16[128,384]{1,0:T(8,128)(2,1)S(1)}, bf16[128,384]{1,0:T(8,128)(2,1)S(1)}, u32[]{:S(2)}, u32[]{:S(2)}) collective-permute-start(bf16[128,384]{1,0:T(8,128)(2,1)S(1)} %pack.1.refs_0_), channel_id=1, source_target_pairs={{0,3},{1,0},{2,1},{3,2},{4,7},{5,4},{6,5},{7,6},{8,11},{9,8},{10,9... | collective-permute-start | bytes 294920 | tf_op jit(solution)/shard_map/ppermute | solution.py:38
  9.2 2.6 %collective-permute-done.2.refs_3_ = bf16[128,384]{1,0:T(8,128)(2,1)S(1)} collective-permute-done((bf16[128,384]{1,0:T(8,128)(2,1)S(1)}, bf16[128,384]{1,0:T(8,128)(2,1)S(1)}, u32[]{:S(2)}, u32[]{:S(2)}) %collective-permute-start.2) | collective-permute-done | bytes 98336 | tf_op jit(solution)/shard_map/ppermute | solution.py:38
  12.8 2.6 %collective-permute-done.refs_1_ = bf16[128,384]{1,0:T(8,128)(2,1)S(1)} collective-permute-done((bf16[128,384]{1,0:T(8,128)(2,1)S(1)}, bf16[128,384]{1,0:T(8,128)(2,1)S(1)}, u32[]{:S(2)}, u32[]{:S(2)}) %collective-permute-start) | collective-permute-done | bytes 98336 | tf_op jit(solution)/shard_map/ppermute | solution.py:38
  17.3 2.5 %collective-permute-start.8 = (bf16[64,1536]{1,0:T(8,128)(2,1)S(1)}, bf16[64,1536]{1,0:T(8,128)(2,1)S(1)}, u32[]{:S(2)}, u32[]{:S(2)}) collective-permute-start(bf16[64,1536]{1,0:T(8,128)(2,1)S(1)} %get-tuple-element.56.refs_5_), channel_id=1, source_target_pairs={{0,96},{1,97},{2,98},{3,99},{4,100},{5,101},{6,102},{7,103},{8,104... | collective-permute-start | bytes 589832 | tf_op jit(solution)/shard_map/ppermute | solution.py:38
  19.8 2.7 %collective-permute-start.6 = (bf16[16,6144]{1,0:T(8,128)(2,1)S(1)}, bf16[16,6144]{1,0:T(8,128)(2,1)S(1)}, u32[]{:S(2)}, u32[]{:S(2)}) collective-permute-start(bf16[16,6144]{1,0:T(8,128)(2,1)S(1)} %get-tuple-element.55.refs_0_.refs_1_), channel_id=1, source_target_pairs={{0,12},{1,13},{2,14},{3,15},{4,0},{5,1},{6,2},{7,3},{8,4},{9,5},{1... | collective-permute-start | bytes 589832 | tf_op jit(solution)/shard_map/ppermute | solution.py:38
  22.5 1.5 %collective-permute-done.8.g_high.refs_7_ = bf16[64,1536]{1,0:T(8,128)(2,1)S(1)} collective-permute-done((bf16[64,1536]{1,0:T(8,128)(2,1)S(1)}, bf16[64,1536]{1,0:T(8,128)(2,1)S(1)}, u32[]{:S(2)}, u32[]{:S(2)}) %collective-permute-start.8) | collective-permute-done | bytes 196640 | tf_op jit(solution)/shard_map/ppermute | solution.py:38
  24.1 3.1 %collective-permute-done.7.g_low.refs_6_ = bf16[64,1536]{1,0:T(8,128)(2,1)S(1)} collective-permute-done((bf16[64,1536]{1,0:T(8,128)(2,1)S(1)}, bf16[64,1536]{1,0:T(8,128)(2,1)S(1)}, u32[]{:S(2)}, u32[]{:S(2)}) %collective-permute-start.7) | collective-permute-done | bytes 196640 | tf_op jit(solution)/shard_map/ppermute | solution.py:38
  27.1 2.4 %collective-permute-done.5.t_low.refs_1_ = bf16[16,6144]{1,0:T(8,128)(2,1)S(1)} collective-permute-done((bf16[16,6144]{1,0:T(8,128)(2,1)S(1)}, bf16[16,6144]{1,0:T(8,128)(2,1)S(1)}, u32[]{:S(2)}, u32[]{:S(2)}) %collective-permute-start.5) | collective-permute-done | bytes 196640 | tf_op jit(solution)/shard_map/ppermute | solution.py:38
  29.7 2.7 %collective-permute-start.10 = (bf16[16,3072]{1,0:T(8,128)(2,1)S(1)}, bf16[16,3072]{1,0:T(8,128)(2,1)S(1)}, u32[]{:S(2)}, u32[]{:S(2)}) collective-permute-start(bf16[16,3072]{1,0:T(8,128)(2,1)S(1)} %get-tuple-element.58), channel_id=1, source_target_pairs={{0,12},{1,13},{2,14},{3,15},{4,0},{5,1},{6,2},{7,3},{8,4},{9,5},{1... | collective-permute-start | bytes 294920 | tf_op jit(solution)/shard_map/ppermute | solution.py:38
  32.3 2.7 %collective-permute-start.12 = (bf16[32,1536]{1,0:T(8,128)(2,1)S(1)}, bf16[32,1536]{1,0:T(8,128)(2,1)S(1)}, u32[]{:S(2)}, u32[]{:S(2)}) collective-permute-start(bf16[32,1536]{1,0:T(8,128)(2,1)S(1)} %get-tuple-element.60), channel_id=1, source_target_pairs={{0,96},{1,97},{2,98},{3,99},{4,100},{5,101},{6,102},{7,103},{8,104... | collective-permute-start | bytes 294920 | tf_op jit(solution)/shard_map/ppermute | solution.py:38
  35.0 2.0 %collective-permute-done.11.refs_8_ = bf16[32,1536]{1,0:T(8,128)(2,1)S(1)} collective-permute-done((bf16[32,1536]{1,0:T(8,128)(2,1)S(1)}, bf16[32,1536]{1,0:T(8,128)(2,1)S(1)}, u32[]{:S(2)}, u32[]{:S(2)}) %collective-permute-start.11) | collective-permute-done | bytes 98336 | tf_op jit(solution)/shard_map/ppermute | solution.py:38
  37.7 2.7 %collective-permute-start.14 = (bf16[64,6144]{1,0:T(8,128)(2,1)S(1)}, bf16[64,6144]{1,0:T(8,128)(2,1)S(1)}, u32[]{:S(2)}, u32[]{:S(2)}) collective-permute-start(bf16[64,6144]{1,0:T(8,128)(2,1)S(1)} %get-tuple-element.61.refs_0_), channel_id=1, source_target_pairs={{0,96},{1,97},{2,98},{3,99},{4,100},{5,101},{6,102},{7,103},{8,104... | collective-permute-start | bytes 2359304 | tf_op jit(solution)/shard_map/ppermute | solution.py:38
  40.4 1.5 %collective-permute-start.15 = (bf16[256,1536]{1,0:T(8,128)(2,1)S(1)}, bf16[256,1536]{1,0:T(8,128)(2,1)S(1)}, u32[]{:S(2)}, u32[]{:S(2)}) collective-permute-start(bf16[256,1536]{1,0:T(8,128)(2,1)S(1)} %get-tuple-element.62.refs_3_.refs_5_), channel_id=1, source_target_pairs={{0,4},{1,5},{2,6},{3,7},{4,8},{5,9},{6,10},{7,11},{8,12},{9,13},{1... | collective-permute-start | bytes 2359304 | tf_op jit(solution)/shard_map/ppermute | solution.py:38
  41.9 11.9 %collective-permute-done.14.t_high.refs_2_ = bf16[64,6144]{1,0:T(8,128)(2,1)S(1)} collective-permute-done((bf16[64,6144]{1,0:T(8,128)(2,1)S(1)}, bf16[64,6144]{1,0:T(8,128)(2,1)S(1)}, u32[]{:S(2)}, u32[]{:S(2)}) %collective-permute-start.14) | collective-permute-done | bytes 786464 | tf_op jit(solution)/shard_map/ppermute | solution.py:38
  53.8 3.1 %collective-permute-done.13.t_low.refs_1_ = bf16[64,6144]{1,0:T(8,128)(2,1)S(1)} collective-permute-done((bf16[64,6144]{1,0:T(8,128)(2,1)S(1)}, bf16[64,6144]{1,0:T(8,128)(2,1)S(1)}, u32[]{:S(2)}, u32[]{:S(2)}) %collective-permute-start.13) | collective-permute-done | bytes 786464 | tf_op jit(solution)/shard_map/ppermute | solution.py:38
  57.1 2.7 %collective-permute-start.18 = (bf16[32,6144]{1,0:T(8,128)(2,1)S(1)}, bf16[32,6144]{1,0:T(8,128)(2,1)S(1)}, u32[]{:S(2)}, u32[]{:S(2)}) collective-permute-start(bf16[32,6144]{1,0:T(8,128)(2,1)S(1)} %get-tuple-element.64), channel_id=1, source_target_pairs={{0,96},{1,97},{2,98},{3,99},{4,100},{5,101},{6,102},{7,103},{8,104... | collective-permute-start | bytes 1179656 | tf_op jit(solution)/shard_map/ppermute | solution.py:38
  59.8 2.7 %collective-permute-start.20 = (bf16[128,1536]{1,0:T(8,128)(2,1)S(1)}, bf16[128,1536]{1,0:T(8,128)(2,1)S(1)}, u32[]{:S(2)}, u32[]{:S(2)}) collective-permute-start(bf16[128,1536]{1,0:T(8,128)(2,1)S(1)} %get-tuple-element.66), channel_id=1, source_target_pairs={{0,12},{1,13},{2,14},{3,15},{4,0},{5,1},{6,2},{7,3},{8,4},{9,5},{1... | collective-permute-start | bytes 1179656 | tf_op jit(solution)/shard_map/ppermute | solution.py:38
  62.5 7.2 %early.1 = (f32[192,1024]{1,0:T(8,128)S(1)}, f32[256,512]{1,0:T(8,128)S(1)}) custom-call(s32[7]{0:T(128)S(1)} %stack.20.where, bf16[64,6144]{1,0:T(8,128)(2,1)S(1)} %get-tuple-element.61.refs_0_, bf16[64,6144]{1,0:T(8,128)(2,1)S(1)} %collective-permute-done.13.t_low.refs_1_, bf16[64,6144]{1,0:T(8,128)(2,1)S(1)} %collective-permute-done.14.t_high.refs_2_, ...), custom_call_target="tpu_custom_call" | custom-call | flops 3600000000 | bytes 20000000 | tf_op jit(solution)/shard_map/early/pallas_call | solution.py:302
  69.7 14.0 %main.1 = (bf16[64,3456]{1,0:T(8,128)(2,1)S(1)}, bf16[64,3456]{1,0:T(8,128)(2,1)S(1)}, bf16[64,3456]{1,0:T(8,128)(2,1)S(1)}, bf16[32,3456]{1,0:T(8,128)(2,1)S(1)...) custom-call(s32[7]{0:T(128)S(1)} %stack.20.where, ...), custom_call_target="tpu_custom_call" | custom-call | flops 8000000000 | bytes 30000000 | tf_op jit(solution)/shard_map/main/pallas_call | solution.py:458
  83.7 6.0 %collective-permute-start.30 = (bf16[256,6912]{1,0:T(8,128)(2,1)}, bf16[256,6912]{1,0:T(8,128)(2,1)S(1)}, u32[]{:S(2)}, u32[]{:S(2)}) collective-permute-start(bf16[256,6912]{1,0:T(8,128)(2,1)} %get-tuple-element.83.refs_0_), channel_id=1, source_target_pairs={{0,16},{1,17},{2,18},{3,19},{4,20},{5,21},{6,22},{7,23},{8,24},{9,... | collective-permute-start | bytes 10616840 | tf_op jit(solution)/shard_map/ppermute | solution.py:49
  91.2 2.7 %collective-permute-start.25 = (bf16[2,16,3072]{2,1,0:T(8,128)(2,1)S(1)}, bf16[2,16,3072]{2,1,0:T(8,128)(2,1)S(1)}, u32[]{:S(2)}, u32[]{:S(2)}) collective-permute-start(bf16[2,16,3072]{2,1,0:T(8,128)(2,1)S(1)} %get-tuple-element.77), channel_id=1, source_target_pairs={{0,12},{1,13},{2,14},{3,15},{4,0},{5,1},{6,2},{7,3},{8,4},{9,5},{1... | collective-permute-start | bytes 589832 | tf_op jit(solution)/shard_map/ppermute | solution.py:38
  93.9 4.4 %collective-permute-done.24.refs_6_.refs_3_ = bf16[2,16,3072]{2,1,0:T(8,128)(2,1)S(1)} collective-permute-done((bf16[2,16,3072]{2,1,0:T(8,128)(2,1)S(1)}, bf16[2,16,3072]{2,1,0:T(8,128)(2,1)S(1)}, u32[]{:S(2)}, u32[]{:S(2)}) %collective-permute-start.24) | collective-permute-done | bytes 196640 | tf_op jit(solution)/shard_map/ppermute | solution.py:38
  100.7 2.7 %collective-permute-start.26 = (bf16[64,3456]{1,0:T(8,128)(2,1)S(1)}, bf16[64,3456]{1,0:T(8,128)(2,1)S(1)}, u32[]{:S(2)}, u32[]{:S(2)}) collective-permute-start(bf16[64,3456]{1,0:T(8,128)(2,1)S(1)} %get-tuple-element.78.refs_4_), channel_id=1, source_target_pairs={{0,96},{1,97},{2,98},{3,99},{4,100},{5,101},{6,102},{7,103},{8,104... | collective-permute-start | bytes 1327112 | tf_op jit(solution)/shard_map/ppermute | solution.py:38
  103.4 2.7 %collective-permute-start.29 = (bf16[4,16,3072]{2,1,0:T(8,128)(2,1)S(1)}, bf16[4,16,3072]{2,1,0:T(8,128)(2,1)S(1)}, u32[]{:S(2)}, u32[]{:S(2)}) collective-permute-start(bf16[4,16,3072]{2,1,0:T(8,128)(2,1)S(1)} %get-tuple-element.82), channel_id=1, source_target_pairs={{0,12},{1,13},{2,14},{3,15},{4,0},{5,1},{6,2},{7,3},{8,4},{9,5},{1... | collective-permute-start | bytes 1179656 | tf_op jit(solution)/shard_map/ppermute | solution.py:38
  106.1 8.6 %up_grads.1 = (bf16[2,6144,128]{2,1,0:T(8,128)(2,1)}, bf16[2,6144,128]{2,1,0:T(8,128)(2,1)}, f32[8,128]{1,0:T(8,128)S(1)}) custom-call(bf16[256,6912]{1,0:T(8,128)(2,1)S(1)} %copy-done.6, bf16[256,6912]{1,0:T(8,128)(2,1)S(1)} %collective-permute-done.30.refs_1_.refs_3_.sib, bf16[256,768]{1,0:T(8,128)(2,1)S(1)} %get-tuple-element.84.refs_2_.own, ...), custom_call_target="tpu_custom_call" | custom-call | flops 3200000000 | bytes 13000000 | tf_op jit(solution)/shard_map/up_grads/pallas_call | solution.py:499
  118.5 2.8 %collective-permute-start.32 = (bf16[16,3456]{1,0:T(8,128)(2,1)S(1)}, bf16[16,3456]{1,0:T(8,128)(2,1)S(1)}, u32[]{:S(2)}, u32[]{:S(2)}) collective-permute-start(bf16[16,3456]{1,0:T(8,128)(2,1)S(1)} %get-tuple-element.88), channel_id=1, source_target_pairs={{0,8},{1,9},{2,10},{3,11},{4,12},{5,13},{6,14},{7,15},{8,0},{9,1},... | collective-permute-start | bytes 331784 | tf_op jit(solution)/shard_map/ppermute | solution.py:38
  122.1 4.6 %down_grads.1 = (bf16[2,128,6144]{2,1,0:T(8,128)(2,1)}, f32[8,128]{1,0:T(8,128)S(1)}) custom-call(bf16[256,6144]{1,0:T(8,128)(2,1)S(1)} %get-tuple-element.94.refs_0_.grads_own, bf16[256,6144]{1,0:T(8,128)(2,1)S(1)} %collective-permute-done.37.grads_sib, bf16[256,768]{1,0:T(8,128)(2,1)S(1)} %get-tuple-element.84.refs_2_.own, ...), custom_call_target="tpu_custom_call" | custom-call | flops 1600000000 | bytes 10000000 | tf_op jit(solution)/shard_map/down_grads/pallas_call | solution.py:538
  127.5 1.8 %collective-permute-start.39 = (bf16[4,6528]{1,0:T(4,128)(2,1)S(1)}, bf16[4,6528]{1,0:T(4,128)(2,1)S(1)}, u32[]{:S(2)}, u32[]{:S(2)}) collective-permute-start(bf16[4,6528]{1,0:T(4,128)(2,1)S(1)} %get-tuple-element.98), channel_id=1, source_target_pairs={{0,2},{1,3},{2,0},{3,1},{4,6},{5,7},{6,4},{7,5},{8,10},{9,11},{10,... | collective-permute-start | bytes 156680 | tf_op jit(solution)/shard_map/ppermute | solution.py:38
  130.2 2.1 %collective-permute-done.38.refs_0_ = bf16[4,6528]{1,0:T(4,128)(2,1)S(1)} collective-permute-done((bf16[4,6528]{1,0:T(4,128)(2,1)S(1)}, bf16[4,6528]{1,0:T(4,128)(2,1)S(1)}, u32[]{:S(2)}, u32[]{:S(2)}) %collective-permute-start.38) | collective-permute-done | bytes 52256 | tf_op jit(solution)/shard_map/ppermute | solution.py:38
  133.5 4.6 %collective-permute-start.41 = (f32[8,128]{1,0:T(8,128)S(1)}, f32[8,128]{1,0:T(8,128)S(1)}, u32[]{:S(2)}, u32[]{:S(2)}) collective-permute-start(f32[8,128]{1,0:T(8,128)S(1)} %get-tuple-element.104.own), channel_id=1, source_target_pairs={{0,16},{1,17},{2,18},{3,19},{4,20},{5,21},{6,22},{7,23},{8,24},{9,... | collective-permute-start | bytes 12296 | tf_op jit(solution)/shard_map/ppermute | solution.py:49
  138.9 1.8 %router.1 = f32[2,256]{1,0:T(2,128)} custom-call(s32[7]{0:T(128)S(1)} %stack.20.where, f32[8,128]{1,0:T(8,128)S(1)} %get-tuple-element.104.own, f32[8,128]{1,0:T(8,128)S(1)} %collective-permute-done.41.other, s32[2,256]{1,0:T(2,128)S(1)} %copy-done.5), custom_call_target="tpu_custom_call" | custom-call | tf_op jit(solution)/shard_map/router/pallas_call | solution.py:699
  (85 shorter events, 19.1 us)
Async XLA Ops:
  0.6 14.9 %collective-permute-start.3 = (bf16[2,6144,128]{2,1,0:T(8,128)(2,1)}, bf16[2,6144,128]{2,1,0:T(8,128)(2,1)S(1)}, u32[]{:S(2)}, u32[]{:S(2)}) collective-permute-start(bf16[2,6144,128]{2,1,0:T(8,128)(2,1)} %refs_10_.1), channel_id=1, source_target_pairs={{0,16},{1,17},{2,18},{3,19},{4,20},{5,21},{6,22},{7,23},{8,24},{9,... | collective-permute-start | bytes 9437192 | tf_op jit(solution)/shard_map/ppermute | solution.py:49
  2.1 13.4 %collective-permute-start.4 = (bf16[2,6144,128]{2,1,0:T(8,128)(2,1)}, bf16[2,6144,128]{2,1,0:T(8,128)(2,1)}, u32[]{:S(2)}, u32[]{:S(2)}) collective-permute-start(bf16[2,6144,128]{2,1,0:T(8,128)(2,1)} %refs_11_.1), channel_id=1, source_target_pairs={{0,16},{1,17},{2,18},{3,19},{4,20},{5,21},{6,22},{7,23},{8,24},{9,... | collective-permute-start | bytes 9437192 | tf_op jit(solution)/shard_map/ppermute | solution.py:49
  3.8 8.0 %collective-permute-start.2 = (bf16[128,384]{1,0:T(8,128)(2,1)S(1)}, bf16[128,384]{1,0:T(8,128)(2,1)S(1)}, u32[]{:S(2)}, u32[]{:S(2)}) collective-permute-start(bf16[128,384]{1,0:T(8,128)(2,1)S(1)} %pack.1.refs_0_), channel_id=1, source_target_pairs={{0,3},{1,0},{2,1},{3,2},{4,7},{5,4},{6,5},{7,6},{8,11},{9,8},{10,9... | collective-permute-start | bytes 294920 | tf_op jit(solution)/shard_map/ppermute | solution.py:38
  7.8 7.7 %collective-permute-start = (bf16[128,384]{1,0:T(8,128)(2,1)S(1)}, bf16[128,384]{1,0:T(8,128)(2,1)S(1)}, u32[]{:S(2)}, u32[]{:S(2)}) collective-permute-start(bf16[128,384]{1,0:T(8,128)(2,1)S(1)} %pack.1.refs_0_), channel_id=1, source_target_pairs={{0,1},{1,2},{2,3},{3,0},{4,5},{5,6},{6,7},{7,4},{8,9},{9,10},{10,1... | collective-permute-start | bytes 294920 | tf_op jit(solution)/shard_map/ppermute | solution.py:38
  16.4 46.0 %collective-permute-start.21 = (bf16[2,128,6144]{2,1,0:T(8,128)(2,1)S(1)}, bf16[2,128,6144]{2,1,0:T(8,128)(2,1)S(1)}, u32[]{:S(2)}, u32[]{:S(2)}) collective-permute-start(bf16[2,128,6144]{2,1,0:T(8,128)(2,1)S(1)} %relay.2), channel_id=1, source_target_pairs={{0,16},{1,17},{2,18},{3,19},{4,20},{5,21},{6,22},{7,23},{8,24},{9,... | collective-permute-start | bytes 9437192 | tf_op jit(solution)/shard_map/ppermute | solution.py:49
  17.3 6.7 %collective-permute-start.8 = (bf16[64,1536]{1,0:T(8,128)(2,1)S(1)}, bf16[64,1536]{1,0:T(8,128)(2,1)S(1)}, u32[]{:S(2)}, u32[]{:S(2)}) collective-permute-start(bf16[64,1536]{1,0:T(8,128)(2,1)S(1)} %get-tuple-element.56.refs_5_), channel_id=1, source_target_pairs={{0,96},{1,97},{2,98},{3,99},{4,100},{5,101},{6,102},{7,103},{8,104... | collective-permute-start | bytes 589832 | tf_op jit(solution)/shard_map/ppermute | solution.py:38
  19.8 7.3 %collective-permute-start.7 = (bf16[64,1536]{1,0:T(8,128)(2,1)S(1)}, bf16[64,1536]{1,0:T(8,128)(2,1)S(1)}, u32[]{:S(2)}, u32[]{:S(2)}) collective-permute-start(bf16[64,1536]{1,0:T(8,128)(2,1)S(1)} %get-tuple-element.56.refs_5_), channel_id=1, source_target_pairs={{0,32},{1,33},{2,34},{3,35},{4,36},{5,37},{6,38},{7,39},{8,40},{9,... | collective-permute-start | bytes 589832 | tf_op jit(solution)/shard_map/ppermute | solution.py:38
  19.8 7.3 %collective-permute-start.6 = (bf16[16,6144]{1,0:T(8,128)(2,1)S(1)}, bf16[16,6144]{1,0:T(8,128)(2,1)S(1)}, u32[]{:S(2)}, u32[]{:S(2)}) collective-permute-start(bf16[16,6144]{1,0:T(8,128)(2,1)S(1)} %get-tuple-element.55.refs_0_.refs_1_), channel_id=1, source_target_pairs={{0,12},{1,13},{2,14},{3,15},{4,0},{5,1},{6,2},{7,3},{8,4},{9,5},{1... | collective-permute-start | bytes 589832 | tf_op jit(solution)/shard_map/ppermute | solution.py:38
  22.5 7.0 %collective-permute-start.5 = (bf16[16,6144]{1,0:T(8,128)(2,1)S(1)}, bf16[16,6144]{1,0:T(8,128)(2,1)S(1)}, u32[]{:S(2)}, u32[]{:S(2)}) collective-permute-start(bf16[16,6144]{1,0:T(8,128)(2,1)S(1)} %get-tuple-element.55.refs_0_.refs_1_), channel_id=1, source_target_pairs={{0,4},{1,5},{2,6},{3,7},{4,8},{5,9},{6,10},{7,11},{8,12},{9,13},{1... | collective-permute-start | bytes 589832 | tf_op jit(solution)/shard_map/ppermute | solution.py:38
  37.7 16.1 %collective-permute-start.14 = (bf16[64,6144]{1,0:T(8,128)(2,1)S(1)}, bf16[64,6144]{1,0:T(8,128)(2,1)S(1)}, u32[]{:S(2)}, u32[]{:S(2)}) collective-permute-start(bf16[64,6144]{1,0:T(8,128)(2,1)S(1)} %get-tuple-element.61.refs_0_), channel_id=1, source_target_pairs={{0,96},{1,97},{2,98},{3,99},{4,100},{5,101},{6,102},{7,103},{8,104... | collective-permute-start | bytes 2359304 | tf_op jit(solution)/shard_map/ppermute | solution.py:38
  40.4 16.5 %collective-permute-start.13 = (bf16[64,6144]{1,0:T(8,128)(2,1)S(1)}, bf16[64,6144]{1,0:T(8,128)(2,1)S(1)}, u32[]{:S(2)}, u32[]{:S(2)}) collective-permute-start(bf16[64,6144]{1,0:T(8,128)(2,1)S(1)} %get-tuple-element.61.refs_0_), channel_id=1, source_target_pairs={{0,32},{1,33},{2,34},{3,35},{4,36},{5,37},{6,38},{7,39},{8,40},{9,... | collective-permute-start | bytes 2359304 | tf_op jit(solution)/shard_map/ppermute | solution.py:38
  40.4 16.5 %collective-permute-start.16 = (bf16[256,1536]{1,0:T(8,128)(2,1)S(1)}, bf16[256,1536]{1,0:T(8,128)(2,1)S(1)}, u32[]{:S(2)}, u32[]{:S(2)}) collective-permute-start(bf16[256,1536]{1,0:T(8,128)(2,1)S(1)} %get-tuple-element.62.refs_3_.refs_5_), channel_id=1, source_target_pairs={{0,12},{1,13},{2,14},{3,15},{4,0},{5,1},{6,2},{7,3},{8,4},{9,5},{1... | collective-permute-start | bytes 2359304 | tf_op jit(solution)/shard_map/ppermute | solution.py:38
  40.4 16.5 %collective-permute-start.15 = (bf16[256,1536]{1,0:T(8,128)(2,1)S(1)}, bf16[256,1536]{1,0:T(8,128)(2,1)S(1)}, u32[]{:S(2)}, u32[]{:S(2)}) collective-permute-start(bf16[256,1536]{1,0:T(8,128)(2,1)S(1)} %get-tuple-element.62.refs_3_.refs_5_), channel_id=1, source_target_pairs={{0,4},{1,5},{2,6},{3,7},{4,8},{5,9},{6,10},{7,11},{8,12},{9,13},{1... | collective-permute-start | bytes 2359304 | tf_op jit(solution)/shard_map/ppermute | solution.py:38
  57.0 12.6 %collective-permute-start.17 = (bf16[32,6144]{1,0:T(8,128)(2,1)S(1)}, bf16[32,6144]{1,0:T(8,128)(2,1)S(1)}, u32[]{:S(2)}, u32[]{:S(2)}) collective-permute-start(bf16[32,6144]{1,0:T(8,128)(2,1)S(1)} %get-tuple-element.63), channel_id=1, source_target_pairs={{0,32},{1,33},{2,34},{3,35},{4,36},{5,37},{6,38},{7,39},{8,40},{9,... | collective-permute-start | bytes 1179656 | tf_op jit(solution)/shard_map/ppermute | solution.py:38
  57.1 12.5 %collective-permute-start.18 = (bf16[32,6144]{1,0:T(8,128)(2,1)S(1)}, bf16[32,6144]{1,0:T(8,128)(2,1)S(1)}, u32[]{:S(2)}, u32[]{:S(2)}) collective-permute-start(bf16[32,6144]{1,0:T(8,128)(2,1)S(1)} %get-tuple-element.64), channel_id=1, source_target_pairs={{0,96},{1,97},{2,98},{3,99},{4,100},{5,101},{6,102},{7,103},{8,104... | collective-permute-start | bytes 1179656 | tf_op jit(solution)/shard_map/ppermute | solution.py:38
  59.8 9.9 %collective-permute-start.19 = (bf16[128,1536]{1,0:T(8,128)(2,1)S(1)}, bf16[128,1536]{1,0:T(8,128)(2,1)S(1)}, u32[]{:S(2)}, u32[]{:S(2)}) collective-permute-start(bf16[128,1536]{1,0:T(8,128)(2,1)S(1)} %get-tuple-element.65), channel_id=1, source_target_pairs={{0,4},{1,5},{2,6},{3,7},{4,8},{5,9},{6,10},{7,11},{8,12},{9,13},{1... | collective-permute-start | bytes 1179656 | tf_op jit(solution)/shard_map/ppermute | solution.py:38
  59.8 9.9 %collective-permute-start.20 = (bf16[128,1536]{1,0:T(8,128)(2,1)S(1)}, bf16[128,1536]{1,0:T(8,128)(2,1)S(1)}, u32[]{:S(2)}, u32[]{:S(2)}) collective-permute-start(bf16[128,1536]{1,0:T(8,128)(2,1)S(1)} %get-tuple-element.66), channel_id=1, source_target_pairs={{0,12},{1,13},{2,14},{3,15},{4,0},{5,1},{6,2},{7,3},{8,4},{9,5},{1... | collective-permute-start | bytes 1179656 | tf_op jit(solution)/shard_map/ppermute | solution.py:38
  83.7 19.7 %collective-permute-start.30 = (bf16[256,6912]{1,0:T(8,128)(2,1)}, bf16[256,6912]{1,0:T(8,128)(2,1)S(1)}, u32[]{:S(2)}, u32[]{:S(2)}) collective-permute-start(bf16[256,6912]{1,0:T(8,128)(2,1)} %get-tuple-element.83.refs_0_), channel_id=1, source_target_pairs={{0,16},{1,17},{2,18},{3,19},{4,20},{5,21},{6,22},{7,23},{8,24},{9,... | collective-permute-start | bytes 10616840 | tf_op jit(solution)/shard_map/ppermute | solution.py:49
  89.7 8.5 %collective-permute-start.22 = (bf16[32,3456]{1,0:T(8,128)(2,1)S(1)}, bf16[32,3456]{1,0:T(8,128)(2,1)S(1)}, u32[]{:S(2)}, u32[]{:S(2)}) collective-permute-start(bf16[32,3456]{1,0:T(8,128)(2,1)S(1)} %get-tuple-element.74), channel_id=1, source_target_pairs={{0,96},{1,97},{2,98},{3,99},{4,100},{5,101},{6,102},{7,103},{8,104... | collective-permute-start | bytes 663560 | tf_op jit(solution)/shard_map/ppermute | solution.py:38
  91.1 7.9 %collective-permute-start.23 = (bf16[32,3456]{1,0:T(8,128)(2,1)S(1)}, bf16[32,3456]{1,0:T(8,128)(2,1)S(1)}, u32[]{:S(2)}, u32[]{:S(2)}) collective-permute-start(bf16[32,3456]{1,0:T(8,128)(2,1)S(1)} %get-tuple-element.75), channel_id=1, source_target_pairs={{0,32},{1,33},{2,34},{3,35},{4,36},{5,37},{6,38},{7,39},{8,40},{9,... | collective-permute-start | bytes 663560 | tf_op jit(solution)/shard_map/ppermute | solution.py:38
  91.2 7.0 %collective-permute-start.24 = (bf16[2,16,3072]{2,1,0:T(8,128)(2,1)S(1)}, bf16[2,16,3072]{2,1,0:T(8,128)(2,1)S(1)}, u32[]{:S(2)}, u32[]{:S(2)}) collective-permute-start(bf16[2,16,3072]{2,1,0:T(8,128)(2,1)S(1)} %get-tuple-element.76), channel_id=1, source_target_pairs={{0,4},{1,5},{2,6},{3,7},{4,8},{5,9},{6,10},{7,11},{8,12},{9,13},{1... | collective-permute-start | bytes 589832 | tf_op jit(solution)/shard_map/ppermute | solution.py:38
  91.2 7.0 %collective-permute-start.25 = (bf16[2,16,3072]{2,1,0:T(8,128)(2,1)S(1)}, bf16[2,16,3072]{2,1,0:T(8,128)(2,1)S(1)}, u32[]{:S(2)}, u32[]{:S(2)}) collective-permute-start(bf16[2,16,3072]{2,1,0:T(8,128)(2,1)S(1)} %get-tuple-element.77), channel_id=1, source_target_pairs={{0,12},{1,13},{2,14},{3,15},{4,0},{5,1},{6,2},{7,3},{8,4},{9,5},{1... | collective-permute-start | bytes 589832 | tf_op jit(solution)/shard_map/ppermute | solution.py:38
  99.2 19.4 %collective-permute-start.37 = (bf16[256,6144]{1,0:T(8,128)(2,1)S(1)}, bf16[256,6144]{1,0:T(8,128)(2,1)S(1)}, u32[]{:S(2)}, u32[]{:S(2)}) collective-permute-start(bf16[256,6144]{1,0:T(8,128)(2,1)S(1)} %relay.3), channel_id=1, source_target_pairs={{0,16},{1,17},{2,18},{3,19},{4,20},{5,21},{6,22},{7,23},{8,24},{9,... | collective-permute-start | bytes 9437192 | tf_op jit(solution)/shard_map/ppermute | solution.py:49
  100.7 14.1 %collective-permute-start.27 = (bf16[64,3456]{1,0:T(8,128)(2,1)S(1)}, bf16[64,3456]{1,0:T(8,128)(2,1)S(1)}, u32[]{:S(2)}, u32[]{:S(2)}) collective-permute-start(bf16[64,3456]{1,0:T(8,128)(2,1)S(1)} %get-tuple-element.79), channel_id=1, source_target_pairs={{0,32},{1,33},{2,34},{3,35},{4,36},{5,37},{6,38},{7,39},{8,40},{9,... | collective-permute-start | bytes 1327112 | tf_op jit(solution)/shard_map/ppermute | solution.py:38
  100.7 14.0 %collective-permute-start.26 = (bf16[64,3456]{1,0:T(8,128)(2,1)S(1)}, bf16[64,3456]{1,0:T(8,128)(2,1)S(1)}, u32[]{:S(2)}, u32[]{:S(2)}) collective-permute-start(bf16[64,3456]{1,0:T(8,128)(2,1)S(1)} %get-tuple-element.78.refs_4_), channel_id=1, source_target_pairs={{0,96},{1,97},{2,98},{3,99},{4,100},{5,101},{6,102},{7,103},{8,104... | collective-permute-start | bytes 1327112 | tf_op jit(solution)/shard_map/ppermute | solution.py:38
  103.4 11.3 %collective-permute-start.28 = (bf16[4,16,3072]{2,1,0:T(8,128)(2,1)S(1)}, bf16[4,16,3072]{2,1,0:T(8,128)(2,1)S(1)}, u32[]{:S(2)}, u32[]{:S(2)}) collective-permute-start(bf16[4,16,3072]{2,1,0:T(8,128)(2,1)S(1)} %get-tuple-element.81), channel_id=1, source_target_pairs={{0,4},{1,5},{2,6},{3,7},{4,8},{5,9},{6,10},{7,11},{8,12},{9,13},{1... | collective-permute-start | bytes 1179656 | tf_op jit(solution)/shard_map/ppermute | solution.py:38
  103.4 11.3 %collective-permute-start.29 = (bf16[4,16,3072]{2,1,0:T(8,128)(2,1)S(1)}, bf16[4,16,3072]{2,1,0:T(8,128)(2,1)S(1)}, u32[]{:S(2)}, u32[]{:S(2)}) collective-permute-start(bf16[4,16,3072]{2,1,0:T(8,128)(2,1)S(1)} %get-tuple-element.82), channel_id=1, source_target_pairs={{0,12},{1,13},{2,14},{3,15},{4,0},{5,1},{6,2},{7,3},{8,4},{9,5},{1... | collective-permute-start | bytes 1179656 | tf_op jit(solution)/shard_map/ppermute | solution.py:38
  115.8 5.6 %collective-permute-start.34 = (bf16[16,3072]{1,0:T(8,128)(2,1)S(1)}, bf16[16,3072]{1,0:T(8,128)(2,1)S(1)}, u32[]{:S(2)}, u32[]{:S(2)}) collective-permute-start(bf16[16,3072]{1,0:T(8,128)(2,1)S(1)} %get-tuple-element.91), channel_id=1, source_target_pairs={{0,96},{1,97},{2,98},{3,99},{4,100},{5,101},{6,102},{7,103},{8,104... | collective-permute-start | bytes 294920 | tf_op jit(solution)/shard_map/ppermute | solution.py:38
  117.2 9.5 %collective-permute-start.35 = (bf16[16,3072]{1,0:T(8,128)(2,1)S(1)}, bf16[16,3072]{1,0:T(8,128)(2,1)S(1)}, u32[]{:S(2)}, u32[]{:S(2)}) collective-permute-start(bf16[16,3072]{1,0:T(8,128)(2,1)S(1)} %get-tuple-element.92), channel_id=1, source_target_pairs={{0,64},{1,65},{2,66},{3,67},{4,68},{5,69},{6,70},{7,71},{8,72},{9,... | collective-permute-start | bytes 294920 | tf_op jit(solution)/shard_map/ppermute | solution.py:38
  117.2 9.5 %collective-permute-start.36 = (bf16[16,3072]{1,0:T(8,128)(2,1)S(1)}, bf16[16,3072]{1,0:T(8,128)(2,1)S(1)}, u32[]{:S(2)}, u32[]{:S(2)}) collective-permute-start(bf16[16,3072]{1,0:T(8,128)(2,1)S(1)} %get-tuple-element.93), channel_id=1, source_target_pairs={{0,32},{1,33},{2,34},{3,35},{4,36},{5,37},{6,38},{7,39},{8,40},{9,... | collective-permute-start | bytes 294920 | tf_op jit(solution)/shard_map/ppermute | solution.py:38
  117.9 8.8 %collective-permute-start.31 = (bf16[16,3456]{1,0:T(8,128)(2,1)S(1)}, bf16[16,3456]{1,0:T(8,128)(2,1)S(1)}, u32[]{:S(2)}, u32[]{:S(2)}) collective-permute-start(bf16[16,3456]{1,0:T(8,128)(2,1)S(1)} %get-tuple-element.87), channel_id=1, source_target_pairs={{0,4},{1,5},{2,6},{3,7},{4,8},{5,9},{6,10},{7,11},{8,12},{9,13},{1... | collective-permute-start | bytes 331784 | tf_op jit(solution)/shard_map/ppermute | solution.py:38
  118.5 8.1 %collective-permute-start.32 = (bf16[16,3456]{1,0:T(8,128)(2,1)S(1)}, bf16[16,3456]{1,0:T(8,128)(2,1)S(1)}, u32[]{:S(2)}, u32[]{:S(2)}) collective-permute-start(bf16[16,3456]{1,0:T(8,128)(2,1)S(1)} %get-tuple-element.88), channel_id=1, source_target_pairs={{0,8},{1,9},{2,10},{3,11},{4,12},{5,13},{6,14},{7,15},{8,0},{9,1},... | collective-permute-start | bytes 331784 | tf_op jit(solution)/shard_map/ppermute | solution.py:38
  (18 other events, 176.8 us)

commit v7 on v6

--- a/solution.py
+++ b/solution.py
@@ -492,13 +492,13 @@
 
 
 def run_up(rows_own, rows_sib, own, before):
-    tile = pl.BlockSpec((HALF, FT), lambda i: (0, i))
+    tile = pl.BlockSpec((HALF, 3 * FT), lambda i: (0, i))
     whole = pl.BlockSpec((HALF, 768), lambda i: (0, 0))
     tail = pl.BlockSpec((HALF, 768), lambda i: (0, D // 768))
-    out = pl.BlockSpec((2, FT, H), lambda i: (0, i, 0))
+    out = pl.BlockSpec((2, 3 * FT, H), lambda i: (0, i, 0))
     return pl.pallas_call(
         up_kernel,
-        grid=(D // FT,),
+        grid=(D // (3 * FT),),
         out_shape=[
             jax.ShapeDtypeStruct((2, D, H), BF),
             jax.ShapeDtypeStruct((2, D, H), BF),
@@ -532,19 +532,19 @@
 
 
 def run_down(grads_own, grads_sib, own, rows_sib):
-    tile = pl.BlockSpec((HALF, 2 * FT), lambda i: (0, i))
+    tile = pl.BlockSpec((HALF, 4 * FT), lambda i: (0, i))
     whole = pl.BlockSpec((HALF, 768), lambda i: (0, 0))
     tail = pl.BlockSpec((HALF, 768), lambda i: (0, D // 768))
     return pl.pallas_call(
         down_kernel,
-        grid=(D // FT // 2,),
+        grid=(D // (4 * FT),),
         out_shape=[
             jax.ShapeDtypeStruct((2, H, D), BF),
             jax.ShapeDtypeStruct((8, 128), F32),
         ],
         in_specs=[tile, tile, whole, tail],
         out_specs=[
-            pl.BlockSpec((2, H, 2 * FT), lambda i: (0, 0, i)),
+            pl.BlockSpec((2, H, 4 * FT), lambda i: (0, 0, i)),
             pl.BlockSpec((8, 128), lambda i: (0, 0)),
         ],
         scratch_shapes=[pltpu.VMEM((256, 512), BF)],

time: 141 us -> 140 us (level)
  Pallas kernels: 40.8 us -> 37.3 us
  waiting for transfers between devices: 38.9 us -> 41.5 us
    pallas_call x2, Pallas kernels: 13.2 us -> 9.76 us  [the longest x1 5.97 us: run_up(): pl.pallas_call(up_kernel, grid=(D // (3 * FT),), out_shape=[jax.ShapeDtyp...]
    ppermute x36, waiting for transfers between devices: 38.1 us -> 40.7 us  [shift(): return lax.ppermute(value, AXES, shift_pairs(axis, step))]
  transfers between devices with their start and end apart: 42 -> 42, of which waited for: 14 -> 15; matrix products, arithmetic and copies ran while one was open for 1% -> 1% of each run, Pallas kernels for 16% -> 14%
where the time goes in v7:
time: 140 us
  starting transfers between devices  57.8 us (41%)
  waiting for transfers between devices  41.5 us (30%)
  Pallas kernels  37.3 us (27%)
  local copies, waits for them, and re-layouts  2.36 us (2%)
    ppermute x36, starting transfers between devices, shift(): return lax.ppermute(value, AXES, shift_pairs(axis, step))  43.5 us
    ppermute x36, waiting for transfers between devices, shift(): return lax.ppermute(value, AXES, shift_pairs(axis, step))  40.7 us
    ppermute x6, starting transfers between devices, swap(): return lax.ppermute(value, AXES, pairs)  14.3 us
    pallas_call x1, Pallas kernels, run_main(): pl.pallas_call(main_kernel, out_shape=out_shape, in_specs=[SMEM_SPEC] + h...  14 us
    pallas_call x1, Pallas kernels, run_early(): pl.pallas_call(early_kernel, out_shape=[jax.ShapeDtypeStruct((192, 1024),...  7.16 us
    pallas_call x1, Pallas kernels, run_up(): pl.pallas_call(up_kernel, grid=(D // (3 * FT),), out_shape=[jax.ShapeDtyp...  5.97 us
    pallas_call x1, Pallas kernels, run_down(): pl.pallas_call(down_kernel, grid=(D // (4 * FT),), out_shape=[jax.ShapeDt...  3.79 us
  transfers between devices with their start and end apart: 42, of which 15 were waited for; matrix products, arithmetic and copies ran while one was open for 1% of the time, Pallas kernels for 14%

profile of v7, /device:TPU:1, one launch (start us, length us, event | category | flops | bytes accessed | tf_op | source)
XLA Modules:
  0.0 139.9 jit_solution(13819216054375923817)
XLA Ops:
  0.6 1.5 %collective-permute-start.3 = (bf16[2,6144,128]{2,1,0:T(8,128)(2,1)}, bf16[2,6144,128]{2,1,0:T(8,128)(2,1)S(1)}, u32[]{:S(2)}, u32[]{:S(2)}) collective-permute-start(bf16[2,6144,128]{2,1,0:T(8,128)(2,1)} %refs_10_.1), channel_id=1, source_target_pairs={{0,16},{1,17},{2,18},{3,19},{4,20},{5,21},{6,22},{7,23},{8,24},{9,... | collective-permute-start | bytes 9437192 | tf_op jit(solution)/shard_map/ppermute | solution.py:49
  3.8 3.9 %collective-permute-start.2 = (bf16[128,384]{1,0:T(8,128)(2,1)S(1)}, bf16[128,384]{1,0:T(8,128)(2,1)S(1)}, u32[]{:S(2)}, u32[]{:S(2)}) collective-permute-start(bf16[128,384]{1,0:T(8,128)(2,1)S(1)} %pack.1.refs_0_), channel_id=1, source_target_pairs={{0,3},{1,0},{2,1},{3,2},{4,7},{5,4},{6,5},{7,6},{8,11},{9,8},{10,9... | collective-permute-start | bytes 294920 | tf_op jit(solution)/shard_map/ppermute | solution.py:38
  9.2 2.6 %collective-permute-done.2.refs_3_ = bf16[128,384]{1,0:T(8,128)(2,1)S(1)} collective-permute-done((bf16[128,384]{1,0:T(8,128)(2,1)S(1)}, bf16[128,384]{1,0:T(8,128)(2,1)S(1)}, u32[]{:S(2)}, u32[]{:S(2)}) %collective-permute-start.2) | collective-permute-done | bytes 98336 | tf_op jit(solution)/shard_map/ppermute | solution.py:38
  12.8 2.6 %collective-permute-done.refs_1_ = bf16[128,384]{1,0:T(8,128)(2,1)S(1)} collective-permute-done((bf16[128,384]{1,0:T(8,128)(2,1)S(1)}, bf16[128,384]{1,0:T(8,128)(2,1)S(1)}, u32[]{:S(2)}, u32[]{:S(2)}) %collective-permute-start) | collective-permute-done | bytes 98336 | tf_op jit(solution)/shard_map/ppermute | solution.py:38
  17.3 2.5 %collective-permute-start.8 = (bf16[64,1536]{1,0:T(8,128)(2,1)S(1)}, bf16[64,1536]{1,0:T(8,128)(2,1)S(1)}, u32[]{:S(2)}, u32[]{:S(2)}) collective-permute-start(bf16[64,1536]{1,0:T(8,128)(2,1)S(1)} %get-tuple-element.56.refs_5_), channel_id=1, source_target_pairs={{0,96},{1,97},{2,98},{3,99},{4,100},{5,101},{6,102},{7,103},{8,104... | collective-permute-start | bytes 589832 | tf_op jit(solution)/shard_map/ppermute | solution.py:38
  19.8 2.7 %collective-permute-start.6 = (bf16[16,6144]{1,0:T(8,128)(2,1)S(1)}, bf16[16,6144]{1,0:T(8,128)(2,1)S(1)}, u32[]{:S(2)}, u32[]{:S(2)}) collective-permute-start(bf16[16,6144]{1,0:T(8,128)(2,1)S(1)} %get-tuple-element.55.refs_0_.refs_1_), channel_id=1, source_target_pairs={{0,12},{1,13},{2,14},{3,15},{4,0},{5,1},{6,2},{7,3},{8,4},{9,5},{1... | collective-permute-start | bytes 589832 | tf_op jit(solution)/shard_map/ppermute | solution.py:38
  22.5 1.5 %collective-permute-done.8.g_high.refs_7_ = bf16[64,1536]{1,0:T(8,128)(2,1)S(1)} collective-permute-done((bf16[64,1536]{1,0:T(8,128)(2,1)S(1)}, bf16[64,1536]{1,0:T(8,128)(2,1)S(1)}, u32[]{:S(2)}, u32[]{:S(2)}) %collective-permute-start.8) | collective-permute-done | bytes 196640 | tf_op jit(solution)/shard_map/ppermute | solution.py:38
  24.1 3.1 %collective-permute-done.7.g_low.refs_6_ = bf16[64,1536]{1,0:T(8,128)(2,1)S(1)} collective-permute-done((bf16[64,1536]{1,0:T(8,128)(2,1)S(1)}, bf16[64,1536]{1,0:T(8,128)(2,1)S(1)}, u32[]{:S(2)}, u32[]{:S(2)}) %collective-permute-start.7) | collective-permute-done | bytes 196640 | tf_op jit(solution)/shard_map/ppermute | solution.py:38
  27.1 2.4 %collective-permute-done.5.t_low.refs_1_ = bf16[16,6144]{1,0:T(8,128)(2,1)S(1)} collective-permute-done((bf16[16,6144]{1,0:T(8,128)(2,1)S(1)}, bf16[16,6144]{1,0:T(8,128)(2,1)S(1)}, u32[]{:S(2)}, u32[]{:S(2)}) %collective-permute-start.5) | collective-permute-done | bytes 196640 | tf_op jit(solution)/shard_map/ppermute | solution.py:38
  29.7 2.7 %collective-permute-start.10 = (bf16[16,3072]{1,0:T(8,128)(2,1)S(1)}, bf16[16,3072]{1,0:T(8,128)(2,1)S(1)}, u32[]{:S(2)}, u32[]{:S(2)}) collective-permute-start(bf16[16,3072]{1,0:T(8,128)(2,1)S(1)} %get-tuple-element.58), channel_id=1, source_target_pairs={{0,12},{1,13},{2,14},{3,15},{4,0},{5,1},{6,2},{7,3},{8,4},{9,5},{1... | collective-permute-start | bytes 294920 | tf_op jit(solution)/shard_map/ppermute | solution.py:38
  32.3 2.7 %collective-permute-start.12 = (bf16[32,1536]{1,0:T(8,128)(2,1)S(1)}, bf16[32,1536]{1,0:T(8,128)(2,1)S(1)}, u32[]{:S(2)}, u32[]{:S(2)}) collective-permute-start(bf16[32,1536]{1,0:T(8,128)(2,1)S(1)} %get-tuple-element.60), channel_id=1, source_target_pairs={{0,96},{1,97},{2,98},{3,99},{4,100},{5,101},{6,102},{7,103},{8,104... | collective-permute-start | bytes 294920 | tf_op jit(solution)/shard_map/ppermute | solution.py:38
  35.0 2.0 %collective-permute-done.11.refs_8_ = bf16[32,1536]{1,0:T(8,128)(2,1)S(1)} collective-permute-done((bf16[32,1536]{1,0:T(8,128)(2,1)S(1)}, bf16[32,1536]{1,0:T(8,128)(2,1)S(1)}, u32[]{:S(2)}, u32[]{:S(2)}) %collective-permute-start.11) | collective-permute-done | bytes 98336 | tf_op jit(solution)/shard_map/ppermute | solution.py:38
  37.7 2.7 %collective-permute-start.14 = (bf16[64,6144]{1,0:T(8,128)(2,1)S(1)}, bf16[64,6144]{1,0:T(8,128)(2,1)S(1)}, u32[]{:S(2)}, u32[]{:S(2)}) collective-permute-start(bf16[64,6144]{1,0:T(8,128)(2,1)S(1)} %get-tuple-element.61.refs_0_), channel_id=1, source_target_pairs={{0,96},{1,97},{2,98},{3,99},{4,100},{5,101},{6,102},{7,103},{8,104... | collective-permute-start | bytes 2359304 | tf_op jit(solution)/shard_map/ppermute | solution.py:38
  41.9 11.9 %collective-permute-done.14.t_high.refs_2_ = bf16[64,6144]{1,0:T(8,128)(2,1)S(1)} collective-permute-done((bf16[64,6144]{1,0:T(8,128)(2,1)S(1)}, bf16[64,6144]{1,0:T(8,128)(2,1)S(1)}, u32[]{:S(2)}, u32[]{:S(2)}) %collective-permute-start.14) | collective-permute-done | bytes 786464 | tf_op jit(solution)/shard_map/ppermute | solution.py:38
  53.8 3.1 %collective-permute-done.13.t_low.refs_1_ = bf16[64,6144]{1,0:T(8,128)(2,1)S(1)} collective-permute-done((bf16[64,6144]{1,0:T(8,128)(2,1)S(1)}, bf16[64,6144]{1,0:T(8,128)(2,1)S(1)}, u32[]{:S(2)}, u32[]{:S(2)}) %collective-permute-start.13) | collective-permute-done | bytes 786464 | tf_op jit(solution)/shard_map/ppermute | solution.py:38
  57.1 2.7 %collective-permute-start.18 = (bf16[32,6144]{1,0:T(8,128)(2,1)S(1)}, bf16[32,6144]{1,0:T(8,128)(2,1)S(1)}, u32[]{:S(2)}, u32[]{:S(2)}) collective-permute-start(bf16[32,6144]{1,0:T(8,128)(2,1)S(1)} %get-tuple-element.64), channel_id=1, source_target_pairs={{0,96},{1,97},{2,98},{3,99},{4,100},{5,101},{6,102},{7,103},{8,104... | collective-permute-start | bytes 1179656 | tf_op jit(solution)/shard_map/ppermute | solution.py:38
  59.8 2.7 %collective-permute-start.20 = (bf16[128,1536]{1,0:T(8,128)(2,1)S(1)}, bf16[128,1536]{1,0:T(8,128)(2,1)S(1)}, u32[]{:S(2)}, u32[]{:S(2)}) collective-permute-start(bf16[128,1536]{1,0:T(8,128)(2,1)S(1)} %get-tuple-element.66), channel_id=1, source_target_pairs={{0,12},{1,13},{2,14},{3,15},{4,0},{5,1},{6,2},{7,3},{8,4},{9,5},{1... | collective-permute-start | bytes 1179656 | tf_op jit(solution)/shard_map/ppermute | solution.py:38
  62.5 7.2 %early.1 = (f32[192,1024]{1,0:T(8,128)S(1)}, f32[256,512]{1,0:T(8,128)S(1)}) custom-call(s32[7]{0:T(128)S(1)} %stack.20.where, bf16[64,6144]{1,0:T(8,128)(2,1)S(1)} %get-tuple-element.61.refs_0_, bf16[64,6144]{1,0:T(8,128)(2,1)S(1)} %collective-permute-done.13.t_low.refs_1_, bf16[64,6144]{1,0:T(8,128)(2,1)S(1)} %collective-permute-done.14.t_high.refs_2_, ...), custom_call_target="tpu_custom_call" | custom-call | flops 3600000000 | bytes 20000000 | tf_op jit(solution)/shard_map/early/pallas_call | solution.py:302
  69.7 14.0 %main.1 = (bf16[64,3456]{1,0:T(8,128)(2,1)S(1)}, bf16[64,3456]{1,0:T(8,128)(2,1)S(1)}, bf16[64,3456]{1,0:T(8,128)(2,1)S(1)}, bf16[32,3456]{1,0:T(8,128)(2,1)S(1)...) custom-call(s32[7]{0:T(128)S(1)} %stack.20.where, ...), custom_call_target="tpu_custom_call" | custom-call | flops 8000000000 | bytes 30000000 | tf_op jit(solution)/shard_map/main/pallas_call | solution.py:458
  83.7 6.0 %collective-permute-start.30 = (bf16[256,6912]{1,0:T(8,128)(2,1)}, bf16[256,6912]{1,0:T(8,128)(2,1)S(1)}, u32[]{:S(2)}, u32[]{:S(2)}) collective-permute-start(bf16[256,6912]{1,0:T(8,128)(2,1)} %get-tuple-element.83.refs_0_), channel_id=1, source_target_pairs={{0,16},{1,17},{2,18},{3,19},{4,20},{5,21},{6,22},{7,23},{8,24},{9,... | collective-permute-start | bytes 10616840 | tf_op jit(solution)/shard_map/ppermute | solution.py:49
  91.2 2.7 %collective-permute-start.25 = (bf16[2,16,3072]{2,1,0:T(8,128)(2,1)S(1)}, bf16[2,16,3072]{2,1,0:T(8,128)(2,1)S(1)}, u32[]{:S(2)}, u32[]{:S(2)}) collective-permute-start(bf16[2,16,3072]{2,1,0:T(8,128)(2,1)S(1)} %get-tuple-element.77), channel_id=1, source_target_pairs={{0,12},{1,13},{2,14},{3,15},{4,0},{5,1},{6,2},{7,3},{8,4},{9,5},{1... | collective-permute-start | bytes 589832 | tf_op jit(solution)/shard_map/ppermute | solution.py:38
  93.9 4.4 %collective-permute-done.24.refs_6_.refs_3_ = bf16[2,16,3072]{2,1,0:T(8,128)(2,1)S(1)} collective-permute-done((bf16[2,16,3072]{2,1,0:T(8,128)(2,1)S(1)}, bf16[2,16,3072]{2,1,0:T(8,128)(2,1)S(1)}, u32[]{:S(2)}, u32[]{:S(2)}) %collective-permute-start.24) | collective-permute-done | bytes 196640 | tf_op jit(solution)/shard_map/ppermute | solution.py:38
  100.7 2.7 %collective-permute-start.26 = (bf16[64,3456]{1,0:T(8,128)(2,1)S(1)}, bf16[64,3456]{1,0:T(8,128)(2,1)S(1)}, u32[]{:S(2)}, u32[]{:S(2)}) collective-permute-start(bf16[64,3456]{1,0:T(8,128)(2,1)S(1)} %get-tuple-element.78.refs_4_), channel_id=1, source_target_pairs={{0,96},{1,97},{2,98},{3,99},{4,100},{5,101},{6,102},{7,103},{8,104... | collective-permute-start | bytes 1327112 | tf_op jit(solution)/shard_map/ppermute | solution.py:38
  103.4 2.7 %collective-permute-start.29 = (bf16[4,16,3072]{2,1,0:T(8,128)(2,1)S(1)}, bf16[4,16,3072]{2,1,0:T(8,128)(2,1)S(1)}, u32[]{:S(2)}, u32[]{:S(2)}) collective-permute-start(bf16[4,16,3072]{2,1,0:T(8,128)(2,1)S(1)} %get-tuple-element.82), channel_id=1, source_target_pairs={{0,12},{1,13},{2,14},{3,15},{4,0},{5,1},{6,2},{7,3},{8,4},{9,5},{1... | collective-permute-start | bytes 1179656 | tf_op jit(solution)/shard_map/ppermute | solution.py:38
  106.1 6.0 %up_grads.1 = (bf16[2,6144,128]{2,1,0:T(8,128)(2,1)}, bf16[2,6144,128]{2,1,0:T(8,128)(2,1)}, f32[8,128]{1,0:T(8,128)S(1)}) custom-call(bf16[256,6912]{1,0:T(8,128)(2,1)S(1)} %copy-done.6, bf16[256,6912]{1,0:T(8,128)(2,1)S(1)} %collective-permute-done.30.refs_1_.refs_3_.sib, bf16[256,768]{1,0:T(8,128)(2,1)S(1)} %get-tuple-element.84.refs_2_.own, ...), custom_call_target="tpu_custom_call" | custom-call | flops 3200000000 | bytes 13000000 | tf_op jit(solution)/shard_map/up_grads/pallas_call | solution.py:499
  112.1 2.6 %collective-permute-done.28.refs_4_ = bf16[4,16,3072]{2,1,0:T(8,128)(2,1)S(1)} collective-permute-done((bf16[4,16,3072]{2,1,0:T(8,128)(2,1)S(1)}, bf16[4,16,3072]{2,1,0:T(8,128)(2,1)S(1)}, u32[]{:S(2)}, u32[]{:S(2)}) %collective-permute-start.28) | collective-permute-done | bytes 393248 | tf_op jit(solution)/shard_map/ppermute | solution.py:38
  118.5 2.8 %collective-permute-start.32 = (bf16[16,3456]{1,0:T(8,128)(2,1)S(1)}, bf16[16,3456]{1,0:T(8,128)(2,1)S(1)}, u32[]{:S(2)}, u32[]{:S(2)}) collective-permute-start(bf16[16,3456]{1,0:T(8,128)(2,1)S(1)} %get-tuple-element.88), channel_id=1, source_target_pairs={{0,8},{1,9},{2,10},{3,11},{4,12},{5,13},{6,14},{7,15},{8,0},{9,1},... | collective-permute-start | bytes 331784 | tf_op jit(solution)/shard_map/ppermute | solution.py:38
  122.1 3.8 %down_grads.1 = (bf16[2,128,6144]{2,1,0:T(8,128)(2,1)}, f32[8,128]{1,0:T(8,128)S(1)}) custom-call(bf16[256,6144]{1,0:T(8,128)(2,1)S(1)} %get-tuple-element.94.refs_0_.grads_own, bf16[256,6144]{1,0:T(8,128)(2,1)S(1)} %collective-permute-done.37.grads_sib, bf16[256,768]{1,0:T(8,128)(2,1)S(1)} %get-tuple-element.84.refs_2_.own, ...), custom_call_target="tpu_custom_call" | custom-call | flops 1600000000 | bytes 10000000 | tf_op jit(solution)/shard_map/down_grads/pallas_call | solution.py:538
  126.7 1.8 %collective-permute-start.39 = (bf16[4,6528]{1,0:T(4,128)(2,1)S(1)}, bf16[4,6528]{1,0:T(4,128)(2,1)S(1)}, u32[]{:S(2)}, u32[]{:S(2)}) collective-permute-start(bf16[4,6528]{1,0:T(4,128)(2,1)S(1)} %get-tuple-element.98), channel_id=1, source_target_pairs={{0,2},{1,3},{2,0},{3,1},{4,6},{5,7},{6,4},{7,5},{8,10},{9,11},{10,... | collective-permute-start | bytes 156680 | tf_op jit(solution)/shard_map/ppermute | solution.py:38
  129.4 2.1 %collective-permute-done.38.refs_0_ = bf16[4,6528]{1,0:T(4,128)(2,1)S(1)} collective-permute-done((bf16[4,6528]{1,0:T(4,128)(2,1)S(1)}, bf16[4,6528]{1,0:T(4,128)(2,1)S(1)}, u32[]{:S(2)}, u32[]{:S(2)}) %collective-permute-start.38) | collective-permute-done | bytes 52256 | tf_op jit(solution)/shard_map/ppermute | solution.py:38
  132.7 4.6 %collective-permute-start.41 = (f32[8,128]{1,0:T(8,128)S(1)}, f32[8,128]{1,0:T(8,128)S(1)}, u32[]{:S(2)}, u32[]{:S(2)}) collective-permute-start(f32[8,128]{1,0:T(8,128)S(1)} %get-tuple-element.104.own), channel_id=1, source_target_pairs={{0,16},{1,17},{2,18},{3,19},{4,20},{5,21},{6,22},{7,23},{8,24},{9,... | collective-permute-start | bytes 12296 | tf_op jit(solution)/shard_map/ppermute | solution.py:49
  138.1 1.8 %router.1 = f32[2,256]{1,0:T(2,128)} custom-call(s32[7]{0:T(128)S(1)} %stack.20.where, f32[8,128]{1,0:T(8,128)S(1)} %get-tuple-element.104.own, f32[8,128]{1,0:T(8,128)S(1)} %collective-permute-done.41.other, s32[2,256]{1,0:T(2,128)S(1)} %copy-done.5), custom_call_target="tpu_custom_call" | custom-call | tf_op jit(solution)/shard_map/router/pallas_call | solution.py:699
  (85 shorter events, 20.6 us)
Async XLA Ops:
  0.6 14.9 %collective-permute-start.3 = (bf16[2,6144,128]{2,1,0:T(8,128)(2,1)}, bf16[2,6144,128]{2,1,0:T(8,128)(2,1)S(1)}, u32[]{:S(2)}, u32[]{:S(2)}) collective-permute-start(bf16[2,6144,128]{2,1,0:T(8,128)(2,1)} %refs_10_.1), channel_id=1, source_target_pairs={{0,16},{1,17},{2,18},{3,19},{4,20},{5,21},{6,22},{7,23},{8,24},{9,... | collective-permute-start | bytes 9437192 | tf_op jit(solution)/shard_map/ppermute | solution.py:49
  2.1 13.4 %collective-permute-start.4 = (bf16[2,6144,128]{2,1,0:T(8,128)(2,1)}, bf16[2,6144,128]{2,1,0:T(8,128)(2,1)}, u32[]{:S(2)}, u32[]{:S(2)}) collective-permute-start(bf16[2,6144,128]{2,1,0:T(8,128)(2,1)} %refs_11_.1), channel_id=1, source_target_pairs={{0,16},{1,17},{2,18},{3,19},{4,20},{5,21},{6,22},{7,23},{8,24},{9,... | collective-permute-start | bytes 9437192 | tf_op jit(solution)/shard_map/ppermute | solution.py:49
  3.8 8.0 %collective-permute-start.2 = (bf16[128,384]{1,0:T(8,128)(2,1)S(1)}, bf16[128,384]{1,0:T(8,128)(2,1)S(1)}, u32[]{:S(2)}, u32[]{:S(2)}) collective-permute-start(bf16[128,384]{1,0:T(8,128)(2,1)S(1)} %pack.1.refs_0_), channel_id=1, source_target_pairs={{0,3},{1,0},{2,1},{3,2},{4,7},{5,4},{6,5},{7,6},{8,11},{9,8},{10,9... | collective-permute-start | bytes 294920 | tf_op jit(solution)/shard_map/ppermute | solution.py:38
  7.8 7.7 %collective-permute-start = (bf16[128,384]{1,0:T(8,128)(2,1)S(1)}, bf16[128,384]{1,0:T(8,128)(2,1)S(1)}, u32[]{:S(2)}, u32[]{:S(2)}) collective-permute-start(bf16[128,384]{1,0:T(8,128)(2,1)S(1)} %pack.1.refs_0_), channel_id=1, source_target_pairs={{0,1},{1,2},{2,3},{3,0},{4,5},{5,6},{6,7},{7,4},{8,9},{9,10},{10,1... | collective-permute-start | bytes 294920 | tf_op jit(solution)/shard_map/ppermute | solution.py:38
  16.4 46.0 %collective-permute-start.21 = (bf16[2,128,6144]{2,1,0:T(8,128)(2,1)S(1)}, bf16[2,128,6144]{2,1,0:T(8,128)(2,1)S(1)}, u32[]{:S(2)}, u32[]{:S(2)}) collective-permute-start(bf16[2,128,6144]{2,1,0:T(8,128)(2,1)S(1)} %relay.2), channel_id=1, source_target_pairs={{0,16},{1,17},{2,18},{3,19},{4,20},{5,21},{6,22},{7,23},{8,24},{9,... | collective-permute-start | bytes 9437192 | tf_op jit(solution)/shard_map/ppermute | solution.py:49
  17.3 6.7 %collective-permute-start.8 = (bf16[64,1536]{1,0:T(8,128)(2,1)S(1)}, bf16[64,1536]{1,0:T(8,128)(2,1)S(1)}, u32[]{:S(2)}, u32[]{:S(2)}) collective-permute-start(bf16[64,1536]{1,0:T(8,128)(2,1)S(1)} %get-tuple-element.56.refs_5_), channel_id=1, source_target_pairs={{0,96},{1,97},{2,98},{3,99},{4,100},{5,101},{6,102},{7,103},{8,104... | collective-permute-start | bytes 589832 | tf_op jit(solution)/shard_map/ppermute | solution.py:38
  19.8 7.3 %collective-permute-start.7 = (bf16[64,1536]{1,0:T(8,128)(2,1)S(1)}, bf16[64,1536]{1,0:T(8,128)(2,1)S(1)}, u32[]{:S(2)}, u32[]{:S(2)}) collective-permute-start(bf16[64,1536]{1,0:T(8,128)(2,1)S(1)} %get-tuple-element.56.refs_5_), channel_id=1, source_target_pairs={{0,32},{1,33},{2,34},{3,35},{4,36},{5,37},{6,38},{7,39},{8,40},{9,... | collective-permute-start | bytes 589832 | tf_op jit(solution)/shard_map/ppermute | solution.py:38
  19.8 7.3 %collective-permute-start.6 = (bf16[16,6144]{1,0:T(8,128)(2,1)S(1)}, bf16[16,6144]{1,0:T(8,128)(2,1)S(1)}, u32[]{:S(2)}, u32[]{:S(2)}) collective-permute-start(bf16[16,6144]{1,0:T(8,128)(2,1)S(1)} %get-tuple-element.55.refs_0_.refs_1_), channel_id=1, source_target_pairs={{0,12},{1,13},{2,14},{3,15},{4,0},{5,1},{6,2},{7,3},{8,4},{9,5},{1... | collective-permute-start | bytes 589832 | tf_op jit(solution)/shard_map/ppermute | solution.py:38
  22.5 7.0 %collective-permute-start.5 = (bf16[16,6144]{1,0:T(8,128)(2,1)S(1)}, bf16[16,6144]{1,0:T(8,128)(2,1)S(1)}, u32[]{:S(2)}, u32[]{:S(2)}) collective-permute-start(bf16[16,6144]{1,0:T(8,128)(2,1)S(1)} %get-tuple-element.55.refs_0_.refs_1_), channel_id=1, source_target_pairs={{0,4},{1,5},{2,6},{3,7},{4,8},{5,9},{6,10},{7,11},{8,12},{9,13},{1... | collective-permute-start | bytes 589832 | tf_op jit(solution)/shard_map/ppermute | solution.py:38
  37.7 16.1 %collective-permute-start.14 = (bf16[64,6144]{1,0:T(8,128)(2,1)S(1)}, bf16[64,6144]{1,0:T(8,128)(2,1)S(1)}, u32[]{:S(2)}, u32[]{:S(2)}) collective-permute-start(bf16[64,6144]{1,0:T(8,128)(2,1)S(1)} %get-tuple-element.61.refs_0_), channel_id=1, source_target_pairs={{0,96},{1,97},{2,98},{3,99},{4,100},{5,101},{6,102},{7,103},{8,104... | collective-permute-start | bytes 2359304 | tf_op jit(solution)/shard_map/ppermute | solution.py:38
  40.4 16.5 %collective-permute-start.13 = (bf16[64,6144]{1,0:T(8,128)(2,1)S(1)}, bf16[64,6144]{1,0:T(8,128)(2,1)S(1)}, u32[]{:S(2)}, u32[]{:S(2)}) collective-permute-start(bf16[64,6144]{1,0:T(8,128)(2,1)S(1)} %get-tuple-element.61.refs_0_), channel_id=1, source_target_pairs={{0,32},{1,33},{2,34},{3,35},{4,36},{5,37},{6,38},{7,39},{8,40},{9,... | collective-permute-start | bytes 2359304 | tf_op jit(solution)/shard_map/ppermute | solution.py:38
  40.4 16.5 %collective-permute-start.16 = (bf16[256,1536]{1,0:T(8,128)(2,1)S(1)}, bf16[256,1536]{1,0:T(8,128)(2,1)S(1)}, u32[]{:S(2)}, u32[]{:S(2)}) collective-permute-start(bf16[256,1536]{1,0:T(8,128)(2,1)S(1)} %get-tuple-element.62.refs_3_.refs_5_), channel_id=1, source_target_pairs={{0,12},{1,13},{2,14},{3,15},{4,0},{5,1},{6,2},{7,3},{8,4},{9,5},{1... | collective-permute-start | bytes 2359304 | tf_op jit(solution)/shard_map/ppermute | solution.py:38
  40.4 16.5 %collective-permute-start.15 = (bf16[256,1536]{1,0:T(8,128)(2,1)S(1)}, bf16[256,1536]{1,0:T(8,128)(2,1)S(1)}, u32[]{:S(2)}, u32[]{:S(2)}) collective-permute-start(bf16[256,1536]{1,0:T(8,128)(2,1)S(1)} %get-tuple-element.62.refs_3_.refs_5_), channel_id=1, source_target_pairs={{0,4},{1,5},{2,6},{3,7},{4,8},{5,9},{6,10},{7,11},{8,12},{9,13},{1... | collective-permute-start | bytes 2359304 | tf_op jit(solution)/shard_map/ppermute | solution.py:38
  57.0 12.6 %collective-permute-start.17 = (bf16[32,6144]{1,0:T(8,128)(2,1)S(1)}, bf16[32,6144]{1,0:T(8,128)(2,1)S(1)}, u32[]{:S(2)}, u32[]{:S(2)}) collective-permute-start(bf16[32,6144]{1,0:T(8,128)(2,1)S(1)} %get-tuple-element.63), channel_id=1, source_target_pairs={{0,32},{1,33},{2,34},{3,35},{4,36},{5,37},{6,38},{7,39},{8,40},{9,... | collective-permute-start | bytes 1179656 | tf_op jit(solution)/shard_map/ppermute | solution.py:38
  57.1 12.5 %collective-permute-start.18 = (bf16[32,6144]{1,0:T(8,128)(2,1)S(1)}, bf16[32,6144]{1,0:T(8,128)(2,1)S(1)}, u32[]{:S(2)}, u32[]{:S(2)}) collective-permute-start(bf16[32,6144]{1,0:T(8,128)(2,1)S(1)} %get-tuple-element.64), channel_id=1, source_target_pairs={{0,96},{1,97},{2,98},{3,99},{4,100},{5,101},{6,102},{7,103},{8,104... | collective-permute-start | bytes 1179656 | tf_op jit(solution)/shard_map/ppermute | solution.py:38
  59.8 9.9 %collective-permute-start.19 = (bf16[128,1536]{1,0:T(8,128)(2,1)S(1)}, bf16[128,1536]{1,0:T(8,128)(2,1)S(1)}, u32[]{:S(2)}, u32[]{:S(2)}) collective-permute-start(bf16[128,1536]{1,0:T(8,128)(2,1)S(1)} %get-tuple-element.65), channel_id=1, source_target_pairs={{0,4},{1,5},{2,6},{3,7},{4,8},{5,9},{6,10},{7,11},{8,12},{9,13},{1... | collective-permute-start | bytes 1179656 | tf_op jit(solution)/shard_map/ppermute | solution.py:38
  59.8 9.9 %collective-permute-start.20 = (bf16[128,1536]{1,0:T(8,128)(2,1)S(1)}, bf16[128,1536]{1,0:T(8,128)(2,1)S(1)}, u32[]{:S(2)}, u32[]{:S(2)}) collective-permute-start(bf16[128,1536]{1,0:T(8,128)(2,1)S(1)} %get-tuple-element.66), channel_id=1, source_target_pairs={{0,12},{1,13},{2,14},{3,15},{4,0},{5,1},{6,2},{7,3},{8,4},{9,5},{1... | collective-permute-start | bytes 1179656 | tf_op jit(solution)/shard_map/ppermute | solution.py:38
  83.7 19.7 %collective-permute-start.30 = (bf16[256,6912]{1,0:T(8,128)(2,1)}, bf16[256,6912]{1,0:T(8,128)(2,1)S(1)}, u32[]{:S(2)}, u32[]{:S(2)}) collective-permute-start(bf16[256,6912]{1,0:T(8,128)(2,1)} %get-tuple-element.83.refs_0_), channel_id=1, source_target_pairs={{0,16},{1,17},{2,18},{3,19},{4,20},{5,21},{6,22},{7,23},{8,24},{9,... | collective-permute-start | bytes 10616840 | tf_op jit(solution)/shard_map/ppermute | solution.py:49
  89.7 8.5 %collective-permute-start.22 = (bf16[32,3456]{1,0:T(8,128)(2,1)S(1)}, bf16[32,3456]{1,0:T(8,128)(2,1)S(1)}, u32[]{:S(2)}, u32[]{:S(2)}) collective-permute-start(bf16[32,3456]{1,0:T(8,128)(2,1)S(1)} %get-tuple-element.74), channel_id=1, source_target_pairs={{0,96},{1,97},{2,98},{3,99},{4,100},{5,101},{6,102},{7,103},{8,104... | collective-permute-start | bytes 663560 | tf_op jit(solution)/shard_map/ppermute | solution.py:38
  91.1 7.9 %collective-permute-start.23 = (bf16[32,3456]{1,0:T(8,128)(2,1)S(1)}, bf16[32,3456]{1,0:T(8,128)(2,1)S(1)}, u32[]{:S(2)}, u32[]{:S(2)}) collective-permute-start(bf16[32,3456]{1,0:T(8,128)(2,1)S(1)} %get-tuple-element.75), channel_id=1, source_target_pairs={{0,32},{1,33},{2,34},{3,35},{4,36},{5,37},{6,38},{7,39},{8,40},{9,... | collective-permute-start | bytes 663560 | tf_op jit(solution)/shard_map/ppermute | solution.py:38
  91.2 7.0 %collective-permute-start.24 = (bf16[2,16,3072]{2,1,0:T(8,128)(2,1)S(1)}, bf16[2,16,3072]{2,1,0:T(8,128)(2,1)S(1)}, u32[]{:S(2)}, u32[]{:S(2)}) collective-permute-start(bf16[2,16,3072]{2,1,0:T(8,128)(2,1)S(1)} %get-tuple-element.76), channel_id=1, source_target_pairs={{0,4},{1,5},{2,6},{3,7},{4,8},{5,9},{6,10},{7,11},{8,12},{9,13},{1... | collective-permute-start | bytes 589832 | tf_op jit(solution)/shard_map/ppermute | solution.py:38
  91.2 7.0 %collective-permute-start.25 = (bf16[2,16,3072]{2,1,0:T(8,128)(2,1)S(1)}, bf16[2,16,3072]{2,1,0:T(8,128)(2,1)S(1)}, u32[]{:S(2)}, u32[]{:S(2)}) collective-permute-start(bf16[2,16,3072]{2,1,0:T(8,128)(2,1)S(1)} %get-tuple-element.77), channel_id=1, source_target_pairs={{0,12},{1,13},{2,14},{3,15},{4,0},{5,1},{6,2},{7,3},{8,4},{9,5},{1... | collective-permute-start | bytes 589832 | tf_op jit(solution)/shard_map/ppermute | solution.py:38
  99.2 19.4 %collective-permute-start.37 = (bf16[256,6144]{1,0:T(8,128)(2,1)S(1)}, bf16[256,6144]{1,0:T(8,128)(2,1)S(1)}, u32[]{:S(2)}, u32[]{:S(2)}) collective-permute-start(bf16[256,6144]{1,0:T(8,128)(2,1)S(1)} %relay.3), channel_id=1, source_target_pairs={{0,16},{1,17},{2,18},{3,19},{4,20},{5,21},{6,22},{7,23},{8,24},{9,... | collective-permute-start | bytes 9437192 | tf_op jit(solution)/shard_map/ppermute | solution.py:49
  100.7 14.1 %collective-permute-start.27 = (bf16[64,3456]{1,0:T(8,128)(2,1)S(1)}, bf16[64,3456]{1,0:T(8,128)(2,1)S(1)}, u32[]{:S(2)}, u32[]{:S(2)}) collective-permute-start(bf16[64,3456]{1,0:T(8,128)(2,1)S(1)} %get-tuple-element.79), channel_id=1, source_target_pairs={{0,32},{1,33},{2,34},{3,35},{4,36},{5,37},{6,38},{7,39},{8,40},{9,... | collective-permute-start | bytes 1327112 | tf_op jit(solution)/shard_map/ppermute | solution.py:38
  100.7 14.0 %collective-permute-start.26 = (bf16[64,3456]{1,0:T(8,128)(2,1)S(1)}, bf16[64,3456]{1,0:T(8,128)(2,1)S(1)}, u32[]{:S(2)}, u32[]{:S(2)}) collective-permute-start(bf16[64,3456]{1,0:T(8,128)(2,1)S(1)} %get-tuple-element.78.refs_4_), channel_id=1, source_target_pairs={{0,96},{1,97},{2,98},{3,99},{4,100},{5,101},{6,102},{7,103},{8,104... | collective-permute-start | bytes 1327112 | tf_op jit(solution)/shard_map/ppermute | solution.py:38
  103.4 11.3 %collective-permute-start.28 = (bf16[4,16,3072]{2,1,0:T(8,128)(2,1)S(1)}, bf16[4,16,3072]{2,1,0:T(8,128)(2,1)S(1)}, u32[]{:S(2)}, u32[]{:S(2)}) collective-permute-start(bf16[4,16,3072]{2,1,0:T(8,128)(2,1)S(1)} %get-tuple-element.81), channel_id=1, source_target_pairs={{0,4},{1,5},{2,6},{3,7},{4,8},{5,9},{6,10},{7,11},{8,12},{9,13},{1... | collective-permute-start | bytes 1179656 | tf_op jit(solution)/shard_map/ppermute | solution.py:38
  103.4 11.3 %collective-permute-start.29 = (bf16[4,16,3072]{2,1,0:T(8,128)(2,1)S(1)}, bf16[4,16,3072]{2,1,0:T(8,128)(2,1)S(1)}, u32[]{:S(2)}, u32[]{:S(2)}) collective-permute-start(bf16[4,16,3072]{2,1,0:T(8,128)(2,1)S(1)} %get-tuple-element.82), channel_id=1, source_target_pairs={{0,12},{1,13},{2,14},{3,15},{4,0},{5,1},{6,2},{7,3},{8,4},{9,5},{1... | collective-permute-start | bytes 1179656 | tf_op jit(solution)/shard_map/ppermute | solution.py:38
  115.8 5.6 %collective-permute-start.34 = (bf16[16,3072]{1,0:T(8,128)(2,1)S(1)}, bf16[16,3072]{1,0:T(8,128)(2,1)S(1)}, u32[]{:S(2)}, u32[]{:S(2)}) collective-permute-start(bf16[16,3072]{1,0:T(8,128)(2,1)S(1)} %get-tuple-element.91), channel_id=1, source_target_pairs={{0,96},{1,97},{2,98},{3,99},{4,100},{5,101},{6,102},{7,103},{8,104... | collective-permute-start | bytes 294920 | tf_op jit(solution)/shard_map/ppermute | solution.py:38
  117.2 8.7 %collective-permute-start.35 = (bf16[16,3072]{1,0:T(8,128)(2,1)S(1)}, bf16[16,3072]{1,0:T(8,128)(2,1)S(1)}, u32[]{:S(2)}, u32[]{:S(2)}) collective-permute-start(bf16[16,3072]{1,0:T(8,128)(2,1)S(1)} %get-tuple-element.92), channel_id=1, source_target_pairs={{0,64},{1,65},{2,66},{3,67},{4,68},{5,69},{6,70},{7,71},{8,72},{9,... | collective-permute-start | bytes 294920 | tf_op jit(solution)/shard_map/ppermute | solution.py:38
  117.2 8.7 %collective-permute-start.36 = (bf16[16,3072]{1,0:T(8,128)(2,1)S(1)}, bf16[16,3072]{1,0:T(8,128)(2,1)S(1)}, u32[]{:S(2)}, u32[]{:S(2)}) collective-permute-start(bf16[16,3072]{1,0:T(8,128)(2,1)S(1)} %get-tuple-element.93), channel_id=1, source_target_pairs={{0,32},{1,33},{2,34},{3,35},{4,36},{5,37},{6,38},{7,39},{8,40},{9,... | collective-permute-start | bytes 294920 | tf_op jit(solution)/shard_map/ppermute | solution.py:38
  117.9 8.0 %collective-permute-start.31 = (bf16[16,3456]{1,0:T(8,128)(2,1)S(1)}, bf16[16,3456]{1,0:T(8,128)(2,1)S(1)}, u32[]{:S(2)}, u32[]{:S(2)}) collective-permute-start(bf16[16,3456]{1,0:T(8,128)(2,1)S(1)} %get-tuple-element.87), channel_id=1, source_target_pairs={{0,4},{1,5},{2,6},{3,7},{4,8},{5,9},{6,10},{7,11},{8,12},{9,13},{1... | collective-permute-start | bytes 331784 | tf_op jit(solution)/shard_map/ppermute | solution.py:38
  118.5 7.3 %collective-permute-start.32 = (bf16[16,3456]{1,0:T(8,128)(2,1)S(1)}, bf16[16,3456]{1,0:T(8,128)(2,1)S(1)}, u32[]{:S(2)}, u32[]{:S(2)}) collective-permute-start(bf16[16,3456]{1,0:T(8,128)(2,1)S(1)} %get-tuple-element.88), channel_id=1, source_target_pairs={{0,8},{1,9},{2,10},{3,11},{4,12},{5,13},{6,14},{7,15},{8,0},{9,1},... | collective-permute-start | bytes 331784 | tf_op jit(solution)/shard_map/ppermute | solution.py:38
  (18 other events, 176.0 us)

commit v8 on v7

--- a/solution.py
+++ b/solution.py
@@ -590,7 +590,7 @@
 
 
 def first_sum_kernel(where, *refs):
-    ra, rb, qa, qb, buf = refs[0:3], refs[3:6], refs[7:11], refs[11:15], refs[15]
+    ra, rb, qa, qb, buf = refs[0:3], refs[3:6], refs[8:12], refs[12:16], refs[16]
     half = D // 2
     buf[...] = total(ra[0][:, 0:half], [r[:, 0:half] for r in ra[1:]]).astype(BF)
     sums = join_three(ra[0][0:16, half:])
@@ -605,21 +605,21 @@
         qb[k][...] = total(rb[0][k], [r[k] for r in rb[1:]]).astype(BF)
 
 
-def run_first_sum(where, ra, rb, token):
+def run_first_sum(where, ra, rb, token, other):
     return pl.pallas_call(
         first_sum_kernel,
         out_shape=[jax.ShapeDtypeStruct((16, WIDE), BF)] * 4
         + [jax.ShapeDtypeStruct((16, D // 2), BF)] * 4,
-        in_specs=[SMEM_SPEC] + vmem_specs(7),
+        in_specs=[SMEM_SPEC] + vmem_specs(8),
         out_specs=vmem_specs(8),
         scratch_shapes=[pltpu.VMEM((64, D // 2), BF)],
         compiler_params=pltpu.CompilerParams(vmem_limit_bytes=8 * MIB),
         name="first_sum",
-    )(where, *ra, *rb, token)
+    )(where, *ra, *rb, token, other)
 
 
 def second_sum_kernel(where, *refs):
-    ra, rb, own, out, buf = refs[0:4], refs[4:8], refs[9], refs[10:13], refs[13]
+    ra, rb, own, out, buf = refs[0:4], refs[4:8], refs[8], refs[9:12], refs[12]
     half = D // 2
     for n, r in enumerate((ra, rb)):
         part = total(r[0][:, 0:half], [p[:, 0:half] for p in r[1:]])
@@ -639,17 +639,17 @@
             out[k - 1][:, D:] = parts
 
 
-def run_second_sum(where, ra, rb, token):
+def run_second_sum(where, ra, rb):
     return pl.pallas_call(
         second_sum_kernel,
         out_shape=[jax.ShapeDtypeStruct((4, D + 128), F32)]
         + [jax.ShapeDtypeStruct((4, D + 384), BF)] * 3,
-        in_specs=[SMEM_SPEC] + vmem_specs(9),
+        in_specs=[SMEM_SPEC] + vmem_specs(8),
         out_specs=vmem_specs(4),
         scratch_shapes=[pltpu.VMEM((NZ, 4, D), F32)],
         compiler_params=pltpu.CompilerParams(vmem_limit_bytes=8 * MIB),
         name="second_sum",
-    )(where, *ra, *rb, token)
+    )(where, *ra, *rb)
 
 
 def last_sum_kernel(own, *refs):
@@ -743,12 +743,12 @@
     gate_grad, up_grad, token = run_up(rows, rows_sib, dl_own, [a_down])
     ra = [a_own, shift(a_down, "x", -1), shift(a_up, "x", 1)]
     rb = [b_own, shift(b_up, "y", 1), shift(b_down, "y", -1)]
-    q = run_first_sum(where, ra, rb, token)
+    down_grad, other = run_down(grads, grads_sib, dl_own, rows_sib)
+    q = run_first_sum(where, ra, rb, token, other)
     qa, qb = q[0:4], q[4:8]
     ra = [qa[0]] + [shift(qa[k], "y", k) for k in (1, 2, 3)]
     rb = [qb[0]] + [shift(qb[k], "x", -k) for k in (1, 2, 3)]
-    down_grad, token = run_down(grads, grads_sib, dl_own, rows_sib)
-    q = run_second_sum(where, ra, rb, token)
+    q = run_second_sum(where, ra, rb)
     input_grad, sums = run_last_sum([q[0]] + [shift(q[k], "z", k) for k in (1, 2, 3)])
     router_grad = run_router(where, sums, swap(sums), slot_tokens)
     return (input_grad, gate_grad, up_grad, down_grad, router_grad)

time: 140 us -> 146 us (1.043)
  waiting for transfers between devices: 41.5 us -> 46.5 us
    ppermute x36, waiting for transfers between devices: 40.7 us -> 43.4 us  [shift(): return lax.ppermute(value, AXES, shift_pairs(axis, step))]
    ppermute x6, waiting for transfers between devices: 0.84 us -> 3.15 us  [swap(): return lax.ppermute(value, AXES, pairs)]
  transfers between devices with their start and end apart: 42 -> 42, of which waited for: 15 -> 17; matrix products, arithmetic and copies ran while one was open for 1% -> 1% of each run, Pallas kernels for 14% -> 13%
where the time goes in v8:
time: 146 us; the launch traced here: 145 us
  starting transfers between devices  58.3 us (40%)
  waiting for transfers between devices  46.5 us (32%)
  Pallas kernels  37.3 us (26%)
  local copies, waits for them, and re-layouts  2.36 us (2%)
    ppermute x36, starting transfers between devices, shift(): return lax.ppermute(value, AXES, shift_pairs(axis, step))  44.1 us
    ppermute x36, waiting for transfers between devices, shift(): return lax.ppermute(value, AXES, shift_pairs(axis, step))  43.4 us
    ppermute x6, starting transfers between devices, swap(): return lax.ppermute(value, AXES, pairs)  14.2 us
    pallas_call x1, Pallas kernels, run_main(): pl.pallas_call(main_kernel, out_shape=out_shape, in_specs=[SMEM_SPEC] + h...  14 us
    pallas_call x1, Pallas kernels, run_early(): pl.pallas_call(early_kernel, out_shape=[jax.ShapeDtypeStruct((192, 1024),...  7.16 us
    pallas_call x1, Pallas kernels, run_up(): pl.pallas_call(up_kernel, grid=(D // (3 * FT),), out_shape=[jax.ShapeDtyp...  5.98 us
    pallas_call x1, Pallas kernels, run_down(): pl.pallas_call(down_kernel, grid=(D // (4 * FT),), out_shape=[jax.ShapeDt...  3.79 us
    ppermute x6, waiting for transfers between devices, swap(): return lax.ppermute(value, AXES, pairs)  3.15 us
  transfers between devices with their start and end apart: 42, of which 17 were waited for; matrix products, arithmetic and copies ran while one was open for 1% of the time, Pallas kernels for 13%

profile of v8, /device:TPU:1, one launch (start us, length us, event | category | flops | bytes accessed | tf_op | source)
XLA Modules:
  0.0 145.3 jit_solution(10611128710494351040)
XLA Ops:
  3.8 3.9 %collective-permute-start.2 = (bf16[128,384]{1,0:T(8,128)(2,1)S(1)}, bf16[128,384]{1,0:T(8,128)(2,1)S(1)}, u32[]{:S(2)}, u32[]{:S(2)}) collective-permute-start(bf16[128,384]{1,0:T(8,128)(2,1)S(1)} %pack.1.refs_0_), channel_id=1, source_target_pairs={{0,3},{1,0},{2,1},{3,2},{4,7},{5,4},{6,5},{7,6},{8,11},{9,8},{10,9... | collective-permute-start | bytes 294920 | tf_op jit(solution)/shard_map/ppermute | solution.py:38
  9.2 2.6 %collective-permute-done.2.refs_3_ = bf16[128,384]{1,0:T(8,128)(2,1)S(1)} collective-permute-done((bf16[128,384]{1,0:T(8,128)(2,1)S(1)}, bf16[128,384]{1,0:T(8,128)(2,1)S(1)}, u32[]{:S(2)}, u32[]{:S(2)}) %collective-permute-start.2) | collective-permute-done | bytes 98336 | tf_op jit(solution)/shard_map/ppermute | solution.py:38
  12.8 2.6 %collective-permute-done.refs_1_ = bf16[128,384]{1,0:T(8,128)(2,1)S(1)} collective-permute-done((bf16[128,384]{1,0:T(8,128)(2,1)S(1)}, bf16[128,384]{1,0:T(8,128)(2,1)S(1)}, u32[]{:S(2)}, u32[]{:S(2)}) %collective-permute-start) | collective-permute-done | bytes 98336 | tf_op jit(solution)/shard_map/ppermute | solution.py:38
  17.3 2.5 %collective-permute-start.8 = (bf16[64,1536]{1,0:T(8,128)(2,1)S(1)}, bf16[64,1536]{1,0:T(8,128)(2,1)S(1)}, u32[]{:S(2)}, u32[]{:S(2)}) collective-permute-start(bf16[64,1536]{1,0:T(8,128)(2,1)S(1)} %get-tuple-element.56.refs_5_), channel_id=1, source_target_pairs={{0,96},{1,97},{2,98},{3,99},{4,100},{5,101},{6,102},{7,103},{8,104... | collective-permute-start | bytes 589832 | tf_op jit(solution)/shard_map/ppermute | solution.py:38
  19.8 2.7 %collective-permute-start.6 = (bf16[16,6144]{1,0:T(8,128)(2,1)S(1)}, bf16[16,6144]{1,0:T(8,128)(2,1)S(1)}, u32[]{:S(2)}, u32[]{:S(2)}) collective-permute-start(bf16[16,6144]{1,0:T(8,128)(2,1)S(1)} %get-tuple-element.55.refs_0_.refs_1_), channel_id=1, source_target_pairs={{0,12},{1,13},{2,14},{3,15},{4,0},{5,1},{6,2},{7,3},{8,4},{9,5},{1... | collective-permute-start | bytes 589832 | tf_op jit(solution)/shard_map/ppermute | solution.py:38
  24.1 3.1 %collective-permute-done.7.g_low.refs_6_ = bf16[64,1536]{1,0:T(8,128)(2,1)S(1)} collective-permute-done((bf16[64,1536]{1,0:T(8,128)(2,1)S(1)}, bf16[64,1536]{1,0:T(8,128)(2,1)S(1)}, u32[]{:S(2)}, u32[]{:S(2)}) %collective-permute-start.7) | collective-permute-done | bytes 196640 | tf_op jit(solution)/shard_map/ppermute | solution.py:38
  27.1 2.4 %collective-permute-done.5.t_low.refs_1_ = bf16[16,6144]{1,0:T(8,128)(2,1)S(1)} collective-permute-done((bf16[16,6144]{1,0:T(8,128)(2,1)S(1)}, bf16[16,6144]{1,0:T(8,128)(2,1)S(1)}, u32[]{:S(2)}, u32[]{:S(2)}) %collective-permute-start.5) | collective-permute-done | bytes 196640 | tf_op jit(solution)/shard_map/ppermute | solution.py:38
  29.7 2.7 %collective-permute-start.10 = (bf16[16,3072]{1,0:T(8,128)(2,1)S(1)}, bf16[16,3072]{1,0:T(8,128)(2,1)S(1)}, u32[]{:S(2)}, u32[]{:S(2)}) collective-permute-start(bf16[16,3072]{1,0:T(8,128)(2,1)S(1)} %get-tuple-element.58), channel_id=1, source_target_pairs={{0,12},{1,13},{2,14},{3,15},{4,0},{5,1},{6,2},{7,3},{8,4},{9,5},{1... | collective-permute-start | bytes 294920 | tf_op jit(solution)/shard_map/ppermute | solution.py:38
  32.3 2.7 %collective-permute-start.12 = (bf16[32,1536]{1,0:T(8,128)(2,1)S(1)}, bf16[32,1536]{1,0:T(8,128)(2,1)S(1)}, u32[]{:S(2)}, u32[]{:S(2)}) collective-permute-start(bf16[32,1536]{1,0:T(8,128)(2,1)S(1)} %get-tuple-element.60), channel_id=1, source_target_pairs={{0,96},{1,97},{2,98},{3,99},{4,100},{5,101},{6,102},{7,103},{8,104... | collective-permute-start | bytes 294920 | tf_op jit(solution)/shard_map/ppermute | solution.py:38
  35.0 2.0 %collective-permute-done.11.refs_8_ = bf16[32,1536]{1,0:T(8,128)(2,1)S(1)} collective-permute-done((bf16[32,1536]{1,0:T(8,128)(2,1)S(1)}, bf16[32,1536]{1,0:T(8,128)(2,1)S(1)}, u32[]{:S(2)}, u32[]{:S(2)}) %collective-permute-start.11) | collective-permute-done | bytes 98336 | tf_op jit(solution)/shard_map/ppermute | solution.py:38
  37.7 2.7 %collective-permute-start.14 = (bf16[64,6144]{1,0:T(8,128)(2,1)S(1)}, bf16[64,6144]{1,0:T(8,128)(2,1)S(1)}, u32[]{:S(2)}, u32[]{:S(2)}) collective-permute-start(bf16[64,6144]{1,0:T(8,128)(2,1)S(1)} %get-tuple-element.61.refs_0_), channel_id=1, source_target_pairs={{0,96},{1,97},{2,98},{3,99},{4,100},{5,101},{6,102},{7,103},{8,104... | collective-permute-start | bytes 2359304 | tf_op jit(solution)/shard_map/ppermute | solution.py:38
  41.9 11.9 %collective-permute-done.14.t_high.refs_2_ = bf16[64,6144]{1,0:T(8,128)(2,1)S(1)} collective-permute-done((bf16[64,6144]{1,0:T(8,128)(2,1)S(1)}, bf16[64,6144]{1,0:T(8,128)(2,1)S(1)}, u32[]{:S(2)}, u32[]{:S(2)}) %collective-permute-start.14) | collective-permute-done | bytes 786464 | tf_op jit(solution)/shard_map/ppermute | solution.py:38
  53.8 3.1 %collective-permute-done.13.t_low.refs_1_ = bf16[64,6144]{1,0:T(8,128)(2,1)S(1)} collective-permute-done((bf16[64,6144]{1,0:T(8,128)(2,1)S(1)}, bf16[64,6144]{1,0:T(8,128)(2,1)S(1)}, u32[]{:S(2)}, u32[]{:S(2)}) %collective-permute-start.13) | collective-permute-done | bytes 786464 | tf_op jit(solution)/shard_map/ppermute | solution.py:38
  57.1 2.7 %collective-permute-start.18 = (bf16[32,6144]{1,0:T(8,128)(2,1)S(1)}, bf16[32,6144]{1,0:T(8,128)(2,1)S(1)}, u32[]{:S(2)}, u32[]{:S(2)}) collective-permute-start(bf16[32,6144]{1,0:T(8,128)(2,1)S(1)} %get-tuple-element.64), channel_id=1, source_target_pairs={{0,96},{1,97},{2,98},{3,99},{4,100},{5,101},{6,102},{7,103},{8,104... | collective-permute-start | bytes 1179656 | tf_op jit(solution)/shard_map/ppermute | solution.py:38
  59.8 2.7 %collective-permute-start.20 = (bf16[128,1536]{1,0:T(8,128)(2,1)S(1)}, bf16[128,1536]{1,0:T(8,128)(2,1)S(1)}, u32[]{:S(2)}, u32[]{:S(2)}) collective-permute-start(bf16[128,1536]{1,0:T(8,128)(2,1)S(1)} %get-tuple-element.66), channel_id=1, source_target_pairs={{0,12},{1,13},{2,14},{3,15},{4,0},{5,1},{6,2},{7,3},{8,4},{9,5},{1... | collective-permute-start | bytes 1179656 | tf_op jit(solution)/shard_map/ppermute | solution.py:38
  62.5 7.2 %early.1 = (f32[192,1024]{1,0:T(8,128)S(1)}, f32[256,512]{1,0:T(8,128)S(1)}) custom-call(s32[7]{0:T(128)S(1)} %stack.20.where, bf16[64,6144]{1,0:T(8,128)(2,1)S(1)} %get-tuple-element.61.refs_0_, bf16[64,6144]{1,0:T(8,128)(2,1)S(1)} %collective-permute-done.13.t_low.refs_1_, bf16[64,6144]{1,0:T(8,128)(2,1)S(1)} %collective-permute-done.14.t_high.refs_2_, ...), custom_call_target="tpu_custom_call" | custom-call | flops 3600000000 | bytes 20000000 | tf_op jit(solution)/shard_map/early/pallas_call | solution.py:302
  69.7 14.0 %main.1 = (bf16[64,3456]{1,0:T(8,128)(2,1)S(1)}, bf16[64,3456]{1,0:T(8,128)(2,1)S(1)}, bf16[64,3456]{1,0:T(8,128)(2,1)S(1)}, bf16[32,3456]{1,0:T(8,128)(2,1)S(1)...) custom-call(s32[7]{0:T(128)S(1)} %stack.20.where, ...), custom_call_target="tpu_custom_call" | custom-call | flops 8000000000 | bytes 30000000 | tf_op jit(solution)/shard_map/main/pallas_call | solution.py:458
  83.7 6.0 %collective-permute-start.30 = (bf16[256,6912]{1,0:T(8,128)(2,1)}, bf16[256,6912]{1,0:T(8,128)(2,1)S(1)}, u32[]{:S(2)}, u32[]{:S(2)}) collective-permute-start(bf16[256,6912]{1,0:T(8,128)(2,1)} %get-tuple-element.83.refs_0_), channel_id=1, source_target_pairs={{0,16},{1,17},{2,18},{3,19},{4,20},{5,21},{6,22},{7,23},{8,24},{9,... | collective-permute-start | bytes 10616840 | tf_op jit(solution)/shard_map/ppermute | solution.py:49
  91.2 2.7 %collective-permute-start.25 = (bf16[2,16,3072]{2,1,0:T(8,128)(2,1)S(1)}, bf16[2,16,3072]{2,1,0:T(8,128)(2,1)S(1)}, u32[]{:S(2)}, u32[]{:S(2)}) collective-permute-start(bf16[2,16,3072]{2,1,0:T(8,128)(2,1)S(1)} %get-tuple-element.77), channel_id=1, source_target_pairs={{0,12},{1,13},{2,14},{3,15},{4,0},{5,1},{6,2},{7,3},{8,4},{9,5},{1... | collective-permute-start | bytes 589832 | tf_op jit(solution)/shard_map/ppermute | solution.py:38
  93.9 4.4 %collective-permute-done.24.refs_6_.refs_3_ = bf16[2,16,3072]{2,1,0:T(8,128)(2,1)S(1)} collective-permute-done((bf16[2,16,3072]{2,1,0:T(8,128)(2,1)S(1)}, bf16[2,16,3072]{2,1,0:T(8,128)(2,1)S(1)}, u32[]{:S(2)}, u32[]{:S(2)}) %collective-permute-start.24) | collective-permute-done | bytes 196640 | tf_op jit(solution)/shard_map/ppermute | solution.py:38
  100.7 2.7 %collective-permute-start.29 = (bf16[4,16,3072]{2,1,0:T(8,128)(2,1)S(1)}, bf16[4,16,3072]{2,1,0:T(8,128)(2,1)S(1)}, u32[]{:S(2)}, u32[]{:S(2)}) collective-permute-start(bf16[4,16,3072]{2,1,0:T(8,128)(2,1)S(1)} %get-tuple-element.82), channel_id=1, source_target_pairs={{0,12},{1,13},{2,14},{3,15},{4,0},{5,1},{6,2},{7,3},{8,4},{9,5},{1... | collective-permute-start | bytes 1179656 | tf_op jit(solution)/shard_map/ppermute | solution.py:38
  103.4 2.3 %collective-permute-done.31.grads_sib = bf16[256,6144]{1,0:T(8,128)(2,1)S(1)} collective-permute-done((bf16[256,6144]{1,0:T(8,128)(2,1)S(1)}, bf16[256,6144]{1,0:T(8,128)(2,1)S(1)}, u32[]{:S(2)}, u32[]{:S(2)}) %collective-permute-start.31) | collective-permute-done | bytes 3145760 | tf_op jit(solution)/shard_map/ppermute | solution.py:49
  105.7 2.2 %collective-permute-start.26 = (bf16[64,3456]{1,0:T(8,128)(2,1)S(1)}, bf16[64,3456]{1,0:T(8,128)(2,1)S(1)}, u32[]{:S(2)}, u32[]{:S(2)}) collective-permute-start(bf16[64,3456]{1,0:T(8,128)(2,1)S(1)} %get-tuple-element.78.refs_4_), channel_id=1, source_target_pairs={{0,96},{1,97},{2,98},{3,99},{4,100},{5,101},{6,102},{7,103},{8,104... | collective-permute-start | bytes 1327112 | tf_op jit(solution)/shard_map/ppermute | solution.py:38
  107.9 3.8 %down_grads.1 = (bf16[2,128,6144]{2,1,0:T(8,128)(2,1)}, f32[8,128]{1,0:T(8,128)S(1)}) custom-call(bf16[256,6144]{1,0:T(8,128)(2,1)S(1)} %get-tuple-element.86.refs_0_.grads_own, bf16[256,6144]{1,0:T(8,128)(2,1)S(1)} %collective-permute-done.31.grads_sib, bf16[256,768]{1,0:T(8,128)(2,1)S(1)} %get-tuple-element.84.refs_2_.own, ...), custom_call_target="tpu_custom_call" | custom-call | flops 1600000000 | bytes 10000000 | tf_op jit(solution)/shard_map/down_grads/pallas_call | solution.py:538
  111.7 6.0 %up_grads.1 = (bf16[2,6144,128]{2,1,0:T(8,128)(2,1)}, bf16[2,6144,128]{2,1,0:T(8,128)(2,1)}, f32[8,128]{1,0:T(8,128)S(1)}) custom-call(bf16[256,6912]{1,0:T(8,128)(2,1)S(1)} %copy-done.6, bf16[256,6912]{1,0:T(8,128)(2,1)S(1)} %collective-permute-done.30.refs_1_.refs_3_.sib, bf16[256,768]{1,0:T(8,128)(2,1)S(1)} %get-tuple-element.84.refs_2_.own, ...), custom_call_target="tpu_custom_call" | custom-call | flops 3200000000 | bytes 13000000 | tf_op jit(solution)/shard_map/up_grads/pallas_call | solution.py:499
  118.7 2.9 %collective-permute-start.35 = (bf16[16,3072]{1,0:T(8,128)(2,1)S(1)}, bf16[16,3072]{1,0:T(8,128)(2,1)S(1)}, u32[]{:S(2)}, u32[]{:S(2)}) collective-permute-start(bf16[16,3072]{1,0:T(8,128)(2,1)S(1)} %get-tuple-element.93), channel_id=1, source_target_pairs={{0,96},{1,97},{2,98},{3,99},{4,100},{5,101},{6,102},{7,103},{8,104... | collective-permute-start | bytes 294920 | tf_op jit(solution)/shard_map/ppermute | solution.py:38
  121.6 3.9 %collective-permute-start.33 = (bf16[16,3456]{1,0:T(8,128)(2,1)S(1)}, bf16[16,3456]{1,0:T(8,128)(2,1)S(1)}, u32[]{:S(2)}, u32[]{:S(2)}) collective-permute-start(bf16[16,3456]{1,0:T(8,128)(2,1)S(1)} %get-tuple-element.90), channel_id=1, source_target_pairs={{0,8},{1,9},{2,10},{3,11},{4,12},{5,13},{6,14},{7,15},{8,0},{9,1},... | collective-permute-start | bytes 331784 | tf_op jit(solution)/shard_map/ppermute | solution.py:38
  126.1 4.6 %collective-permute-done.36.refs_6_ = bf16[16,3072]{1,0:T(8,128)(2,1)S(1)} collective-permute-done((bf16[16,3072]{1,0:T(8,128)(2,1)S(1)}, bf16[16,3072]{1,0:T(8,128)(2,1)S(1)}, u32[]{:S(2)}, u32[]{:S(2)}) %collective-permute-start.36) | collective-permute-done | bytes 98336 | tf_op jit(solution)/shard_map/ppermute | solution.py:38
  132.2 1.8 %collective-permute-start.39 = (bf16[4,6528]{1,0:T(4,128)(2,1)S(1)}, bf16[4,6528]{1,0:T(4,128)(2,1)S(1)}, u32[]{:S(2)}, u32[]{:S(2)}) collective-permute-start(bf16[4,6528]{1,0:T(4,128)(2,1)S(1)} %get-tuple-element.98), channel_id=1, source_target_pairs={{0,2},{1,3},{2,0},{3,1},{4,6},{5,7},{6,4},{7,5},{8,10},{9,11},{10,... | collective-permute-start | bytes 156680 | tf_op jit(solution)/shard_map/ppermute | solution.py:38
  134.9 2.1 %collective-permute-done.38.refs_0_ = bf16[4,6528]{1,0:T(4,128)(2,1)S(1)} collective-permute-done((bf16[4,6528]{1,0:T(4,128)(2,1)S(1)}, bf16[4,6528]{1,0:T(4,128)(2,1)S(1)}, u32[]{:S(2)}, u32[]{:S(2)}) %collective-permute-start.38) | collective-permute-done | bytes 52256 | tf_op jit(solution)/shard_map/ppermute | solution.py:38
  138.2 4.5 %collective-permute-start.41 = (f32[8,128]{1,0:T(8,128)S(1)}, f32[8,128]{1,0:T(8,128)S(1)}, u32[]{:S(2)}, u32[]{:S(2)}) collective-permute-start(f32[8,128]{1,0:T(8,128)S(1)} %get-tuple-element.104.own), channel_id=1, source_target_pairs={{0,16},{1,17},{2,18},{3,19},{4,20},{5,21},{6,22},{7,23},{8,24},{9,... | collective-permute-start | bytes 12296 | tf_op jit(solution)/shard_map/ppermute | solution.py:49
  143.5 1.8 %router.1 = f32[2,256]{1,0:T(2,128)} custom-call(s32[7]{0:T(128)S(1)} %stack.20.where, f32[8,128]{1,0:T(8,128)S(1)} %get-tuple-element.104.own, f32[8,128]{1,0:T(8,128)S(1)} %collective-permute-done.41.other, s32[2,256]{1,0:T(2,128)S(1)} %copy-done.5), custom_call_target="tpu_custom_call" | custom-call | tf_op jit(solution)/shard_map/router/pallas_call | solution.py:699
  (85 shorter events, 21.5 us)
Async XLA Ops:
  0.6 14.9 %collective-permute-start.3 = (bf16[2,6144,128]{2,1,0:T(8,128)(2,1)}, bf16[2,6144,128]{2,1,0:T(8,128)(2,1)S(1)}, u32[]{:S(2)}, u32[]{:S(2)}) collective-permute-start(bf16[2,6144,128]{2,1,0:T(8,128)(2,1)} %refs_10_.1), channel_id=1, source_target_pairs={{0,16},{1,17},{2,18},{3,19},{4,20},{5,21},{6,22},{7,23},{8,24},{9,... | collective-permute-start | bytes 9437192 | tf_op jit(solution)/shard_map/ppermute | solution.py:49
  2.1 13.4 %collective-permute-start.4 = (bf16[2,6144,128]{2,1,0:T(8,128)(2,1)}, bf16[2,6144,128]{2,1,0:T(8,128)(2,1)}, u32[]{:S(2)}, u32[]{:S(2)}) collective-permute-start(bf16[2,6144,128]{2,1,0:T(8,128)(2,1)} %refs_11_.1), channel_id=1, source_target_pairs={{0,16},{1,17},{2,18},{3,19},{4,20},{5,21},{6,22},{7,23},{8,24},{9,... | collective-permute-start | bytes 9437192 | tf_op jit(solution)/shard_map/ppermute | solution.py:49
  3.8 8.0 %collective-permute-start.2 = (bf16[128,384]{1,0:T(8,128)(2,1)S(1)}, bf16[128,384]{1,0:T(8,128)(2,1)S(1)}, u32[]{:S(2)}, u32[]{:S(2)}) collective-permute-start(bf16[128,384]{1,0:T(8,128)(2,1)S(1)} %pack.1.refs_0_), channel_id=1, source_target_pairs={{0,3},{1,0},{2,1},{3,2},{4,7},{5,4},{6,5},{7,6},{8,11},{9,8},{10,9... | collective-permute-start | bytes 294920 | tf_op jit(solution)/shard_map/ppermute | solution.py:38
  7.8 7.7 %collective-permute-start = (bf16[128,384]{1,0:T(8,128)(2,1)S(1)}, bf16[128,384]{1,0:T(8,128)(2,1)S(1)}, u32[]{:S(2)}, u32[]{:S(2)}) collective-permute-start(bf16[128,384]{1,0:T(8,128)(2,1)S(1)} %pack.1.refs_0_), channel_id=1, source_target_pairs={{0,1},{1,2},{2,3},{3,0},{4,5},{5,6},{6,7},{7,4},{8,9},{9,10},{10,1... | collective-permute-start | bytes 294920 | tf_op jit(solution)/shard_map/ppermute | solution.py:38
  16.4 46.0 %collective-permute-start.21 = (bf16[2,128,6144]{2,1,0:T(8,128)(2,1)S(1)}, bf16[2,128,6144]{2,1,0:T(8,128)(2,1)S(1)}, u32[]{:S(2)}, u32[]{:S(2)}) collective-permute-start(bf16[2,128,6144]{2,1,0:T(8,128)(2,1)S(1)} %relay.2), channel_id=1, source_target_pairs={{0,16},{1,17},{2,18},{3,19},{4,20},{5,21},{6,22},{7,23},{8,24},{9,... | collective-permute-start | bytes 9437192 | tf_op jit(solution)/shard_map/ppermute | solution.py:49
  17.3 6.7 %collective-permute-start.8 = (bf16[64,1536]{1,0:T(8,128)(2,1)S(1)}, bf16[64,1536]{1,0:T(8,128)(2,1)S(1)}, u32[]{:S(2)}, u32[]{:S(2)}) collective-permute-start(bf16[64,1536]{1,0:T(8,128)(2,1)S(1)} %get-tuple-element.56.refs_5_), channel_id=1, source_target_pairs={{0,96},{1,97},{2,98},{3,99},{4,100},{5,101},{6,102},{7,103},{8,104... | collective-permute-start | bytes 589832 | tf_op jit(solution)/shard_map/ppermute | solution.py:38
  19.8 7.3 %collective-permute-start.7 = (bf16[64,1536]{1,0:T(8,128)(2,1)S(1)}, bf16[64,1536]{1,0:T(8,128)(2,1)S(1)}, u32[]{:S(2)}, u32[]{:S(2)}) collective-permute-start(bf16[64,1536]{1,0:T(8,128)(2,1)S(1)} %get-tuple-element.56.refs_5_), channel_id=1, source_target_pairs={{0,32},{1,33},{2,34},{3,35},{4,36},{5,37},{6,38},{7,39},{8,40},{9,... | collective-permute-start | bytes 589832 | tf_op jit(solution)/shard_map/ppermute | solution.py:38
  19.8 7.3 %collective-permute-start.6 = (bf16[16,6144]{1,0:T(8,128)(2,1)S(1)}, bf16[16,6144]{1,0:T(8,128)(2,1)S(1)}, u32[]{:S(2)}, u32[]{:S(2)}) collective-permute-start(bf16[16,6144]{1,0:T(8,128)(2,1)S(1)} %get-tuple-element.55.refs_0_.refs_1_), channel_id=1, source_target_pairs={{0,12},{1,13},{2,14},{3,15},{4,0},{5,1},{6,2},{7,3},{8,4},{9,5},{1... | collective-permute-start | bytes 589832 | tf_op jit(solution)/shard_map/ppermute | solution.py:38
  22.5 7.0 %collective-permute-start.5 = (bf16[16,6144]{1,0:T(8,128)(2,1)S(1)}, bf16[16,6144]{1,0:T(8,128)(2,1)S(1)}, u32[]{:S(2)}, u32[]{:S(2)}) collective-permute-start(bf16[16,6144]{1,0:T(8,128)(2,1)S(1)} %get-tuple-element.55.refs_0_.refs_1_), channel_id=1, source_target_pairs={{0,4},{1,5},{2,6},{3,7},{4,8},{5,9},{6,10},{7,11},{8,12},{9,13},{1... | collective-permute-start | bytes 589832 | tf_op jit(solution)/shard_map/ppermute | solution.py:38
  37.7 16.1 %collective-permute-start.14 = (bf16[64,6144]{1,0:T(8,128)(2,1)S(1)}, bf16[64,6144]{1,0:T(8,128)(2,1)S(1)}, u32[]{:S(2)}, u32[]{:S(2)}) collective-permute-start(bf16[64,6144]{1,0:T(8,128)(2,1)S(1)} %get-tuple-element.61.refs_0_), channel_id=1, source_target_pairs={{0,96},{1,97},{2,98},{3,99},{4,100},{5,101},{6,102},{7,103},{8,104... | collective-permute-start | bytes 2359304 | tf_op jit(solution)/shard_map/ppermute | solution.py:38
  40.4 16.5 %collective-permute-start.13 = (bf16[64,6144]{1,0:T(8,128)(2,1)S(1)}, bf16[64,6144]{1,0:T(8,128)(2,1)S(1)}, u32[]{:S(2)}, u32[]{:S(2)}) collective-permute-start(bf16[64,6144]{1,0:T(8,128)(2,1)S(1)} %get-tuple-element.61.refs_0_), channel_id=1, source_target_pairs={{0,32},{1,33},{2,34},{3,35},{4,36},{5,37},{6,38},{7,39},{8,40},{9,... | collective-permute-start | bytes 2359304 | tf_op jit(solution)/shard_map/ppermute | solution.py:38
  40.4 16.5 %collective-permute-start.16 = (bf16[256,1536]{1,0:T(8,128)(2,1)S(1)}, bf16[256,1536]{1,0:T(8,128)(2,1)S(1)}, u32[]{:S(2)}, u32[]{:S(2)}) collective-permute-start(bf16[256,1536]{1,0:T(8,128)(2,1)S(1)} %get-tuple-element.62.refs_3_.refs_5_), channel_id=1, source_target_pairs={{0,12},{1,13},{2,14},{3,15},{4,0},{5,1},{6,2},{7,3},{8,4},{9,5},{1... | collective-permute-start | bytes 2359304 | tf_op jit(solution)/shard_map/ppermute | solution.py:38
  40.4 16.5 %collective-permute-start.15 = (bf16[256,1536]{1,0:T(8,128)(2,1)S(1)}, bf16[256,1536]{1,0:T(8,128)(2,1)S(1)}, u32[]{:S(2)}, u32[]{:S(2)}) collective-permute-start(bf16[256,1536]{1,0:T(8,128)(2,1)S(1)} %get-tuple-element.62.refs_3_.refs_5_), channel_id=1, source_target_pairs={{0,4},{1,5},{2,6},{3,7},{4,8},{5,9},{6,10},{7,11},{8,12},{9,13},{1... | collective-permute-start | bytes 2359304 | tf_op jit(solution)/shard_map/ppermute | solution.py:38
  57.0 12.6 %collective-permute-start.17 = (bf16[32,6144]{1,0:T(8,128)(2,1)S(1)}, bf16[32,6144]{1,0:T(8,128)(2,1)S(1)}, u32[]{:S(2)}, u32[]{:S(2)}) collective-permute-start(bf16[32,6144]{1,0:T(8,128)(2,1)S(1)} %get-tuple-element.63), channel_id=1, source_target_pairs={{0,32},{1,33},{2,34},{3,35},{4,36},{5,37},{6,38},{7,39},{8,40},{9,... | collective-permute-start | bytes 1179656 | tf_op jit(solution)/shard_map/ppermute | solution.py:38
  57.1 12.5 %collective-permute-start.18 = (bf16[32,6144]{1,0:T(8,128)(2,1)S(1)}, bf16[32,6144]{1,0:T(8,128)(2,1)S(1)}, u32[]{:S(2)}, u32[]{:S(2)}) collective-permute-start(bf16[32,6144]{1,0:T(8,128)(2,1)S(1)} %get-tuple-element.64), channel_id=1, source_target_pairs={{0,96},{1,97},{2,98},{3,99},{4,100},{5,101},{6,102},{7,103},{8,104... | collective-permute-start | bytes 1179656 | tf_op jit(solution)/shard_map/ppermute | solution.py:38
  59.8 9.9 %collective-permute-start.19 = (bf16[128,1536]{1,0:T(8,128)(2,1)S(1)}, bf16[128,1536]{1,0:T(8,128)(2,1)S(1)}, u32[]{:S(2)}, u32[]{:S(2)}) collective-permute-start(bf16[128,1536]{1,0:T(8,128)(2,1)S(1)} %get-tuple-element.65), channel_id=1, source_target_pairs={{0,4},{1,5},{2,6},{3,7},{4,8},{5,9},{6,10},{7,11},{8,12},{9,13},{1... | collective-permute-start | bytes 1179656 | tf_op jit(solution)/shard_map/ppermute | solution.py:38
  59.8 9.9 %collective-permute-start.20 = (bf16[128,1536]{1,0:T(8,128)(2,1)S(1)}, bf16[128,1536]{1,0:T(8,128)(2,1)S(1)}, u32[]{:S(2)}, u32[]{:S(2)}) collective-permute-start(bf16[128,1536]{1,0:T(8,128)(2,1)S(1)} %get-tuple-element.66), channel_id=1, source_target_pairs={{0,12},{1,13},{2,14},{3,15},{4,0},{5,1},{6,2},{7,3},{8,4},{9,5},{1... | collective-permute-start | bytes 1179656 | tf_op jit(solution)/shard_map/ppermute | solution.py:38
  83.7 24.2 %collective-permute-start.30 = (bf16[256,6912]{1,0:T(8,128)(2,1)}, bf16[256,6912]{1,0:T(8,128)(2,1)S(1)}, u32[]{:S(2)}, u32[]{:S(2)}) collective-permute-start(bf16[256,6912]{1,0:T(8,128)(2,1)} %get-tuple-element.83.refs_0_), channel_id=1, source_target_pairs={{0,16},{1,17},{2,18},{3,19},{4,20},{5,21},{6,22},{7,23},{8,24},{9,... | collective-permute-start | bytes 10616840 | tf_op jit(solution)/shard_map/ppermute | solution.py:49
  89.7 8.5 %collective-permute-start.22 = (bf16[32,3456]{1,0:T(8,128)(2,1)S(1)}, bf16[32,3456]{1,0:T(8,128)(2,1)S(1)}, u32[]{:S(2)}, u32[]{:S(2)}) collective-permute-start(bf16[32,3456]{1,0:T(8,128)(2,1)S(1)} %get-tuple-element.74), channel_id=1, source_target_pairs={{0,96},{1,97},{2,98},{3,99},{4,100},{5,101},{6,102},{7,103},{8,104... | collective-permute-start | bytes 663560 | tf_op jit(solution)/shard_map/ppermute | solution.py:38
  91.1 7.9 %collective-permute-start.23 = (bf16[32,3456]{1,0:T(8,128)(2,1)S(1)}, bf16[32,3456]{1,0:T(8,128)(2,1)S(1)}, u32[]{:S(2)}, u32[]{:S(2)}) collective-permute-start(bf16[32,3456]{1,0:T(8,128)(2,1)S(1)} %get-tuple-element.75), channel_id=1, source_target_pairs={{0,32},{1,33},{2,34},{3,35},{4,36},{5,37},{6,38},{7,39},{8,40},{9,... | collective-permute-start | bytes 663560 | tf_op jit(solution)/shard_map/ppermute | solution.py:38
  91.2 7.0 %collective-permute-start.24 = (bf16[2,16,3072]{2,1,0:T(8,128)(2,1)S(1)}, bf16[2,16,3072]{2,1,0:T(8,128)(2,1)S(1)}, u32[]{:S(2)}, u32[]{:S(2)}) collective-permute-start(bf16[2,16,3072]{2,1,0:T(8,128)(2,1)S(1)} %get-tuple-element.76), channel_id=1, source_target_pairs={{0,4},{1,5},{2,6},{3,7},{4,8},{5,9},{6,10},{7,11},{8,12},{9,13},{1... | collective-permute-start | bytes 589832 | tf_op jit(solution)/shard_map/ppermute | solution.py:38
  91.2 7.0 %collective-permute-start.25 = (bf16[2,16,3072]{2,1,0:T(8,128)(2,1)S(1)}, bf16[2,16,3072]{2,1,0:T(8,128)(2,1)S(1)}, u32[]{:S(2)}, u32[]{:S(2)}) collective-permute-start(bf16[2,16,3072]{2,1,0:T(8,128)(2,1)S(1)} %get-tuple-element.77), channel_id=1, source_target_pairs={{0,12},{1,13},{2,14},{3,15},{4,0},{5,1},{6,2},{7,3},{8,4},{9,5},{1... | collective-permute-start | bytes 589832 | tf_op jit(solution)/shard_map/ppermute | solution.py:38
  99.2 6.5 %collective-permute-start.31 = (bf16[256,6144]{1,0:T(8,128)(2,1)S(1)}, bf16[256,6144]{1,0:T(8,128)(2,1)S(1)}, u32[]{:S(2)}, u32[]{:S(2)}) collective-permute-start(bf16[256,6144]{1,0:T(8,128)(2,1)S(1)} %relay.3), channel_id=1, source_target_pairs={{0,16},{1,17},{2,18},{3,19},{4,20},{5,21},{6,22},{7,23},{8,24},{9,... | collective-permute-start | bytes 9437192 | tf_op jit(solution)/shard_map/ppermute | solution.py:49
  100.7 17.0 %collective-permute-start.28 = (bf16[4,16,3072]{2,1,0:T(8,128)(2,1)S(1)}, bf16[4,16,3072]{2,1,0:T(8,128)(2,1)S(1)}, u32[]{:S(2)}, u32[]{:S(2)}) collective-permute-start(bf16[4,16,3072]{2,1,0:T(8,128)(2,1)S(1)} %get-tuple-element.81), channel_id=1, source_target_pairs={{0,4},{1,5},{2,6},{3,7},{4,8},{5,9},{6,10},{7,11},{8,12},{9,13},{1... | collective-permute-start | bytes 1179656 | tf_op jit(solution)/shard_map/ppermute | solution.py:38
  100.7 16.9 %collective-permute-start.29 = (bf16[4,16,3072]{2,1,0:T(8,128)(2,1)S(1)}, bf16[4,16,3072]{2,1,0:T(8,128)(2,1)S(1)}, u32[]{:S(2)}, u32[]{:S(2)}) collective-permute-start(bf16[4,16,3072]{2,1,0:T(8,128)(2,1)S(1)} %get-tuple-element.82), channel_id=1, source_target_pairs={{0,12},{1,13},{2,14},{3,15},{4,0},{5,1},{6,2},{7,3},{8,4},{9,5},{1... | collective-permute-start | bytes 1179656 | tf_op jit(solution)/shard_map/ppermute | solution.py:38
  103.4 14.3 %collective-permute-start.27 = (bf16[64,3456]{1,0:T(8,128)(2,1)S(1)}, bf16[64,3456]{1,0:T(8,128)(2,1)S(1)}, u32[]{:S(2)}, u32[]{:S(2)}) collective-permute-start(bf16[64,3456]{1,0:T(8,128)(2,1)S(1)} %get-tuple-element.79), channel_id=1, source_target_pairs={{0,32},{1,33},{2,34},{3,35},{4,36},{5,37},{6,38},{7,39},{8,40},{9,... | collective-permute-start | bytes 1327112 | tf_op jit(solution)/shard_map/ppermute | solution.py:38
  105.7 12.0 %collective-permute-start.26 = (bf16[64,3456]{1,0:T(8,128)(2,1)S(1)}, bf16[64,3456]{1,0:T(8,128)(2,1)S(1)}, u32[]{:S(2)}, u32[]{:S(2)}) collective-permute-start(bf16[64,3456]{1,0:T(8,128)(2,1)S(1)} %get-tuple-element.78.refs_4_), channel_id=1, source_target_pairs={{0,96},{1,97},{2,98},{3,99},{4,100},{5,101},{6,102},{7,103},{8,104... | collective-permute-start | bytes 1327112 | tf_op jit(solution)/shard_map/ppermute | solution.py:38
  118.7 6.7 %collective-permute-start.35 = (bf16[16,3072]{1,0:T(8,128)(2,1)S(1)}, bf16[16,3072]{1,0:T(8,128)(2,1)S(1)}, u32[]{:S(2)}, u32[]{:S(2)}) collective-permute-start(bf16[16,3072]{1,0:T(8,128)(2,1)S(1)} %get-tuple-element.93), channel_id=1, source_target_pairs={{0,96},{1,97},{2,98},{3,99},{4,100},{5,101},{6,102},{7,103},{8,104... | collective-permute-start | bytes 294920 | tf_op jit(solution)/shard_map/ppermute | solution.py:38
  121.6 9.8 %collective-permute-start.32 = (bf16[16,3456]{1,0:T(8,128)(2,1)S(1)}, bf16[16,3456]{1,0:T(8,128)(2,1)S(1)}, u32[]{:S(2)}, u32[]{:S(2)}) collective-permute-start(bf16[16,3456]{1,0:T(8,128)(2,1)S(1)} %get-tuple-element.89), channel_id=1, source_target_pairs={{0,4},{1,5},{2,6},{3,7},{4,8},{5,9},{6,10},{7,11},{8,12},{9,13},{1... | collective-permute-start | bytes 331784 | tf_op jit(solution)/shard_map/ppermute | solution.py:38
  121.6 9.8 %collective-permute-start.33 = (bf16[16,3456]{1,0:T(8,128)(2,1)S(1)}, bf16[16,3456]{1,0:T(8,128)(2,1)S(1)}, u32[]{:S(2)}, u32[]{:S(2)}) collective-permute-start(bf16[16,3456]{1,0:T(8,128)(2,1)S(1)} %get-tuple-element.90), channel_id=1, source_target_pairs={{0,8},{1,9},{2,10},{3,11},{4,12},{5,13},{6,14},{7,15},{8,0},{9,1},... | collective-permute-start | bytes 331784 | tf_op jit(solution)/shard_map/ppermute | solution.py:38
  125.4 6.0 %collective-permute-start.34 = (bf16[16,3456]{1,0:T(8,128)(2,1)S(1)}, bf16[16,3456]{1,0:T(8,128)(2,1)S(1)}, u32[]{:S(2)}, u32[]{:S(2)}) collective-permute-start(bf16[16,3456]{1,0:T(8,128)(2,1)S(1)} %get-tuple-element.91), channel_id=1, source_target_pairs={{0,12},{1,13},{2,14},{3,15},{4,0},{5,1},{6,2},{7,3},{8,4},{9,5},{1... | collective-permute-start | bytes 331784 | tf_op jit(solution)/shard_map/ppermute | solution.py:38
  125.4 6.0 %collective-permute-start.37 = (bf16[16,3072]{1,0:T(8,128)(2,1)S(1)}, bf16[16,3072]{1,0:T(8,128)(2,1)S(1)}, u32[]{:S(2)}, u32[]{:S(2)}) collective-permute-start(bf16[16,3072]{1,0:T(8,128)(2,1)S(1)} %get-tuple-element.95), channel_id=1, source_target_pairs={{0,32},{1,33},{2,34},{3,35},{4,36},{5,37},{6,38},{7,39},{8,40},{9,... | collective-permute-start | bytes 294920 | tf_op jit(solution)/shard_map/ppermute | solution.py:38
  (18 other events, 173.4 us)

commit v9 on v7

--- a/solution.py
+++ b/solution.py
@@ -72,6 +72,7 @@
 
 KT = 1024
 FT = 512
+WT = 1024
 MIB = 2**20
 WIDE = D // 2 + 384
 
@@ -419,24 +420,24 @@
         out[0:16, D // 2 :] = sums
 
     def partial(i):
-        f = pl.ds(pl.multiple_of(i * FT, FT), FT)
+        f = pl.ds(pl.multiple_of(i * WT, WT), WT)
         wide = jnp.concatenate(
             [wv[s, n, e, f, :] for s in range(2) for e in range(2) for n in range(2)], axis=1
         )
         return nt(deltas[...], wide)
 
-    half = D // 2 // FT
+    half = D // 2 // WT
 
     @pl.loop(0, half)
     def _(i):
-        f = pl.ds(pl.multiple_of(i * FT, FT), FT)
+        f = pl.ds(pl.multiple_of(i * WT, WT), WT)
         part = partial(i).astype(BF)
         for out, at in zip(pa_out, (0, 64, 192, 128, 160)):
             out[:, f] = part[at : at + out.shape[0], :]
 
     @pl.loop(0, half)
     def _(i):
-        f = pl.ds(pl.multiple_of(i * FT, FT), FT)
+        f = pl.ds(pl.multiple_of(i * WT, WT), WT)
         tile[...] = partial(i + half).astype(BF)
         for out, k, first in zip(pb_out, (0, 1, 3, 2, 2), (0, 0, 0, 0, 2)):
             for b in range(out.shape[0]):
@@ -466,14 +467,14 @@
             pltpu.VMEM((HALF, 1024), F32),
             pltpu.VMEM((HALF, 512), F32),
             pltpu.VMEM((HALF, 1024), BF),
-            pltpu.VMEM((HALF, FT), BF),
+            pltpu.VMEM((HALF, WT), BF),
             pltpu.VMEM((HALF, 128), F32),
             pltpu.SemaphoreType.DMA((5,)),
             pltpu.SemaphoreType.DMA((5,)),
             pltpu.SemaphoreType.DMA((D // KT, 4)),
             pltpu.SemaphoreType.DMA((2,)),
         ],
-        compiler_params=pltpu.CompilerParams(vmem_limit_bytes=21 * MIB),
+        compiler_params=pltpu.CompilerParams(vmem_limit_bytes=24 * MIB),
         cost_estimate=pl.CostEstimate(
             flops=8_000_000_000, bytes_accessed=30_000_000, transcendentals=262144
         ),

time: 140 us -> 139 us (level)
  no operation moved by 1% of the time
where the time goes in v9:
time: 139 us
  starting transfers between devices  57.8 us (42%)
  waiting for transfers between devices  41.5 us (30%)
  Pallas kernels  36.4 us (26%)
  local copies, waits for them, and re-layouts  2.36 us (2%)
    ppermute x36, starting transfers between devices, shift(): return lax.ppermute(value, AXES, shift_pairs(axis, step))  43.5 us
    ppermute x36, waiting for transfers between devices, shift(): return lax.ppermute(value, AXES, shift_pairs(axis, step))  40.7 us
    ppermute x6, starting transfers between devices, swap(): return lax.ppermute(value, AXES, pairs)  14.3 us
    pallas_call x1, Pallas kernels, run_main(): pl.pallas_call(main_kernel, out_shape=out_shape, in_specs=[SMEM_SPEC] + h...  12.8 us
    pallas_call x1, Pallas kernels, run_early(): pl.pallas_call(early_kernel, out_shape=[jax.ShapeDtypeStruct((192, 1024),...  7.56 us
    pallas_call x1, Pallas kernels, run_up(): pl.pallas_call(up_kernel, grid=(D // (3 * FT),), out_shape=[jax.ShapeDtyp...  5.98 us
    pallas_call x1, Pallas kernels, run_down(): pl.pallas_call(down_kernel, grid=(D // (4 * FT),), out_shape=[jax.ShapeDt...  3.79 us
  transfers between devices with their start and end apart: 42, of which 15 were waited for; matrix products, arithmetic and copies ran while one was open for 1% of the time, Pallas kernels for 14%

profile of v9, /device:TPU:1, one launch (start us, length us, event | category | flops | bytes accessed | tf_op | source)
XLA Modules:
  0.0 139.1 jit_solution(9980840310189423589)
XLA Ops:
  0.6 1.5 %collective-permute-start.3 = (bf16[2,6144,128]{2,1,0:T(8,128)(2,1)}, bf16[2,6144,128]{2,1,0:T(8,128)(2,1)S(1)}, u32[]{:S(2)}, u32[]{:S(2)}) collective-permute-start(bf16[2,6144,128]{2,1,0:T(8,128)(2,1)} %refs_10_.1), channel_id=1, source_target_pairs={{0,16},{1,17},{2,18},{3,19},{4,20},{5,21},{6,22},{7,23},{8,24},{9,... | collective-permute-start | bytes 9437192 | tf_op jit(solution)/shard_map/ppermute | solution.py:49
  3.8 3.9 %collective-permute-start.2 = (bf16[128,384]{1,0:T(8,128)(2,1)S(1)}, bf16[128,384]{1,0:T(8,128)(2,1)S(1)}, u32[]{:S(2)}, u32[]{:S(2)}) collective-permute-start(bf16[128,384]{1,0:T(8,128)(2,1)S(1)} %pack.1.refs_0_), channel_id=1, source_target_pairs={{0,3},{1,0},{2,1},{3,2},{4,7},{5,4},{6,5},{7,6},{8,11},{9,8},{10,9... | collective-permute-start | bytes 294920 | tf_op jit(solution)/shard_map/ppermute | solution.py:38
  9.2 2.6 %collective-permute-done.2.refs_3_ = bf16[128,384]{1,0:T(8,128)(2,1)S(1)} collective-permute-done((bf16[128,384]{1,0:T(8,128)(2,1)S(1)}, bf16[128,384]{1,0:T(8,128)(2,1)S(1)}, u32[]{:S(2)}, u32[]{:S(2)}) %collective-permute-start.2) | collective-permute-done | bytes 98336 | tf_op jit(solution)/shard_map/ppermute | solution.py:38
  12.8 2.6 %collective-permute-done.refs_1_ = bf16[128,384]{1,0:T(8,128)(2,1)S(1)} collective-permute-done((bf16[128,384]{1,0:T(8,128)(2,1)S(1)}, bf16[128,384]{1,0:T(8,128)(2,1)S(1)}, u32[]{:S(2)}, u32[]{:S(2)}) %collective-permute-start) | collective-permute-done | bytes 98336 | tf_op jit(solution)/shard_map/ppermute | solution.py:38
  17.3 2.5 %collective-permute-start.8 = (bf16[64,1536]{1,0:T(8,128)(2,1)S(1)}, bf16[64,1536]{1,0:T(8,128)(2,1)S(1)}, u32[]{:S(2)}, u32[]{:S(2)}) collective-permute-start(bf16[64,1536]{1,0:T(8,128)(2,1)S(1)} %get-tuple-element.56.refs_5_), channel_id=1, source_target_pairs={{0,96},{1,97},{2,98},{3,99},{4,100},{5,101},{6,102},{7,103},{8,104... | collective-permute-start | bytes 589832 | tf_op jit(solution)/shard_map/ppermute | solution.py:38
  19.8 2.7 %collective-permute-start.6 = (bf16[16,6144]{1,0:T(8,128)(2,1)S(1)}, bf16[16,6144]{1,0:T(8,128)(2,1)S(1)}, u32[]{:S(2)}, u32[]{:S(2)}) collective-permute-start(bf16[16,6144]{1,0:T(8,128)(2,1)S(1)} %get-tuple-element.55.refs_0_.refs_1_), channel_id=1, source_target_pairs={{0,12},{1,13},{2,14},{3,15},{4,0},{5,1},{6,2},{7,3},{8,4},{9,5},{1... | collective-permute-start | bytes 589832 | tf_op jit(solution)/shard_map/ppermute | solution.py:38
  22.5 1.5 %collective-permute-done.8.g_high.refs_7_ = bf16[64,1536]{1,0:T(8,128)(2,1)S(1)} collective-permute-done((bf16[64,1536]{1,0:T(8,128)(2,1)S(1)}, bf16[64,1536]{1,0:T(8,128)(2,1)S(1)}, u32[]{:S(2)}, u32[]{:S(2)}) %collective-permute-start.8) | collective-permute-done | bytes 196640 | tf_op jit(solution)/shard_map/ppermute | solution.py:38
  24.1 3.1 %collective-permute-done.7.g_low.refs_6_ = bf16[64,1536]{1,0:T(8,128)(2,1)S(1)} collective-permute-done((bf16[64,1536]{1,0:T(8,128)(2,1)S(1)}, bf16[64,1536]{1,0:T(8,128)(2,1)S(1)}, u32[]{:S(2)}, u32[]{:S(2)}) %collective-permute-start.7) | collective-permute-done | bytes 196640 | tf_op jit(solution)/shard_map/ppermute | solution.py:38
  27.1 2.4 %collective-permute-done.5.t_low.refs_1_ = bf16[16,6144]{1,0:T(8,128)(2,1)S(1)} collective-permute-done((bf16[16,6144]{1,0:T(8,128)(2,1)S(1)}, bf16[16,6144]{1,0:T(8,128)(2,1)S(1)}, u32[]{:S(2)}, u32[]{:S(2)}) %collective-permute-start.5) | collective-permute-done | bytes 196640 | tf_op jit(solution)/shard_map/ppermute | solution.py:38
  29.7 2.7 %collective-permute-start.10 = (bf16[16,3072]{1,0:T(8,128)(2,1)S(1)}, bf16[16,3072]{1,0:T(8,128)(2,1)S(1)}, u32[]{:S(2)}, u32[]{:S(2)}) collective-permute-start(bf16[16,3072]{1,0:T(8,128)(2,1)S(1)} %get-tuple-element.58), channel_id=1, source_target_pairs={{0,12},{1,13},{2,14},{3,15},{4,0},{5,1},{6,2},{7,3},{8,4},{9,5},{1... | collective-permute-start | bytes 294920 | tf_op jit(solution)/shard_map/ppermute | solution.py:38
  32.3 2.7 %collective-permute-start.12 = (bf16[32,1536]{1,0:T(8,128)(2,1)S(1)}, bf16[32,1536]{1,0:T(8,128)(2,1)S(1)}, u32[]{:S(2)}, u32[]{:S(2)}) collective-permute-start(bf16[32,1536]{1,0:T(8,128)(2,1)S(1)} %get-tuple-element.60), channel_id=1, source_target_pairs={{0,96},{1,97},{2,98},{3,99},{4,100},{5,101},{6,102},{7,103},{8,104... | collective-permute-start | bytes 294920 | tf_op jit(solution)/shard_map/ppermute | solution.py:38
  35.0 2.0 %collective-permute-done.11.refs_8_ = bf16[32,1536]{1,0:T(8,128)(2,1)S(1)} collective-permute-done((bf16[32,1536]{1,0:T(8,128)(2,1)S(1)}, bf16[32,1536]{1,0:T(8,128)(2,1)S(1)}, u32[]{:S(2)}, u32[]{:S(2)}) %collective-permute-start.11) | collective-permute-done | bytes 98336 | tf_op jit(solution)/shard_map/ppermute | solution.py:38
  37.7 2.7 %collective-permute-start.14 = (bf16[64,6144]{1,0:T(8,128)(2,1)S(1)}, bf16[64,6144]{1,0:T(8,128)(2,1)S(1)}, u32[]{:S(2)}, u32[]{:S(2)}) collective-permute-start(bf16[64,6144]{1,0:T(8,128)(2,1)S(1)} %get-tuple-element.61.refs_0_), channel_id=1, source_target_pairs={{0,96},{1,97},{2,98},{3,99},{4,100},{5,101},{6,102},{7,103},{8,104... | collective-permute-start | bytes 2359304 | tf_op jit(solution)/shard_map/ppermute | solution.py:38
  41.9 11.9 %collective-permute-done.14.t_high.refs_2_ = bf16[64,6144]{1,0:T(8,128)(2,1)S(1)} collective-permute-done((bf16[64,6144]{1,0:T(8,128)(2,1)S(1)}, bf16[64,6144]{1,0:T(8,128)(2,1)S(1)}, u32[]{:S(2)}, u32[]{:S(2)}) %collective-permute-start.14) | collective-permute-done | bytes 786464 | tf_op jit(solution)/shard_map/ppermute | solution.py:38
  53.8 3.1 %collective-permute-done.13.t_low.refs_1_ = bf16[64,6144]{1,0:T(8,128)(2,1)S(1)} collective-permute-done((bf16[64,6144]{1,0:T(8,128)(2,1)S(1)}, bf16[64,6144]{1,0:T(8,128)(2,1)S(1)}, u32[]{:S(2)}, u32[]{:S(2)}) %collective-permute-start.13) | collective-permute-done | bytes 786464 | tf_op jit(solution)/shard_map/ppermute | solution.py:38
  57.1 2.7 %collective-permute-start.18 = (bf16[32,6144]{1,0:T(8,128)(2,1)S(1)}, bf16[32,6144]{1,0:T(8,128)(2,1)S(1)}, u32[]{:S(2)}, u32[]{:S(2)}) collective-permute-start(bf16[32,6144]{1,0:T(8,128)(2,1)S(1)} %get-tuple-element.64), channel_id=1, source_target_pairs={{0,96},{1,97},{2,98},{3,99},{4,100},{5,101},{6,102},{7,103},{8,104... | collective-permute-start | bytes 1179656 | tf_op jit(solution)/shard_map/ppermute | solution.py:38
  59.8 2.7 %collective-permute-start.20 = (bf16[128,1536]{1,0:T(8,128)(2,1)S(1)}, bf16[128,1536]{1,0:T(8,128)(2,1)S(1)}, u32[]{:S(2)}, u32[]{:S(2)}) collective-permute-start(bf16[128,1536]{1,0:T(8,128)(2,1)S(1)} %get-tuple-element.66), channel_id=1, source_target_pairs={{0,12},{1,13},{2,14},{3,15},{4,0},{5,1},{6,2},{7,3},{8,4},{9,5},{1... | collective-permute-start | bytes 1179656 | tf_op jit(solution)/shard_map/ppermute | solution.py:38
  62.5 7.6 %early.1 = (f32[192,1024]{1,0:T(8,128)S(1)}, f32[256,512]{1,0:T(8,128)S(1)}) custom-call(s32[7]{0:T(128)S(1)} %stack.20.where, bf16[64,6144]{1,0:T(8,128)(2,1)S(1)} %get-tuple-element.61.refs_0_, bf16[64,6144]{1,0:T(8,128)(2,1)S(1)} %collective-permute-done.13.t_low.refs_1_, bf16[64,6144]{1,0:T(8,128)(2,1)S(1)} %collective-permute-done.14.t_high.refs_2_, ...), custom_call_target="tpu_custom_call" | custom-call | flops 3600000000 | bytes 20000000 | tf_op jit(solution)/shard_map/early/pallas_call | solution.py:303
  70.1 12.8 %main.1 = (bf16[64,3456]{1,0:T(8,128)(2,1)S(1)}, bf16[64,3456]{1,0:T(8,128)(2,1)S(1)}, bf16[64,3456]{1,0:T(8,128)(2,1)S(1)}, bf16[32,3456]{1,0:T(8,128)(2,1)S(1)...) custom-call(s32[7]{0:T(128)S(1)} %stack.20.where, ...), custom_call_target="tpu_custom_call" | custom-call | flops 8000000000 | bytes 30000000 | tf_op jit(solution)/shard_map/main/pallas_call | solution.py:459
  82.9 6.0 %collective-permute-start.30 = (bf16[256,6912]{1,0:T(8,128)(2,1)}, bf16[256,6912]{1,0:T(8,128)(2,1)S(1)}, u32[]{:S(2)}, u32[]{:S(2)}) collective-permute-start(bf16[256,6912]{1,0:T(8,128)(2,1)} %get-tuple-element.83.refs_0_), channel_id=1, source_target_pairs={{0,16},{1,17},{2,18},{3,19},{4,20},{5,21},{6,22},{7,23},{8,24},{9,... | collective-permute-start | bytes 10616840 | tf_op jit(solution)/shard_map/ppermute | solution.py:49
  90.4 2.7 %collective-permute-start.25 = (bf16[2,16,3072]{2,1,0:T(8,128)(2,1)S(1)}, bf16[2,16,3072]{2,1,0:T(8,128)(2,1)S(1)}, u32[]{:S(2)}, u32[]{:S(2)}) collective-permute-start(bf16[2,16,3072]{2,1,0:T(8,128)(2,1)S(1)} %get-tuple-element.77), channel_id=1, source_target_pairs={{0,12},{1,13},{2,14},{3,15},{4,0},{5,1},{6,2},{7,3},{8,4},{9,5},{1... | collective-permute-start | bytes 589832 | tf_op jit(solution)/shard_map/ppermute | solution.py:38
  93.1 4.4 %collective-permute-done.24.refs_6_.refs_3_ = bf16[2,16,3072]{2,1,0:T(8,128)(2,1)S(1)} collective-permute-done((bf16[2,16,3072]{2,1,0:T(8,128)(2,1)S(1)}, bf16[2,16,3072]{2,1,0:T(8,128)(2,1)S(1)}, u32[]{:S(2)}, u32[]{:S(2)}) %collective-permute-start.24) | collective-permute-done | bytes 196640 | tf_op jit(solution)/shard_map/ppermute | solution.py:38
  99.9 2.7 %collective-permute-start.26 = (bf16[64,3456]{1,0:T(8,128)(2,1)S(1)}, bf16[64,3456]{1,0:T(8,128)(2,1)S(1)}, u32[]{:S(2)}, u32[]{:S(2)}) collective-permute-start(bf16[64,3456]{1,0:T(8,128)(2,1)S(1)} %get-tuple-element.78.refs_4_), channel_id=1, source_target_pairs={{0,96},{1,97},{2,98},{3,99},{4,100},{5,101},{6,102},{7,103},{8,104... | collective-permute-start | bytes 1327112 | tf_op jit(solution)/shard_map/ppermute | solution.py:38
  102.6 2.7 %collective-permute-start.29 = (bf16[4,16,3072]{2,1,0:T(8,128)(2,1)S(1)}, bf16[4,16,3072]{2,1,0:T(8,128)(2,1)S(1)}, u32[]{:S(2)}, u32[]{:S(2)}) collective-permute-start(bf16[4,16,3072]{2,1,0:T(8,128)(2,1)S(1)} %get-tuple-element.82), channel_id=1, source_target_pairs={{0,12},{1,13},{2,14},{3,15},{4,0},{5,1},{6,2},{7,3},{8,4},{9,5},{1... | collective-permute-start | bytes 1179656 | tf_op jit(solution)/shard_map/ppermute | solution.py:38
  105.3 6.0 %up_grads.1 = (bf16[2,6144,128]{2,1,0:T(8,128)(2,1)}, bf16[2,6144,128]{2,1,0:T(8,128)(2,1)}, f32[8,128]{1,0:T(8,128)S(1)}) custom-call(bf16[256,6912]{1,0:T(8,128)(2,1)S(1)} %copy-done.7, bf16[256,6912]{1,0:T(8,128)(2,1)S(1)} %collective-permute-done.30.refs_1_.refs_3_.sib, bf16[256,768]{1,0:T(8,128)(2,1)S(1)} %get-tuple-element.84.refs_2_.own, ...), custom_call_target="tpu_custom_call" | custom-call | flops 3200000000 | bytes 13000000 | tf_op jit(solution)/shard_map/up_grads/pallas_call | solution.py:500
  111.2 2.6 %collective-permute-done.28.refs_4_ = bf16[4,16,3072]{2,1,0:T(8,128)(2,1)S(1)} collective-permute-done((bf16[4,16,3072]{2,1,0:T(8,128)(2,1)S(1)}, bf16[4,16,3072]{2,1,0:T(8,128)(2,1)S(1)}, u32[]{:S(2)}, u32[]{:S(2)}) %collective-permute-start.28) | collective-permute-done | bytes 393248 | tf_op jit(solution)/shard_map/ppermute | solution.py:38
  117.7 2.8 %collective-permute-start.32 = (bf16[16,3456]{1,0:T(8,128)(2,1)S(1)}, bf16[16,3456]{1,0:T(8,128)(2,1)S(1)}, u32[]{:S(2)}, u32[]{:S(2)}) collective-permute-start(bf16[16,3456]{1,0:T(8,128)(2,1)S(1)} %get-tuple-element.88), channel_id=1, source_target_pairs={{0,8},{1,9},{2,10},{3,11},{4,12},{5,13},{6,14},{7,15},{8,0},{9,1},... | collective-permute-start | bytes 331784 | tf_op jit(solution)/shard_map/ppermute | solution.py:38
  121.2 3.8 %down_grads.1 = (bf16[2,128,6144]{2,1,0:T(8,128)(2,1)}, f32[8,128]{1,0:T(8,128)S(1)}) custom-call(bf16[256,6144]{1,0:T(8,128)(2,1)S(1)} %get-tuple-element.94.refs_0_.grads_own, bf16[256,6144]{1,0:T(8,128)(2,1)S(1)} %collective-permute-done.37.grads_sib, bf16[256,768]{1,0:T(8,128)(2,1)S(1)} %get-tuple-element.84.refs_2_.own, ...), custom_call_target="tpu_custom_call" | custom-call | flops 1600000000 | bytes 10000000 | tf_op jit(solution)/shard_map/down_grads/pallas_call | solution.py:539
  125.9 1.8 %collective-permute-start.39 = (bf16[4,6528]{1,0:T(4,128)(2,1)S(1)}, bf16[4,6528]{1,0:T(4,128)(2,1)S(1)}, u32[]{:S(2)}, u32[]{:S(2)}) collective-permute-start(bf16[4,6528]{1,0:T(4,128)(2,1)S(1)} %get-tuple-element.98), channel_id=1, source_target_pairs={{0,2},{1,3},{2,0},{3,1},{4,6},{5,7},{6,4},{7,5},{8,10},{9,11},{10,... | collective-permute-start | bytes 156680 | tf_op jit(solution)/shard_map/ppermute | solution.py:38
  128.6 2.1 %collective-permute-done.38.refs_0_ = bf16[4,6528]{1,0:T(4,128)(2,1)S(1)} collective-permute-done((bf16[4,6528]{1,0:T(4,128)(2,1)S(1)}, bf16[4,6528]{1,0:T(4,128)(2,1)S(1)}, u32[]{:S(2)}, u32[]{:S(2)}) %collective-permute-start.38) | collective-permute-done | bytes 52256 | tf_op jit(solution)/shard_map/ppermute | solution.py:38
  131.9 4.6 %collective-permute-start.41 = (f32[8,128]{1,0:T(8,128)S(1)}, f32[8,128]{1,0:T(8,128)S(1)}, u32[]{:S(2)}, u32[]{:S(2)}) collective-permute-start(f32[8,128]{1,0:T(8,128)S(1)} %get-tuple-element.104.own), channel_id=1, source_target_pairs={{0,16},{1,17},{2,18},{3,19},{4,20},{5,21},{6,22},{7,23},{8,24},{9,... | collective-permute-start | bytes 12296 | tf_op jit(solution)/shard_map/ppermute | solution.py:49
  137.2 1.8 %router.1 = f32[2,256]{1,0:T(2,128)} custom-call(s32[7]{0:T(128)S(1)} %stack.20.where, f32[8,128]{1,0:T(8,128)S(1)} %get-tuple-element.104.own, f32[8,128]{1,0:T(8,128)S(1)} %collective-permute-done.41.other, s32[2,256]{1,0:T(2,128)S(1)} %copy-done.6), custom_call_target="tpu_custom_call" | custom-call | tf_op jit(solution)/shard_map/router/pallas_call | solution.py:700
  (87 shorter events, 20.6 us)
Async XLA Ops:
  0.6 14.9 %collective-permute-start.3 = (bf16[2,6144,128]{2,1,0:T(8,128)(2,1)}, bf16[2,6144,128]{2,1,0:T(8,128)(2,1)S(1)}, u32[]{:S(2)}, u32[]{:S(2)}) collective-permute-start(bf16[2,6144,128]{2,1,0:T(8,128)(2,1)} %refs_10_.1), channel_id=1, source_target_pairs={{0,16},{1,17},{2,18},{3,19},{4,20},{5,21},{6,22},{7,23},{8,24},{9,... | collective-permute-start | bytes 9437192 | tf_op jit(solution)/shard_map/ppermute | solution.py:49
  2.1 13.4 %collective-permute-start.4 = (bf16[2,6144,128]{2,1,0:T(8,128)(2,1)}, bf16[2,6144,128]{2,1,0:T(8,128)(2,1)}, u32[]{:S(2)}, u32[]{:S(2)}) collective-permute-start(bf16[2,6144,128]{2,1,0:T(8,128)(2,1)} %refs_11_.1), channel_id=1, source_target_pairs={{0,16},{1,17},{2,18},{3,19},{4,20},{5,21},{6,22},{7,23},{8,24},{9,... | collective-permute-start | bytes 9437192 | tf_op jit(solution)/shard_map/ppermute | solution.py:49
  3.8 8.0 %collective-permute-start.2 = (bf16[128,384]{1,0:T(8,128)(2,1)S(1)}, bf16[128,384]{1,0:T(8,128)(2,1)S(1)}, u32[]{:S(2)}, u32[]{:S(2)}) collective-permute-start(bf16[128,384]{1,0:T(8,128)(2,1)S(1)} %pack.1.refs_0_), channel_id=1, source_target_pairs={{0,3},{1,0},{2,1},{3,2},{4,7},{5,4},{6,5},{7,6},{8,11},{9,8},{10,9... | collective-permute-start | bytes 294920 | tf_op jit(solution)/shard_map/ppermute | solution.py:38
  7.8 7.7 %collective-permute-start = (bf16[128,384]{1,0:T(8,128)(2,1)S(1)}, bf16[128,384]{1,0:T(8,128)(2,1)S(1)}, u32[]{:S(2)}, u32[]{:S(2)}) collective-permute-start(bf16[128,384]{1,0:T(8,128)(2,1)S(1)} %pack.1.refs_0_), channel_id=1, source_target_pairs={{0,1},{1,2},{2,3},{3,0},{4,5},{5,6},{6,7},{7,4},{8,9},{9,10},{10,1... | collective-permute-start | bytes 294920 | tf_op jit(solution)/shard_map/ppermute | solution.py:38
  16.4 46.0 %collective-permute-start.21 = (bf16[2,128,6144]{2,1,0:T(8,128)(2,1)S(1)}, bf16[2,128,6144]{2,1,0:T(8,128)(2,1)S(1)}, u32[]{:S(2)}, u32[]{:S(2)}) collective-permute-start(bf16[2,128,6144]{2,1,0:T(8,128)(2,1)S(1)} %relay.2), channel_id=1, source_target_pairs={{0,16},{1,17},{2,18},{3,19},{4,20},{5,21},{6,22},{7,23},{8,24},{9,... | collective-permute-start | bytes 9437192 | tf_op jit(solution)/shard_map/ppermute | solution.py:49
  17.3 6.7 %collective-permute-start.8 = (bf16[64,1536]{1,0:T(8,128)(2,1)S(1)}, bf16[64,1536]{1,0:T(8,128)(2,1)S(1)}, u32[]{:S(2)}, u32[]{:S(2)}) collective-permute-start(bf16[64,1536]{1,0:T(8,128)(2,1)S(1)} %get-tuple-element.56.refs_5_), channel_id=1, source_target_pairs={{0,96},{1,97},{2,98},{3,99},{4,100},{5,101},{6,102},{7,103},{8,104... | collective-permute-start | bytes 589832 | tf_op jit(solution)/shard_map/ppermute | solution.py:38
  19.8 7.3 %collective-permute-start.7 = (bf16[64,1536]{1,0:T(8,128)(2,1)S(1)}, bf16[64,1536]{1,0:T(8,128)(2,1)S(1)}, u32[]{:S(2)}, u32[]{:S(2)}) collective-permute-start(bf16[64,1536]{1,0:T(8,128)(2,1)S(1)} %get-tuple-element.56.refs_5_), channel_id=1, source_target_pairs={{0,32},{1,33},{2,34},{3,35},{4,36},{5,37},{6,38},{7,39},{8,40},{9,... | collective-permute-start | bytes 589832 | tf_op jit(solution)/shard_map/ppermute | solution.py:38
  19.8 7.3 %collective-permute-start.6 = (bf16[16,6144]{1,0:T(8,128)(2,1)S(1)}, bf16[16,6144]{1,0:T(8,128)(2,1)S(1)}, u32[]{:S(2)}, u32[]{:S(2)}) collective-permute-start(bf16[16,6144]{1,0:T(8,128)(2,1)S(1)} %get-tuple-element.55.refs_0_.refs_1_), channel_id=1, source_target_pairs={{0,12},{1,13},{2,14},{3,15},{4,0},{5,1},{6,2},{7,3},{8,4},{9,5},{1... | collective-permute-start | bytes 589832 | tf_op jit(solution)/shard_map/ppermute | solution.py:38
  22.5 7.0 %collective-permute-start.5 = (bf16[16,6144]{1,0:T(8,128)(2,1)S(1)}, bf16[16,6144]{1,0:T(8,128)(2,1)S(1)}, u32[]{:S(2)}, u32[]{:S(2)}) collective-permute-start(bf16[16,6144]{1,0:T(8,128)(2,1)S(1)} %get-tuple-element.55.refs_0_.refs_1_), channel_id=1, source_target_pairs={{0,4},{1,5},{2,6},{3,7},{4,8},{5,9},{6,10},{7,11},{8,12},{9,13},{1... | collective-permute-start | bytes 589832 | tf_op jit(solution)/shard_map/ppermute | solution.py:38
  37.7 16.1 %collective-permute-start.14 = (bf16[64,6144]{1,0:T(8,128)(2,1)S(1)}, bf16[64,6144]{1,0:T(8,128)(2,1)S(1)}, u32[]{:S(2)}, u32[]{:S(2)}) collective-permute-start(bf16[64,6144]{1,0:T(8,128)(2,1)S(1)} %get-tuple-element.61.refs_0_), channel_id=1, source_target_pairs={{0,96},{1,97},{2,98},{3,99},{4,100},{5,101},{6,102},{7,103},{8,104... | collective-permute-start | bytes 2359304 | tf_op jit(solution)/shard_map/ppermute | solution.py:38
  40.4 16.5 %collective-permute-start.13 = (bf16[64,6144]{1,0:T(8,128)(2,1)S(1)}, bf16[64,6144]{1,0:T(8,128)(2,1)S(1)}, u32[]{:S(2)}, u32[]{:S(2)}) collective-permute-start(bf16[64,6144]{1,0:T(8,128)(2,1)S(1)} %get-tuple-element.61.refs_0_), channel_id=1, source_target_pairs={{0,32},{1,33},{2,34},{3,35},{4,36},{5,37},{6,38},{7,39},{8,40},{9,... | collective-permute-start | bytes 2359304 | tf_op jit(solution)/shard_map/ppermute | solution.py:38
  40.4 16.5 %collective-permute-start.16 = (bf16[256,1536]{1,0:T(8,128)(2,1)S(1)}, bf16[256,1536]{1,0:T(8,128)(2,1)S(1)}, u32[]{:S(2)}, u32[]{:S(2)}) collective-permute-start(bf16[256,1536]{1,0:T(8,128)(2,1)S(1)} %get-tuple-element.62.refs_3_.refs_5_), channel_id=1, source_target_pairs={{0,12},{1,13},{2,14},{3,15},{4,0},{5,1},{6,2},{7,3},{8,4},{9,5},{1... | collective-permute-start | bytes 2359304 | tf_op jit(solution)/shard_map/ppermute | solution.py:38
  40.4 16.5 %collective-permute-start.15 = (bf16[256,1536]{1,0:T(8,128)(2,1)S(1)}, bf16[256,1536]{1,0:T(8,128)(2,1)S(1)}, u32[]{:S(2)}, u32[]{:S(2)}) collective-permute-start(bf16[256,1536]{1,0:T(8,128)(2,1)S(1)} %get-tuple-element.62.refs_3_.refs_5_), channel_id=1, source_target_pairs={{0,4},{1,5},{2,6},{3,7},{4,8},{5,9},{6,10},{7,11},{8,12},{9,13},{1... | collective-permute-start | bytes 2359304 | tf_op jit(solution)/shard_map/ppermute | solution.py:38
  57.0 13.0 %collective-permute-start.17 = (bf16[32,6144]{1,0:T(8,128)(2,1)S(1)}, bf16[32,6144]{1,0:T(8,128)(2,1)S(1)}, u32[]{:S(2)}, u32[]{:S(2)}) collective-permute-start(bf16[32,6144]{1,0:T(8,128)(2,1)S(1)} %get-tuple-element.63), channel_id=1, source_target_pairs={{0,32},{1,33},{2,34},{3,35},{4,36},{5,37},{6,38},{7,39},{8,40},{9,... | collective-permute-start | bytes 1179656 | tf_op jit(solution)/shard_map/ppermute | solution.py:38
  57.1 13.0 %collective-permute-start.18 = (bf16[32,6144]{1,0:T(8,128)(2,1)S(1)}, bf16[32,6144]{1,0:T(8,128)(2,1)S(1)}, u32[]{:S(2)}, u32[]{:S(2)}) collective-permute-start(bf16[32,6144]{1,0:T(8,128)(2,1)S(1)} %get-tuple-element.64), channel_id=1, source_target_pairs={{0,96},{1,97},{2,98},{3,99},{4,100},{5,101},{6,102},{7,103},{8,104... | collective-permute-start | bytes 1179656 | tf_op jit(solution)/shard_map/ppermute | solution.py:38
  59.8 10.3 %collective-permute-start.19 = (bf16[128,1536]{1,0:T(8,128)(2,1)S(1)}, bf16[128,1536]{1,0:T(8,128)(2,1)S(1)}, u32[]{:S(2)}, u32[]{:S(2)}) collective-permute-start(bf16[128,1536]{1,0:T(8,128)(2,1)S(1)} %get-tuple-element.65), channel_id=1, source_target_pairs={{0,4},{1,5},{2,6},{3,7},{4,8},{5,9},{6,10},{7,11},{8,12},{9,13},{1... | collective-permute-start | bytes 1179656 | tf_op jit(solution)/shard_map/ppermute | solution.py:38
  59.8 10.3 %collective-permute-start.20 = (bf16[128,1536]{1,0:T(8,128)(2,1)S(1)}, bf16[128,1536]{1,0:T(8,128)(2,1)S(1)}, u32[]{:S(2)}, u32[]{:S(2)}) collective-permute-start(bf16[128,1536]{1,0:T(8,128)(2,1)S(1)} %get-tuple-element.66), channel_id=1, source_target_pairs={{0,12},{1,13},{2,14},{3,15},{4,0},{5,1},{6,2},{7,3},{8,4},{9,5},{1... | collective-permute-start | bytes 1179656 | tf_op jit(solution)/shard_map/ppermute | solution.py:38
  82.9 19.7 %collective-permute-start.30 = (bf16[256,6912]{1,0:T(8,128)(2,1)}, bf16[256,6912]{1,0:T(8,128)(2,1)S(1)}, u32[]{:S(2)}, u32[]{:S(2)}) collective-permute-start(bf16[256,6912]{1,0:T(8,128)(2,1)} %get-tuple-element.83.refs_0_), channel_id=1, source_target_pairs={{0,16},{1,17},{2,18},{3,19},{4,20},{5,21},{6,22},{7,23},{8,24},{9,... | collective-permute-start | bytes 10616840 | tf_op jit(solution)/shard_map/ppermute | solution.py:49
  88.9 8.5 %collective-permute-start.22 = (bf16[32,3456]{1,0:T(8,128)(2,1)S(1)}, bf16[32,3456]{1,0:T(8,128)(2,1)S(1)}, u32[]{:S(2)}, u32[]{:S(2)}) collective-permute-start(bf16[32,3456]{1,0:T(8,128)(2,1)S(1)} %get-tuple-element.74), channel_id=1, source_target_pairs={{0,96},{1,97},{2,98},{3,99},{4,100},{5,101},{6,102},{7,103},{8,104... | collective-permute-start | bytes 663560 | tf_op jit(solution)/shard_map/ppermute | solution.py:38
  90.2 7.9 %collective-permute-start.23 = (bf16[32,3456]{1,0:T(8,128)(2,1)S(1)}, bf16[32,3456]{1,0:T(8,128)(2,1)S(1)}, u32[]{:S(2)}, u32[]{:S(2)}) collective-permute-start(bf16[32,3456]{1,0:T(8,128)(2,1)S(1)} %get-tuple-element.75), channel_id=1, source_target_pairs={{0,32},{1,33},{2,34},{3,35},{4,36},{5,37},{6,38},{7,39},{8,40},{9,... | collective-permute-start | bytes 663560 | tf_op jit(solution)/shard_map/ppermute | solution.py:38
  90.4 7.0 %collective-permute-start.24 = (bf16[2,16,3072]{2,1,0:T(8,128)(2,1)S(1)}, bf16[2,16,3072]{2,1,0:T(8,128)(2,1)S(1)}, u32[]{:S(2)}, u32[]{:S(2)}) collective-permute-start(bf16[2,16,3072]{2,1,0:T(8,128)(2,1)S(1)} %get-tuple-element.76), channel_id=1, source_target_pairs={{0,4},{1,5},{2,6},{3,7},{4,8},{5,9},{6,10},{7,11},{8,12},{9,13},{1... | collective-permute-start | bytes 589832 | tf_op jit(solution)/shard_map/ppermute | solution.py:38
  90.4 7.0 %collective-permute-start.25 = (bf16[2,16,3072]{2,1,0:T(8,128)(2,1)S(1)}, bf16[2,16,3072]{2,1,0:T(8,128)(2,1)S(1)}, u32[]{:S(2)}, u32[]{:S(2)}) collective-permute-start(bf16[2,16,3072]{2,1,0:T(8,128)(2,1)S(1)} %get-tuple-element.77), channel_id=1, source_target_pairs={{0,12},{1,13},{2,14},{3,15},{4,0},{5,1},{6,2},{7,3},{8,4},{9,5},{1... | collective-permute-start | bytes 589832 | tf_op jit(solution)/shard_map/ppermute | solution.py:38
  98.4 19.4 %collective-permute-start.37 = (bf16[256,6144]{1,0:T(8,128)(2,1)S(1)}, bf16[256,6144]{1,0:T(8,128)(2,1)S(1)}, u32[]{:S(2)}, u32[]{:S(2)}) collective-permute-start(bf16[256,6144]{1,0:T(8,128)(2,1)S(1)} %relay.3), channel_id=1, source_target_pairs={{0,16},{1,17},{2,18},{3,19},{4,20},{5,21},{6,22},{7,23},{8,24},{9,... | collective-permute-start | bytes 9437192 | tf_op jit(solution)/shard_map/ppermute | solution.py:49
  99.8 14.1 %collective-permute-start.27 = (bf16[64,3456]{1,0:T(8,128)(2,1)S(1)}, bf16[64,3456]{1,0:T(8,128)(2,1)S(1)}, u32[]{:S(2)}, u32[]{:S(2)}) collective-permute-start(bf16[64,3456]{1,0:T(8,128)(2,1)S(1)} %get-tuple-element.79), channel_id=1, source_target_pairs={{0,32},{1,33},{2,34},{3,35},{4,36},{5,37},{6,38},{7,39},{8,40},{9,... | collective-permute-start | bytes 1327112 | tf_op jit(solution)/shard_map/ppermute | solution.py:38
  99.9 14.0 %collective-permute-start.26 = (bf16[64,3456]{1,0:T(8,128)(2,1)S(1)}, bf16[64,3456]{1,0:T(8,128)(2,1)S(1)}, u32[]{:S(2)}, u32[]{:S(2)}) collective-permute-start(bf16[64,3456]{1,0:T(8,128)(2,1)S(1)} %get-tuple-element.78.refs_4_), channel_id=1, source_target_pairs={{0,96},{1,97},{2,98},{3,99},{4,100},{5,101},{6,102},{7,103},{8,104... | collective-permute-start | bytes 1327112 | tf_op jit(solution)/shard_map/ppermute | solution.py:38
  102.6 11.3 %collective-permute-start.28 = (bf16[4,16,3072]{2,1,0:T(8,128)(2,1)S(1)}, bf16[4,16,3072]{2,1,0:T(8,128)(2,1)S(1)}, u32[]{:S(2)}, u32[]{:S(2)}) collective-permute-start(bf16[4,16,3072]{2,1,0:T(8,128)(2,1)S(1)} %get-tuple-element.81), channel_id=1, source_target_pairs={{0,4},{1,5},{2,6},{3,7},{4,8},{5,9},{6,10},{7,11},{8,12},{9,13},{1... | collective-permute-start | bytes 1179656 | tf_op jit(solution)/shard_map/ppermute | solution.py:38
  102.6 11.3 %collective-permute-start.29 = (bf16[4,16,3072]{2,1,0:T(8,128)(2,1)S(1)}, bf16[4,16,3072]{2,1,0:T(8,128)(2,1)S(1)}, u32[]{:S(2)}, u32[]{:S(2)}) collective-permute-start(bf16[4,16,3072]{2,1,0:T(8,128)(2,1)S(1)} %get-tuple-element.82), channel_id=1, source_target_pairs={{0,12},{1,13},{2,14},{3,15},{4,0},{5,1},{6,2},{7,3},{8,4},{9,5},{1... | collective-permute-start | bytes 1179656 | tf_op jit(solution)/shard_map/ppermute | solution.py:38
  114.9 5.6 %collective-permute-start.34 = (bf16[16,3072]{1,0:T(8,128)(2,1)S(1)}, bf16[16,3072]{1,0:T(8,128)(2,1)S(1)}, u32[]{:S(2)}, u32[]{:S(2)}) collective-permute-start(bf16[16,3072]{1,0:T(8,128)(2,1)S(1)} %get-tuple-element.91), channel_id=1, source_target_pairs={{0,96},{1,97},{2,98},{3,99},{4,100},{5,101},{6,102},{7,103},{8,104... | collective-permute-start | bytes 294920 | tf_op jit(solution)/shard_map/ppermute | solution.py:38
  116.3 8.7 %collective-permute-start.35 = (bf16[16,3072]{1,0:T(8,128)(2,1)S(1)}, bf16[16,3072]{1,0:T(8,128)(2,1)S(1)}, u32[]{:S(2)}, u32[]{:S(2)}) collective-permute-start(bf16[16,3072]{1,0:T(8,128)(2,1)S(1)} %get-tuple-element.92), channel_id=1, source_target_pairs={{0,64},{1,65},{2,66},{3,67},{4,68},{5,69},{6,70},{7,71},{8,72},{9,... | collective-permute-start | bytes 294920 | tf_op jit(solution)/shard_map/ppermute | solution.py:38
  116.4 8.7 %collective-permute-start.36 = (bf16[16,3072]{1,0:T(8,128)(2,1)S(1)}, bf16[16,3072]{1,0:T(8,128)(2,1)S(1)}, u32[]{:S(2)}, u32[]{:S(2)}) collective-permute-start(bf16[16,3072]{1,0:T(8,128)(2,1)S(1)} %get-tuple-element.93), channel_id=1, source_target_pairs={{0,32},{1,33},{2,34},{3,35},{4,36},{5,37},{6,38},{7,39},{8,40},{9,... | collective-permute-start | bytes 294920 | tf_op jit(solution)/shard_map/ppermute | solution.py:38
  117.0 8.0 %collective-permute-start.31 = (bf16[16,3456]{1,0:T(8,128)(2,1)S(1)}, bf16[16,3456]{1,0:T(8,128)(2,1)S(1)}, u32[]{:S(2)}, u32[]{:S(2)}) collective-permute-start(bf16[16,3456]{1,0:T(8,128)(2,1)S(1)} %get-tuple-element.87), channel_id=1, source_target_pairs={{0,4},{1,5},{2,6},{3,7},{4,8},{5,9},{6,10},{7,11},{8,12},{9,13},{1... | collective-permute-start | bytes 331784 | tf_op jit(solution)/shard_map/ppermute | solution.py:38
  117.7 7.3 %collective-permute-start.32 = (bf16[16,3456]{1,0:T(8,128)(2,1)S(1)}, bf16[16,3456]{1,0:T(8,128)(2,1)S(1)}, u32[]{:S(2)}, u32[]{:S(2)}) collective-permute-start(bf16[16,3456]{1,0:T(8,128)(2,1)S(1)} %get-tuple-element.88), channel_id=1, source_target_pairs={{0,8},{1,9},{2,10},{3,11},{4,12},{5,13},{6,14},{7,15},{8,0},{9,1},... | collective-permute-start | bytes 331784 | tf_op jit(solution)/shard_map/ppermute | solution.py:38
  (19 other events, 184.5 us)
